TPU v7x, 32 devices: a whole 2x2x4 slice. The times are simulated.
32 devices in a mesh: fsdp: 4 (over x, core), ctx: 8 (over z, y).
Axes of the slice: x: 2, y: 2, z: 4, core: 2. Of those that a mesh axis runs over, the one named last changes fastest.
Arguments:
- history: bfloat16 [9, 4, 2048, 2048], P(None, 'fsdp', 'ctx'), may hold values from -6 to 6
- dense_mix: float32 [4, 9, 4, 2048], P(None, None, 'fsdp', 'ctx'), may hold values from -2.5 to 2.5
- doc_starts: int32 [4, 8], P('fsdp'), may hold values from 0 to 2048, as said below
- norm_gain: float32 [4, 2048], P(None, ('fsdp', 'ctx')), may hold values from 0.25 to 1.75
- norm_bias: float32 [4, 2048], P(None, ('fsdp', 'ctx')), may hold values from -1.25 to 1.25
- query_key_value_weight: bfloat16 [2048, 3, 2048], P(('fsdp', 'ctx')), may hold values from -0.125 to 0.125
- query_key_value_bias: float32 [3, 2048], P(None, ('fsdp', 'ctx')), may hold values from -1.75 to 1.75
- out_weight: bfloat16 [2048, 2048], P(('fsdp', 'ctx')), may hold values from -0.5 to 0.5
- out_bias: float32 [2048], P(('fsdp', 'ctx')), may hold values from -1.75 to 1.75
- up_weight: bfloat16 [2048, 8192], P(('fsdp', 'ctx')), may hold values from -0.125 to 0.125
- up_bias: float32 [8192], P(('fsdp', 'ctx')), may hold values from -1.75 to 1.75
- down_weight: bfloat16 [8192, 2048], P(('fsdp', 'ctx')), may hold values from -0.0625 to 0.0625
- down_bias: float32 [2048], P(('fsdp', 'ctx')), may hold values from -1.75 to 1.75
- root_gain: float32 [2048], P(('fsdp', 'ctx')), may hold values from 0.25 to 1.75
- mix_in_weight: float32 [2048, 40], P(('fsdp', 'ctx')), may hold values from -0.125 to 0.125
- mix_out_weight: float32 [40, 40], replicated, may hold values from -1 to 1
- mix_out_bias: float32 [40], replicated, may hold values from -3 to 3
- out_cotangent: bfloat16 [4, 2048, 2048], P('fsdp', 'ctx'), may hold values from -6 to 6
- mix_cotangent: float32 [40, 4, 2048], P(None, 'fsdp', 'ctx'), may hold values from -6 to 6
Outputs:
- block_out: bfloat16 [4, 2048, 2048], P('fsdp', 'ctx')
- next_mix: float32 [40, 4, 2048], P(None, 'fsdp', 'ctx')
- grad_history: float32 [9, 4, 2048, 2048], P(None, 'fsdp', 'ctx')
- grad_mix: float32 [4, 9, 4, 2048], P(None, None, 'fsdp', 'ctx')
- grad_norm_gain: float32 [4, 2048], P(None, ('fsdp', 'ctx'))
- grad_norm_bias: float32 [4, 2048], P(None, ('fsdp', 'ctx'))
- grad_qkv_weight: float32 [2048, 3, 2048], P(('fsdp', 'ctx'))
- grad_qkv_bias: float32 [3, 2048], P(None, ('fsdp', 'ctx'))
- grad_out_weight: float32 [2048, 2048], P(('fsdp', 'ctx'))
- grad_out_bias: float32 [2048], P(('fsdp', 'ctx'))
- grad_up_weight: float32 [2048, 8192], P(('fsdp', 'ctx'))
- grad_up_bias: float32 [8192], P(('fsdp', 'ctx'))
- grad_down_weight: float32 [8192, 2048], P(('fsdp', 'ctx'))
- grad_down_bias: float32 [2048], P(('fsdp', 'ctx'))
- grad_root_gain: float32 [2048], P(('fsdp', 'ctx'))
- grad_mix_in_weight: float32 [2048, 40], P(('fsdp', 'ctx'))
- grad_mix_out_weight: float32 [40, 40], replicated
- grad_mix_out_bias: float32 [40], replicated
Inputs may be any that keep to these rules, and one draw needn't show every extreme that they name: doc_starts[g, 0] = 0 and each row never falls; sequence g's documents begin at its distinct entries below 2048; entries equal to 2048 begin none. Of the one consecutive sequence (those of one index of fsdp) one, drawn from the seed, is a single document.
All inputs are finite; a program needn't handle non-finite values.
Results may differ from a plain program's by a relative error of at most 0.013.
Values may be sent and summed in bfloat16 or wider, within the bound.
A program may use at most 576 MiB of HBM per device.

v0:
```python
import math

import jax
import jax.numpy as jnp
from jax import lax
from jax.sharding import PartitionSpec as P

HEAD_DIM = 128
ROT = 32


TOP_PRECISION = lax.Precision.HIGHEST
EPS_NORM = 1e-05
EPS_ROOT = 1e-06
NEG_BIG = -1e30


def layer_norm(values, gain_row, shift_row):
    centre = values - jnp.mean(values, axis=-1, keepdims=True)
    spread = jnp.mean(centre * centre, axis=-1, keepdims=True)
    return centre * lax.rsqrt(spread + EPS_NORM) * gain_row + shift_row


def precise_gelu_curve(values):
    return jax.nn.gelu(values, approximate=False)


def rotary(values, positions, turning):
    half_rot = ROT // 2
    frequency = jnp.exp(jnp.arange(half_rot, dtype=jnp.float32) * (-2.0 * math.log(10000.0) / ROT))
    angles = positions[:, None] * frequency[None, :]
    cosine = jnp.cos(angles)[:, None, :]
    sine_part = turning * jnp.sin(angles)[:, None, :]
    front_part = values[..., :half_rot]
    back_part = values[..., half_rot:ROT]
    return jnp.concatenate(
        [
            front_part * cosine - back_part * sine_part,
            back_part * cosine + front_part * sine_part,
            values[..., ROT:],
        ],
        axis=-1,
    )


def mixer(out_rows, gain_row, opening_layer, closing_layer, closing_bias):
    inverse_rms = lax.rsqrt(jnp.mean(out_rows * out_rows, axis=-1, keepdims=True) + EPS_ROOT)
    square_rooted = out_rows * inverse_rms * gain_row
    hidden_units = jnp.einsum("evw,wr->evr", square_rooted, opening_layer, precision=TOP_PRECISION)
    return (
        jnp.einsum(
            "hjn,nr->hjr", precise_gelu_curve(hidden_units), closing_layer, precision=TOP_PRECISION
        )
        + closing_bias
    )


def matrix_product(pattern, left_side, right_side):
    return jnp.einsum(pattern, left_side, right_side, preferred_element_type=jnp.float32)


def body(
    history,
    dense_mix,
    doc_starts,
    norm_gain,
    norm_bias,
    query_key_value_weight,
    query_key_value_bias,
    out_weight,
    out_bias,
    up_weight,
    up_bias,
    down_weight,
    down_bias,
    root_gain,
    mix_in_weight,
    mix_out_weight,
    mix_out_bias,
    out_cotangent,
    mix_cotangent,
):
    small_set = (
        lax.all_gather(norm_gain, ("fsdp", "ctx"), axis=1, tiled=True),
        lax.all_gather(norm_bias, ("fsdp", "ctx"), axis=1, tiled=True),
        lax.all_gather(query_key_value_bias, ("fsdp", "ctx"), axis=1, tiled=True),
        lax.all_gather(out_bias, ("fsdp", "ctx"), axis=0, tiled=True),
        lax.all_gather(up_bias, ("fsdp", "ctx"), axis=0, tiled=True),
        lax.all_gather(down_bias, ("fsdp", "ctx"), axis=0, tiled=True),
        lax.all_gather(root_gain, ("fsdp", "ctx"), axis=0, tiled=True),
        lax.all_gather(mix_in_weight, ("fsdp", "ctx"), axis=0, tiled=True),
    )
    (
        gain_all,
        shift_all,
        query_key_value_offset,
        out_shift,
        up_shift,
        down_shift,
        root_full,
        mix_in_full,
    ) = small_set
    query_key_value_whole, out_full, up_full, down_full = (
        lax.all_gather(query_key_value_weight, ("fsdp", "ctx"), axis=0, tiled=True),
        lax.all_gather(out_weight, ("fsdp", "ctx"), axis=0, tiled=True),
        lax.all_gather(up_weight, ("fsdp", "ctx"), axis=0, tiled=True),
        lax.all_gather(down_weight, ("fsdp", "ctx"), axis=0, tiled=True),
    )
    seq_count, local_len, model_width = out_cotangent.shape
    head_count = model_width // HEAD_DIM
    scaling = HEAD_DIM ** (-0.5)
    first_pos = lax.axis_index("ctx") * local_len
    query_pos = first_pos + jnp.arange(local_len, dtype=jnp.int32)
    positions = query_pos.astype(jnp.float32)
    streams = jnp.zeros((dense_mix.shape[0], seq_count, local_len, model_width), jnp.float32)
    for layer_id in range(history.shape[0]):
        streams = (
            streams
            + dense_mix[:, layer_id][..., None] * history[layer_id].astype(jnp.float32)[None]
        )

    def front_norm(values, gain_rows, shift_rows):
        return layer_norm(values, gain_rows[:, None, None, :], shift_rows[:, None, None, :])

    normalized_input, front_pull = jax.vjp(front_norm, streams[:3], gain_all[:3], shift_all[:3])
    normalized_lowered = normalized_input.astype(jnp.bfloat16)
    mapped_output = (
        matrix_product("tbpr,rth->tbph", normalized_lowered, query_key_value_whole)
        + query_key_value_offset[:, None, None, :]
    )
    heads_shape = (seq_count, local_len, head_count, HEAD_DIM)
    queries = rotary(mapped_output[0].reshape(heads_shape), positions, 1.0).astype(jnp.bfloat16)
    keys_local = rotary(mapped_output[1].reshape(heads_shape), positions, 1.0).astype(jnp.bfloat16)
    values_local = mapped_output[2].reshape(heads_shape).astype(jnp.bfloat16)
    keys_all, values_all = (
        lax.all_gather(keys_local, "ctx", axis=1, tiled=True),
        lax.all_gather(values_local, "ctx", axis=1, tiled=True),
    )
    total_len = keys_all.shape[1]
    key_pos = jnp.arange(total_len, dtype=jnp.int32)
    key_doc = jnp.sum((doc_starts[:, None, :] <= key_pos[None, :, None]).astype(jnp.int32), axis=-1)
    query_doc = lax.dynamic_slice_in_dim(key_doc, first_pos, local_len, 1)

    def visible_of(query_ids, key_ids):
        return (query_ids[:, None] == key_ids[None, :]) & (key_pos[None, :] <= query_pos[:, None])

    def attend_one(seq_items):
        query_seq, key_seq, value_seq, query_ids, key_ids = seq_items
        scores = matrix_product("qhe,khe->hqk", query_seq, key_seq) * scaling
        scores = jnp.where(visible_of(query_ids, key_ids)[None], scores, NEG_BIG)
        row_peak = jnp.max(scores, axis=-1, keepdims=True)
        raised = jnp.exp(scores - row_peak)
        totals = jnp.sum(raised, axis=-1, keepdims=True)
        prob_low = (raised / totals).astype(jnp.bfloat16)
        mixed_rows = matrix_product("hqk,khe->qhe", prob_low, value_seq)
        return (mixed_rows, (row_peak + jnp.log(totals))[..., 0])

    attended, log_totals = lax.map(attend_one, (queries, keys_all, values_all, query_doc, key_doc))
    attended_low = attended.reshape(seq_count, local_len, model_width).astype(jnp.bfloat16)
    hidden_res = streams[3] + matrix_product("gld,de->gle", attended_low, out_full) + out_shift
    normed_mlp, mid_pull = jax.vjp(layer_norm, hidden_res, gain_all[3], shift_all[3])
    normed_mlp_low = normed_mlp.astype(jnp.bfloat16)
    upward = matrix_product("gld,df->glf", normed_mlp_low, up_full) + up_shift
    activated, gelu_pull = jax.vjp(precise_gelu_curve, upward)
    activated_low = activated.astype(jnp.bfloat16)
    result = hidden_res + matrix_product("glf,fd->gld", activated_low, down_full) + down_shift
    block_out = result.astype(jnp.bfloat16)
    next_rows, mixer_pull = jax.vjp(
        mixer, result, root_full, mix_in_full, mix_out_weight, mix_out_bias
    )
    next_mix = jnp.transpose(next_rows, (2, 0, 1))
    grad_result, grad_root, grad_mix_in, grad_mix_out, grad_mix_bias = mixer_pull(
        jnp.transpose(mix_cotangent, (1, 2, 0))
    )
    grad_result = grad_result + out_cotangent.astype(jnp.float32)
    query_key_value_whole, out_full, up_full, down_full = (
        lax.all_gather(query_key_value_weight, ("fsdp", "ctx"), axis=0, tiled=True),
        lax.all_gather(out_weight, ("fsdp", "ctx"), axis=0, tiled=True),
        lax.all_gather(up_weight, ("fsdp", "ctx"), axis=0, tiled=True),
        lax.all_gather(down_weight, ("fsdp", "ctx"), axis=0, tiled=True),
    )
    grad_branch = grad_result.astype(jnp.bfloat16)
    grad_down = matrix_product("glf,gld->fd", activated_low, grad_branch)
    grad_down_shift = jnp.sum(grad_branch.astype(jnp.float32), axis=(0, 1))
    grad_active = matrix_product("gld,fd->glf", grad_branch, down_full)
    grad_upward = gelu_pull(grad_active)[0].astype(jnp.bfloat16)
    grad_up = matrix_product("gld,glf->df", normed_mlp_low, grad_upward)
    grad_up_shift = jnp.sum(grad_upward.astype(jnp.float32), axis=(0, 1))
    grad_normed_mlp = matrix_product("glf,df->gld", grad_upward, up_full)
    grad_hidden, grad_gain_mid, grad_shift_mid = mid_pull(grad_normed_mlp)
    grad_hidden = grad_hidden + grad_result
    grad_attn_branch = grad_hidden.astype(jnp.bfloat16)
    grad_out = matrix_product("gld,gle->de", attended_low, grad_attn_branch)
    grad_out_shift = jnp.sum(grad_attn_branch.astype(jnp.float32), axis=(0, 1))
    grad_attended = (
        matrix_product("gle,de->gld", grad_attn_branch, out_full)
        .astype(jnp.bfloat16)
        .reshape(heads_shape)
    )

    def back_one(seq_items):
        query_seq, key_seq, value_seq, query_ids, key_ids, grad_seq, log_seq = seq_items
        scores = matrix_product("qhe,khe->hqk", query_seq, key_seq) * scaling
        prob_rows = jnp.where(
            visible_of(query_ids, key_ids)[None], jnp.exp(scores - log_seq[..., None]), 0.0
        )
        grad_probs = matrix_product("qhe,khe->hqk", grad_seq, value_seq)
        centre = jnp.sum(prob_rows * grad_probs, axis=-1, keepdims=True)
        grad_scores = (prob_rows * (grad_probs - centre)).astype(jnp.bfloat16)
        grad_query = matrix_product("hqk,khe->qhe", grad_scores, key_seq) * scaling
        grad_key = matrix_product("hqk,qhe->khe", grad_scores, query_seq) * scaling
        grad_value = matrix_product("hqk,qhe->khe", prob_rows.astype(jnp.bfloat16), grad_seq)
        return (grad_query, grad_key, grad_value)

    grad_queries, key_terms, value_terms = lax.map(
        back_one, (queries, keys_all, values_all, query_doc, key_doc, grad_attended, log_totals)
    )
    grad_keys, grad_values = (
        lax.psum_scatter(
            key_terms.astype(jnp.bfloat16), "ctx", scatter_dimension=1, tiled=True
        ).astype(jnp.float32),
        lax.psum_scatter(
            value_terms.astype(jnp.bfloat16), "ctx", scatter_dimension=1, tiled=True
        ).astype(jnp.float32),
    )
    gradient_mapped = jnp.stack(
        [rotary(grad_queries, positions, -1.0), rotary(grad_keys, positions, -1.0), grad_values]
    )
    gradient_mapped = gradient_mapped.reshape(3, seq_count, local_len, model_width).astype(
        jnp.bfloat16
    )
    gradient_query_key_value = matrix_product("ctbp,ctbm->pcm", normalized_lowered, gradient_mapped)
    grad_qkv_shift = jnp.sum(gradient_mapped.astype(jnp.float32), axis=(1, 2))
    gradient_normalized = matrix_product("cqtb,ycb->cqty", gradient_mapped, query_key_value_whole)
    grad_front, grad_gain_front, grad_shift_front = front_pull(gradient_normalized)
    grad_streams = jnp.concatenate([grad_front, grad_hidden[None]], axis=0)
    hist_grads = []
    mix_grads = []
    for layer_id in range(history.shape[0]):
        hist_grads.append(jnp.sum(dense_mix[:, layer_id][..., None] * grad_streams, axis=0))
        mix_grads.append(
            jnp.sum(history[layer_id].astype(jnp.float32)[None] * grad_streams, axis=-1)
        )
    grad_history = jnp.stack(hist_grads, axis=0)
    grad_mix = jnp.stack(mix_grads, axis=1)
    grad_gain = jnp.concatenate([grad_gain_front, grad_gain_mid[None]], axis=0)
    grad_shift = jnp.concatenate([grad_shift_front, grad_shift_mid[None]], axis=0)
    reduced = (
        lax.psum_scatter(
            gradient_query_key_value, ("fsdp", "ctx"), scatter_dimension=0, tiled=True
        ),
        lax.psum_scatter(grad_out, ("fsdp", "ctx"), scatter_dimension=0, tiled=True),
        lax.psum_scatter(grad_up, ("fsdp", "ctx"), scatter_dimension=0, tiled=True),
        lax.psum_scatter(grad_down, ("fsdp", "ctx"), scatter_dimension=0, tiled=True),
        lax.psum_scatter(grad_gain, ("fsdp", "ctx"), scatter_dimension=1, tiled=True),
        lax.psum_scatter(grad_shift, ("fsdp", "ctx"), scatter_dimension=1, tiled=True),
        lax.psum_scatter(grad_qkv_shift, ("fsdp", "ctx"), scatter_dimension=1, tiled=True),
        lax.psum_scatter(grad_out_shift, ("fsdp", "ctx"), scatter_dimension=0, tiled=True),
        lax.psum_scatter(grad_up_shift, ("fsdp", "ctx"), scatter_dimension=0, tiled=True),
        lax.psum_scatter(grad_down_shift, ("fsdp", "ctx"), scatter_dimension=0, tiled=True),
        lax.psum_scatter(grad_root, ("fsdp", "ctx"), scatter_dimension=0, tiled=True),
        lax.psum_scatter(grad_mix_in, ("fsdp", "ctx"), scatter_dimension=0, tiled=True),
    )
    mixer_sums = lax.psum((grad_mix_out, grad_mix_bias), ("fsdp", "ctx"))
    return (
        block_out,
        next_mix,
        grad_history,
        grad_mix,
        reduced[4],
        reduced[5],
        reduced[0],
        reduced[6],
        reduced[1],
        reduced[7],
        reduced[2],
        reduced[8],
        reduced[3],
        reduced[9],
        reduced[10],
        reduced[11],
        mixer_sums[0],
        mixer_sums[1],
    )


def solution(mesh):
    placed = (
        P(None, "fsdp", "ctx", None),
        P(None, None, "fsdp", "ctx"),
        P("fsdp", None),
        P(None, ("fsdp", "ctx")),
        P(None, ("fsdp", "ctx")),
        P(("fsdp", "ctx"), None, None),
        P(None, ("fsdp", "ctx")),
        P(("fsdp", "ctx"), None),
        P(("fsdp", "ctx")),
        P(("fsdp", "ctx"), None),
        P(("fsdp", "ctx")),
        P(("fsdp", "ctx"), None),
        P(("fsdp", "ctx")),
        P(("fsdp", "ctx")),
        P(("fsdp", "ctx"), None),
        P(),
        P(),
        P("fsdp", "ctx", None),
        P(None, "fsdp", "ctx"),
    )
    return jax.shard_map(
        body,
        mesh=mesh,
        in_specs=placed,
        out_specs=(
            P("fsdp", "ctx", None),
            P(None, "fsdp", "ctx"),
            P(None, "fsdp", "ctx", None),
            P(None, None, "fsdp", "ctx"),
            P(None, ("fsdp", "ctx")),
            P(None, ("fsdp", "ctx")),
            P(("fsdp", "ctx"), None, None),
            P(None, ("fsdp", "ctx")),
            P(("fsdp", "ctx"), None),
            P(("fsdp", "ctx")),
            P(("fsdp", "ctx"), None),
            P(("fsdp", "ctx")),
            P(("fsdp", "ctx"), None),
            P(("fsdp", "ctx")),
            P(("fsdp", "ctx")),
            P(("fsdp", "ctx"), None),
            P(),
            P(),
        ),
        check_vma=False,
    )
```

profile of v0, /device:TPU:1, one launch (start us, length us, event | category | flops | bytes accessed | tf_op | source)
XLA Modules:
  0.0 6095.1 jit_solution(656544450056032121)
XLA Ops:
  8.8 63.7 %all-gather = f32[32,64,4]{1,2,0:T(4,128)S(1)} all-gather(f32[1,64,4]{1,2,0:T(4,128)} %bitcast.300), channel_id=1, replica_groups=mesh['fsdp'=4,'ctx'=8] {'fsdp','ctx'}, dimensions={0}, use_global_device_ids=true | all-gather | bytes 33792 | tf_op jit(solution)/shard_map/all_gather | solution.py:84
  72.7 66.0 %all-gather.1 = f32[32,64,4]{1,2,0:T(4,128)S(1)} all-gather(f32[1,64,4]{1,2,0:T(4,128)} %bitcast.301), channel_id=1, replica_groups=mesh['fsdp'=4,'ctx'=8] {'fsdp','ctx'}, dimensions={0}, use_global_device_ids=true | all-gather | bytes 33792 | tf_op jit(solution)/shard_map/all_gather | solution.py:85
  138.7 66.0 %all-gather.2 = f32[32,64,3]{1,2,0:T(4,128)S(1)} all-gather(f32[1,64,3]{1,2,0:T(4,128)} %bitcast.302), channel_id=1, replica_groups=mesh['fsdp'=4,'ctx'=8] {'fsdp','ctx'}, dimensions={0}, use_global_device_ids=true | all-gather | bytes 25344 | tf_op jit(solution)/shard_map/all_gather | solution.py:86
  205.9 4.9 bitcast_convert_fusion.8
  211.0 5.9 multiply_add_fusion
  217.7 3.0 copy-done.1
  222.1 14.2 convolution_add_fusion.1
  240.4 4.1 fusion.46
  244.5 1.9 pad_maximum_fusion.5
  246.5 2.7 slice.244
  249.2 2.3 copy.184
  253.4 76.5 %all-gather.4 = f32[32,64,40]{1,2,0:T(8,128)S(1)} all-gather(f32[1,64,40]{1,2,0:T(8,128)S(1)} %bitcast.297), channel_id=1, replica_groups=mesh['fsdp'=4,'ctx'=8] {'fsdp','ctx'}, dimensions={0}, use_global_device_ids=true | all-gather | bytes 337920 | tf_op jit(solution)/shard_map/all_gather | solution.py:91
  332.0 45.5 all-reduce.9
  377.5 62.7 %all-gather.3 = f32[32,1,256]{2,1,0:T(1,128)S(1)} all-gather(f32[1,1,256]{2,1,0:T(1,128)S(1)} %bitcast.303), channel_id=1, replica_groups=mesh['fsdp'=4,'ctx'=8] {'fsdp','ctx'}, dimensions={0}, use_global_device_ids=true | all-gather | bytes 33792 | tf_op jit(solution)/shard_map/all_gather | solution.py:88
  441.6 19.0 select_reduce_fusion
  460.5 15.1 fusion
  475.7 34.9 all-gather.14.cloned.1.call-done
  510.5 17.5 fusion.39
  528.0 61.9 %all-gather.18.cloned.1.call-done = bf16[2048,2048]{1,0:T(8,128)(2,1)} async-done(((bf16[64,2048]{1,0:T(8,128)(2,1)}), bf16[2048,2048]{1,0:T(8,128)(2,1)}) %all-gather.18.cloned.1.call-update) | async-done | bytes 8388624 | tf_op jit(solution)/shard_map/all_gather | solution.py:105
  589.9 6.6 fusion.102
  597.8 188.4 %all-gather.20.cloned.1.call-done = bf16[2048,8192]{1,0:T(8,128)(2,1)} async-done(((bf16[64,8192]{1,0:T(8,128)(2,1)}), bf16[2048,8192]{1,0:T(8,128)(2,1)}) %all-gather.20.cloned.1.call-update) | async-done | bytes 33554448 | tf_op jit(solution)/shard_map/all_gather | solution.py:106
  786.2 18.4 convolution_add_fusion
  804.6 177.5 %all-gather.22.cloned.1.call-done = bf16[8192,2048]{1,0:T(8,128)(2,1)} async-done(((bf16[256,2048]{1,0:T(8,128)(2,1)}), bf16[8192,2048]{1,0:T(8,128)(2,1)}) %all-gather.22.cloned.1.call-update) | async-done | bytes 33554448 | tf_op jit(solution)/shard_map/all_gather | solution.py:107
  982.0 30.9 multiply_reduce_fusion.24
  1013.0 2.1 fusion.65
  1015.3 1.8 fusion.103
  1017.2 2.3 multiply_reduce_fusion.20
  1021.0 34.3 convert_reduce_fusion
  1055.3 17.8 multiply_reduce_fusion.21
  1073.1 2.2 fusion.98
  1075.4 4.0 convert_reduce_fusion.3
  1080.4 5.8 convolution_convert_fusion
  1086.7 19.0 convert_bitcast_fusion
  1105.8 28.5 multiply_reduce_fusion
  1134.3 28.8 multiply_convert_fusion
  1163.1 13.2 fusion.10
  1177.2 11.0 multiply_bitcast_fusion
  1189.5 4.5 fusion.33
  1194.1 59.0 reduce-scatter.20.cloned.1.call-done
  1253.0 2.6 copy.170
  1255.7 149.8 %reduce-scatter.18.cloned.1.call-done = bf16[1,256,16,128]{3,1,2,0:T(8,128)(2,1)} async-done(((bf16[1,2048,16,128]{3,1,2,0:T(8,128)(2,1)}), bf16[1,256,16,128]{3,1,2,0:T(8,128)(2,1)}) %reduce-scatter.18.cloned.1.call-update) | async-done | bytes 1048592 | tf_op jit(solution)/shard_map/reduce_scatter | solution.py:219
  1407.0 2.3 multiply_subtract_fusion.1
  1409.8 1.9 maximum_convert_fusion.1
  1413.2 3.2 maximum_convert_fusion
  1420.8 16.7 fusion.24
  1440.3 6.6 fusion.23
  1446.9 3.3 reduce_sum.448
  1453.1 22.8 convolution_bitcast_fusion
  1475.9 71.2 %copy.173 = f32[2048,3,2048]{2,1,0:T(4,128)} copy(f32[2048,3,2048]{0,2,1:T(8,128)} %convolution_bitcast_fusion) | data formatting | bytes 100663296 | tf_op jit(solution)/shard_map/ctbp,ctbm->pcm/transpose | solution.py:59
  1548.7 8.1 fusion.49
  1558.3 34.1 fusion.52
  1594.0 25.6 fusion.95
  1621.8 40.9 all-reduce.8
  1666.7 7.6 broadcast_add_fusion
  1674.3 21.7 multiply_reduce_fusion.2
  1696.1 8.8 multiply_reduce_fusion.3
  1719.7 81.7 %reduce-scatter.28.cloned.1.call-done = f32[64,4]{1,0:T(8,128)} async-done(((f32[2048,4]{1,0:T(8,128)}), f32[64,4]{1,0:T(8,128)}) %reduce-scatter.28.cloned.1.call-update) | async-done | bytes 1040
  1802.8 132.3 %reduce-scatter.30.cloned.1.call-done = f32[64,4]{1,0:T(8,128)} async-done(((f32[2048,4]{1,0:T(8,128)}), f32[64,4]{1,0:T(8,128)}) %reduce-scatter.30.cloned.1.call-update) | async-done | bytes 1040
  1936.5 981.6 %all-reduce.12.cloned.1.call-done = f32[2048,3,2048]{2,1,0:T(4,128)} async-done(((f32[2048,3,2048]{2,1,0:T(4,128)}), f32[2048,3,2048]{2,1,0:T(4,128)}) %all-reduce.12.cloned.1.call-update) | async-done | bytes 50331664
  2918.1 2.0 constant_dynamic-slice_fusion
  2920.1 2.1 copy.177
  2922.2 355.6 %reduce-scatter.22.cloned.1.call-done = f32[64,2048]{1,0:T(8,128)} async-done(((f32[2048,2048]{1,0:T(8,128)}), f32[64,2048]{1,0:T(8,128)}) %reduce-scatter.22.cloned.1.call-update) | async-done | bytes 524304 | tf_op jit(solution)/shard_map/reduce_scatter | solution.py:252
  3277.7 1405.0 %reduce-scatter.26.cloned.1.call-done = f32[256,2048]{1,0:T(8,128)} async-done(((f32[8192,2048]{1,0:T(8,128)}), f32[256,2048]{1,0:T(8,128)}) %reduce-scatter.26.cloned.1.call-update) | async-done | bytes 2097168 | tf_op jit(solution)/shard_map/reduce_scatter | solution.py:254
  4682.7 1405.3 %reduce-scatter.24.cloned.1.call-done = f32[64,8192]{1,0:T(8,128)} async-done(((f32[2048,8192]{1,0:T(8,128)}), f32[64,8192]{1,0:T(8,128)}) %reduce-scatter.24.cloned.1.call-update) | async-done | bytes 2097168 | tf_op jit(solution)/shard_map/reduce_scatter | solution.py:253
  (374 shorter events, 62.8 us)
Async XLA Ops:
  7.2 1007.9 %copy-start = (f32[40,40]{1,0:T(8,128)S(1)}, f32[40,40]{1,0:T(8,128)}, u32[]{:S(2)}) copy-start(f32[40,40]{1,0:T(8,128)} %param.34) | copy-start | bytes 19204
  7.2 214.9 %all-gather.12.cloned.1.call-start = ((), (), s32[]{:S(2)}) async-start(), calls=%async_computation.9 | async-start | bytes 25952256 | tf_op jit(solution)/shard_map/all_gather | solution.py:104
  7.9 433.6 %all-gather.16.cloned.1.call-start = ((), (), s32[]{:S(2)}) async-start(), calls=%async_computation.11 | async-start | bytes 9437184 | tf_op jit(solution)/shard_map/all_gather | solution.py:136
  8.8 202.1 %copy-start.100 = (f32[4,1,1,256]{3,0,1,2:T(4,128)}, f32[4,1,1,256]{3,0,1,2:T(4,128)S(1)}, u32[]{:S(2)}) copy-start(f32[4,1,1,256]{3,0,1,2:T(4,128)S(1)} %copy.253) | copy-start | bytes 12292
  72.7 180.6 %copy-start.43 = (f32[2048,4]{0,1:T(4,128)}, f32[2048,4]{0,1:T(4,128)S(1)}, u32[]{:S(2)}) copy-start(f32[2048,4]{0,1:T(4,128)S(1)} %reshape.1634) | copy-start | bytes 98308
  138.7 114.6 %copy-start.49 = (f32[2048,4]{0,1:T(4,128)}, f32[2048,4]{0,1:T(4,128)S(1)}, u32[]{:S(2)}) copy-start(f32[2048,4]{0,1:T(4,128)S(1)} %reshape.1636) | copy-start | bytes 98308
  205.7 34.7 copy-start.46
  220.7 15.6 copy-start.65
  222.1 14.2 copy-start.68
  244.5 86.6 %copy-start.114 = (s32[1,8]{1,0:T(1,128)S(1)}, s32[1,8]{1,0:T(1,128)}, u32[]{:S(2)}) copy-start(s32[1,8]{1,0:T(1,128)} %param.21) | copy-start | bytes 100
  244.5 86.7 %copy-start.116 = (f32[64]{0:T(128)S(1)}, f32[64]{0:T(128)}, u32[]{:S(2)}) copy-start(f32[64]{0:T(128)} %param.31) | copy-start | bytes 772
  244.5 87.0 %copy-start.117 = (f32[64]{0:T(128)S(1)}, f32[64]{0:T(128)}, u32[]{:S(2)}) copy-start(f32[64]{0:T(128)} %param.27) | copy-start | bytes 772
  244.5 87.2 %copy-start.118 = (f32[64]{0:T(128)S(1)}, f32[64]{0:T(128)}, u32[]{:S(2)}) copy-start(f32[64]{0:T(128)} %param.32) | copy-start | bytes 772
  244.5 133.0 %copy-start.112 = (f32[256]{0:T(256)S(1)}, f32[256]{0:T(256)}, u32[]{:S(2)}) copy-start(f32[256]{0:T(256)} %param.29) | copy-start | bytes 3076
  246.5 264.1 %all-gather.14.cloned.1.call-start = ((), (), s32[]{:S(2)}) async-start(), calls=%async_computation.10 | async-start | bytes 9437184 | tf_op jit(solution)/shard_map/all_gather | solution.py:137
  251.5 338.4 %all-gather.18.cloned.1.call-start = ((), (), s32[]{:S(2)}) async-start(), calls=%async_computation.12 | async-start | bytes 8650752 | tf_op jit(solution)/shard_map/all_gather | solution.py:105
  252.1 534.1 %all-gather.20.cloned.1.call-start = ((), (), s32[]{:S(2)}) async-start(), calls=%async_computation.13 | async-start | bytes 34603008 | tf_op jit(solution)/shard_map/all_gather | solution.py:106
  252.7 729.3 %all-gather.22.cloned.1.call-start = ((), (), s32[]{:S(2)}) async-start(), calls=%async_computation.14 | async-start | bytes 34603008 | tf_op jit(solution)/shard_map/all_gather | solution.py:107
  253.3 999.8 %reduce-scatter.20.cloned.1.call-start = ((), (), s32[]{:S(2)}) async-start(), calls=%async_computation.16 | async-start | bytes 9437184 | tf_op jit(solution)/shard_map/reduce_scatter | solution.py:222
  253.3 532.8 %copy-start.51 = (f32[1,2048]{1,0:T(1,128)}, f32[1,2048]{1,0:T(1,128)S(1)}, u32[]{:S(2)}) copy-start(f32[1,2048]{1,0:T(1,128)S(1)} %slice.193) | copy-start | bytes 24580
  253.4 532.8 %copy-start.55 = (f32[1,2048]{1,0:T(1,128)}, f32[1,2048]{1,0:T(1,128)S(1)}, u32[]{:S(2)}) copy-start(f32[1,2048]{1,0:T(1,128)S(1)} %slice.194) | copy-start | bytes 24580
  440.9 69.6 %copy-start.4 = (pred[256,2048]{1,0:T(8,128)(4,1)}, pred[256,2048]{1,0:T(8,128)(4,1)S(1)}, u32[]{:S(2)}) copy-start(pred[256,2048]{1,0:T(8,128)(4,1)S(1)} %fusion.32) | copy-start | bytes 1572868
  441.5 19.0 copy-start.20
  528.0 68.5 %copy-start.31 = (bf16[16,128,256]{2,1,0:T(8,128)(2,1)}, bf16[16,128,256]{2,1,0:T(8,128)(2,1)S(1)}, u32[]{:S(2)}) copy-start(bf16[16,128,256]{2,1,0:T(8,128)(2,1)S(1)} %fusion.39) | copy-start | bytes 3145732
  596.5 476.6 %copy-start.2 = (f32[256,2048]{1,0:T(8,128)}, f32[256,2048]{1,0:T(8,128)S(1)}, u32[]{:S(2)}) copy-start(f32[256,2048]{1,0:T(8,128)S(1)} %get-tuple-element.267) | copy-start | bytes 6291460
  596.5 208.0 %copy-start.71 = (f32[256]{0:T(256)}, f32[256]{0:T(256)S(1)}, u32[]{:S(2)}) copy-start(f32[256]{0:T(256)S(1)} %broadcast_multiply_fusion.2) | copy-start | bytes 3076
  596.9 207.7 %copy-start.110 = (f32[256]{0:T(256)}, f32[256]{0:T(256)S(1)}, u32[]{:S(2)}) copy-start(f32[256]{0:T(256)S(1)} %multiply_reduce_fusion.25) | copy-start | bytes 3076
  596.9 207.6 %copy-start.77 = (f32[256]{0:T(256)}, f32[256]{0:T(256)S(1)}, u32[]{:S(2)}) copy-start(f32[256]{0:T(256)S(1)} %fusion.80) | copy-start | bytes 3076
  982.0 30.9 copy-start.42
  982.0 30.9 copy-start.74
  982.0 33.1 copy-start.57
  1015.1 40.2 copy-start.59
  1015.1 40.2 copy-start.61
  1015.3 39.9 copy-start.63
  1020.9 34.3 copy-start.29
  1020.9 34.3 copy-start.52
  1020.9 34.3 copy-start.72
  1020.9 34.3 copy-start.78
  1055.3 17.8 copy-start.111
  1105.7 299.8 %reduce-scatter.18.cloned.1.call-start = ((), (), s32[]{:S(2)}) async-start(), calls=%async_computation.15 | async-start | bytes 9437184 | tf_op jit(solution)/shard_map/reduce_scatter | solution.py:219
  1134.3 28.8 copy-start.18
  1134.3 28.8 copy-start.19
  1176.3 488.7 %reduce-scatter.34.cloned.1.call-start = ((), (), s32[]{:S(2)}) async-start(), calls=%async_computation.23 | async-start | bytes 1081344
  1177.1 12.4 copy-start.12
  1177.1 12.4 copy-start.64
  1177.2 12.4 copy-start.75
  1177.2 12.4 copy-start.108
  1188.1 218.9 %copy-start.47 = (f32[256,16]{1,0:T(8,128)S(1)}, f32[256,16]{1,0:T(8,128)}, u32[]{:S(2)}) copy-start(f32[256,16]{1,0:T(8,128)} %copy-done.46) | copy-start | bytes 49156
  1194.0 524.3 %reduce-scatter.32.cloned.1.call-start = ((), (), s32[]{:S(2)}) async-start(), calls=%async_computation.22 | async-start | bytes 1081344
  1420.7 16.7 copy-start.36
  1420.7 18.9 copy-start.97
  1420.7 19.5 copy-start.69
  1439.7 361.6 %reduce-scatter.28.cloned.1.call-start = ((), (), s32[]{:S(2)}) async-start(), calls=%async_computation.20 | async-start | bytes 1081344
  1451.5 483.5 %reduce-scatter.30.cloned.1.call-start = ((), (), s32[]{:S(2)}) async-start(), calls=%async_computation.21 | async-start | bytes 1081344
  1453.0 1465.1 %all-reduce.12.cloned.1.call-start = ((), (), s32[]{:S(2)}) async-start(), calls=%async_computation.24 | async-start | bytes 134217728
  1547.1 1730.6 %reduce-scatter.22.cloned.1.call-start = ((), (), s32[]{:S(2)}) async-start(), calls=%async_computation.17 | async-start | bytes 17301504 | tf_op jit(solution)/shard_map/reduce_scatter | solution.py:252
  1556.7 3126.0 %reduce-scatter.26.cloned.1.call-start = ((), (), s32[]{:S(2)}) async-start(), calls=%async_computation.19 | async-start | bytes 69206016 | tf_op jit(solution)/shard_map/reduce_scatter | solution.py:254
  1592.4 4495.6 %reduce-scatter.24.cloned.1.call-start = ((), (), s32[]{:S(2)}) async-start(), calls=%async_computation.18 | async-start | bytes 69206016 | tf_op jit(solution)/shard_map/reduce_scatter | solution.py:253
  1619.6 46.9 copy-start.109
  1619.6 46.9 copy-start.45
  1619.6 46.9 copy-start.67
  1619.7 46.9 copy-start.70
  1619.7 46.9 copy-start.99
  1674.3 21.7 copy-start.101
  (71 other events, 351.7 us)
Sparse Core Ops, SparseCore 0:
  11.1 158.4 all-gather.11
  246.6 137.6 all-gather.15
  386.9 123.6 all-gather.13
  513.4 76.5 all-gather.17
  592.7 193.3 all-gather.19
  789.0 192.9 all-gather.21
  1105.8 147.1 reduce-scatter.19
  1257.1 148.3 reduce-scatter.17
  1407.8 126.1 reduce-scatter.33
  1536.1 131.4 reduce-scatter.31
  1669.9 131.4 reduce-scatter.27
  1803.5 131.4 reduce-scatter.29
  1941.5 976.5 all-reduce.11
  2920.9 356.8 reduce-scatter.21
  3280.5 1402.1 reduce-scatter.25
  4685.5 1402.4 reduce-scatter.23
where the time goes:
time: 6100 us
  waiting for transfers between devices  5040 us (83%)
  blocking collectives  421 us (7%)
  matrix products  352 us (6%)
  local copies, waits for them, and re-layouts  137 us (2%)
  other arithmetic  133 us (2%)
    reduce_scatter x1, waiting for transfers between devices, body(): lax.psum_scatter(grad_up, ('fsdp', 'ctx'), scatter_dimension=0, tiled=True)  1410 us
    reduce_scatter x1, waiting for transfers between devices, body(): lax.psum_scatter(grad_down, ('fsdp', 'ctx'), scatter_dimension=0, tiled=T...  1400 us
    unnamed x21, waiting for transfers between devices  1200 us
    reduce_scatter x1, waiting for transfers between devices, body(): lax.psum_scatter(grad_out, ('fsdp', 'ctx'), scatter_dimension=0, tiled=True)  356 us
    dot_general x18, matrix products, matrix_product(): jnp.einsum(pattern, left_side, right_side, preferred_element_type=jnp.flo...  343 us
    all_gather x1, waiting for transfers between devices, body(): lax.all_gather(up_weight, ('fsdp', 'ctx'), axis=0, tiled=True)  188 us
    all_gather x1, waiting for transfers between devices, body(): lax.all_gather(down_weight, ('fsdp', 'ctx'), axis=0, tiled=True)  177 us
    reduce_scatter x1, waiting for transfers between devices, body(): lax.psum_scatter(key_terms.astype(jnp.bfloat16), 'ctx', scatter_dimension...  150 us
  transfers between devices with their start and end apart: 16, of which 12 were waited for; matrix products, arithmetic and copies ran while one was open for 8% of the time, Pallas kernels for 0%

commit v1 on v0

v1 whole, which is shorter than its diff:
```python
import math

import jax
import jax.numpy as jnp
from jax import lax
from jax.experimental import pallas as pl
from jax.experimental.pallas import tpu as pltpu
from jax.sharding import PartitionSpec as P

HEAD_DIM = 128
ROT = 32
TOP_PRECISION = lax.Precision.HIGHEST
EPS_NORM = 1e-05
EPS_ROOT = 1e-06
NEG_BIG = -1e30
BOTH = ("fsdp", "ctx")
BF16 = jnp.bfloat16
F32 = jnp.float32
MESH = pl.DeviceIdType.MESH
ANY = pl.BlockSpec(memory_space=pl.ANY)
VMEM = pl.BlockSpec(memory_space=pltpu.VMEM)
LOG2E = 1.4426950408889634


def layer_norm(values, gain_row, shift_row):
    centre = values - jnp.mean(values, axis=-1, keepdims=True)
    spread = jnp.mean(centre * centre, axis=-1, keepdims=True)
    return centre * lax.rsqrt(spread + EPS_NORM) * gain_row + shift_row


def gelu(values):
    return jax.nn.gelu(values, approximate=False)


def rotary_tables(positions, turning):
    half = ROT // 2
    frequency = jnp.exp(jnp.arange(half, dtype=F32) * (-2.0 * math.log(10000.0) / ROT))
    angles = positions[:, None] * frequency[None, :]
    return jnp.cos(angles), turning * jnp.sin(angles)


def rotary(values, cosine, sine):
    half = ROT // 2
    front, back = values[..., :half], values[..., half:ROT]
    return jnp.concatenate(
        [front * cosine - back * sine, back * cosine + front * sine, values[..., ROT:]], axis=-1
    )


def mixer(rows, gain_row, opening, closing, closing_bias):
    inverse_rms = lax.rsqrt(jnp.mean(rows * rows, axis=-1, keepdims=True) + EPS_ROOT)
    rooted = rows * inverse_rms * gain_row
    hidden = jnp.dot(rooted, opening, precision=TOP_PRECISION)
    return jnp.dot(gelu(hidden), closing, precision=TOP_PRECISION) + closing_bias


def dot(pattern, left, right):
    return jnp.einsum(pattern, left, right, preferred_element_type=F32)


def remote(src, dst, send_sem, recv_sem, target):
    return pltpu.make_async_remote_copy(
        src_ref=src,
        dst_ref=dst,
        send_sem=send_sem,
        recv_sem=recv_sem,
        device_id=target,
        device_id_type=MESH,
    )


def greet(targets):
    barrier = pltpu.get_barrier_semaphore()
    for t in targets:
        pl.semaphore_signal(barrier, inc=1, device_id=t, device_id_type=MESH)
    pl.semaphore_wait(barrier, len(targets))


def greet_all(fn, cn, me):
    barrier = pltpu.get_barrier_semaphore()

    def hello(k, _):
        t = lax.rem(me + k, fn * cn)
        pl.semaphore_signal(
            barrier, inc=1, device_id=(t // cn, lax.rem(t, cn)), device_id_type=MESH
        )
        return 0

    lax.fori_loop(1, fn * cn, hello, 0)
    pl.semaphore_wait(barrier, fn * cn - 1)


def gather_small(x):
    fn, cn = lax.axis_size("fsdp"), lax.axis_size("ctx")
    dn = fn * cn

    def kernel(x_ref, o_ref, send, recv):
        me = lax.axis_index("fsdp") * cn + lax.axis_index("ctx")
        greet_all(fn, cn, me)

        def copy(k, slot):
            t = lax.rem(me + k, dn)
            return remote(
                x_ref, o_ref.at[slot], send.at[k], recv.at[k], (t // cn, lax.rem(t, cn))
            )

        def go(k, _):
            copy(k, me).start()
            return 0

        lax.fori_loop(1, dn, go, 0)
        o_ref[me] = x_ref[...]

        def end(k, _):
            c = copy(k, lax.rem(me + dn - k, dn))
            c.wait_send()
            c.wait_recv()
            return 0

        lax.fori_loop(1, dn, end, 0)

    return pl.pallas_call(
        kernel,
        out_shape=jax.ShapeDtypeStruct((dn, *x.shape), x.dtype),
        in_specs=[VMEM],
        out_specs=VMEM,
        scratch_shapes=[pltpu.SemaphoreType.DMA((dn,)), pltpu.SemaphoreType.DMA((dn,))],
        compiler_params=pltpu.CompilerParams(collective_id=1, has_side_effects=True),
    )(x)


def scatter_small(x):
    fn, cn = lax.axis_size("fsdp"), lax.axis_size("ctx")
    dn = fn * cn

    def kernel(x_ref, o_ref, got, send, recv):
        me = lax.axis_index("fsdp") * cn + lax.axis_index("ctx")
        greet_all(fn, cn, me)

        def copy(k):
            t = lax.rem(me + k, dn)
            return remote(
                x_ref.at[t], got.at[k], send.at[k], recv.at[k], (t // cn, lax.rem(t, cn))
            )

        def go(k, _):
            copy(k).start()
            return 0

        lax.fori_loop(1, dn, go, 0)
        o_ref[...] = x_ref[me]

        def end(k, _):
            copy(k).wait_recv()
            o_ref[...] += got[k]
            return 0

        lax.fori_loop(1, dn, end, 0)

        def sent(k, _):
            copy(k).wait_send()
            return 0

        lax.fori_loop(1, dn, sent, 0)

    return pl.pallas_call(
        kernel,
        out_shape=jax.ShapeDtypeStruct(x.shape[1:], x.dtype),
        in_specs=[VMEM],
        out_specs=VMEM,
        scratch_shapes=[
            pltpu.VMEM(x.shape, x.dtype),
            pltpu.SemaphoreType.DMA((dn,)),
            pltpu.SemaphoreType.DMA((dn,)),
        ],
        compiler_params=pltpu.CompilerParams(collective_id=2, has_side_effects=True),
    )(x)


def gather_fsdp(x, cid, parts=4):
    fn = lax.axis_size("fsdp")
    chips = fn // 2
    k_count, n, d = x.shape
    step = n // parts
    pieces = [(k, pl.ds(p * step, step)) for k in range(k_count) for p in range(parts)]
    many = len(pieces)

    def kernel(x_ref, o_ref, own_sem, s_link, r_link, s_core, r_core):
        f, c = lax.axis_index("fsdp"), lax.axis_index("ctx")
        chip, core = f // 2, lax.rem(f, 2)
        twin = (chip * 2 + 1 - core, c)

        def to(j):
            return (lax.rem(chip + j, chips) * 2 + core, c)

        def slot(j, core_id):
            return lax.rem(chip + chips - j, chips) * 2 + core_id

        greet([to(j) for j in range(1, chips)] + [twin])
        links, cores = {}, {}
        for i, (k, rows) in enumerate(pieces):
            for j in range(1, chips):
                links[i, j] = remote(
                    x_ref.at[k, rows],
                    o_ref.at[k, f, rows],
                    s_link.at[j, i],
                    r_link.at[j, i],
                    to(j),
                )
                links[i, j].start()
        for i, (k, rows) in enumerate(pieces):
            cores[i, 0] = remote(
                x_ref.at[k, rows], o_ref.at[k, f, rows], s_core.at[0, i], r_core.at[0, i], twin
            )
            cores[i, 0].start()
        own = pltpu.make_async_copy(x_ref, o_ref.at[:, f], own_sem)
        own.start()
        for i, (k, rows) in enumerate(pieces):
            for j in range(1, chips):
                here = o_ref.at[k, slot(j, core), rows]
                remote(here, here, s_link.at[j, i], r_link.at[j, i], to(j)).wait_recv()
                cores[i, j] = remote(here, here, s_core.at[j, i], r_core.at[j, i], twin)
                cores[i, j].start()
        own.wait()
        for i, (k, rows) in enumerate(pieces):
            for j in range(chips):
                there = o_ref.at[k, slot(j, 1 - core), rows]
                cores[i, j].wait_send()
                remote(there, there, s_core.at[j, i], r_core.at[j, i], twin).wait_recv()
            for j in range(1, chips):
                links[i, j].wait_send()

    return pl.pallas_call(
        kernel,
        out_shape=jax.ShapeDtypeStruct((k_count, fn, n, d), x.dtype),
        in_specs=[ANY],
        out_specs=ANY,
        scratch_shapes=[
            pltpu.SemaphoreType.DMA,
            pltpu.SemaphoreType.DMA((chips, many)),
            pltpu.SemaphoreType.DMA((chips, many)),
            pltpu.SemaphoreType.DMA((chips, many)),
            pltpu.SemaphoreType.DMA((chips, many)),
        ],
        compiler_params=pltpu.CompilerParams(collective_id=cid, has_side_effects=True),
    )(x)


def scatter_fsdp(x, cid, parts=4):
    fn = lax.axis_size("fsdp")
    chips = fn // 2
    k_count, _, n, d = x.shape
    step = n // parts
    pieces = [(k, p) for k in range(k_count) for p in range(parts)]
    many = len(pieces)

    def kernel(x_ref, o_ref, own, near, mine, far, ss, s_own, s_near, r_near, s_far, r_far):
        f, c = lax.axis_index("fsdp"), lax.axis_index("ctx")
        chip, core = f // 2, lax.rem(f, 2)
        twin = (chip * 2 + 1 - core, c)

        def chip_at(j):
            return lax.rem(chip + j, chips)

        def to(j):
            return (chip_at(j) * 2 + core, c)

        order = list(range(1, chips)) + [0]
        greet([to(j) for j in range(1, chips)] + [twin])
        nears, owns, fars, outs = {}, {}, {}, []
        for i, (k, p) in enumerate(pieces):
            rows = pl.ds(p * step, step)
            for j in order:
                owns[i, j] = pltpu.make_async_copy(
                    x_ref.at[k, chip_at(j) * 2 + core, rows], own.at[j, i], s_own.at[j, i]
                )
                owns[i, j].start()
                nears[i, j] = remote(
                    x_ref.at[k, chip_at(j) * 2 + 1 - core, rows],
                    near.at[j, i],
                    s_near.at[j, i],
                    r_near.at[j, i],
                    twin,
                )
                nears[i, j].start()
        for i in range(many):
            for j in range(1, chips):
                owns[i, j].wait()
                nears[i, j].wait_recv()
                mine[j, i] = (own[j, i].astype(F32) + near[j, i].astype(F32)).astype(BF16)
                fars[i, j] = remote(
                    mine.at[j, i], far.at[j, i], s_far.at[j, i], r_far.at[j, i], to(j)
                )
                fars[i, j].start()
        for i, (k, p) in enumerate(pieces):
            owns[i, 0].wait()
            nears[i, 0].wait_recv()
            ss[i] = own[0, i].astype(F32) + near[0, i].astype(F32)
        for i, (k, p) in enumerate(pieces):
            for j in range(1, chips):
                fars[i, j].wait_recv()
                ss[i] += far[j, i].astype(F32)
            outs.append(
                pltpu.make_async_copy(
                    ss.at[i], o_ref.at[k, pl.ds(p * step, step)], s_far.at[0, i]
                )
            )
            outs[-1].start()
        for i in range(many):
            outs[i].wait()
            for j in range(chips):
                nears[i, j].wait_send()
            for j in range(1, chips):
                fars[i, j].wait_send()

    blocks = (chips, many, step, d)
    sems = pltpu.SemaphoreType.DMA((chips, many))
    return pl.pallas_call(
        kernel,
        out_shape=jax.ShapeDtypeStruct((k_count, n, d), F32),
        in_specs=[ANY],
        out_specs=ANY,
        scratch_shapes=[
            pltpu.VMEM(blocks, BF16),
            pltpu.VMEM(blocks, BF16),
            pltpu.VMEM(blocks, BF16),
            pltpu.VMEM(blocks, BF16),
            pltpu.VMEM((many, step, d), F32),
            sems,
            sems,
            sems,
            sems,
            sems,
        ],
        compiler_params=pltpu.CompilerParams(
            collective_id=cid, has_side_effects=True, vmem_limit_bytes=56 * 2**20
        ),
    )(x)


def nt(a, b):
    return lax.dot_general(a, b, (((1,), (1,)), ((), ())), preferred_element_type=F32)


def nn(a, b):
    return lax.dot_general(a, b, (((1,), (0,)), ((), ())), preferred_element_type=F32)


def attend(q, k, v, starts, block=512):
    u, t, _ = q.shape
    scale = HEAD_DIM**-0.5 * LOG2E

    def kernel(q_ref, k_ref, v_ref, s_ref, o_ref, l_ref, vt):
        i = pl.program_id(1)

        @pl.when(i == 0)
        def _():
            vt[...] = v_ref[0].T

        rows = q_ref[0]
        first = s_ref[0]
        base = lax.broadcasted_iota(jnp.int32, (block, block), 0)
        qpos = i * block + lax.broadcasted_iota(jnp.int32, (1, block), 1)

        def one(j, carry, diagonal):
            peak, total, acc = carry
            at = pl.multiple_of(j * block, block)
            s = nt(k_ref[0, pl.ds(at, block)], rows) * scale
            kpos = base + at
            keep = kpos >= first
            if diagonal:
                keep = keep & (kpos <= qpos)
            s = jnp.where(keep, s, NEG_BIG)
            new = jnp.maximum(peak, jnp.max(s, axis=0, keepdims=True))
            p = jnp.exp2(s - new)
            shrink = jnp.exp2(peak - new)
            total = total * shrink + jnp.sum(p, axis=0, keepdims=True)
            acc = acc * shrink + nn(vt[:, pl.ds(at, block)], p.astype(BF16))
            return new, total, acc

        start = (
            jnp.full((1, block), NEG_BIG, F32),
            jnp.zeros((1, block), F32),
            jnp.zeros((HEAD_DIM, block), F32),
        )
        start = one(i, start, True)
        peak, total, acc = lax.fori_loop(0, i, lambda j, c: one(j, c, False), start)
        o_ref[0] = (acc / total).T.astype(BF16)
        l_ref[0] = peak + jnp.log2(total)

    return pl.pallas_call(
        kernel,
        grid=(u, t // block),
        in_specs=[
            pl.BlockSpec((1, block, HEAD_DIM), lambda a, b: (a, b, 0)),
            pl.BlockSpec((1, t, HEAD_DIM), lambda a, b: (a, 0, 0)),
            pl.BlockSpec((1, t, HEAD_DIM), lambda a, b: (a, 0, 0)),
            pl.BlockSpec((1, 1, block), lambda a, b: (a, 0, b)),
        ],
        out_specs=[
            pl.BlockSpec((1, block, HEAD_DIM), lambda a, b: (a, b, 0)),
            pl.BlockSpec((1, 1, block), lambda a, b: (a, 0, b)),
        ],
        out_shape=[
            jax.ShapeDtypeStruct((u, t, HEAD_DIM), BF16),
            jax.ShapeDtypeStruct((u, 1, t), F32),
        ],
        scratch_shapes=[pltpu.VMEM((HEAD_DIM, t), BF16)],
        compiler_params=pltpu.CompilerParams(vmem_limit_bytes=32 * 2**20),
        cost_estimate=pl.CostEstimate(
            flops=2 * u * t * t * HEAD_DIM, bytes_accessed=8 * u * t * 256, transcendentals=u * t * t // 2
        ),
    )(q, k, v, starts)


def attend_back(q, k, v, starts, lse, o, g, block=512):
    u, t, _ = q.shape
    scale = HEAD_DIM**-0.5

    def kernel(q_ref, k_ref, v_ref, s_ref, l_ref, o_ref, g_ref, dq_ref, dk_ref, dv_ref, kt):
        i = pl.program_id(1)

        @pl.when(i == 0)
        def _():
            kt[...] = k_ref[0].T
            dk_ref[...] = jnp.zeros_like(dk_ref)
            dv_ref[...] = jnp.zeros_like(dv_ref)

        rows, grows = q_ref[0], g_ref[0]
        first, logs = s_ref[0], l_ref[0]
        prod = o_ref[0].astype(F32) * grows.astype(F32)
        centre = jnp.sum(prod.T, axis=0, keepdims=True)
        base = lax.broadcasted_iota(jnp.int32, (block, block), 0)
        qpos = i * block + lax.broadcasted_iota(jnp.int32, (1, block), 1)

        def one(j, acc, diagonal):
            at = pl.multiple_of(j * block, block)
            here = pl.ds(at, block)
            p = jnp.exp2(nt(k_ref[0, here], rows) * (scale * LOG2E) - logs)
            kpos = base + at
            keep = kpos >= first
            if diagonal:
                keep = keep & (kpos <= qpos)
            p = jnp.where(keep, p, 0.0)
            gp = nt(v_ref[0, here], grows)
            ds = (p * (gp - centre)).astype(BF16)
            dv_ref[0, here] += nn(p.astype(BF16), grows)
            dk_ref[0, here] += nn(ds, rows) * scale
            return acc + nn(kt[:, here], ds)

        acc = one(i, jnp.zeros((HEAD_DIM, block), F32), True)
        acc = lax.fori_loop(0, i, lambda j, a: one(j, a, False), acc)
        dq_ref[0] = (acc * scale).T

    def whole(a, b):
        return (a, 0, 0)

    def part(a, b):
        return (a, b, 0)

    def row(a, b):
        return (a, 0, b)

    spec, full, line = (1, block, HEAD_DIM), (1, t, HEAD_DIM), (1, 1, block)
    return pl.pallas_call(
        kernel,
        grid=(u, t // block),
        in_specs=[
            pl.BlockSpec(spec, part),
            pl.BlockSpec(full, whole),
            pl.BlockSpec(full, whole),
            pl.BlockSpec(line, row),
            pl.BlockSpec(line, row),
            pl.BlockSpec(spec, part),
            pl.BlockSpec(spec, part),
        ],
        out_specs=[
            pl.BlockSpec(spec, part),
            pl.BlockSpec(full, whole),
            pl.BlockSpec(full, whole),
        ],
        out_shape=[jax.ShapeDtypeStruct((u, t, HEAD_DIM), F32)] * 3,
        scratch_shapes=[pltpu.VMEM((HEAD_DIM, t), BF16)],
        compiler_params=pltpu.CompilerParams(vmem_limit_bytes=48 * 2**20),
        cost_estimate=pl.CostEstimate(
            flops=5 * u * t * t * HEAD_DIM, bytes_accessed=20 * u * t * 256, transcendentals=u * t * t // 2
        ),
    )(q, k, v, starts, lse, o, g)


def body(
    history,
    dense_mix,
    doc_starts,
    norm_gain,
    norm_bias,
    qkv_weight,
    qkv_bias,
    out_weight,
    out_bias,
    up_weight,
    up_bias,
    down_weight,
    down_bias,
    root_gain,
    mix_in_weight,
    mix_out_weight,
    mix_out_bias,
    out_cotangent,
    mix_cotangent,
):
    fn, cn = lax.axis_size("fsdp"), lax.axis_size("ctx")
    dn = fn * cn
    fi, ci = lax.axis_index("fsdp"), lax.axis_index("ctx")
    hist, seqs, length, width = history.shape
    nloc = seqs * length
    ntp = fn * nloc
    rows = qkv_weight.shape[0]
    ff = up_weight.shape[1]
    wcol, fcol = width // fn, ff // fn
    heads = wcol // HEAD_DIM
    units = fn * seqs * heads // cn
    total = cn * length
    mixn = mix_in_weight.shape[1]

    def to_columns(w, cols):
        w = w.reshape(rows, fn, cols).transpose(1, 0, 2)
        return lax.all_to_all(w, "fsdp", 0, 0, tiled=True)

    def rows_over_ctx(w):
        g = lax.all_gather(w, "ctx", axis=0)
        return g.transpose(1, 0, 2, 3).reshape(fn * cn * w.shape[1], w.shape[2])

    qkv_cols = lax.all_to_all(
        qkv_weight.reshape(rows, 3, fn, wcol).transpose(2, 1, 0, 3), "fsdp", 0, 0, tiled=True
    )
    qkv_g = lax.all_gather(qkv_cols, "ctx", axis=0)
    wqkv = qkv_g.transpose(2, 1, 0, 3, 4).reshape(3, width, wcol)
    wup = rows_over_ctx(to_columns(up_weight, fcol))
    wout = lax.all_gather(out_weight, "ctx", axis=0, tiled=True)
    wdown = lax.all_gather(down_weight, "ctx", axis=0, tiled=True)

    parts = [
        norm_gain,
        norm_bias,
        qkv_bias,
        out_bias,
        up_bias,
        down_bias,
        root_gain,
        mix_in_weight,
        doc_starts.astype(F32),
    ]
    flat = jnp.concatenate([a.reshape(-1) for a in parts])
    flat = jnp.pad(flat, (0, -flat.size % 1024)).reshape(-1, 128)
    flats = gather_small(flat).reshape(dn, -1)
    pieces, at = [], 0
    for a in parts:
        pieces.append(flats[:, at : at + a.size])
        at += a.size

    def joined(piece, lead):
        return piece.reshape(dn, lead, -1).transpose(1, 0, 2).reshape(lead, -1)

    gain_all = joined(pieces[0], 4)
    shift_all = joined(pieces[1], 4)
    qkv_shift = joined(pieces[2], 3)
    out_shift = pieces[3].reshape(-1)
    up_shift = pieces[4].reshape(-1)
    down_shift = pieces[5].reshape(-1)
    root_full = pieces[6].reshape(-1)
    mix_in_full = pieces[7].reshape(width, mixn)
    starts = pieces[8].reshape(fn, cn, seqs, -1)[:, 0].astype(jnp.int32)

    hist2 = history.reshape(hist, nloc, width)
    mix2 = dense_mix.reshape(dense_mix.shape[0], hist, nloc)
    streams = jnp.zeros((dense_mix.shape[0], nloc, width), F32)
    for j in range(hist):
        streams = streams + mix2[:, j][..., None] * hist2[j].astype(F32)[None]

    def front_norm(values, gains, shifts):
        return layer_norm(values, gains[:, None, :], shifts[:, None, :])

    normed, front_pull = jax.vjp(front_norm, streams[:3], gain_all[:3], shift_all[:3])
    normed_g = gather_fsdp(normed.astype(BF16), 3).reshape(3, ntp, width)

    bias_cols = lax.dynamic_slice_in_dim(qkv_shift, fi * wcol, wcol, 1)
    projected = dot("snd,sdc->snc", normed_g, wqkv) + bias_cols[:, None, :]
    pos_local = (ci * length + jnp.arange(length, dtype=jnp.int32)).astype(F32)
    cos_l, sin_l = rotary_tables(pos_local, 1.0)
    split = projected.reshape(3, fn * seqs, length, heads, HEAD_DIM)
    turned = rotary(split[:2], cos_l[None, None, :, None], sin_l[None, None, :, None])
    low = jnp.concatenate([turned, split[2:]], axis=0).astype(BF16)

    def to_units(x):
        k = x.shape[0]
        x = x.transpose(1, 3, 0, 2, 4).reshape(cn, units, k, length, HEAD_DIM)
        x = lax.all_to_all(x, "ctx", 0, 0, tiled=True)
        return x.transpose(2, 1, 0, 3, 4).reshape(k, units, total, HEAD_DIM)

    def from_units(x):
        k = x.shape[0]
        x = x.reshape(k, units, cn, length, HEAD_DIM).transpose(2, 1, 0, 3, 4)
        x = lax.all_to_all(x, "ctx", 0, 0, tiled=True)
        x = x.reshape(fn * seqs, heads, k, length, HEAD_DIM).transpose(2, 0, 3, 1, 4)
        return x.reshape(k, ntp, wcol)

    q_u, k_u, v_u = to_units(low)
    pos_all = jnp.arange(total, dtype=jnp.int32)
    unit_ids = ci * units + jnp.arange(units, dtype=jnp.int32)
    seq_ids = unit_ids // heads
    unit_starts = starts.reshape(fn * seqs, -1)[seq_ids]
    first_key = jnp.max(
        jnp.where(unit_starts[:, None, :] <= pos_all[None, :, None], unit_starts[:, None, :], 0),
        axis=-1,
    )[:, None, :]
    att_u, lse_u = attend(q_u, k_u, v_u, first_key)
    attended = from_units(att_u[None])[0]

    def scatter_tokens(x):
        k = x.shape[0]
        x = x.astype(BF16).reshape(k, fn, nloc, width)
        return scatter_fsdp(x, 5 if k == 1 else 6)

    def gather_tokens(x):
        return gather_fsdp(x[None], 4).reshape(ntp, width)

    hidden_res = streams[3] + scatter_tokens(dot("nd,de->ne", attended, wout)[None])[0] + out_shift
    normed_mlp, mid_pull = jax.vjp(layer_norm, hidden_res, gain_all[3], shift_all[3])
    mlp_g = gather_tokens(normed_mlp.astype(BF16))
    up_cols = lax.dynamic_slice_in_dim(up_shift, fi * fcol, fcol, 0)
    upward = dot("nd,df->nf", mlp_g, wup) + up_cols
    activated, gelu_pull = jax.vjp(gelu, upward)
    act_low = activated.astype(BF16)
    result = hidden_res + scatter_tokens(dot("nf,fd->nd", act_low, wdown)[None])[0] + down_shift
    block_out = result.astype(BF16).reshape(seqs, length, width)

    next_rows, mixer_pull = jax.vjp(
        mixer, result, root_full, mix_in_full, mix_out_weight, mix_out_bias
    )
    next_mix = next_rows.T.reshape(-1, seqs, length)
    grad_result, grad_root, grad_mix_in, grad_mix_out, grad_mix_bias = mixer_pull(
        mix_cotangent.reshape(-1, nloc).T
    )
    grad_result = grad_result + out_cotangent.reshape(nloc, width).astype(F32)

    grad_branch = grad_result.astype(BF16)
    branch_g = gather_tokens(grad_branch)
    grad_down_shift = jnp.sum(grad_branch.astype(F32), axis=0)

    def scatter_ctx(x):
        return lax.psum_scatter(x.astype(BF16), "ctx", scatter_dimension=0, tiled=True)

    grad_down = scatter_ctx(dot("nf,nd->fd", act_low, branch_g)).astype(F32)
    grad_active = dot("nd,fd->nf", branch_g, wdown)
    grad_upward = gelu_pull(grad_active)[0].astype(BF16)
    grad_up_shift = jnp.sum(grad_upward.astype(F32), axis=0)

    grad_up_part = dot("nd,nf->df", mlp_g, grad_upward).reshape(fn, cn, rows, fcol)
    grad_up = scatter_ctx(grad_up_part.transpose(1, 0, 2, 3).reshape(-1, fcol))
    grad_up = grad_up.reshape(fn, rows, fcol)
    grad_up = lax.all_to_all(grad_up, "fsdp", 0, 0, tiled=True)
    grad_up = grad_up.transpose(1, 0, 2).reshape(rows, ff).astype(F32)

    grad_mlp = scatter_tokens(dot("nf,df->nd", grad_upward, wup)[None])[0]
    grad_hidden, grad_gain_mid, grad_shift_mid = mid_pull(grad_mlp)
    grad_hidden = grad_hidden + grad_result
    grad_attn = grad_hidden.astype(BF16)
    grad_out_shift = jnp.sum(grad_attn.astype(F32), axis=0)
    attn_g = gather_tokens(grad_attn)
    grad_out = scatter_ctx(dot("nd,ne->de", attended, attn_g)).astype(F32)
    grad_att = dot("ne,de->nd", attn_g, wout).astype(BF16)
    (g_u,) = to_units(grad_att.reshape(1, fn * seqs, length, heads, HEAD_DIM))
    gq, gk, gv = attend_back(q_u, k_u, v_u, first_key, lse_u, att_u, g_u)
    cos_a, sin_a = rotary_tables(pos_all.astype(F32), -1.0)
    grad_units = jnp.stack([rotary(gq, cos_a, sin_a), rotary(gk, cos_a, sin_a), gv]).astype(BF16)
    grad_proj = from_units(grad_units)
    grad_qkv_shift = jnp.sum(grad_proj.astype(F32), axis=1)

    grad_qkv_part = dot("snd,snc->sdc", normed_g, grad_proj).reshape(3, fn, cn, rows, wcol)
    grad_qkv = scatter_ctx(grad_qkv_part.transpose(2, 1, 0, 3, 4).reshape(-1, wcol))
    grad_qkv = grad_qkv.reshape(fn, 3, rows, wcol)
    grad_qkv = lax.all_to_all(grad_qkv, "fsdp", 0, 0, tiled=True)
    grad_qkv = grad_qkv.transpose(2, 1, 0, 3).reshape(rows, 3, width).astype(F32)

    grad_normed = scatter_tokens(dot("snc,sdc->snd", grad_proj, wqkv))
    grad_front, grad_gain_front, grad_shift_front = front_pull(grad_normed)
    grad_streams = jnp.concatenate([grad_front, grad_hidden[None]], axis=0)
    hist_grads, mix_grads = [], []
    for j in range(hist):
        hist_grads.append(jnp.sum(mix2[:, j][..., None] * grad_streams, axis=0))
        mix_grads.append(jnp.sum(hist2[j].astype(F32)[None] * grad_streams, axis=-1))
    grad_history = jnp.stack(hist_grads, axis=0).reshape(history.shape)
    grad_mix = jnp.stack(mix_grads, axis=1).reshape(dense_mix.shape)

    def own_columns(x, full):
        zero = jnp.zeros((x.shape[0], full), F32)
        return lax.dynamic_update_slice_in_dim(zero, x, fi * x.shape[1], 1)

    def parted(x):
        k = x.shape[0]
        return x.reshape(k, dn, -1).transpose(1, 0, 2).reshape(dn, -1)

    sums = [
        parted(jnp.concatenate([grad_gain_front, grad_gain_mid[None]], axis=0)),
        parted(jnp.concatenate([grad_shift_front, grad_shift_mid[None]], axis=0)),
        parted(own_columns(grad_qkv_shift, width)),
        parted(grad_out_shift[None]),
        parted(own_columns(grad_up_shift[None], ff)),
        parted(grad_down_shift[None]),
        parted(grad_root[None]),
        grad_mix_in.reshape(dn, -1),
    ]
    same = jnp.concatenate([grad_mix_out.reshape(-1), grad_mix_bias])
    sums.append(jnp.broadcast_to(same[None], (dn, same.size)))
    flat = jnp.concatenate(sums, axis=1)
    flat = jnp.pad(flat, ((0, 0), (0, -flat.shape[1] % 1024)))
    small = scatter_small(flat.reshape(dn, -1, 128)).reshape(-1)
    out_small, at = [], 0
    for s, shape in zip(sums[:-1], [a.shape for a in parts[:-1]], strict=True):
        out_small.append(small[at : at + s.shape[1]].reshape(shape))
        at += s.shape[1]
    (g_gain, g_shift, g_qkv_b, g_out_b, g_up_b, g_down_b, g_root, g_mix_in) = out_small
    mix_sums = small[at : at + same.size]
    cut = grad_mix_out.size
    return (
        block_out,
        next_mix,
        grad_history,
        grad_mix,
        g_gain,
        g_shift,
        grad_qkv,
        g_qkv_b,
        grad_out,
        g_out_b,
        grad_up,
        g_up_b,
        grad_down,
        g_down_b,
        g_root,
        g_mix_in,
        mix_sums[:cut].reshape(grad_mix_out.shape),
        mix_sums[cut:],
    )


def solution(mesh):
    token = P(None, "fsdp", "ctx")
    both = P(BOTH)
    cols = P(None, BOTH)
    placed = (
        token,
        P(None, None, "fsdp", "ctx"),
        P("fsdp"),
        cols,
        cols,
        both,
        cols,
        both,
        both,
        both,
        both,
        both,
        both,
        both,
        both,
        P(),
        P(),
        P("fsdp", "ctx"),
        token,
    )
    outs = (
        P("fsdp", "ctx"),
        token,
        token,
        P(None, None, "fsdp", "ctx"),
        cols,
        cols,
        both,
        cols,
        both,
        both,
        both,
        both,
        both,
        both,
        both,
        both,
        P(),
        P(),
    )
    return jax.shard_map(body, mesh=mesh, in_specs=placed, out_specs=outs, check_vma=False)
```

time: 6100 us -> 1300 us (0.21)
  waiting for transfers between devices: 5040 us -> 228 us
  Pallas kernels: 0 us -> 457 us
  blocking collectives: 421 us -> 143 us
  matrix products: 352 us -> 172 us
    reduce_scatter x5 -> x4, waiting for transfers between devices: 3370 us -> 51.6 us  [scatter_ctx(): lax.psum_scatter(x.astype(BF16), 'ctx', scatter_dimension=0, tiled=True)]
    unnamed x21 -> x8, waiting for transfers between devices: 1200 us -> 1.3 us
    all_gather x6 -> x4, waiting for transfers between devices: 463 us -> 0.06 us  [the longest x1 0.02 us: rows_over_ctx(): g = lax.all_gather(w, 'ctx', axis=0)]
    pallas_call x0 -> x12, Pallas kernels: none -> 457 us  [the longest x4 201 us: gather_fsdp(): pl.pallas_call(kernel, out_shape=jax.ShapeDtypeStruct((k_count, fn, n, d)...]
    all_gather x5 -> x0, blocking collectives: 335 us -> none  [the longest x1 76.5 us: body(): lax.all_gather(mix_in_weight, ('fsdp', 'ctx'), axis=0, tiled=True)]
    dot_general x23 -> x18, matrix products: 348 us -> 172 us  [the longest x12 159 us: dot(): return jnp.einsum(pattern, left, right, preferred_element_type=F32)]
    all_to_all x0 -> x5, waiting for transfers between devices: none -> 175 us  [the longest x2 123 us: to_units(): x = lax.all_to_all(x, 'ctx', 0, 0, tiled=True)]
    all_to_all x0 -> x3, blocking collectives: none -> 143 us  [the longest x1 111 us: from_units(): x = lax.all_to_all(x, 'ctx', 0, 0, tiled=True)]
  transfers between devices with their start and end apart: 16 -> 13, of which waited for: 12 -> 5; matrix products, arithmetic and copies ran while one was open for 8% -> 26% of each run, Pallas kernels for 0% -> 26%
where the time goes in v1:
time: 1300 us
  Pallas kernels  457 us (35%)
  waiting for transfers between devices  228 us (18%)
  matrix products  172 us (13%)
  local copies, waits for them, and re-layouts  149 us (11%)
  blocking collectives  143 us (11%)
  other arithmetic  108 us (8%)
  starting transfers between devices  22.9 us (2%)
  between operations  16.1 us (1%)
    pallas_call x4, Pallas kernels, gather_fsdp(): pl.pallas_call(kernel, out_shape=jax.ShapeDtypeStruct((k_count, fn, n, d)...  201 us
    pallas_call x4, Pallas kernels, scatter_fsdp(): pl.pallas_call(kernel, out_shape=jax.ShapeDtypeStruct((k_count, n, d), F3...  161 us
    dot_general x12, matrix products, dot(): return jnp.einsum(pattern, left, right, preferred_element_type=F32)  159 us
    all_to_all x2, waiting for transfers between devices, to_units(): x = lax.all_to_all(x, 'ctx', 0, 0, tiled=True)  123 us
    all_to_all x1, blocking collectives, from_units(): x = lax.all_to_all(x, 'ctx', 0, 0, tiled=True)  111 us
    reduce_scatter x4, waiting for transfers between devices, scatter_ctx(): lax.psum_scatter(x.astype(BF16), 'ctx', scatter_dimension=0, tiled=True)  51.6 us
    all_to_all x1, waiting for transfers between devices, from_units(): x = lax.all_to_all(x, 'ctx', 0, 0, tiled=True)  39.9 us
    unnamed x239, local copies, waits for them, and re-layouts  33.4 us
  transfers between devices with their start and end apart: 13, of which 5 were waited for; matrix products, arithmetic and copies ran while one was open for 26% of the time, Pallas kernels for 26%

profile of v1, /device:TPU:1, one launch (start us, length us, event | category | flops | bytes accessed | tf_op | source)
XLA Modules:
  0.0 1297.0 jit_solution(14669289774622007009)
XLA Ops:
  9.8 14.8 %all_to_all.40 = bf16[4,3,64,512]{3,2,1,0:T(8,128)(2,1)} all-to-all(bf16[4,3,64,512]{3,2,1,0:T(8,128)(2,1)S(1)} %copy.236), channel_id=1, replica_groups=mesh['fsdp'=4,'ctx'=8] {'fsdp'}, dimensions={0} | all-to-all | bytes 1572864 | tf_op jit(solution)/shard_map/all_to_all | solution.py:534
  27.1 17.9 %all_to_all.41 = bf16[4,64,2048]{2,1,0:T(8,128)(2,1)} all-to-all(bf16[4,64,2048]{2,1,0:T(8,128)(2,1)S(1)} %copy.252), channel_id=1, replica_groups=mesh['fsdp'=4,'ctx'=8] {'fsdp'}, dimensions={0} | all-to-all | bytes 2097152 | tf_op jit(solution)/shard_map/all_to_all | solution.py:528
  46.9 29.3 %shard_map.322 = f32[32,32,128]{2,1,0:T(8,128)} custom-call(f32[32,128]{1,0:T(8,128)} %pad_bitcast_fusion.1.x_ref), custom_call_target="tpu_custom_call" | custom-call | tf_op jit(solution)/shard_map/pallas_call | solution.py:122
  78.4 5.4 bitcast_convert_fusion.8
  84.1 5.9 multiply_add_fusion
  94.1 5.0 add_convert_fusion.1.x_ref
  99.1 98.7 %shard_map.323 = bf16[3,4,256,2048]{3,2,1,0:T(8,128)(2,1)} custom-call(bf16[3,256,2048]{2,1,0:T(8,128)(2,1)} %add_convert_fusion.1.x_ref), custom_call_target="tpu_custom_call" | custom-call | tf_op jit(solution)/shard_map/pallas_call | solution.py:233
  198.5 6.9 copy.237
  207.2 10.5 broadcast_add_fusion.1
  217.7 4.6 slice.298
  224.0 5.2 slice.247
  229.3 3.3 slice.301
  235.9 6.0 fusion.56
  243.1 3.1 pad_maximum_fusion.1
  246.3 3.7 all-to-all-start.1
  252.0 93.1 %all-to-all-done.1 = bf16[8,2,3,256,128]{4,3,2,1,0:T(8,128)(2,1)S(1)} async-done(((bf16[8,2,3,256,128]{4,3,2,1,0:T(8,128)(2,1)}), bf16[8,2,3,256,128]{4,3,2,1,0:T(8,128)(2,1)S(1)}, u32[]{:S(2)}, u32[]{:S(2)}) %all-to-all-start.1) | async-done | bytes 3145760 | tf_op jit(solution)/shard_map/all_to_all | solution.py:598
  346.6 15.3 %shard_map.324 = (bf16[2,2048,128]{2,1,0:T(8,128)(2,1)S(1)}, f32[2,1,2048]{2,1,0:T(1,128)S(1)}) custom-call(bf16[2,2048,128]{2,1,0:T(8,128)(2,1)S(1)} %bitcast.289, bf16[2,2048,128]{2,1,0:T(8,128)(2,1)S(1)} %bitcast.291, bf16[2,2048,128]{2,1,0:T(8,128)(2,1)S(1)} %bitcast.293, s32[2,1,2048]{2,1,0:T(1,128)S(1)} %broadcast_in_dim.37.s_ref), custom_call_target="tpu_custom_call" | custom-call | flops 2147483648 | bytes 8388608 | tf_op jit(solution)/shard_map/pallas_call | solution.py:391
  364.0 3.6 all-to-all-start.2
  370.2 8.5 copy.253
  378.7 39.9 %all-to-all-done.2 = bf16[8,2,1,256,128]{4,3,1,2,0:T(8,128)(2,1)S(1)} async-done(((bf16[8,2,1,256,128]{4,3,1,2,0:T(8,128)(2,1)}), bf16[8,2,1,256,128]{4,3,1,2,0:T(8,128)(2,1)S(1)}, u32[]{:S(2)}, u32[]{:S(2)}) %all-to-all-start.2) | async-done | bytes 1048608 | tf_op jit(solution)/shard_map/all_to_all | solution.py:604
  419.5 6.3 convolution_convert_fusion.5
  425.8 29.8 %shard_map.325 = f32[1,256,2048]{2,1,0:T(8,128)} custom-call(bf16[1,4,256,2048]{3,2,1,0:T(8,128)(2,1)} %bitcast.322), custom_call_target="tpu_custom_call" | custom-call | tf_op jit(solution)/shard_map/pallas_call | solution.py:318
  455.6 2.6 fusion.18
  460.0 34.4 %shard_map.326 = bf16[1,4,256,2048]{3,2,1,0:T(8,128)(2,1)} custom-call(bf16[1,256,2048]{2,1,0:T(8,128)(2,1)} %add_convert_fusion.5.x_ref), custom_call_target="tpu_custom_call" | custom-call | tf_op jit(solution)/shard_map/pallas_call | solution.py:233
  494.5 31.9 %multiply_convert_fusion = (bf16[1024,2048]{1,0:T(8,128)(2,1)}, f32[1024,2048]{1,0:T(8,128)}, f32[1024,2048]{1,0:T(8,128)}) fusion(f32[2048]{0:T(1024)S(1)} %dynamic_slice.7, bf16[1024,2048]{1,0:T(8,128)(2,1)} %bitcast.303, bf16[2048,2048]{1,0:T(8,128)(2,1)} %bitcast.311), kind=kOutput, calls=%fused_computation.26 | convolution fusion | flops 8728346624 | bytes 33562624 | tf_op jit(solution)/shard_map/nd,df->nf/dot_general | solution.py:58
  526.4 14.0 %convolution_convert_fusion.4 = bf16[1024,2048]{1,0:T(8,128)(2,1)} fusion(bf16[1024,2048]{1,0:T(8,128)(2,1)} %get-tuple-element.190, bf16[2048,2048]{1,0:T(8,128)(2,1)} %all-gather.9.cloned.1.call-done), kind=kOutput, calls=%fused_computation.56 | convolution fusion | flops 8592031744 | bytes 16777216 | tf_op jit(solution)/shard_map/nf,fd->nd/dot_general | solution.py:58
  540.4 28.4 %shard_map.327 = f32[1,256,2048]{2,1,0:T(8,128)} custom-call(bf16[1,4,256,2048]{3,2,1,0:T(8,128)(2,1)} %bitcast.323), custom_call_target="tpu_custom_call" | custom-call | tf_op jit(solution)/shard_map/pallas_call | solution.py:318
  573.6 3.0 multiply_reduce_fusion.21
  580.6 33.7 %shard_map.328 = bf16[1,4,256,2048]{3,2,1,0:T(8,128)(2,1)} custom-call(bf16[1,256,2048]{2,1,0:T(8,128)(2,1)} %convert_bitcast_fusion.4.x_ref), custom_call_target="tpu_custom_call" | custom-call | tf_op jit(solution)/shard_map/pallas_call | solution.py:233
  614.2 19.4 %convert_reduce_fusion = (f32[2048]{0:T(1024)}, bf16[1024,2048]{1,0:T(8,128)(2,1)S(1)}) fusion(f32[1024,2048]{1,0:T(8,128)} %get-tuple-element.191, f32[1024,2048]{1,0:T(8,128)} %get-tuple-element.247, f32[2048]{0:T(1024)S(1)} %dynamic_slice.7, bf16[1024,2048]{1,0:T(8,128)(2,1)} %bitcast.317, bf16[2048,2048]{1,0:T(8,128)(2,1)} %all-gather.9.cloned.1.call-done), kind=kOutput, calls=%fused_computation.6 | convolution fusion | flops 8625584128 | bytes 33570816 | tf_op jit(solution)/shard_map/nd,fd->nf/dot_general | solution.py:58
  633.6 14.1 %convolution_convert_fusion.3 = bf16[1024,2048]{1,0:T(8,128)(2,1)} fusion(bf16[1024,2048]{1,0:T(8,128)(2,1)S(1)} %get-tuple-element.183, bf16[2048,2048]{1,0:T(8,128)(2,1)} %bitcast.312), kind=kOutput, calls=%fused_computation.55 | convolution fusion | flops 8592031744 | bytes 16777216 | tf_op jit(solution)/shard_map/nf,df->nd/dot_general | solution.py:58
  647.7 28.5 %shard_map.329 = f32[1,256,2048]{2,1,0:T(8,128)} custom-call(bf16[1,4,256,2048]{3,2,1,0:T(8,128)(2,1)} %bitcast.321), custom_call_target="tpu_custom_call" | custom-call | tf_op jit(solution)/shard_map/pallas_call | solution.py:318
  676.3 3.1 fusion.8
  685.1 34.1 %shard_map.330 = bf16[1,4,256,2048]{3,2,1,0:T(8,128)(2,1)} custom-call(bf16[1,256,2048]{2,1,0:T(8,128)(2,1)} %convert_bitcast_fusion.3.x_ref), custom_call_target="tpu_custom_call" | custom-call | tf_op jit(solution)/shard_map/pallas_call | solution.py:233
  719.2 5.9 convolution_convert_fusion.6
  725.2 6.8 copy.270
  732.0 13.9 %convert_bitcast_fusion = bf16[8,4,64,2048]{3,2,0,1:T(8,128)(2,1)} fusion(bf16[4,8,64,1024]{3,2,1,0:T(8,128)(2,1)} %bitcast.324, bf16[1024,2048]{1,0:T(8,128)(2,1)} %copy-done.105), kind=kOutput, calls=%fused_computation.5 | convolution fusion | flops 8594128896 | bytes 16777216 | tf_op jit(solution)/shard_map/nd,nf->df/dot_general | solution.py:58
  745.9 8.4 copy.271
  755.8 5.6 convolution_convert_fusion.7
  763.7 2.4 copy.254
  766.1 4.2 all-to-all-start.4
  773.7 30.3 %all-to-all-done.4 = bf16[8,2,1,256,128]{4,3,1,2,0:T(8,128)(2,1)} async-done(((bf16[8,2,1,256,128]{4,3,1,2,0:T(8,128)(2,1)}), bf16[8,2,1,256,128]{4,3,1,2,0:T(8,128)(2,1)}, u32[]{:S(2)}, u32[]{:S(2)}) %all-to-all-start.4) | async-done | bytes 1048608 | tf_op jit(solution)/shard_map/all_to_all | solution.py:598
  806.6 20.7 %shard_map.331 = (f32[2,2048,128]{2,1,0:T(8,128)}, f32[2,2048,128]{2,1,0:T(8,128)}, f32[2,2048,128]{2,1,0:T(8,128)}) custom-call(bf16[2,2048,128]{2,1,0:T(8,128)(2,1)S(1)} %bitcast.290, bf16[2,2048,128]{2,1,0:T(8,128)(2,1)S(1)} %bitcast.292, bf16[2,2048,128]{2,1,0:T(8,128)(2,1)S(1)} %bitcast.294, s32[2,1,2048]{2,1,0:T(1,128)S(1)} %copy-done.10, ...), custom_call_target="tpu_custom_call" | custom-call | flops 5368709120 | bytes 20971520 | tf_op jit(solution)/shard_map/pallas_call | solution.py:465
  837.4 110.8 %all_to_all.42 = bf16[8,2,3,256,128]{4,3,2,1,0:T(8,128)(2,1)S(1)} all-to-all(bf16[8,2,3,256,128]{4,3,2,1,0:T(8,128)(2,1)S(1)} %copy_bitcast_fusion), channel_id=1, replica_groups=mesh['fsdp'=4,'ctx'=8] {'ctx'}, dimensions={0} | all-to-all | bytes 6291456 | tf_op jit(solution)/shard_map/all_to_all | solution.py:604
  949.8 2.4 copy.262
  952.3 3.2 reshape.743
  955.5 10.6 convolution_convert_fusion.2
  966.2 3.1 copy.268
  971.6 14.4 %convolution_convert_fusion = bf16[2048,2048]{1,0:T(8,128)(2,1)} fusion(bf16[1024,2048]{1,0:T(8,128)(2,1)} %get-tuple-element.190, bf16[1024,2048]{1,0:T(8,128)(2,1)} %bitcast.318), kind=kOutput, calls=%fused_computation.41 | convolution fusion | flops 8594128896 | bytes 16777216 | tf_op jit(solution)/shard_map/nf,nd->fd/dot_general | solution.py:58
  986.7 5.2 fusion.12
  1005.3 3.1 fusion.28
  1010.2 12.9 convolution_convert_fusion.1
  1023.1 73.9 %shard_map.332 = f32[3,256,2048]{2,1,0:T(8,128)} custom-call(bf16[3,4,256,2048]{3,2,1,0:T(8,128)(2,1)} %bitcast.305), custom_call_target="tpu_custom_call" | custom-call | tf_op jit(solution)/shard_map/pallas_call | solution.py:318
  1097.0 6.2 fusion.51
  1103.4 5.2 multiply_reduce_fusion.18
  1121.1 30.4 %shard_map.333 = f32[48,128]{1,0:T(8,128)} custom-call(f32[32,48,128]{2,1,0:T(8,128)} %bitcast.331), custom_call_target="tpu_custom_call" | custom-call | tf_op jit(solution)/shard_map/pallas_call | solution.py:166
  1152.3 7.6 broadcast_add_fusion
  1160.0 22.3 %multiply_reduce_fusion.1 = (f32[4,256]{1,0:T(4,128)S(1)}, f32[256,2048]{1,0:T(8,128)}, f32[256,2048]{1,0:T(8,128)}, f32[256,2048]{1,0:T(8,128)}, f32[4,256]{1,0...) fusion(f32[256,2048]{1,0:T(8,128)} %copy-done.25, ...), kind=kLoop, calls=%fused_computation.8 | loop fusion | flops 48230400 | bytes 33603584 | tf_op jit(solution)/shard_map/reduce_sum | solution.py:692
  1182.3 8.4 multiply_reduce_fusion.2
  1202.7 6.5 all-to-all-start.7
  1211.2 11.5 all-to-all-done.7
  1222.8 4.3 all-to-all-start.6
  1232.3 51.6 %reduce-scatter.11.cloned.1.call-done = bf16[256,2048]{1,0:T(8,128)(2,1)} async-done(((bf16[2048,2048]{1,0:T(8,128)(2,1)}), bf16[256,2048]{1,0:T(8,128)(2,1)}) %reduce-scatter.11.cloned.1.call-update) | async-done | bytes 1048592 | tf_op jit(solution)/shard_map/reduce_scatter | solution.py:652
  1283.9 2.8 convert_element_type.314
  (405 shorter events, 122.4 us)
Async XLA Ops:
  7.2 566.2 %copy-start = (f32[40,40]{1,0:T(8,128)S(1)}, f32[40,40]{1,0:T(8,128)}, u32[]{:S(2)}) copy-start(f32[40,40]{1,0:T(8,128)} %param.34) | copy-start | bytes 19204
  7.2 38.6 %copy-start.93 = (f32[64,40]{0,1:T(8,128)S(1)}, f32[64,40]{0,1:T(8,128)}, u32[]{:S(2)}) copy-start(f32[64,40]{0,1:T(8,128)} %param.33) | copy-start | bytes 30724
  7.2 38.7 %copy-start.96 = (f32[4,64]{1,0:T(4,128)S(1)}, f32[4,64]{1,0:T(4,128)}, u32[]{:S(2)}) copy-start(f32[4,64]{1,0:T(4,128)} %param.22) | copy-start | bytes 3076
  7.2 38.8 %copy-start.97 = (f32[4,64]{1,0:T(4,128)S(1)}, f32[4,64]{1,0:T(4,128)}, u32[]{:S(2)}) copy-start(f32[4,64]{1,0:T(4,128)} %param.23) | copy-start | bytes 3076
  7.2 38.9 %copy-start.98 = (f32[3,64]{1,0:T(4,128)S(1)}, f32[3,64]{1,0:T(4,128)}, u32[]{:S(2)}) copy-start(f32[3,64]{1,0:T(4,128)} %param.25) | copy-start | bytes 2308
  7.2 39.0 %copy-start.104 = (s32[1,8]{1,0:T(1,128)S(1)}, s32[1,8]{1,0:T(1,128)}, u32[]{:S(2)}) copy-start(s32[1,8]{1,0:T(1,128)} %param.21) | copy-start | bytes 100
  7.3 39.0 %copy-start.99 = (f32[256]{0:T(256)S(1)}, f32[256]{0:T(256)}, u32[]{:S(2)}) copy-start(f32[256]{0:T(256)} %param.29) | copy-start | bytes 3076
  7.3 39.0 %copy-start.100 = (f32[64]{0:T(128)S(1)}, f32[64]{0:T(128)}, u32[]{:S(2)}) copy-start(f32[64]{0:T(128)} %param.27) | copy-start | bytes 772
  7.3 39.0 %copy-start.101 = (f32[64]{0:T(128)S(1)}, f32[64]{0:T(128)}, u32[]{:S(2)}) copy-start(f32[64]{0:T(128)} %param.31) | copy-start | bytes 772
  7.3 39.0 %copy-start.102 = (f32[64]{0:T(128)S(1)}, f32[64]{0:T(128)}, u32[]{:S(2)}) copy-start(f32[64]{0:T(128)} %param.32) | copy-start | bytes 772
  7.3 191.2 %all-gather.11.cloned.1.call-start = ((), (), s32[]{:S(2)}) async-start(), calls=%async_computation.18 | async-start | bytes 7077888 | tf_op jit(solution)/shard_map/all_gather | solution.py:537
  24.6 345.6 %all-gather.13.cloned.1.call-start = ((), (), s32[]{:S(2)}) async-start(), calls=%async_computation.19 | async-start | bytes 9437184 | tf_op jit(solution)/shard_map/all_gather | solution.py:531
  45.0 374.4 %all-gather.7.cloned.1.call-start = ((), (), s32[]{:S(2)}) async-start(), calls=%async_computation.12 | async-start | bytes 2359296 | tf_op jit(solution)/shard_map/all_gather | solution.py:540
  78.4 119.7 %copy-start.94 = (f32[16]{0:T(128)}, f32[16]{0:T(128)S(1)}, u32[]{:S(2)}) copy-start(f32[16]{0:T(128)S(1)} %multiply_exponential_fusion) | copy-start | bytes 196
  90.8 8.3 copy-start.63
  93.6 104.2 %copy-start.86 = (f32[3,256]{1,0:T(4,128)}, f32[3,256]{1,0:T(4,128)S(1)}, u32[]{:S(2)}) copy-start(f32[3,256]{1,0:T(4,128)S(1)} %multiply_reduce_fusion.20) | copy-start | bytes 9220
  93.6 104.2 %copy-start.68 = (f32[3,256]{1,0:T(4,128)}, f32[3,256]{1,0:T(4,128)S(1)}, u32[]{:S(2)}) copy-start(f32[3,256]{1,0:T(4,128)S(1)} %fusion.45) | copy-start | bytes 9220
  93.8 104.0 %copy-start.51 = (f32[3,2048]{1,0:T(4,128)}, f32[3,2048]{1,0:T(4,128)S(1)}, u32[]{:S(2)}) copy-start(f32[3,2048]{1,0:T(4,128)S(1)} %mul.758) | copy-start | bytes 73732
  93.9 103.9 %copy-start.59 = (f32[32,4,64]{2,1,0:T(4,128)}, f32[32,4,64]{2,1,0:T(4,128)S(1)}, u32[]{:S(2)}) copy-start(f32[32,4,64]{2,1,0:T(4,128)S(1)} %reshape.719) | copy-start | bytes 98308
  198.5 8.7 copy-start.35
  246.3 98.8 %all-to-all-start.1 = ((bf16[8,2,3,256,128]{4,3,2,1,0:T(8,128)(2,1)}), bf16[8,2,3,256,128]{4,3,2,1,0:T(8,128)(2,1)S(1)}, u32[]{:S(2)}, u32[]{:S(2)}) async-start(bf16[8,2,3,256,128]{4,3,2,1,0:T(8,128)(2,1)} %bitcast.307), calls=%async_computation.1 | async-start | bytes 6291456 | tf_op jit(solution)/shard_map/all_to_all | solution.py:598
  249.9 276.5 %all-gather.9.cloned.1.call-start = ((), (), s32[]{:S(2)}) async-start(), calls=%async_computation.13 | async-start | bytes 9437184 | tf_op jit(solution)/shard_map/all_gather | solution.py:541
  252.0 93.6 %copy-start.9 = (s32[2,1,2048]{2,1,0:T(1,128)}, s32[2,1,2048]{2,1,0:T(1,128)S(1)}, u32[]{:S(2)}) copy-start(s32[2,1,2048]{2,1,0:T(1,128)S(1)} %broadcast_in_dim.37.s_ref) | copy-start | bytes 49156
  345.4 17.6 %copy-start.1 = (bf16[1,2,8,256,128]{4,3,2,1,0:T(8,128)(2,1)}, bf16[1,2,8,256,128]{4,3,2,1,0:T(8,128)(2,1)S(1)}, u32[]{:S(2)}) copy-start(bf16[1,2,8,256,128]{4,3,2,1,0:T(8,128)(2,1)S(1)} %copy.245) | copy-start | bytes 3145732
  345.6 16.3 %copy-start.5 = (bf16[1,2,8,256,128]{4,3,2,1,0:T(8,128)(2,1)}, bf16[1,2,8,256,128]{4,3,2,1,0:T(8,128)(2,1)S(1)}, u32[]{:S(2)}) copy-start(bf16[1,2,8,256,128]{4,3,2,1,0:T(8,128)(2,1)S(1)} %copy.247) | copy-start | bytes 3145732
  345.6 22.3 %copy-start.47 = (f32[4,8,32,128]{3,1,2,0:T(8,128)S(1)}, f32[4,8,32,128]{3,1,2,0:T(8,128)}, u32[]{:S(2)}) copy-start(f32[4,8,32,128]{3,1,2,0:T(8,128)} %copy-done.46) | copy-start | bytes 1572868
  364.0 54.6 %all-to-all-start.2 = ((bf16[8,2,1,256,128]{4,3,1,2,0:T(8,128)(2,1)}), bf16[8,2,1,256,128]{4,3,1,2,0:T(8,128)(2,1)S(1)}, u32[]{:S(2)}, u32[]{:S(2)}) async-start(bf16[8,2,1,256,128]{4,3,1,2,0:T(8,128)(2,1)} %bitcast.284), calls=%async_computation.2 | async-start | bytes 2097152 | tf_op jit(solution)/shard_map/all_to_all | solution.py:604
  367.6 640.8 %reduce-scatter.7.cloned.1.call-start = ((), (), s32[]{:S(2)}) async-start(), calls=%async_computation.15 | async-start | bytes 2359296 | tf_op jit(solution)/shard_map/reduce_scatter | solution.py:652
  369.2 201.9 %copy-start.65 = (f32[2048]{0:T(1024)}, f32[2048]{0:T(1024)S(1)}, u32[]{:S(2)}) copy-start(f32[2048]{0:T(1024)S(1)} %add.275) | copy-start | bytes 24580
  369.3 207.3 %copy-start.61 = (f32[2048]{0:T(1024)}, f32[2048]{0:T(1024)S(1)}, u32[]{:S(2)}) copy-start(f32[2048]{0:T(1024)S(1)} %mul.787) | copy-start | bytes 24580
  458.1 221.3 %copy-start.12 = (f32[1,256,2048]{2,1,0:T(8,128)}, f32[1,256,2048]{2,1,0:T(8,128)S(1)}, u32[]{:S(2)}) copy-start(f32[1,256,2048]{2,1,0:T(8,128)S(1)} %get-tuple-element.193) | copy-start | bytes 6291460
  633.6 14.1 %copy-start.105 = (bf16[1024,2048]{1,0:T(8,128)(2,1)}, bf16[1024,2048]{1,0:T(8,128)(2,1)S(1)}, u32[]{:S(2)}) copy-start(bf16[1024,2048]{1,0:T(8,128)(2,1)S(1)} %get-tuple-element.183) | copy-start | bytes 12582916
  681.7 37.5 %copy-start.49 = (bf16[1,4,256,4,128]{4,3,2,1,0:T(4,128)(2,1)S(1)}, bf16[1,4,256,4,128]{4,3,2,1,0:T(4,128)(2,1)}, u32[]{:S(2)}) copy-start(bf16[1,4,256,4,128]{4,3,2,1,0:T(4,128)(2,1)} %copy-done.48) | copy-start | bytes 3145732
  725.1 477.6 %reduce-scatter.9.cloned.1.call-start = ((), (), s32[]{:S(2)}) async-start(), calls=%async_computation.16 | async-start | bytes 9437184 | tf_op jit(solution)/shard_map/reduce_scatter | solution.py:652
  761.4 9.0 copy-start.95
  761.4 43.9 %copy-start.2 = (bf16[1,2,8,256,128]{4,3,2,1,0:T(8,128)(2,1)S(1)}, bf16[1,2,8,256,128]{4,3,2,1,0:T(8,128)(2,1)}, u32[]{:S(2)}) copy-start(bf16[1,2,8,256,128]{4,3,2,1,0:T(8,128)(2,1)} %copy-done.1) | copy-start | bytes 3145732
  761.4 43.9 %copy-start.4 = (bf16[1,2,8,256,128]{4,3,2,1,0:T(8,128)(2,1)S(1)}, bf16[1,2,8,256,128]{4,3,2,1,0:T(8,128)(2,1)}, u32[]{:S(2)}) copy-start(bf16[1,2,8,256,128]{4,3,2,1,0:T(8,128)(2,1)} %copy-done.3) | copy-start | bytes 3145732
  761.4 43.9 %copy-start.6 = (bf16[1,2,8,256,128]{4,3,2,1,0:T(8,128)(2,1)S(1)}, bf16[1,2,8,256,128]{4,3,2,1,0:T(8,128)(2,1)}, u32[]{:S(2)}) copy-start(bf16[1,2,8,256,128]{4,3,2,1,0:T(8,128)(2,1)} %copy-done.5) | copy-start | bytes 3145732
  761.4 43.9 %copy-start.10 = (s32[2,1,2048]{2,1,0:T(1,128)S(1)}, s32[2,1,2048]{2,1,0:T(1,128)}, u32[]{:S(2)}) copy-start(s32[2,1,2048]{2,1,0:T(1,128)} %copy-done.9) | copy-start | bytes 49156
  766.1 37.8 %all-to-all-start.4 = ((bf16[8,2,1,256,128]{4,3,1,2,0:T(8,128)(2,1)}), bf16[8,2,1,256,128]{4,3,1,2,0:T(8,128)(2,1)}, u32[]{:S(2)}, u32[]{:S(2)}) async-start(bf16[8,2,1,256,128]{4,3,1,2,0:T(8,128)(2,1)} %bitcast.327), calls=%async_computation.4 | async-start | bytes 2097152 | tf_op jit(solution)/shard_map/all_to_all | solution.py:598
  770.4 452.4 %reduce-scatter.5.cloned.1.call-start = ((), (), s32[]{:S(2)}) async-start(), calls=%async_computation.14 | async-start | bytes 7077888 | tf_op jit(solution)/shard_map/reduce_scatter | solution.py:652
  969.3 314.6 %reduce-scatter.11.cloned.1.call-start = ((), (), s32[]{:S(2)}) async-start(), calls=%async_computation.17 | async-start | bytes 9437184 | tf_op jit(solution)/shard_map/reduce_scatter | solution.py:652
  985.9 9.3 copy-start.54
  985.9 19.4 %copy-start.13 = (f32[1,256,2048]{2,1,0:T(8,128)S(1)}, f32[1,256,2048]{2,1,0:T(8,128)}, u32[]{:S(2)}) copy-start(f32[1,256,2048]{2,1,0:T(8,128)} %copy-done.12) | copy-start | bytes 6291460
  986.0 19.3 %copy-start.66 = (f32[2048]{0:T(1024)S(1)}, f32[2048]{0:T(1024)}, u32[]{:S(2)}) copy-start(f32[2048]{0:T(1024)} %copy-done.65) | copy-start | bytes 24580
  1023.0 73.9 %copy-start.52 = (f32[3,2048]{1,0:T(4,128)S(1)}, f32[3,2048]{1,0:T(4,128)}, u32[]{:S(2)}) copy-start(f32[3,2048]{1,0:T(4,128)} %copy-done.51) | copy-start | bytes 73732
  1023.0 73.9 %copy-start.64 = (f32[3,256]{1,0:T(4,128)S(1)}, f32[3,256]{1,0:T(4,128)}, u32[]{:S(2)}) copy-start(f32[3,256]{1,0:T(4,128)} %copy-done.63) | copy-start | bytes 9220
  1103.4 14.2 %copy-start.21 = (bf16[8,2,3,256,128]{4,3,2,1,0:T(8,128)(2,1)S(1)}, bf16[8,2,3,256,128]{4,3,2,1,0:T(8,128)(2,1)}, u32[]{:S(2)}) copy-start(bf16[8,2,3,256,128]{4,3,2,1,0:T(8,128)(2,1)} %copy-done.20) | copy-start | bytes 9437188
  1103.4 15.7 %copy-start.67 = (f32[32,64]{1,0:T(8,128)S(1)}, f32[32,64]{1,0:T(8,128)}, u32[]{:S(2)}) copy-start(f32[32,64]{1,0:T(8,128)} %reshape_transpose_reshape_broadcast_in_dim.9) | copy-start | bytes 24580
  1152.2 7.7 copy-start.19
  1152.2 7.7 copy-start.71
  1152.2 7.7 copy-start.73
  1152.2 7.7 copy-start.75
  1152.2 7.7 copy-start.77
  1152.2 7.7 copy-start.79
  1152.2 7.7 copy-start.81
  1152.2 7.7 copy-start.83
  1152.3 7.7 copy-start.85
  1160.0 22.3 %copy-start.90 = (f32[4,256]{1,0:T(4,128)S(1)}, f32[4,256]{1,0:T(4,128)}, u32[]{:S(2)}) copy-start(f32[4,256]{1,0:T(4,128)} %copy-done.89) | copy-start | bytes 12292
  1182.3 10.1 copy-start.43
  1199.7 9.4 copy-start.60
  1199.7 10.0 copy-start.36
  1202.7 20.1 %all-to-all-start.7 = ((bf16[4,64,2048]{2,1,0:T(8,128)(2,1)}), bf16[4,64,2048]{2,1,0:T(8,128)(2,1)S(1)}, u32[]{:S(2)}, u32[]{:S(2)}) async-start(bf16[4,64,2048]{2,1,0:T(8,128)(2,1)} %bitcast.341), calls=%async_computation.10 | async-start | bytes 2097152 | tf_op jit(solution)/shard_map/all_to_all | solution.py:662
  1222.8 65.7 %all-to-all-start.6 = ((bf16[4,3,64,512]{3,2,1,0:T(8,128)(2,1)}), bf16[4,3,64,512]{3,2,1,0:T(8,128)(2,1)S(1)}, u32[]{:S(2)}, u32[]{:S(2)}) async-start(bf16[4,3,64,512]{3,2,1,0:T(8,128)(2,1)} %bitcast.344), calls=%async_computation.7 | async-start | bytes 1572864 | tf_op jit(solution)/shard_map/all_to_all | solution.py:683
  (55 other events, 256.9 us)
Sparse Core Ops, SparseCore 0:
  24.7 109.5 all-gather.10
  136.5 125.4 all-gather.12
  264.1 88.9 all-gather.6
  355.1 144.6 all-gather.8
  725.2 77.6 reduce-scatter.6
  806.4 197.8 reduce-scatter.8
  1008.3 116.0 reduce-scatter.4
  1128.5 155.4 reduce-scatter.10

commit v2 on v1

v2 whole, which is shorter than its diff:
```python
import math

import jax
import jax.numpy as jnp
import numpy as np
from jax import lax
from jax.experimental import pallas as pl
from jax.experimental.pallas import tpu as pltpu
from jax.sharding import PartitionSpec as P

HEAD_DIM = 128
ROT = 32
TOP_PRECISION = lax.Precision.HIGHEST
EPS_NORM = 1e-05
EPS_ROOT = 1e-06
NEG_BIG = -1e30
BOTH = ("fsdp", "ctx")
BF16 = jnp.bfloat16
F32 = jnp.float32
MESH = pl.DeviceIdType.MESH
ANY = pl.BlockSpec(memory_space=pl.ANY)
VMEM = pl.BlockSpec(memory_space=pltpu.VMEM)
LOG2E = 1.4426950408889634


def layer_norm(values, gain_row, shift_row):
    centre = values - jnp.mean(values, axis=-1, keepdims=True)
    spread = jnp.mean(centre * centre, axis=-1, keepdims=True)
    return centre * lax.rsqrt(spread + EPS_NORM) * gain_row + shift_row


def gelu(values):
    return jax.nn.gelu(values, approximate=False)


def rotary_tables(count):
    half = ROT // 2
    frequency = np.exp(np.arange(half, dtype=np.float32) * np.float32(-2.0 * math.log(10000.0) / ROT))
    angles = np.arange(count, dtype=np.float32)[:, None] * frequency.astype(np.float32)[None, :]
    cosine = jnp.asarray(np.cos(angles.astype(np.float64)), F32)
    sine = jnp.asarray(np.sin(angles.astype(np.float64)), F32)
    zero, rest = jnp.zeros_like(sine), HEAD_DIM - ROT
    return jnp.stack(
        [
            jnp.pad(jnp.concatenate([cosine, cosine], 1), ((0, 0), (0, rest)), constant_values=1.0),
            jnp.pad(jnp.concatenate([zero, sine], 1), ((0, 0), (0, rest))),
            jnp.pad(jnp.concatenate([-sine, zero], 1), ((0, 0), (0, rest))),
        ]
    )


def turn(x, straight, right, left):
    half = ROT // 2
    return (
        x * straight
        + pltpu.roll(x, half, axis=1) * right
        + pltpu.roll(x, HEAD_DIM - half, axis=1) * left
    )


def mixer(rows, gain_row, opening, closing, closing_bias):
    inverse_rms = lax.rsqrt(jnp.mean(rows * rows, axis=-1, keepdims=True) + EPS_ROOT)
    rooted = rows * inverse_rms * gain_row
    hidden = jnp.dot(rooted, opening, precision=TOP_PRECISION)
    return jnp.dot(gelu(hidden), closing, precision=TOP_PRECISION) + closing_bias


def dot(pattern, left, right):
    return jnp.einsum(pattern, left, right, preferred_element_type=F32)


def remote(src, dst, send_sem, recv_sem, target):
    return pltpu.make_async_remote_copy(
        src_ref=src,
        dst_ref=dst,
        send_sem=send_sem,
        recv_sem=recv_sem,
        device_id=target,
        device_id_type=MESH,
    )


def place():
    return lax.axis_index("fsdp"), lax.axis_index("ctx")


def links_and_twin():
    chips = lax.axis_size("fsdp") // 2
    f, c = place()
    chip, core = f // 2, lax.rem(f, 2)
    return [(lax.rem(chip + j, chips) * 2 + core, c) for j in range(1, chips)] + [
        (chip * 2 + 1 - core, c)
    ]


def along_ctx():
    cn = lax.axis_size("ctx")
    f, c = place()
    return [(f, lax.rem(c + j, cn)) for j in range(1, cn)]


def along_fsdp():
    fn = lax.axis_size("fsdp")
    f, c = place()
    return [(lax.rem(f + j, fn), c) for j in range(1, fn)]


def along_both():
    return along_ctx() + along_fsdp()


def comm(cid, *tasks):
    n = len(tasks)
    counts = [len(t[5]) for t in tasks]

    def kernel(*refs):
        targets, seen = [], []
        covered = [(along_fsdp, [along_both]), (the_pair, [along_ctx])]
        for t in tasks:
            if t[0] not in seen and (t[0], seen[:1]) not in covered:
                seen.append(t[0])
                targets += t[0]()
        barrier = pltpu.get_barrier_semaphore()
        for t in targets:
            pl.semaphore_signal(barrier, inc=1, device_id=t, device_id_type=MESH)
        pl.semaphore_wait(barrier, len(targets))
        scratch = list(refs[2 * n :])
        phases = []
        for i, t in enumerate(tasks):
            mine, scratch = scratch[: counts[i]], scratch[counts[i] :]
            phases.append(t[6](refs[i], refs[n + i], *mine))
        for p in range(3):
            for ph in phases:
                ph[p]()

    out = pl.pallas_call(
        kernel,
        out_shape=[t[2] for t in tasks],
        in_specs=[t[3] for t in tasks],
        out_specs=[t[4] for t in tasks],
        scratch_shapes=[x for t in tasks for x in t[5]],
        compiler_params=pltpu.CompilerParams(
            collective_id=cid, has_side_effects=True, vmem_limit_bytes=40 * 2**20
        ),
        cost_estimate=pl.CostEstimate(flops=0, bytes_accessed=15_000_000, transcendentals=0),
    )(*[t[1] for t in tasks])
    return out


def dma(*shape):
    return pltpu.SemaphoreType.DMA(shape)


def gather_small(x):
    fn, cn = lax.axis_size("fsdp"), lax.axis_size("ctx")

    def body(x_ref, o_ref, s1, r1, s2, r2):
        f, c = place()

        def first(j):
            return remote(
                x_ref, o_ref.at[f, c], s1.at[j], r1.at[j], (f, lax.rem(c + j, cn))
            )

        def second(j):
            return remote(
                o_ref.at[f], o_ref.at[f], s2.at[j], r2.at[j], (lax.rem(f + j, fn), c)
            )

        def start():
            for j in range(1, cn):
                first(j).start()
            o_ref[f, c] = x_ref[...]

        def middle():
            for j in range(1, cn):
                there = o_ref.at[f, lax.rem(c + cn - j, cn)]
                remote(there, there, s1.at[j], r1.at[j], (f, lax.rem(c + j, cn))).wait_recv()
            for j in range(1, fn):
                second(j).start()

        def end():
            for j in range(1, fn):
                there = o_ref.at[lax.rem(f + fn - j, fn)]
                remote(there, there, s2.at[j], r2.at[j], (lax.rem(f + j, fn), c)).wait_recv()
            for j in range(1, cn):
                first(j).wait_send()
            for j in range(1, fn):
                second(j).wait_send()

        return start, middle, end

    shape = jax.ShapeDtypeStruct((fn, cn, *x.shape), x.dtype)
    return (along_both, x, shape, VMEM, VMEM, [dma(cn), dma(cn), dma(fn), dma(fn)], body)


def exchange_fsdp(x):
    fn = lax.axis_size("fsdp")

    def body(x_ref, o_ref, s, r, own):
        f, c = place()

        def copy(j, slot):
            t = lax.rem(f + j, fn)
            return remote(x_ref.at[t], o_ref.at[slot], s.at[j], r.at[j], (t, c))

        mine = pltpu.make_async_copy(x_ref.at[f], o_ref.at[f], own)

        def start():
            for j in range(1, fn):
                copy(j, f).start()
            mine.start()

        def end():
            mine.wait()
            for j in range(1, fn):
                copy(j, lax.rem(f + fn - j, fn)).wait_recv()
            for j in range(1, fn):
                copy(j, f).wait_send()

        return start, lambda: None, end

    shape = jax.ShapeDtypeStruct(x.shape, x.dtype)
    return (along_fsdp, x, shape, ANY, ANY, [dma(fn), dma(fn), dma()], body)


def exchange_ctx(x, to_units):
    cn = lax.axis_size("ctx")
    lead = x.shape[1] if to_units else x.shape[0]

    def body(x_ref, o_ref, s, r, own):
        f, c = place()

        def source(t):
            return x_ref.at[t] if to_units else x_ref.at[:, t]

        def target(slot):
            return o_ref.at[:, slot] if to_units else o_ref.at[slot]

        def copy(j, slot):
            t = lax.rem(c + j, cn)
            return remote(source(t), target(slot), s.at[j], r.at[j], (f, t))

        mine = pltpu.make_async_copy(source(c), target(c), own)

        def start():
            for j in range(1, cn):
                copy(j, c).start()
            mine.start()

        def end():
            mine.wait()
            for j in range(1, cn):
                copy(j, lax.rem(c + cn - j, cn)).wait_recv()
            for j in range(1, cn):
                copy(j, c).wait_send()

        return start, lambda: None, end

    dims = (lead, cn) if to_units else (cn, lead)
    shape = jax.ShapeDtypeStruct((*dims, *x.shape[2:]), x.dtype)
    return (along_ctx, x, shape, ANY, ANY, [dma(cn), dma(cn), dma()], body)


def the_pair():
    f, c = place()
    return [(f, c // 2 * 2 + 1 - lax.rem(c, 2))]


def exchange_pair(x):
    def body(x_ref, o_ref, s, r):
        (pair,) = the_pair()
        copy = remote(x_ref, o_ref, s, r, pair)
        return copy.start, lambda: None, copy.wait

    shape = jax.ShapeDtypeStruct(x.shape, x.dtype)
    return (the_pair, x, shape, ANY, ANY, [dma(), dma()], body)


def gather_fsdp(x, parts=4):
    fn = lax.axis_size("fsdp")
    chips = fn // 2
    n, d = x.shape
    step = n // parts
    pieces = [pl.ds(p * step, step) for p in range(parts)]

    def body(x_ref, o_ref, own_sem, s_link, r_link, s_core, r_core):
        f, c = place()
        chip, core = f // 2, lax.rem(f, 2)
        twin = (chip * 2 + 1 - core, c)
        links, cores = {}, {}

        def to(j):
            return (lax.rem(chip + j, chips) * 2 + core, c)

        def slot(j, core_id):
            return lax.rem(chip + chips - j, chips) * 2 + core_id

        own = pltpu.make_async_copy(x_ref, o_ref.at[f], own_sem)

        def start():
            for i, rows in enumerate(pieces):
                here, there = x_ref.at[rows], o_ref.at[f, rows]
                for j in range(1, chips):
                    links[i, j] = remote(here, there, s_link.at[j, i], r_link.at[j, i], to(j))
                    links[i, j].start()
            for i, rows in enumerate(pieces):
                here, there = x_ref.at[rows], o_ref.at[f, rows]
                cores[i, 0] = remote(here, there, s_core.at[0, i], r_core.at[0, i], twin)
                cores[i, 0].start()
            own.start()

        def middle():
            for i, rows in enumerate(pieces):
                for j in range(1, chips):
                    here = o_ref.at[slot(j, core), rows]
                    remote(here, here, s_link.at[j, i], r_link.at[j, i], to(j)).wait_recv()
                    cores[i, j] = remote(here, here, s_core.at[j, i], r_core.at[j, i], twin)
                    cores[i, j].start()

        def end():
            own.wait()
            for i, rows in enumerate(pieces):
                for j in range(chips):
                    there = o_ref.at[slot(j, 1 - core), rows]
                    cores[i, j].wait_send()
                    remote(there, there, s_core.at[j, i], r_core.at[j, i], twin).wait_recv()
                for j in range(1, chips):
                    links[i, j].wait_send()

        return start, middle, end

    shape = jax.ShapeDtypeStruct((fn, n, d), x.dtype)
    return (links_and_twin, x, shape, ANY, ANY, [dma()] + [dma(chips, parts)] * 4, body)


def gather_ctx(x):
    cn = lax.axis_size("ctx")
    count = cn // 2

    def body(x_ref, o_ref, own_sem, s_up, r_up, s_down, r_down, s_pair, r_pair):
        f, c = place()
        hi, lo = c // 2, lax.rem(c, 2)
        pair = (f, hi * 2 + 1 - lo)
        above = (f, lax.rem(hi + 1, count) * 2 + lo)
        below = (f, lax.rem(hi + count - 1, count) * 2 + lo)
        own = pltpu.make_async_copy(x_ref, o_ref.at[c], own_sem)

        def low(d):
            return lax.rem(hi + count - d, count)

        def high(d):
            return lax.rem(hi + d, count)

        def up(d):
            source = x_ref if d == 0 else o_ref.at[low(d) * 2 + lo]
            return remote(source, o_ref.at[low(d) * 2 + lo], s_up.at[d], r_up.at[d + 1], above)

        def down(d):
            source = x_ref if d == 0 else o_ref.at[high(d) * 2 + lo]
            return remote(
                source, o_ref.at[high(d) * 2 + lo], s_down.at[d], r_down.at[d + 1], below
            )

        def across(k, slot):
            source = x_ref if k == 0 else o_ref.at[slot * 2 + lo]
            return remote(source, o_ref.at[slot * 2 + lo], s_pair.at[k], r_pair.at[k], pair)

        def start():
            pl.when(hi < count - 1)(lambda: up(0).start())
            pl.when(hi > 0)(lambda: down(0).start())
            across(0, hi).start()
            own.start()

        def middle():
            for d in range(1, count):

                @pl.when(hi >= d)
                def _():
                    here = o_ref.at[low(d) * 2 + lo]
                    remote(here, here, s_up.at[d], r_up.at[d], above).wait_recv()
                    across(d, low(d)).start()
                    if d < count - 1:
                        pl.when(hi < count - 1)(lambda: up(d).start())

                @pl.when(hi + d < count)
                def _():
                    here = o_ref.at[high(d) * 2 + lo]
                    remote(here, here, s_down.at[d], r_down.at[d], below).wait_recv()
                    across(count - d, high(d)).start()
                    if d < count - 1:
                        pl.when(hi > 0)(lambda: down(d).start())

        def end():
            own.wait()
            across(0, hi).wait_send()
            for k in range(count):
                there = o_ref.at[low(k) * 2 + 1 - lo]
                remote(there, there, s_pair.at[k], r_pair.at[k], pair).wait_recv()
                if k > 0:
                    across(k, low(k)).wait_send()
            for d in range(count - 1):
                pl.when((hi >= d) & (hi < count - 1))(lambda d=d: up(d).wait_send())
                pl.when((hi + d < count) & (hi > 0))(lambda d=d: down(d).wait_send())

        return start, middle, end

    shape = jax.ShapeDtypeStruct((cn, *x.shape), x.dtype)
    scratch = [dma()] + [dma(count + 1)] * 4 + [dma(count)] * 2
    return (along_ctx, x, shape, ANY, ANY, scratch, body)


def scatter_fsdp(x, parts=4):
    fn = lax.axis_size("fsdp")
    chips = fn // 2
    _, n, d = x.shape
    step = n // parts

    def body(x_ref, o_ref, own, near, mine, far, ss, s_own, s_near, r_near, s_far, r_far):
        f, c = place()
        chip, core = f // 2, lax.rem(f, 2)
        twin = (chip * 2 + 1 - core, c)
        nears, owns, fars, outs = {}, {}, {}, {}

        def chip_at(j):
            return lax.rem(chip + j, chips)

        def start():
            for p in range(parts):
                rows = pl.ds(p * step, step)
                for j in list(range(1, chips)) + [0]:
                    at = chip_at(j) * 2
                    owns[p, j] = pltpu.make_async_copy(
                        x_ref.at[at + core, rows], own.at[j, p], s_own.at[j, p]
                    )
                    owns[p, j].start()
                    nears[p, j] = remote(
                        x_ref.at[at + 1 - core, rows],
                        near.at[j, p],
                        s_near.at[j, p],
                        r_near.at[j, p],
                        twin,
                    )
                    nears[p, j].start()

        def middle():
            for p in range(parts):
                for j in range(1, chips):
                    owns[p, j].wait()
                    nears[p, j].wait_recv()
                    mine[j, p] = (own[j, p].astype(F32) + near[j, p].astype(F32)).astype(BF16)
                    fars[p, j] = remote(
                        mine.at[j, p],
                        far.at[j, p],
                        s_far.at[j, p],
                        r_far.at[j, p],
                        (chip_at(j) * 2 + core, c),
                    )
                    fars[p, j].start()
            for p in range(parts):
                owns[p, 0].wait()
                nears[p, 0].wait_recv()
                ss[p] = own[0, p].astype(F32) + near[0, p].astype(F32)

        def end():
            for p in range(parts):
                for j in range(1, chips):
                    fars[p, j].wait_recv()
                    ss[p] += far[j, p].astype(F32)
                outs[p] = pltpu.make_async_copy(
                    ss.at[p], o_ref.at[pl.ds(p * step, step)], s_far.at[0, p]
                )
                outs[p].start()
            for p in range(parts):
                outs[p].wait()
                for j in range(chips):
                    nears[p, j].wait_send()
                for j in range(1, chips):
                    fars[p, j].wait_send()

        return start, middle, end

    block = pltpu.VMEM((chips, parts, step, d), BF16)
    scratch = [block] * 4 + [pltpu.VMEM((parts, step, d), F32)] + [dma(chips, parts)] * 5
    return (links_and_twin, x, jax.ShapeDtypeStruct((n, d), F32), ANY, ANY, scratch, body)


def scatter_small(x):
    fn, cn = lax.axis_size("fsdp"), lax.axis_size("ctx")

    def body(x_ref, o_ref, got, sums, got2, s1, r1, s2, r2):
        f, c = place()

        def first(j):
            t = lax.rem(f + j, fn)
            return remote(x_ref.at[t], got.at[j], s1.at[j], r1.at[j], (t, c))

        def second(j):
            t = lax.rem(c + j, cn)
            return remote(sums.at[t], got2.at[j], s2.at[j], r2.at[j], (f, t))

        def start():
            for j in range(1, fn):
                first(j).start()
            sums[...] = x_ref[f]

        def middle():
            for j in range(1, fn):
                first(j).wait_recv()
                sums[...] += got[j]
            for j in range(1, cn):
                second(j).start()
            o_ref[...] = sums[c]

        def end():
            for j in range(1, cn):
                second(j).wait_recv()
                o_ref[...] += got2[j]
            for j in range(1, fn):
                first(j).wait_send()
            for j in range(1, cn):
                second(j).wait_send()

        return start, middle, end

    tail = x.shape[2:]
    scratch = [
        pltpu.VMEM(x.shape, x.dtype),
        pltpu.VMEM(x.shape[1:], x.dtype),
        pltpu.VMEM(x.shape[1:], x.dtype),
        dma(fn),
        dma(fn),
        dma(cn),
        dma(cn),
    ]
    return (along_both, x, jax.ShapeDtypeStruct(tail, x.dtype), VMEM, VMEM, scratch, body)


def nt(a, b):
    return lax.dot_general(a, b, (((1,), (1,)), ((), ())), preferred_element_type=F32)


def nn(a, b):
    return lax.dot_general(a, b, (((1,), (0,)), ((), ())), preferred_element_type=F32)


def attend(q, k, v, starts, block=512):
    u, t, _ = q.shape
    scale = HEAD_DIM**-0.5 * LOG2E

    def kernel(q_ref, k_ref, v_ref, s_ref, o_ref, l_ref, vt):
        i = pl.program_id(1)

        @pl.when(i == 0)
        def _():
            vt[...] = v_ref[0].T

        rows = q_ref[0]
        first = s_ref[0]
        base = lax.broadcasted_iota(jnp.int32, (block, block), 0)
        qpos = i * block + lax.broadcasted_iota(jnp.int32, (1, block), 1)

        def one(j, carry, diagonal):
            peak, total, acc = carry
            at = pl.multiple_of(j * block, block)
            s = nt(k_ref[0, pl.ds(at, block)], rows) * scale
            kpos = base + at
            keep = kpos >= first
            if diagonal:
                keep = keep & (kpos <= qpos)
            s = jnp.where(keep, s, NEG_BIG)
            new = jnp.maximum(peak, jnp.max(s, axis=0, keepdims=True))
            p = jnp.exp2(s - new)
            shrink = jnp.exp2(peak - new)
            total = total * shrink + jnp.sum(p, axis=0, keepdims=True)
            acc = acc * shrink + nn(vt[:, pl.ds(at, block)], p.astype(BF16))
            return new, total, acc

        start = (
            jnp.full((1, block), NEG_BIG, F32),
            jnp.zeros((1, block), F32),
            jnp.zeros((HEAD_DIM, block), F32),
        )
        start = one(i, start, True)
        peak, total, acc = lax.fori_loop(0, i, lambda j, c: one(j, c, False), start)
        o_ref[0] = (acc / total).T.astype(BF16)
        l_ref[0] = peak + jnp.log2(total)

    return pl.pallas_call(
        kernel,
        grid=(u, t // block),
        in_specs=[
            pl.BlockSpec((1, block, HEAD_DIM), lambda a, b: (a, b, 0)),
            pl.BlockSpec((1, t, HEAD_DIM), lambda a, b: (a, 0, 0)),
            pl.BlockSpec((1, t, HEAD_DIM), lambda a, b: (a, 0, 0)),
            pl.BlockSpec((1, 1, block), lambda a, b: (a, 0, b)),
        ],
        out_specs=[
            pl.BlockSpec((1, block, HEAD_DIM), lambda a, b: (a, b, 0)),
            pl.BlockSpec((1, 1, block), lambda a, b: (a, 0, b)),
        ],
        out_shape=[
            jax.ShapeDtypeStruct((u, t, HEAD_DIM), BF16),
            jax.ShapeDtypeStruct((u, 1, t), F32),
        ],
        scratch_shapes=[pltpu.VMEM((HEAD_DIM, t), BF16)],
        compiler_params=pltpu.CompilerParams(vmem_limit_bytes=32 * 2**20),
        cost_estimate=pl.CostEstimate(
            flops=2 * u * t * t * HEAD_DIM, bytes_accessed=8 * u * t * 256, transcendentals=u * t * t // 2
        ),
    )(q, k, v, starts)


def attend_back(q, k, v, starts, lse, o, g, tables, block=512):
    u, t, _ = q.shape
    scale = HEAD_DIM**-0.5

    def kernel(
        q_ref, k_ref, v_ref, s_ref, l_ref, o_ref, g_ref, t_ref, dq_ref, dk_ref, dv_ref, kt, dk, dv
    ):
        i = pl.program_id(1)

        @pl.when(i == 0)
        def _():
            kt[...] = k_ref[0].T
            dk[...] = jnp.zeros_like(dk)
            dv[...] = jnp.zeros_like(dv)

        rows, grows = q_ref[0], g_ref[0]
        first, logs = s_ref[0], l_ref[0]
        prod = o_ref[0].astype(F32) * grows.astype(F32)
        centre = jnp.sum(prod.T, axis=0, keepdims=True)
        base = lax.broadcasted_iota(jnp.int32, (block, block), 0)
        qpos = i * block + lax.broadcasted_iota(jnp.int32, (1, block), 1)

        def one(j, acc, diagonal):
            at = pl.multiple_of(j * block, block)
            here = pl.ds(at, block)
            p = jnp.exp2(nt(k_ref[0, here], rows) * (scale * LOG2E) - logs)
            kpos = base + at
            keep = kpos >= first
            if diagonal:
                keep = keep & (kpos <= qpos)
            p = jnp.where(keep, p, 0.0)
            gp = nt(v_ref[0, here], grows)
            ds = (p * (gp - centre)).astype(BF16)
            dv[here] += nn(p.astype(BF16), grows)
            dk[here] += nn(ds, rows)
            return acc + nn(kt[:, here], ds)

        acc = one(i, jnp.zeros((HEAD_DIM, block), F32), True)
        acc = lax.fori_loop(0, i, lambda j, a: one(j, a, False), acc)
        there = pl.ds(pl.multiple_of(i * block, block), block)
        straight, right, left = t_ref[0, there], t_ref[1, there], t_ref[2, there]
        dq_ref[0] = turn((acc * scale).T, straight, -right, -left).astype(BF16)

        @pl.when(i == t // block - 1)
        def _():
            for b in range(t // block):
                at = pl.ds(b * block, block)
                dk_ref[0, at] = turn(
                    dk[at] * scale, t_ref[0, at], -t_ref[1, at], -t_ref[2, at]
                ).astype(BF16)
                dv_ref[0, at] = dv[at].astype(BF16)

    def whole(a, b):
        return (a, 0, 0)

    def part(a, b):
        return (a, b, 0)

    def row(a, b):
        return (a, 0, b)

    spec, full, line = (1, block, HEAD_DIM), (1, t, HEAD_DIM), (1, 1, block)
    return pl.pallas_call(
        kernel,
        grid=(u, t // block),
        in_specs=[
            pl.BlockSpec(spec, part),
            pl.BlockSpec(full, whole),
            pl.BlockSpec(full, whole),
            pl.BlockSpec(line, row),
            pl.BlockSpec(line, row),
            pl.BlockSpec(spec, part),
            pl.BlockSpec(spec, part),
            pl.BlockSpec((3, t, HEAD_DIM), lambda a, b: (0, 0, 0)),
        ],
        out_specs=[
            pl.BlockSpec(spec, part),
            pl.BlockSpec(full, whole),
            pl.BlockSpec(full, whole),
        ],
        out_shape=[jax.ShapeDtypeStruct((u, t, HEAD_DIM), BF16)] * 3,
        scratch_shapes=[
            pltpu.VMEM((HEAD_DIM, t), BF16),
            pltpu.VMEM((t, HEAD_DIM), F32),
            pltpu.VMEM((t, HEAD_DIM), F32),
        ],
        compiler_params=pltpu.CompilerParams(vmem_limit_bytes=48 * 2**20),
        cost_estimate=pl.CostEstimate(
            flops=5 * u * t * t * HEAD_DIM, bytes_accessed=20 * u * t * 256, transcendentals=u * t * t // 2
        ),
    )(q, k, v, starts, lse, o, g, tables)


def project(x, w, bias, tables):
    count, length, width = x.shape
    cn, fn, rows, cols = w.shape
    heads = cols // HEAD_DIM

    def kernel(*refs):
        x_ref, w_ref, b_ref = refs[:3]
        o_ref, held, sem = refs[-3:]

        @pl.when(pl.program_id(0) == 0)
        def _():
            copies = [
                pltpu.make_async_copy(w_ref.at[:, f], held.at[f], sem.at[f])
                for f in range(fn)
            ]
            for c in copies:
                c.start()
            for c in copies:
                c.wait()

        y = nn(x_ref[0], held[...].reshape(width, cols)) + b_ref[...]
        for h in range(heads):
            part = y[:, h * HEAD_DIM : (h + 1) * HEAD_DIM]
            if tables is not None:
                t_ref = refs[3]
                part = turn(part, t_ref[0], t_ref[1], t_ref[2])
            o_ref[h] = part.astype(BF16)

    extra = [] if tables is None else [tables]
    return pl.pallas_call(
        kernel,
        grid=(count,),
        in_specs=[
            pl.BlockSpec((1, length, width), lambda i: (i, 0, 0)),
            ANY,
            pl.BlockSpec((1, cols), lambda i: (0, 0)),
        ]
        + [pl.BlockSpec((3, length, HEAD_DIM), lambda i: (0, 0, 0)) for _ in extra],
        out_specs=pl.BlockSpec((heads, length, HEAD_DIM), lambda i: (i, 0, 0)),
        out_shape=jax.ShapeDtypeStruct((count * heads, length, HEAD_DIM), BF16),
        scratch_shapes=[pltpu.VMEM((fn, cn, rows, cols), BF16), dma(fn)],
        compiler_params=pltpu.CompilerParams(vmem_limit_bytes=32 * 2**20),
        cost_estimate=pl.CostEstimate(
            flops=2 * count * length * width * cols,
            bytes_accessed=2 * (count * length * (width + cols) + width * cols),
            transcendentals=0,
        ),
    )(x, w, bias, *extra)


def widen(x, w, bias, tile=256, rows_at_once=512):
    n, d = x.shape
    cn, fn, rows, cols = w.shape
    tiles = cols // tile

    def kernel(x_ref, w_ref, b_ref, a_ref, g_ref, o_ref, held, sem):
        i = pl.program_id(0)

        def copy(j, f):
            at = pl.ds(pl.multiple_of(j * tile, tile), tile)
            return pltpu.make_async_copy(w_ref.at[:, f, :, at], held.at[j, f], sem.at[j, f])

        @pl.when(i == 0)
        def _():
            for j in range(tiles):
                for f in range(fn):
                    copy(j, f).start()

        for f in range(fn):
            copy(i, f).wait()
        w_tile = held[i].reshape(d, tile)
        o_ref[...] = w_tile
        for r in range(0, n, rows_at_once):
            part = pl.ds(r, rows_at_once)
            y = nn(x_ref[part], w_tile) + b_ref[...]
            t = y * math.sqrt(0.5)
            below = 0.5 + 0.5 * lax.erf(t)
            a_ref[part] = (y * below).astype(BF16)
            density = jnp.exp(-t * t) * (1.0 / math.sqrt(2.0 * math.pi))
            g_ref[part] = (below + y * density).astype(BF16)

    column = pl.BlockSpec((n, tile), lambda i: (0, i))
    return pl.pallas_call(
        kernel,
        grid=(tiles,),
        in_specs=[
            pl.BlockSpec((n, d), lambda i: (0, 0)),
            ANY,
            pl.BlockSpec((1, tile), lambda i: (0, i)),
        ],
        out_specs=[column, column, pl.BlockSpec((d, tile), lambda i: (0, i))],
        out_shape=[
            jax.ShapeDtypeStruct((n, cols), BF16),
            jax.ShapeDtypeStruct((n, cols), BF16),
            jax.ShapeDtypeStruct((d, cols), BF16),
        ],
        scratch_shapes=[pltpu.VMEM((tiles, fn, cn, rows, tile), BF16), dma(tiles, fn)],
        compiler_params=pltpu.CompilerParams(vmem_limit_bytes=48 * 2**20),
        cost_estimate=pl.CostEstimate(
            flops=2 * n * d * cols, bytes_accessed=60_000_000, transcendentals=0
        ),
    )(x, w, bias)


def front(hist, mix, gain, shift, tokens=16, wide=256):
    h, n, d = hist.shape
    rest = gain.shape[0]

    def kernel(h_ref, m_ref, g_ref, b_ref, s_ref, n_ref):
        m = m_ref[...]
        for at in range(0, d, wide):
            cut = slice(at, at + wide)
            for s in range(4):
                acc = m[:, s * h : s * h + 1] * h_ref[0, :, cut].astype(F32)
                for j in range(1, h):
                    acc += m[:, s * h + j : s * h + j + 1] * h_ref[j, :, cut].astype(F32)
                s_ref[s, :, cut] = acc
        for s in range(rest):
            x = s_ref[s]
            centre = x - jnp.mean(x, axis=-1, keepdims=True)
            spread = jnp.mean(centre * centre, axis=-1, keepdims=True)
            y = centre * lax.rsqrt(spread + EPS_NORM) * g_ref[s : s + 1] + b_ref[s : s + 1]
            n_ref[s] = y.astype(BF16)

    return pl.pallas_call(
        kernel,
        grid=(n // tokens,),
        in_specs=[
            pl.BlockSpec((h, tokens, d), lambda i: (0, i, 0)),
            pl.BlockSpec((tokens, 128), lambda i: (i, 0)),
            pl.BlockSpec((rest, d), lambda i: (0, 0)),
            pl.BlockSpec((rest, d), lambda i: (0, 0)),
        ],
        out_specs=[
            pl.BlockSpec((4, tokens, d), lambda i: (0, i, 0)),
            pl.BlockSpec((rest, tokens, d), lambda i: (0, i, 0)),
        ],
        out_shape=[
            jax.ShapeDtypeStruct((4, n, d), F32),
            jax.ShapeDtypeStruct((rest, n, d), BF16),
        ],
        compiler_params=pltpu.CompilerParams(vmem_limit_bytes=60 * 2**20),
        cost_estimate=pl.CostEstimate(
            flops=2 * 4 * h * n * d, bytes_accessed=n * d * (2 * h + 22), transcendentals=0
        ),
    )(hist, mix, gain, shift)


def last(hist, mix, streams, gain, grads, grad_hidden, tokens=16, wide=256):
    h, n, d = hist.shape
    rest = gain.shape[0]

    def kernel(h_ref, m_ref, s_ref, g_ref, d0, d1, d2, r_ref, gh_ref, gm_ref, gg_ref, gb_ref, ds):
        @pl.when(pl.program_id(0) == 0)
        def _():
            gg_ref[...] = jnp.zeros_like(gg_ref)
            gb_ref[...] = jnp.zeros_like(gb_ref)

        for s, d_ref in enumerate((d0, d1, d2)):
            x = s_ref[s]
            centre = x - jnp.mean(x, axis=-1, keepdims=True)
            inverse = lax.rsqrt(jnp.mean(centre * centre, axis=-1, keepdims=True) + EPS_NORM)
            unit = centre * inverse
            dn = d_ref[...]
            gg_ref[s : s + 1] += jnp.sum(dn * unit, axis=0, keepdims=True)
            gb_ref[s : s + 1] += jnp.sum(dn, axis=0, keepdims=True)
            du = dn * g_ref[s : s + 1]
            ds[s] = inverse * (
                du
                - jnp.mean(du, axis=-1, keepdims=True)
                - unit * jnp.mean(du * unit, axis=-1, keepdims=True)
            )
        ds[rest] = r_ref[...]
        m = m_ref[...]
        sums = [[jnp.zeros((tokens, 128), F32) for _ in range(h)] for _ in range(4)]
        for at in range(0, d, wide):
            cut = slice(at, at + wide)
            parts = [ds[s, :, cut] for s in range(4)]
            for j in range(h):
                row = h_ref[j, :, cut].astype(F32)
                acc = m[:, j : j + 1] * parts[0]
                for s in range(1, 4):
                    acc += m[:, s * h + j : s * h + j + 1] * parts[s]
                gh_ref[j, :, cut] = acc
                for s in range(4):
                    prod = row * parts[s]
                    for b in range(0, wide, 128):
                        sums[s][j] += prod[:, b : b + 128]
        lane = lax.broadcasted_iota(jnp.int32, (tokens, 128), 1)
        total = jnp.zeros((tokens, 128), F32)
        for s in range(4):
            for j in range(h):
                value = jnp.sum(sums[s][j], axis=-1, keepdims=True)
                total = jnp.where(lane == s * h + j, value, total)
        gm_ref[...] = total

    row = pl.BlockSpec((tokens, d), lambda i: (i, 0))
    lines = pl.BlockSpec((rest, d), lambda i: (0, 0))
    return pl.pallas_call(
        kernel,
        grid=(n // tokens,),
        in_specs=[
            pl.BlockSpec((h, tokens, d), lambda i: (0, i, 0)),
            pl.BlockSpec((tokens, 128), lambda i: (i, 0)),
            pl.BlockSpec((4, tokens, d), lambda i: (0, i, 0)),
            lines,
            row,
            row,
            row,
            row,
        ],
        out_specs=[
            pl.BlockSpec((h, tokens, d), lambda i: (0, i, 0)),
            pl.BlockSpec((tokens, 128), lambda i: (i, 0)),
            lines,
            lines,
        ],
        out_shape=[
            jax.ShapeDtypeStruct((h, n, d), F32),
            jax.ShapeDtypeStruct((n, 128), F32),
            jax.ShapeDtypeStruct((rest, d), F32),
            jax.ShapeDtypeStruct((rest, d), F32),
        ],
        scratch_shapes=[pltpu.VMEM((4, tokens, d), F32)],
        compiler_params=pltpu.CompilerParams(vmem_limit_bytes=60 * 2**20),
        cost_estimate=pl.CostEstimate(
            flops=4 * 4 * h * n * d, bytes_accessed=n * d * (6 * h + 32), transcendentals=0
        ),
    )(hist, mix, streams, gain, *grads, grad_hidden)


def body(
    history,
    dense_mix,
    doc_starts,
    norm_gain,
    norm_bias,
    qkv_weight,
    qkv_bias,
    out_weight,
    out_bias,
    up_weight,
    up_bias,
    down_weight,
    down_bias,
    root_gain,
    mix_in_weight,
    mix_out_weight,
    mix_out_bias,
    out_cotangent,
    mix_cotangent,
):
    fn, cn = lax.axis_size("fsdp"), lax.axis_size("ctx")
    dn = fn * cn
    fi, ci = lax.axis_index("fsdp"), lax.axis_index("ctx")
    hist, seqs, length, width = history.shape
    nloc = seqs * length
    ntp = fn * nloc
    rows = qkv_weight.shape[0]
    ff = up_weight.shape[1]
    wcol, fcol = width // fn, ff // fn
    heads = wcol // HEAD_DIM
    units = fn * seqs * heads // cn
    total = cn * length
    mixn = mix_in_weight.shape[1]

    wdown = lax.all_gather(down_weight, "ctx", axis=0, tiled=True)

    parts = [
        norm_gain,
        norm_bias,
        qkv_bias,
        out_bias,
        up_bias,
        down_bias,
        root_gain,
        mix_in_weight,
        doc_starts.astype(F32),
    ]
    flat = jnp.concatenate([a.reshape(-1) for a in parts])
    flat = jnp.pad(flat, (0, -flat.size % 1024)).reshape(-1, 128)
    flats, qkv_cols, up_cols = comm(
        1,
        gather_small(flat),
        exchange_fsdp(qkv_weight.reshape(rows, 3, fn, wcol).transpose(2, 1, 0, 3)),
        exchange_fsdp(up_weight.reshape(rows, fn, fcol).transpose(1, 0, 2)),
    )
    flats = flats.reshape(dn, -1)
    pieces, at = [], 0
    for a in parts:
        pieces.append(flats[:, at : at + a.size])
        at += a.size

    def joined(piece, lead):
        return piece.reshape(dn, lead, -1).transpose(1, 0, 2).reshape(lead, -1)

    gain_all = joined(pieces[0], 4)
    shift_all = joined(pieces[1], 4)
    qkv_shift = joined(pieces[2], 3)
    out_shift = pieces[3].reshape(-1)
    up_shift = pieces[4].reshape(-1)
    down_shift = pieces[5].reshape(-1)
    root_full = pieces[6].reshape(-1)
    mix_in_full = pieces[7].reshape(width, mixn)
    starts = pieces[8].reshape(fn, cn, seqs, -1)[:, 0].astype(jnp.int32)

    hist2 = history.reshape(hist, nloc, width)
    mix2 = dense_mix.reshape(dense_mix.shape[0], hist, nloc)
    mixes = jnp.pad(mix2.reshape(-1, nloc).T, ((0, 0), (0, 128 - mix2.shape[0] * hist)))
    streams, normed = front(hist2, mixes, gain_all[:3], shift_all[:3])

    bias_cols = lax.dynamic_slice_in_dim(qkv_shift, fi * wcol, wcol, 1)
    tables = rotary_tables(total)
    tables_l = lax.dynamic_slice_in_dim(tables, ci * length, length, 1)

    def projected(x, w, s):
        y = project(
            x.reshape(fn * seqs, length, width),
            w,
            bias_cols[s : s + 1],
            tables_l if s < 2 else None,
        )
        return y.reshape(cn, units, length, HEAD_DIM)

    def whole_units(x):
        return x.reshape(units, total, HEAD_DIM)

    def from_units(x):
        return exchange_ctx(x.reshape(units, cn, length, HEAD_DIM), False)

    def columns(x):
        x = x.reshape(fn * seqs, heads, length, HEAD_DIM)
        return x.transpose(0, 2, 1, 3).reshape(ntp, wcol)

    cols_of = [qkv_cols[:, s] for s in range(3)]
    g0, w0 = comm(9, gather_ctx(cols_of[0]), gather_fsdp(normed[0]))[::-1]
    p0 = projected(g0, w0, 0)
    q_u, w1, g1 = comm(4, exchange_ctx(p0, True), gather_ctx(cols_of[1]), gather_fsdp(normed[1]))
    p1 = projected(g1, w1, 1)
    p1, up_cols, out_rows, wdown = lax.optimization_barrier((p1, up_cols, out_weight, wdown))
    wout = lax.all_gather(out_rows, "ctx", axis=0, tiled=True)
    up_g = lax.all_gather(up_cols, "ctx", axis=0)
    k_u, w2, g2 = comm(4, exchange_ctx(p1, True), gather_ctx(cols_of[2]), gather_fsdp(normed[2]))
    p2 = projected(g2, w2, 2)
    (v_u,) = comm(5, exchange_ctx(p2, True))
    wqkv = [w.transpose(1, 0, 2, 3).reshape(width, wcol) for w in (w0, w1, w2)]
    q_u, k_u, v_u = whole_units(q_u), whole_units(k_u), whole_units(v_u)
    normed_g = [g.reshape(ntp, width) for g in (g0, g1, g2)]

    pos_all = jnp.arange(total, dtype=jnp.int32)
    unit_ids = ci * units + jnp.arange(units, dtype=jnp.int32)
    seq_ids = unit_ids // heads
    unit_starts = starts.reshape(fn * seqs, -1)[seq_ids]
    first_key = jnp.max(
        jnp.where(unit_starts[:, None, :] <= pos_all[None, :, None], unit_starts[:, None, :], 0),
        axis=-1,
    )[:, None, :]
    att_u, lse_u = attend(q_u, k_u, v_u, first_key)
    attended = columns(comm(6, from_units(att_u))[0])

    def scatter_tokens(x):
        return comm(10, scatter_fsdp(x.astype(BF16).reshape(fn, nloc, width)))[0]

    def gather_tokens(x):
        return comm(3, gather_fsdp(x))[0].reshape(ntp, width)

    hidden_res = streams[3] + scatter_tokens(dot("nd,de->ne", attended, wout)) + out_shift
    normed_mlp, mid_pull = jax.vjp(layer_norm, hidden_res, gain_all[3], shift_all[3])
    mlp_g = gather_tokens(normed_mlp.astype(BF16))
    up_bias_cols = lax.dynamic_slice_in_dim(up_shift, fi * fcol, fcol, 0)
    act_low, slope, wup = widen(mlp_g, up_g, up_bias_cols[None])
    result = hidden_res + scatter_tokens(dot("nf,fd->nd", act_low, wdown)) + down_shift
    block_out = result.astype(BF16).reshape(seqs, length, width)

    next_rows, mixer_pull = jax.vjp(
        mixer, result, root_full, mix_in_full, mix_out_weight, mix_out_bias
    )
    next_mix = next_rows.T.reshape(-1, seqs, length)
    grad_result, grad_root, grad_mix_in, grad_mix_out, grad_mix_bias = mixer_pull(
        mix_cotangent.reshape(-1, nloc).T
    )
    grad_result = grad_result + out_cotangent.reshape(nloc, width).astype(F32)

    grad_branch = grad_result.astype(BF16)
    branch_g = gather_tokens(grad_branch)
    grad_down_shift = jnp.sum(grad_branch.astype(F32), axis=0)

    low_bit = lax.rem(ci, 2)
    pairs = [(i, i ^ 1) for i in range(cn)]
    lines = [list(range(b, cn, 2)) for b in range(2)]

    def halves(x):
        x = x.reshape(cn // 2, 2, *x.shape[1:])
        away = lax.dynamic_index_in_dim(x, 1 - low_bit, 1, keepdims=False)
        kept = lax.dynamic_index_in_dim(x, low_bit, 1, keepdims=False)
        return away, kept

    def joined_half(kept, come):
        return (kept.astype(F32) + come.astype(F32)).astype(BF16)

    def line_scatter(x):
        y = lax.psum_scatter(
            x.reshape(-1, x.shape[-1]),
            "ctx",
            scatter_dimension=0,
            axis_index_groups=lines,
            tiled=True,
        )
        return y.reshape(x.shape[1:])

    down_part = dot("nf,nd->fd", act_low, branch_g).astype(BF16)
    down_part, wdown = lax.optimization_barrier((down_part, wdown))
    grad_down = lax.psum_scatter(down_part, "ctx", scatter_dimension=0, tiled=True)
    grad_active = dot("nd,fd->nf", branch_g, wdown)
    grad_upward = (grad_active * slope.astype(F32)).astype(BF16)
    grad_up_shift = jnp.sum(grad_upward.astype(F32), axis=0)
    up_part = dot("nd,nf->df", mlp_g, grad_upward).astype(BF16)
    up_part = up_part.reshape(fn, cn // 2, 2, rows, fcol)

    def up_rows(bit):
        x = lax.dynamic_index_in_dim(up_part, bit, 2, keepdims=False)
        return x.transpose(1, 0, 2, 3).reshape(cn // 2, -1, fcol)

    up_away, grad_upward = lax.optimization_barrier((up_rows(1 - low_bit), grad_upward))
    up_half = joined_half(up_rows(low_bit), lax.ppermute(up_away, "ctx", pairs))
    mlp_part = dot("nf,df->nd", grad_upward, wup).astype(BF16)
    grad_mlp = scatter_tokens(mlp_part)
    grad_hidden, grad_gain_mid, grad_shift_mid = mid_pull(grad_mlp)
    grad_hidden = grad_hidden + grad_result
    grad_attn = grad_hidden.astype(BF16)
    grad_out_shift = jnp.sum(grad_attn.astype(F32), axis=0)
    attn_g = gather_tokens(grad_attn)
    out_part = dot("nd,ne->de", attended, attn_g).astype(BF16)
    grad_att = dot("ne,de->nd", attn_g, wout).astype(BF16)
    grad_att = grad_att.reshape(fn * seqs, length, heads, HEAD_DIM).transpose(0, 2, 1, 3)
    out_away, out_kept = halves(out_part.reshape(cn, -1, width))
    (g_u,) = comm(5, exchange_ctx(grad_att.reshape(cn, units, length, HEAD_DIM), True))
    g_u, grad_down, up_half = lax.optimization_barrier((g_u, grad_down, up_half))
    grad_up = line_scatter(up_half)
    gq, gk, gv = attend_back(q_u, k_u, v_u, first_key, lse_u, att_u, whole_units(g_u), tables)

    def qkv_halves(p, s):
        x = dot("nd,nc->dc", normed_g[s], p).astype(BF16).reshape(fn, cn, rows, wcol)
        return halves(x.transpose(1, 0, 2, 3).reshape(cn, -1, wcol))

    def back_part(p, s):
        return dot("nc,dc->nd", p, wqkv[s]).astype(BF16).reshape(fn, nloc, width)

    gp0, out_come = comm(12, from_units(gq), exchange_pair(out_away))
    gp0 = columns(gp0)
    q_away, q_kept = qkv_halves(gp0, 0)
    gp1, q_come, gn0 = comm(
        8, from_units(gk), exchange_pair(q_away), scatter_fsdp(back_part(gp0, 0))
    )
    gp1 = columns(gp1)
    k_away, k_kept = qkv_halves(gp1, 1)
    gp2, k_come, gn1 = comm(
        8, from_units(gv), exchange_pair(k_away), scatter_fsdp(back_part(gp1, 1))
    )
    gp2, grad_up = lax.optimization_barrier((gp2, grad_up))
    out_half = joined_half(out_kept, out_come).reshape(cn // 2, -1, wcol)
    early = [joined_half(q_kept, q_come), joined_half(k_kept, k_come), out_half]
    early = line_scatter(jnp.concatenate(early, axis=1))
    grad_qk, grad_out = early[: 2 * fn * rows], early[2 * fn * rows :].reshape(rows, width)
    gp2 = columns(gp2)
    v_away, v_kept = qkv_halves(gp2, 2)
    gn2, v_come, grad_up = comm(
        7,
        scatter_fsdp(back_part(gp2, 2)),
        exchange_pair(v_away),
        exchange_fsdp(grad_up.reshape(fn, rows, fcol)),
    )
    grad_up = grad_up.transpose(1, 0, 2).reshape(rows, ff)
    grad_v = line_scatter(joined_half(v_kept, v_come))
    grad_proj = (gp0, gp1, gp2)
    grad_qkv = jnp.concatenate(
        [grad_qk.reshape(2, fn, rows, wcol), grad_v.reshape(1, fn, rows, wcol)], axis=0
    )
    grad_qkv = lax.all_to_all(grad_qkv.transpose(1, 0, 2, 3), "fsdp", 0, 0, tiled=True)
    grad_qkv = grad_qkv.transpose(2, 1, 0, 3).reshape(rows, 3, width).astype(F32)
    grad_qkv_shift = jnp.stack([jnp.sum(g.astype(F32), axis=0) for g in grad_proj])

    grad_history, grad_mix, grad_gain_front, grad_shift_front = last(
        hist2, mixes, streams, gain_all[:3], (gn0, gn1, gn2), grad_hidden
    )
    grad_history = grad_history.reshape(history.shape)
    grad_mix = grad_mix[:, : mix2.shape[0] * hist].T.reshape(dense_mix.shape)

    def own_columns(x, full):
        zero = jnp.zeros((x.shape[0], full), F32)
        return lax.dynamic_update_slice_in_dim(zero, x, fi * x.shape[1], 1)

    def parted(x):
        k = x.shape[0]
        return x.reshape(k, dn, -1).transpose(1, 0, 2).reshape(dn, -1)

    sums = [
        parted(jnp.concatenate([grad_gain_front, grad_gain_mid[None]], axis=0)),
        parted(jnp.concatenate([grad_shift_front, grad_shift_mid[None]], axis=0)),
        parted(own_columns(grad_qkv_shift, width)),
        parted(grad_out_shift[None]),
        parted(own_columns(grad_up_shift[None], ff)),
        parted(grad_down_shift[None]),
        parted(grad_root[None]),
        grad_mix_in.reshape(dn, -1),
    ]
    same = jnp.concatenate([grad_mix_out.reshape(-1), grad_mix_bias])
    sums.append(jnp.broadcast_to(same[None], (dn, same.size)))
    flat = jnp.concatenate(sums, axis=1)
    flat = jnp.pad(flat, ((0, 0), (0, -flat.shape[1] % 1024)))
    small = comm(2, scatter_small(flat.reshape(fn, cn, -1, 128)))[0].reshape(-1)
    out_small, at = [], 0
    for s, shape in zip(sums[:-1], [a.shape for a in parts[:-1]], strict=True):
        out_small.append(small[at : at + s.shape[1]].reshape(shape))
        at += s.shape[1]
    (g_gain, g_shift, g_qkv_b, g_out_b, g_up_b, g_down_b, g_root, g_mix_in) = out_small
    mix_sums = small[at : at + same.size]
    cut = grad_mix_out.size
    return (
        block_out,
        next_mix,
        grad_history,
        grad_mix,
        g_gain,
        g_shift,
        grad_qkv,
        g_qkv_b,
        grad_out.astype(F32),
        g_out_b,
        grad_up.astype(F32),
        g_up_b,
        grad_down.astype(F32),
        g_down_b,
        g_root,
        g_mix_in,
        mix_sums[:cut].reshape(grad_mix_out.shape),
        mix_sums[cut:],
    )


def solution(mesh):
    token = P(None, "fsdp", "ctx")
    both = P(BOTH)
    cols = P(None, BOTH)
    placed = (
        token,
        P(None, None, "fsdp", "ctx"),
        P("fsdp"),
        cols,
        cols,
        both,
        cols,
        both,
        both,
        both,
        both,
        both,
        both,
        both,
        both,
        P(),
        P(),
        P("fsdp", "ctx"),
        token,
    )
    outs = (
        P("fsdp", "ctx"),
        token,
        token,
        P(None, None, "fsdp", "ctx"),
        cols,
        cols,
        both,
        cols,
        both,
        both,
        both,
        both,
        both,
        both,
        both,
        both,
        P(),
        P(),
    )
    return jax.shard_map(body, mesh=mesh, in_specs=placed, out_specs=outs, check_vma=False)
```

time: 1300 us -> 1140 us (0.88)
  Pallas kernels: 457 us -> 871 us
  waiting for transfers between devices: 228 us -> 19.1 us
  blocking collectives: 143 us -> 0 us
  matrix products: 172 us -> 97.5 us
  other arithmetic: 108 us -> 34.3 us
  local copies, waits for them, and re-layouts: 149 us -> 94.5 us
  starting transfers between devices: 22.9 us -> 5.03 us
    pallas_call x10 -> x24, Pallas kernels: 421 us -> 831 us  [the longest x18 756 us: comm(): pl.pallas_call(kernel, out_shape=[t[2] for t in tasks], in_specs=[t[3] fo...]
    all_to_all x5 -> x1, waiting for transfers between devices: 175 us -> 8.43 us  [body(): lax.all_to_all(grad_qkv.transpose(1, 0, 2, 3), 'fsdp', 0, 0, tiled=True)]
    all_to_all x3 -> x0, blocking collectives: 143 us -> none  [the longest x1 111 us: from_units(): x = lax.all_to_all(x, 'ctx', 0, 0, tiled=True)]
    dot_general x12 -> x14, matrix products: 159 us -> 86.6 us  [dot(): return jnp.einsum(pattern, left, right, preferred_element_type=F32)]
    reduce_scatter x4, waiting for transfers between devices: 51.6 us -> 9.22 us  [the longest x1 9.2 us: body(): lax.psum_scatter(down_part, 'ctx', scatter_dimension=0, tiled=True)]
    reduce_sum x3, other arithmetic: 31.1 us -> 3.28 us  [body(): jnp.sum(g.astype(F32), axis=0)]
    slice x11 -> x7, local copies, waits for them, and re-layouts: 28.2 us -> 1.51 us  [the longest x4 1.42 us: body(): streams, normed = front(hist2, mixes, gain_all[:3], shift_all[:3])]
    all_to_all x5 -> x1, starting transfers between devices: 22.3 us -> 3.48 us  [body(): lax.all_to_all(grad_qkv.transpose(1, 0, 2, 3), 'fsdp', 0, 0, tiled=True)]
  transfers between devices with their start and end apart: 13 -> 9, of which waited for: 5 -> 2; matrix products, arithmetic and copies ran while one was open for 26% -> 14% of each run, Pallas kernels for 26% -> 70%
where the time goes in v2:
time: 1140 us
  Pallas kernels  871 us (76%)
  matrix products  97.5 us (9%)
  local copies, waits for them, and re-layouts  94.5 us (8%)
  other arithmetic  34.3 us (3%)
  waiting for transfers between devices  19.1 us (2%)
  between operations  15.9 us (1%)
    pallas_call x18, Pallas kernels, comm(): pl.pallas_call(kernel, out_shape=[t[2] for t in tasks], in_specs=[t[3] fo...  756 us
    dot_general x14, matrix products, dot(): return jnp.einsum(pattern, left, right, preferred_element_type=F32)  86.6 us
    unnamed x170, local copies, waits for them, and re-layouts  34.9 us
    pallas_call x1, Pallas kernels, last(): pl.pallas_call(kernel, grid=(n // tokens,), in_specs=[pl.BlockSpec((h, to...  27.2 us
    pallas_call x1, Pallas kernels, attend_back(): pl.pallas_call(kernel, grid=(u, t // block), in_specs=[pl.BlockSpec(spec,...  24.9 us
  transfers between devices with their start and end apart: 9, of which 2 were waited for; matrix products, arithmetic and copies ran while one was open for 14% of the time, Pallas kernels for 70%

profile of v2, /device:TPU:1, one launch (start us, length us, event | category | flops | bytes accessed | tf_op | source)
XLA Modules:
  0.0 1137.6 jit_solution(6219252907121593840)
XLA Ops:
  10.1 33.4 %shard_map.340 = (f32[4,8,32,128]{3,2,1,0:T(8,128)S(1)}, bf16[4,3,64,512]{3,2,1,0:T(8,128)(2,1)S(1)}, bf16[4,64,2048]{2,1,0:T(8,128)(2,1)}) custom-call(f32[32,128]{1,0:T(8,128)S(1)} %pad_bitcast_fusion.1.refs_0_, bf16[4,3,64,512]{3,2,1,0:T(8,128)(2,1)S(1)} %bitcast.298, bf16[4,64,2048]{2,1,0:T(8,128)(2,1)S(1)} %bitcast.289), custom_call_target="tpu_custom_call" | custom-call | bytes 15000000 | tf_op jit(solution)/shard_map/pallas_call | solution.py:136
  46.5 17.6 %shard_map.341 = (f32[4,256,2048]{2,1,0:T(8,128)}, bf16[3,256,2048]{2,1,0:T(8,128)(2,1)}) custom-call(bf16[9,256,2048]{2,1,0:T(8,128)(2,1)} %bitcast.324, f32[256,128]{1,0:T(8,128)} %pad.25.m_ref, f32[3,2048]{1,0:T(4,128)} %slice.134.g_ref, f32[3,2048]{1,0:T(4,128)} %slice.137.b_ref), custom_call_target="tpu_custom_call" | custom-call | flops 37748736 | bytes 20971520 | tf_op jit(solution)/shard_map/pallas_call | solution.py:831
  64.2 2.7 slice_bitcast_fusion
  66.9 66.7 %shard_map.342 = (bf16[8,4,64,512]{3,2,1,0:T(8,128)(2,1)S(1)}, bf16[4,256,2048]{2,1,0:T(8,128)(2,1)S(1)}) custom-call(bf16[4,64,512]{2,1,0:T(8,128)(2,1)S(1)} %get-tuple-element.266.refs_0_, bf16[256,2048]{1,0:T(8,128)(2,1)S(1)} %get-tuple-element.262.refs_1_), custom_call_target="tpu_custom_call" | custom-call | bytes 15000000 | tf_op jit(solution)/shard_map/pallas_call | solution.py:136
  134.9 2.1 copy-done.25
  139.7 2.2 copy-done.26
  141.9 4.1 shard_map.343
  146.0 58.9 %shard_map.344 = (bf16[2,8,256,128]{3,2,1,0:T(8,128)(2,1)S(1)}, bf16[8,4,64,512]{3,2,1,0:T(8,128)(2,1)S(1)}, bf16[4,256,2048]{2,1,0:T(8,128)(2,1)S(1)}) custom-call(bf16[8,2,256,128]{3,2,1,0:T(8,128)(2,1)S(1)} %bitcast.308, bf16[4,64,512]{2,1,0:T(8,128)(2,1)S(1)} %get-tuple-element.265.refs_1_, bf16[256,2048]{1,0:T(8,128)(2,1)S(1)} %get-tuple-element.261.refs_2_), custom_call_target="tpu_custom_call" | custom-call | bytes 15000000 | tf_op jit(solution)/shard_map/pallas_call | solution.py:136
  205.9 4.1 shard_map.345
  211.4 1.9 copy-done.28
  216.7 1.8 reshape.494
  218.5 71.3 %shard_map.346 = (bf16[2,8,256,128]{3,2,1,0:T(8,128)(2,1)S(1)}, bf16[8,4,64,512]{3,2,1,0:T(8,128)(2,1)S(1)}, bf16[4,256,2048]{2,1,0:T(8,128)(2,1)S(1)}) custom-call(bf16[8,2,256,128]{3,2,1,0:T(8,128)(2,1)S(1)} %bitcast.305, bf16[4,64,512]{2,1,0:T(8,128)(2,1)S(1)} %get-tuple-element.264.refs_1_, bf16[256,2048]{1,0:T(8,128)(2,1)S(1)} %get-tuple-element.260.refs_2_), custom_call_target="tpu_custom_call" | custom-call | bytes 15000000 | tf_op jit(solution)/shard_map/pallas_call | solution.py:136
  289.9 3.1 shard_map.347
  293.1 35.4 %shard_map.348 = bf16[2,8,256,128]{3,2,1,0:T(8,128)(2,1)S(1)} custom-call(bf16[8,2,256,128]{3,2,1,0:T(8,128)(2,1)S(1)} %bitcast.309), custom_call_target="tpu_custom_call" | custom-call | bytes 15000000 | tf_op jit(solution)/shard_map/pallas_call | solution.py:136
  328.5 15.4 %shard_map.349 = (bf16[2,2048,128]{2,1,0:T(8,128)(2,1)S(1)}, f32[2,1,2048]{2,1,0:T(1,128)S(1)}) custom-call(bf16[2,2048,128]{2,1,0:T(8,128)(2,1)S(1)} %bitcast.320, bf16[2,2048,128]{2,1,0:T(8,128)(2,1)S(1)} %bitcast.322, bf16[2,2048,128]{2,1,0:T(8,128)(2,1)S(1)} %bitcast.302, s32[2,1,2048]{2,1,0:T(1,128)S(1)} %broadcast_in_dim.29.s_ref), custom_call_target="tpu_custom_call" | custom-call | flops 2147483648 | bytes 8388608 | tf_op jit(solution)/shard_map/pallas_call | solution.py:589
  343.8 41.9 %shard_map.350 = bf16[8,2,256,128]{3,2,1,0:T(8,128)(2,1)S(1)} custom-call(bf16[2,8,256,128]{3,2,1,0:T(8,128)(2,1)S(1)} %bitcast.304), custom_call_target="tpu_custom_call" | custom-call | bytes 15000000 | tf_op jit(solution)/shard_map/pallas_call | solution.py:136
  387.6 4.3 convolution_convert_fusion.7
  391.9 44.7 %shard_map.351 = f32[256,2048]{1,0:T(8,128)S(1)} custom-call(bf16[4,256,2048]{2,1,0:T(8,128)(2,1)S(1)} %bitcast.287), custom_call_target="tpu_custom_call" | custom-call | bytes 15000000 | tf_op jit(solution)/shard_map/pallas_call | solution.py:136
  436.6 1.9 fusion.57
  440.4 27.2 %shard_map.352 = bf16[4,256,2048]{2,1,0:T(8,128)(2,1)S(1)} custom-call(bf16[256,2048]{1,0:T(8,128)(2,1)S(1)} %add_convert_fusion.refs_0_), custom_call_target="tpu_custom_call" | custom-call | bytes 15000000 | tf_op jit(solution)/shard_map/pallas_call | solution.py:136
  467.6 2.0 copy-done.1
  469.5 18.2 %shard_map.353 = (bf16[1024,2048]{1,0:T(8,128)(2,1)S(1)}, bf16[1024,2048]{1,0:T(8,128)(2,1)}, bf16[2048,2048]{1,0:T(8,128)(2,1)}) custom-call(bf16[1024,2048]{1,0:T(8,128)(2,1)} %bitcast.277, bf16[8,4,64,2048]{3,2,1,0:T(8,128)(2,1)} %bitcast.377, f32[1,2048]{1,0:T(1,128)S(1)} %bitcast.316), custom_call_target="tpu_custom_call" | custom-call | flops 8589934592 | bytes 60000000 | tf_op jit(solution)/shard_map/pallas_call | solution.py:789
  487.8 11.5 %convolution_convert_fusion.6 = bf16[1024,2048]{1,0:T(8,128)(2,1)S(1)} fusion(bf16[1024,2048]{1,0:T(8,128)(2,1)S(1)} %get-tuple-element.84, bf16[2048,2048]{1,0:T(8,128)(2,1)} %all-gather.5.cloned.1.call-done), kind=kOutput, calls=%fused_computation.14 | convolution fusion | flops 8592031744 | bytes 16777216 | tf_op jit(solution)/shard_map/nf,fd->nd/dot_general | solution.py:69
  499.3 27.0 %shard_map.354 = f32[256,2048]{1,0:T(8,128)S(1)} custom-call(bf16[4,256,2048]{2,1,0:T(8,128)(2,1)S(1)} %bitcast.288), custom_call_target="tpu_custom_call" | custom-call | bytes 15000000 | tf_op jit(solution)/shard_map/pallas_call | solution.py:136
  526.7 2.0 fusion.35
  528.9 3.0 multiply_reduce_fusion
  533.4 27.5 %shard_map.355 = bf16[4,256,2048]{2,1,0:T(8,128)(2,1)S(1)} custom-call(bf16[256,2048]{1,0:T(8,128)(2,1)S(1)} %get-tuple-element.248.refs_0_), custom_call_target="tpu_custom_call" | custom-call | bytes 15000000 | tf_op jit(solution)/shard_map/pallas_call | solution.py:136
  560.9 1.9 copy-done.3
  562.9 11.8 %convolution_convert_fusion.1 = bf16[2048,2048]{1,0:T(8,128)(2,1)} fusion(bf16[1024,2048]{1,0:T(8,128)(2,1)S(1)} %get-tuple-element.84, bf16[1024,2048]{1,0:T(8,128)(2,1)S(1)} %bitcast.279), kind=kOutput, calls=%fused_computation.6 | convolution fusion | flops 8594128896 | bytes 16777216 | tf_op jit(solution)/shard_map/nf,nd->fd/dot_general | solution.py:69
  574.7 13.4 %convert_reduce_fusion = (f32[2048]{0:T(1024)S(1)}, bf16[1024,2048]{1,0:T(8,128)(2,1)S(1)}) fusion(bf16[1024,2048]{1,0:T(8,128)(2,1)} %get-tuple-element.88, bf16[1024,2048]{1,0:T(8,128)(2,1)} %bitcast.280, bf16[2048,2048]{1,0:T(8,128)(2,1)} %all-gather.5.cloned.1.call-done), kind=kOutput, calls=%fused_computation.3 | convolution fusion | flops 8600418304 | bytes 20979712 | tf_op jit(solution)/shard_map/nd,fd->nf/dot_general | solution.py:69
  588.1 11.3 convolution_convert_fusion
  599.4 7.3 constant_dynamic-slice_fusion.1
  606.7 2.4 copy.273
  609.5 11.7 %convolution_convert_fusion.5 = bf16[1024,2048]{1,0:T(8,128)(2,1)S(1)} fusion(bf16[1024,2048]{1,0:T(8,128)(2,1)S(1)} %get-tuple-element.89, bf16[2048,2048]{1,0:T(8,128)(2,1)} %get-tuple-element.90), kind=kOutput, calls=%fused_computation.13 | convolution fusion | flops 8592031744 | bytes 16777216 | tf_op jit(solution)/shard_map/nf,df->nd/dot_general | solution.py:69
  621.2 27.6 %shard_map.356 = f32[256,2048]{1,0:T(8,128)S(1)} custom-call(bf16[4,256,2048]{2,1,0:T(8,128)(2,1)S(1)} %bitcast.286), custom_call_target="tpu_custom_call" | custom-call | bytes 15000000 | tf_op jit(solution)/shard_map/pallas_call | solution.py:136
  652.1 3.3 convert_reduce_fusion.2
  655.3 26.9 %shard_map.357 = bf16[4,256,2048]{2,1,0:T(8,128)(2,1)S(1)} custom-call(bf16[256,2048]{1,0:T(8,128)(2,1)S(1)} %get-tuple-element.250.refs_0_), custom_call_target="tpu_custom_call" | custom-call | bytes 15000000 | tf_op jit(solution)/shard_map/pallas_call | solution.py:136
  682.3 2.0 copy-done.4
  684.3 2.4 convolution_convert_fusion.12
  687.1 72.1 %shard_map.358 = bf16[2,8,256,128]{3,2,1,0:T(8,128)(2,1)S(1)} custom-call(bf16[8,2,256,128]{3,2,1,0:T(8,128)(2,1)S(1)} %bitcast.296), custom_call_target="tpu_custom_call" | custom-call | bytes 15000000 | tf_op jit(solution)/shard_map/pallas_call | solution.py:136
  760.4 6.5 fusion
  766.9 9.2 reduce-scatter.5.cloned.1.call-done
  782.2 2.5 convolution_convert_fusion.11
  786.2 24.9 %shard_map.359 = (bf16[2,2048,128]{2,1,0:T(8,128)(2,1)S(1)}, bf16[2,2048,128]{2,1,0:T(8,128)(2,1)S(1)}, bf16[2,2048,128]{2,1,0:T(8,128)(2,1)S(1)}) custom-call(bf16[2,2048,128]{2,1,0:T(8,128)(2,1)S(1)} %bitcast.321, bf16[2,2048,128]{2,1,0:T(8,128)(2,1)S(1)} %bitcast.323, bf16[2,2048,128]{2,1,0:T(8,128)(2,1)} %bitcast.303, ...), custom_call_target="tpu_custom_call" | custom-call | flops 5368709120 | bytes 20971520 | tf_op jit(solution)/shard_map/pallas_call | solution.py:676
  811.2 45.2 %shard_map.360 = (bf16[8,2,256,128]{3,2,1,0:T(8,128)(2,1)S(1)}, bf16[4,64,2048]{2,1,0:T(8,128)(2,1)S(1)}) custom-call(bf16[2,8,256,128]{3,2,1,0:T(8,128)(2,1)S(1)} %bitcast.307, bf16[4,64,2048]{2,1,0:T(8,128)(2,1)S(1)} %dynamic-slice_bitcast_fusion.4.refs_1_), custom_call_target="tpu_custom_call" | custom-call | bytes 15000000 | tf_op jit(solution)/shard_map/pallas_call | solution.py:136
  857.2 2.5 convolution_convert_fusion.10
  860.0 2.4 convolution_convert_fusion.4
  862.4 59.2 %shard_map.361 = (bf16[8,2,256,128]{3,2,1,0:T(8,128)(2,1)S(1)}, bf16[4,256,512]{2,1,0:T(8,128)(2,1)S(1)}, f32[256,2048]{1,0:T(8,128)S(1)}) custom-call(bf16[2,8,256,128]{3,2,1,0:T(8,128)(2,1)S(1)} %bitcast.312, bf16[4,256,512]{2,1,0:T(8,128)(2,1)S(1)} %dynamic-slice_bitcast_fusion.3.refs_1_, bf16[4,256,2048]{2,1,0:T(8,128)(2,1)S(1)} %bitcast.284), custom_call_target="tpu_custom_call" | custom-call | bytes 15000000 | tf_op jit(solution)/shard_map/pallas_call | solution.py:136
  922.5 2.5 convolution_convert_fusion.9
  930.4 3.7 convolution_convert_fusion.3
  934.1 36.9 %shard_map.362 = (bf16[8,2,256,128]{3,2,1,0:T(8,128)(2,1)S(1)}, bf16[4,256,512]{2,1,0:T(8,128)(2,1)S(1)}, f32[256,2048]{1,0:T(8,128)S(1)}) custom-call(bf16[2,8,256,128]{3,2,1,0:T(8,128)(2,1)S(1)} %bitcast.311, bf16[4,256,512]{2,1,0:T(8,128)(2,1)S(1)} %dynamic-slice_bitcast_fusion.2.refs_1_, bf16[4,256,2048]{2,1,0:T(8,128)(2,1)S(1)} %bitcast.283), custom_call_target="tpu_custom_call" | custom-call | bytes 15000000 | tf_op jit(solution)/shard_map/pallas_call | solution.py:136
  971.4 2.0 copy-done.46
  973.7 1.8 pad_maximum_fusion
  977.2 3.3 copy.283
  980.7 4.5 fusion.8
  986.0 4.6 convolution_convert_fusion.8
  992.4 2.4 convolution_convert_fusion.2
  994.8 38.0 %shard_map.363 = (f32[256,2048]{1,0:T(8,128)S(1)}, bf16[4,256,512]{2,1,0:T(8,128)(2,1)S(1)}, bf16[4,64,2048]{2,1,0:T(8,128)(2,1)S(1)}) custom-call(bf16[4,256,2048]{2,1,0:T(8,128)(2,1)S(1)} %bitcast.285, bf16[4,256,512]{2,1,0:T(8,128)(2,1)S(1)} %dynamic-slice_bitcast_fusion.1.refs_1_, bf16[4,64,2048]{2,1,0:T(8,128)(2,1)S(1)} %bitcast.310), custom_call_target="tpu_custom_call" | custom-call | bytes 15000000 | tf_op jit(solution)/shard_map/pallas_call | solution.py:136
  1044.1 2.1 reduce.17
  1052.8 2.8 convert_element_type.258
  1061.2 27.2 %shard_map.364 = (f32[9,256,2048]{2,1,0:T(8,128)}, f32[256,128]{1,0:T(8,128)}, f32[3,2048]{1,0:T(4,128)}, f32[3,2048]{1,0:T(4,128)}) custom-call(bf16[9,256,2048]{2,1,0:T(8,128)(2,1)} %bitcast.325, f32[256,128]{1,0:T(8,128)} %pad.25.m_ref, f32[4,256,2048]{2,1,0:T(8,128)} %get-tuple-element.68.s_ref, f32[3,2048]{1,0:T(4,128)} %slice.134.g_ref, ...), custom_call_target="tpu_custom_call" | custom-call | flops 75497472 | bytes 45088768 | tf_op jit(solution)/shard_map/pallas_call | solution.py:905
  1090.8 16.6 %shard_map.365 = f32[48,128]{1,0:T(8,128)S(1)} custom-call(f32[4,8,48,128]{3,2,1,0:T(8,128)S(1)} %copy.377), custom_call_target="tpu_custom_call" | custom-call | bytes 15000000 | tf_op jit(solution)/shard_map/pallas_call | solution.py:136
  1114.8 3.5 all-to-all-start
  1120.6 8.4 all-to-all-done
  (319 shorter events, 83.3 us)
Async XLA Ops:
  7.2 521.5 %copy-start = (f32[40,40]{1,0:T(8,128)S(1)}, f32[40,40]{1,0:T(8,128)}, u32[]{:S(2)}) copy-start(f32[40,40]{1,0:T(8,128)} %param.36) | copy-start | bytes 19204
  7.2 2.2 copy-start.55
  7.2 206.1 %all-gather.5.cloned.1.call-start = ((), (), s32[]{:S(2)}) async-start(), calls=%async_computation.5 | async-start | bytes 9437184 | tf_op jit(solution)/shard_map/all_gather | solution.py:973
  8.0 2.0 copy-start.80
  8.0 2.0 copy-start.75
  8.0 2.0 copy-start.76
  8.0 379.6 %all-gather.7.cloned.1.call-start = ((), (), s32[]{:S(2)}) async-start(), calls=%async_computation.6 | async-start | bytes 2359296 | tf_op jit(solution)/shard_map/all_gather | solution.py:1047
  9.5 35.9 %copy-start.70 = (f32[4,9,1,256]{3,2,1,0:T(1,128)S(1)}, f32[4,9,1,256]{3,2,1,0:T(1,128)}, u32[]{:S(2)}) copy-start(f32[4,9,1,256]{3,2,1,0:T(1,128)} %param.22) | copy-start | bytes 110596
  134.9 2.1 copy-start.25
  139.7 2.2 copy-start.26
  213.4 256.2 %all-gather.9.cloned.1.call-start = ((), (), s32[]{:S(2)}) async-start(), calls=%async_computation.11 | async-start | bytes 9437184 | tf_op jit(solution)/shard_map/all_gather | solution.py:1048
  214.1 562.0 %reduce-scatter.5.cloned.1.call-start = ((), (), s32[]{:S(2)}) async-start(), calls=%async_computation.7 | async-start | bytes 9437184 | tf_op jit(solution)/shard_map/reduce_scatter | solution.py:1119
  289.9 3.2 copy-start.14
  289.9 3.2 copy-start.30
  289.9 38.6 %copy-start.34 = (bf16[2,8,256,128]{3,2,1,0:T(8,128)(2,1)}, bf16[2,8,256,128]{3,2,1,0:T(8,128)(2,1)S(1)}, u32[]{:S(2)}) copy-start(bf16[2,8,256,128]{3,2,1,0:T(8,128)(2,1)S(1)} %get-tuple-element.78) | copy-start | bytes 3145732
  293.0 35.4 %copy-start.32 = (bf16[2,8,256,128]{3,2,1,0:T(8,128)(2,1)S(1)}, bf16[2,8,256,128]{3,2,1,0:T(8,128)(2,1)}, u32[]{:S(2)}) copy-start(bf16[2,8,256,128]{3,2,1,0:T(8,128)(2,1)} %copy-done.31) | copy-start | bytes 3145732
  328.4 15.4 %copy-start.17 = (bf16[2,8,256,128]{3,2,1,0:T(8,128)(2,1)}, bf16[2,8,256,128]{3,2,1,0:T(8,128)(2,1)S(1)}, u32[]{:S(2)}) copy-start(bf16[2,8,256,128]{3,2,1,0:T(8,128)(2,1)S(1)} %shard_map.348) | copy-start | bytes 3145732
  387.6 4.3 copy-start.52
  467.6 2.0 copy-start.1
  499.3 27.0 %copy-start.39 = (f32[256,2048]{1,0:T(8,128)S(1)}, f32[256,2048]{1,0:T(8,128)}, u32[]{:S(2)}) copy-start(f32[256,2048]{1,0:T(8,128)} %copy-done.38) | copy-start | bytes 6291460
  526.7 124.2 %copy-start.36 = (f32[256,2048]{1,0:T(8,128)}, f32[256,2048]{1,0:T(8,128)S(1)}, u32[]{:S(2)}) copy-start(f32[256,2048]{1,0:T(8,128)S(1)} %get-tuple-element.255) | copy-start | bytes 6291460
  526.7 2.1 copy-start.62
  528.7 3.2 copy-start.56
  528.7 3.2 copy-start.58
  528.9 3.0 copy-start.60
  528.9 3.0 copy-start.47
  574.7 410.5 %reduce-scatter.7.cloned.1.call-start = ((), (), s32[]{:S(2)}) async-start(), calls=%async_computation.8 | async-start | bytes 5242880 | tf_op jit(solution)/shard_map/reduce_scatter | solution.py:1108
  574.7 13.4 %copy-start.2 = (bf16[4,256,2048]{2,1,0:T(8,128)(2,1)S(1)}, bf16[4,256,2048]{2,1,0:T(8,128)(2,1)}, u32[]{:S(2)}) copy-start(bf16[4,256,2048]{2,1,0:T(8,128)(2,1)} %copy-done.1) | copy-start | bytes 12582916
  609.1 151.3 %collective-permute-start = (bf16[4,256,2048]{2,1,0:T(8,128)(2,1)}, bf16[4,256,2048]{2,1,0:T(8,128)(2,1)}, u32[]{:S(2)}, u32[]{:S(2)}) collective-permute-start(bf16[4,256,2048]{2,1,0:T(8,128)(2,1)} %bitcast.41), channel_id=1, source_target_pairs={{0,1},{1,0},{2,3},{3,2},{4,5},{5,4},{6,7},{7,6},{8,9},{9,8},{10,11... | collective-permute-start | bytes 12582920 | tf_op jit(solution)/shard_map/ppermute | solution.py:1131
  621.2 27.6 %copy-start.40 = (f32[256,2048]{1,0:T(8,128)S(1)}, f32[256,2048]{1,0:T(8,128)}, u32[]{:S(2)}) copy-start(f32[256,2048]{1,0:T(8,128)} %copy-done.38) | copy-start | bytes 6291460
  655.3 28.9 %copy-start.79 = (bf16[512,2048]{1,0:T(8,128)(2,1)S(1)}, bf16[512,2048]{1,0:T(8,128)(2,1)}, u32[]{:S(2)}) copy-start(bf16[512,2048]{1,0:T(8,128)(2,1)} %all-gather.7.cloned.1.call-done) | copy-start | bytes 6291460
  682.2 2.0 copy-start.4
  686.9 72.3 %copy-start.43 = (bf16[4,4,1,64,2048]{4,3,2,1,0:T(8,128)(2,1)S(1)}, bf16[4,4,1,64,2048]{4,3,2,1,0:T(8,128)(2,1)}, u32[]{:S(2)}) copy-start(bf16[4,4,1,64,2048]{4,3,2,1,0:T(8,128)(2,1)} %get-tuple-element.258) | copy-start | bytes 12582916
  776.1 4.7 copy-start.53
  776.1 281.7 %reduce-scatter.9.cloned.1.call-start = ((), (), s32[]{:S(2)}) async-start(), calls=%async_computation.9 | async-start | bytes 3932160 | tf_op jit(solution)/shard_map/reduce_scatter | solution.py:1108
  779.3 2.9 copy-start.5
  811.2 46.0 %copy-start.23 = (bf16[2,2048,128]{2,1,0:T(8,128)(2,1)}, bf16[2,2048,128]{2,1,0:T(8,128)(2,1)S(1)}, u32[]{:S(2)}) copy-start(bf16[2,2048,128]{2,1,0:T(8,128)(2,1)S(1)} %get-tuple-element.98) | copy-start | bytes 3145732
  811.2 46.0 %copy-start.27 = (bf16[4,256,2048]{2,1,0:T(8,128)(2,1)S(1)}, bf16[4,256,2048]{2,1,0:T(8,128)(2,1)}, u32[]{:S(2)}) copy-start(bf16[4,256,2048]{2,1,0:T(8,128)(2,1)} %copy-done.25) | copy-start | bytes 12582916
  859.9 2.5 copy-start.44
  862.4 60.1 %copy-start.29 = (bf16[4,256,2048]{2,1,0:T(8,128)(2,1)S(1)}, bf16[4,256,2048]{2,1,0:T(8,128)(2,1)}, u32[]{:S(2)}) copy-start(bf16[4,256,2048]{2,1,0:T(8,128)(2,1)} %copy-done.28) | copy-start | bytes 12582916
  921.7 3.3 copy-start.6
  921.7 3.3 copy-start.20
  922.5 2.5 copy-start.54
  930.4 3.7 copy-start.24
  934.1 37.0 %copy-start.21 = (bf16[4,256,512]{2,1,0:T(8,128)(2,1)S(1)}, bf16[4,256,512]{2,1,0:T(8,128)(2,1)}, u32[]{:S(2)}) copy-start(bf16[4,256,512]{2,1,0:T(8,128)(2,1)} %copy-done.20) | copy-start | bytes 3145732
  934.1 37.0 %copy-start.45 = (bf16[4,8,64,512]{3,2,0,1:T(8,128)(2,1)S(1)}, bf16[4,8,64,512]{3,2,0,1:T(8,128)(2,1)}, u32[]{:S(2)}) copy-start(bf16[4,8,64,512]{3,2,0,1:T(8,128)(2,1)} %copy-done.44) | copy-start | bytes 6291460
  971.0 2.7 copy-start.7
  971.0 2.4 copy-start.46
  971.4 2.3 copy-start.49
  975.5 137.2 %reduce-scatter.11.cloned.1.call-start = ((), (), s32[]{:S(2)}) async-start(), calls=%async_computation.10 | async-start | bytes 1310720 | tf_op jit(solution)/shard_map/reduce_scatter | solution.py:1108
  977.2 3.3 copy-start.57
  977.2 3.3 copy-start.59
  977.2 3.5 copy-start.37
  977.2 3.5 copy-start.61
  992.4 2.4 copy-start.22
  1061.2 28.0 %copy-start.69 = (f32[1,32,64]{2,1,0:T(8,128)S(1)}, f32[1,32,64]{2,1,0:T(8,128)}, u32[]{:S(2)}) copy-start(f32[1,32,64]{2,1,0:T(8,128)} %concatenate.48) | copy-start | bytes 24580
  1061.2 29.1 %copy-start.68 = (f32[1,32,64]{2,1,0:T(8,128)S(1)}, f32[1,32,64]{2,1,0:T(8,128)}, u32[]{:S(2)}) copy-start(f32[1,32,64]{2,1,0:T(8,128)} %concatenate.45) | copy-start | bytes 24580
  1061.2 29.3 %copy-start.64 = (f32[32,256]{1,0:T(8,128)S(1)}, f32[32,256]{1,0:T(8,128)}, u32[]{:S(2)}) copy-start(f32[32,256]{1,0:T(8,128)} %reshape_transpose_reshape.3) | copy-start | bytes 98308
  1061.2 29.3 %copy-start.66 = (f32[32,64]{1,0:T(8,128)S(1)}, f32[32,64]{1,0:T(8,128)}, u32[]{:S(2)}) copy-start(f32[32,64]{1,0:T(8,128)} %reshape_transpose_reshape_broadcast_in_dim.10) | copy-start | bytes 24580
  1061.2 29.3 %copy-start.67 = (f32[32,64]{1,0:T(8,128)S(1)}, f32[32,64]{1,0:T(8,128)}, u32[]{:S(2)}) copy-start(f32[32,64]{1,0:T(8,128)} %reshape_transpose_reshape_broadcast_in_dim.11) | copy-start | bytes 24580
  1090.6 21.4 %copy-start.65 = (f32[256,128]{1,0:T(8,128)S(1)}, f32[256,128]{1,0:T(8,128)}, u32[]{:S(2)}) copy-start(f32[256,128]{1,0:T(8,128)} %get-tuple-element.107) | copy-start | bytes 393220
  1090.6 22.2 %slice-start = ((bf16[768,512]{1,0:T(8,128)(2,1)}), bf16[512,512]{1,0:T(8,128)(2,1)S(1)}, s32[]{:S(2)}) async-start(bf16[768,512]{1,0:T(8,128)(2,1)} %reduce-scatter.9.cloned.1.call-done), calls=%async_computation.12 | async-start | bytes 1048576 | tf_op jit(solution)/shard_map/slice | solution.py:1170
  1112.8 5.5 copy-start.16
  1114.8 14.2 %all-to-all-start = ((bf16[4,3,64,512]{3,2,1,0:T(8,128)(2,1)}), bf16[4,3,64,512]{3,2,1,0:T(8,128)(2,1)S(1)}, u32[]{:S(2)}, u32[]{:S(2)}) async-start(bf16[4,3,64,512]{3,2,1,0:T(8,128)(2,1)} %copy.294), calls=%async_computation.4 | async-start | bytes 1572864 | tf_op jit(solution)/shard_map/all_to_all | solution.py:1185
  (27 other events, 41.0 us)
Sparse Core Ops, SparseCore 0:
  10.2 161.3 all-gather.4
  213.5 71.0 all-gather.6
  286.7 164.9 all-gather.8
  574.8 201.2 reduce-scatter.4
  778.3 98.6 reduce-scatter.6
  975.6 59.5 reduce-scatter.8
  1037.5 27.1 reduce-scatter.10

commit v3 on v2

--- a/solution.py
+++ b/solution.py
@@ -115,7 +115,13 @@
 
     def kernel(*refs):
         targets, seen = [], []
-        covered = [(along_fsdp, [along_both]), (the_pair, [along_ctx])]
+        covered = [
+            (along_fsdp, [along_both]),
+            (the_pair, [along_ctx]),
+            (the_pair, [plane_others]),
+            (links_and_twin, [plane_others]),
+            (along_fsdp, [plane_others]),
+        ]
         for t in tasks:
             if t[0] not in seen and (t[0], seen[:1]) not in covered:
                 seen.append(t[0])
@@ -140,7 +146,7 @@
         out_specs=[t[4] for t in tasks],
         scratch_shapes=[x for t in tasks for x in t[5]],
         compiler_params=pltpu.CompilerParams(
-            collective_id=cid, has_side_effects=True, vmem_limit_bytes=40 * 2**20
+            collective_id=cid, has_side_effects=True, vmem_limit_bytes=56 * 2**20
         ),
         cost_estimate=pl.CostEstimate(flops=0, bytes_accessed=15_000_000, transcendentals=0),
     )(*[t[1] for t in tasks])
@@ -483,6 +489,336 @@
     block = pltpu.VMEM((chips, parts, step, d), BF16)
     scratch = [block] * 4 + [pltpu.VMEM((parts, step, d), F32)] + [dma(chips, parts)] * 5
     return (links_and_twin, x, jax.ShapeDtypeStruct((n, d), F32), ANY, ANY, scratch, body)
+
+
+def plane_others():
+    fn = lax.axis_size("fsdp")
+    f, c = place()
+    (pair,) = the_pair()
+    return [(lax.rem(f + a, fn), (c, pair[1])[b]) for a in range(fn) for b in range(2) if a or b]
+
+
+def plane_diagonals():
+    fn = lax.axis_size("fsdp")
+    f, _ = place()
+    (pair,) = the_pair()
+    return [(lax.rem(f + a, fn), pair[1]) for a in range(1, fn)]
+
+
+def exchange_plane(x, peers):
+    fn = lax.axis_size("fsdp")
+
+    def body(x_ref, o_ref, s, r, own):
+        f, c = place()
+        lo = lax.rem(c, 2)
+        (pair,) = the_pair()
+
+        def index(a, b):
+            return lax.rem(f + a + fn, fn), (lo if b == 0 else 1 - lo)
+
+        def copy(a, b, slot):
+            fa, lb = index(a, b)
+            return remote(
+                x_ref.at[fa, lb],
+                o_ref.at[slot[0], slot[1]],
+                s.at[a, b],
+                r.at[a, b],
+                (fa, c if b == 0 else pair[1]),
+            )
+
+        steps = [(a, b) for a in range(fn) for b in range(2) if a or b]
+        mine = pltpu.make_async_copy(x_ref.at[f, lo], o_ref.at[f, lo], own)
+
+        def start():
+            for a, b in steps:
+                copy(a, b, (f, lo)).start()
+            mine.start()
+
+        def end():
+            mine.wait()
+            for a, b in steps:
+                copy(a, b, index(-a, b)).wait_recv()
+            for a, b in steps:
+                copy(a, b, (f, lo)).wait_send()
+
+        return start, lambda: None, end
+
+    shape = jax.ShapeDtypeStruct(x.shape, x.dtype)
+    return (peers, x, shape, ANY, ANY, [dma(fn, 2), dma(fn, 2), dma()], body)
+
+
+def links_twin_pair():
+    return links_and_twin() + the_pair()
+
+
+def gather_plane(x, parts=4):
+    fn = lax.axis_size("fsdp")
+    chips = fn // 2
+    n, d = x.shape
+    step = n // parts
+    first, second = list(range(parts // 2)), list(range(parts // 2, parts))
+    others = list(range(1, chips))
+
+    def body(x_ref, o_ref, own_sem, sx, rx, sy, ry, st, rt):
+        f, c = place()
+        chip, core, lo = f // 2, lax.rem(f, 2), lax.rem(c, 2)
+        twin = (chip * 2 + 1 - core, c)
+        (pair,) = the_pair()
+
+        def rows(p):
+            return pl.ds(p * step, step)
+
+        def block(j, core_id, kind, p):
+            slot = lax.rem(chip + chips - j, chips) * 2 + core_id
+            return o_ref.at[slot, lo if kind == 0 else 1 - lo, rows(p)]
+
+        def source(j, kind, p):
+            return x_ref.at[rows(p)] if j == 0 and kind == 0 else block(j, core, kind, p)
+
+        def to(j):
+            return (lax.rem(chip + j, chips) * 2 + core, c)
+
+        def x_copy(j, kind, p):
+            return remote(
+                source(0, kind, p), block(0, core, kind, p), sx.at[j, kind, p], rx.at[j, kind, p], to(j)
+            )
+
+        def y_copy(j, p):
+            return remote(source(j, 0, p), block(j, core, 0, p), sy.at[j, p], ry.at[j, p], pair)
+
+        def t_copy(j, kind, p):
+            return remote(
+                source(j, kind, p), block(j, core, kind, p), st.at[j, kind, p], rt.at[j, kind, p], twin
+            )
+
+        def x_come(j, kind, p):
+            here = block(j, core, kind, p)
+            remote(here, here, sx.at[j, kind, p], rx.at[j, kind, p], to(j)).wait_recv()
+
+        def y_come(j, p):
+            here = block(j, core, 1, p)
+            remote(here, here, sy.at[j, p], ry.at[j, p], pair).wait_recv()
+
+        own = pltpu.make_async_copy(x_ref, o_ref.at[f, lo], own_sem)
+
+        def start():
+            for p in first:
+                for j in others:
+                    x_copy(j, 0, p).start()
+            for p in second + first:
+                y_copy(0, p).start()
+            for p in second:
+                for j in others:
+                    x_copy(j, 0, p).start()
+            for p in range(parts):
+                t_copy(0, 0, p).start()
+            own.start()
+
+        def middle():
+            for p, q in zip(first, second, strict=True):
+                for j in others:
+                    x_come(j, 0, p)
+                    y_copy(j, p).start()
+                    t_copy(j, 0, p).start()
+                y_come(0, q)
+                for j in others:
+                    x_copy(j, 1, q).start()
+                t_copy(0, 1, q).start()
+            for p, q in zip(first, second, strict=True):
+                y_come(0, p)
+                t_copy(0, 1, p).start()
+                for j in others:
+                    x_come(j, 0, q)
+                    t_copy(j, 0, q).start()
+
+        def end():
+            for p, q in zip(first, second, strict=True):
+                for j in others:
+                    y_come(j, p)
+                    t_copy(j, 1, p).start()
+                    x_come(j, 1, q)
+                    t_copy(j, 1, q).start()
+            own.wait()
+            for p in range(parts):
+                for j in range(chips):
+                    for kind in range(2):
+                        there = block(j, 1 - core, kind, p)
+                        remote(
+                            there, there, st.at[j, kind, p], rt.at[j, kind, p], twin
+                        ).wait_recv()
+                        t_copy(j, kind, p).wait_send()
+                y_copy(0, p).wait_send()
+                for j in others:
+                    x_copy(j, 0, p).wait_send()
+            for p, q in zip(first, second, strict=True):
+                for j in others:
+                    y_copy(j, p).wait_send()
+                    x_copy(j, 1, q).wait_send()
+
+        return start, middle, end
+
+    shape = jax.ShapeDtypeStruct((fn, 2, n, d), x.dtype)
+    scratch = [dma()] + [dma(chips, 2, parts)] * 2 + [dma(chips, parts)] * 2
+    scratch = scratch + [dma(chips, 2, parts)] * 2
+    return (links_twin_pair, x, shape, ANY, ANY, scratch, body)
+
+
+def scatter_plane(x, parts=4):
+    fn = lax.axis_size("fsdp")
+    chips = fn // 2
+    _, _, n, d = x.shape
+    step = n // parts
+    half = parts // 2
+    others = list(range(1, chips))
+
+    def body(
+        x_ref, o_ref, own, near, send1, come_y, send_x, come_x, come_x2, send_y, come_y2, acc,
+        s_own, s_near, r_near, s_1, r_y, r_x, s_2, r_x2, s_3, r_y2, s_out,
+    ):
+        f, c = place()
+        chip, core, lo = f // 2, lax.rem(f, 2), lax.rem(c, 2)
+        twin = (chip * 2 + 1 - core, c)
+        (pair,) = the_pair()
+
+        def chip_at(j):
+            return lax.rem(chip + j, chips)
+
+        def to(j):
+            return (chip_at(j) * 2 + core, c)
+
+        def part(j, core_id, kind, p):
+            return x_ref.at[
+                chip_at(j) * 2 + core_id, lo if kind == 0 else 1 - lo, pl.ds(p * step, step)
+            ]
+
+        def own_copy(j, k, p):
+            return pltpu.make_async_copy(part(j, core, k, p), own.at[j, k, p], s_own.at[j, k, p])
+
+        def near_copy(j, k, p):
+            return remote(
+                part(j, 1 - core, k, p), near.at[j, k, p], s_near.at[j, k, p], r_near.at[j, k, p], twin
+            )
+
+        def both(j, k, p):
+            return own[j, k, p].astype(F32) + near[j, k, p].astype(F32)
+
+        def ready(j, k, p):
+            own_copy(j, k, p).wait()
+            near_copy(j, k, p).wait_recv()
+
+        def y_first(j, p):
+            return remote(send1.at[j, 1, p], come_y.at[j, p], s_1.at[j, 1, p], r_y.at[j, p], pair)
+
+        def x_first(j, k, p):
+            q = p - half
+            return remote(
+                send1.at[j, k, p], come_x.at[j, k, q], s_1.at[j, k, p], r_x.at[j, k, q], to(j)
+            )
+
+        def x_then(j, p):
+            return remote(send_x.at[j, p], come_x2.at[j, p], s_2.at[j, p], r_x2.at[j, p], to(j))
+
+        def y_then(q):
+            return remote(send_y.at[q], come_y2.at[q], s_3.at[q], r_y2.at[q], pair)
+
+        def out(p):
+            return pltpu.make_async_copy(acc.at[p], o_ref.at[pl.ds(p * step, step)], s_out.at[p])
+
+        order = [(j, k, i) for i in range(half) for j in others + [0] for k in (1, 0)]
+
+        def start():
+            for j, k, i in order:
+                for p in (i, i + half):
+                    own_copy(j, k, p).start()
+                    near_copy(j, k, p).start()
+
+        def middle():
+            for i in range(half):
+                for j in range(chips):
+                    ready(j, 1, i)
+                    send1[j, 1, i] = both(j, 1, i).astype(BF16)
+                    y_first(j, i).start()
+                for j in others:
+                    for k in (1, 0):
+                        ready(j, k, i + half)
+                        send1[j, k, i + half] = both(j, k, i + half).astype(BF16)
+                        x_first(j, k, i + half).start()
+            for i in range(half):
+                for j in range(chips):
+                    ready(j, 0, i)
+                for k in range(2):
+                    ready(0, k, i + half)
+
+        def end():
+            for i in range(half):
+                for j in others:
+                    y_first(j, i).wait_recv()
+                    send_x[j, i] = (both(j, 0, i) + come_y[j, i].astype(F32)).astype(BF16)
+                    x_then(j, i).start()
+                total = both(0, 1, i + half)
+                for j in others:
+                    x_first(j, 1, i + half).wait_recv()
+                    total += come_x[j, 1, i].astype(F32)
+                send_y[i] = total.astype(BF16)
+                y_then(i).start()
+            for i in range(half):
+                y_first(0, i).wait_recv()
+                acc[i] = both(0, 0, i) + come_y[0, i].astype(F32)
+                acc[i + half] = both(0, 0, i + half)
+                for j in others:
+                    x_first(j, 0, i + half).wait_recv()
+                    acc[i + half] += come_x[j, 0, i].astype(F32)
+            for i in range(half):
+                for j in others:
+                    x_then(j, i).wait_recv()
+                    acc[i] += come_x2[j, i].astype(F32)
+                out(i).start()
+                y_then(i).wait_recv()
+                acc[i + half] += come_y2[i].astype(F32)
+                out(i + half).start()
+            for i in range(half):
+                out(i).wait()
+                out(i + half).wait()
+                y_then(i).wait_send()
+                for j in others:
+                    x_then(j, i).wait_send()
+                    for k in range(2):
+                        x_first(j, k, i + half).wait_send()
+                for j in range(chips):
+                    y_first(j, i).wait_send()
+                    for k in range(2):
+                        near_copy(j, k, i).wait_send()
+                        near_copy(j, k, i + half).wait_send()
+
+        return start, middle, end
+
+    def buffer(*lead):
+        return pltpu.VMEM((*lead, step, d), BF16)
+
+    scratch = [
+        buffer(chips, 2, parts),
+        buffer(chips, 2, parts),
+        buffer(chips, 2, parts),
+        buffer(chips, half),
+        buffer(chips, half),
+        buffer(chips, 2, half),
+        buffer(chips, half),
+        buffer(half),
+        buffer(half),
+        pltpu.VMEM((parts, step, d), F32),
+        dma(chips, 2, parts),
+        dma(chips, 2, parts),
+        dma(chips, 2, parts),
+        dma(chips, 2, parts),
+        dma(chips, half),
+        dma(chips, 2, half),
+        dma(chips, half),
+        dma(chips, half),
+        dma(half),
+        dma(half),
+        dma(parts),
+    ]
+    return (links_twin_pair, x, jax.ShapeDtypeStruct((n, d), F32), ANY, ANY, scratch, body)
 
 
 def scatter_small(x):
@@ -704,9 +1040,9 @@
     )(q, k, v, starts, lse, o, g, tables)
 
 
-def project(x, w, bias, tables):
+def project(x, w, stream, bias, tables):
     count, length, width = x.shape
-    cn, fn, rows, cols = w.shape
+    cn, fn, _, rows, cols = w.shape
     heads = cols // HEAD_DIM
 
     def kernel(*refs):
@@ -716,7 +1052,7 @@
         @pl.when(pl.program_id(0) == 0)
         def _():
             copies = [
-                pltpu.make_async_copy(w_ref.at[:, f], held.at[f], sem.at[f])
+                pltpu.make_async_copy(w_ref.at[:, f, stream], held.at[f], sem.at[f])
                 for f in range(fn)
             ]
             for c in copies:
@@ -806,6 +1142,55 @@
             flops=2 * n * d * cols, bytes_accessed=60_000_000, transcendentals=0
         ),
     )(x, w, bias)
+
+
+def halved_product(x, g, bit, groups, lines, tile=512, split=True):
+    n, d = g.shape
+    block = x.shape[1] // groups
+    r = block // lines // 2
+    tile = min(tile, d)
+
+    def kernel(bit_ref, x_ref, g_ref, *refs):
+        turned = refs[-1]
+
+        @pl.when(pl.program_id(1) == 0)
+        def _():
+            turned[...] = x_ref[...].T
+
+        y = nn(turned[...], g_ref[...]).astype(BF16)
+        if not split:
+            refs[0][:, 0] = y.reshape(lines, 2 * r, tile)
+            return
+        a_ref, k_ref = refs[:2]
+        y = y.reshape(lines, 2, r, tile)
+        first = bit_ref[0] == 0
+        a_ref[:, 0] = jnp.where(first, y[:, 1], y[:, 0])
+        k_ref[:, 0] = jnp.where(first, y[:, 0], y[:, 1])
+
+    size = r if split else 2 * r
+    half = pl.BlockSpec((lines, 1, size, tile), lambda i, j, b: (0, i, 0, j))
+    shape = jax.ShapeDtypeStruct((lines, groups, size, d), BF16)
+    outs = 2 if split else 1
+    return pl.pallas_call(
+        kernel,
+        grid_spec=pltpu.PrefetchScalarGridSpec(
+            num_scalar_prefetch=1,
+            grid=(groups, d // tile),
+            in_specs=[
+                pl.BlockSpec((n, block), lambda i, j, b: (0, i)),
+                pl.BlockSpec((n, tile), lambda i, j, b: (0, j)),
+            ],
+            out_specs=[half] * outs,
+            scratch_shapes=[pltpu.VMEM((block, n), BF16)],
+        ),
+        out_shape=[shape] * outs,
+        compiler_params=pltpu.CompilerParams(vmem_limit_bytes=48 * 2**20),
+        cost_estimate=pl.CostEstimate(
+            flops=2 * n * d * x.shape[1],
+            bytes_accessed=2 * (n * d + n * x.shape[1] + d * x.shape[1]),
+            transcendentals=0,
+        ),
+    )(bit, x, g)
 
 
 def front(hist, mix, gain, shift, tokens=16, wide=256):
@@ -964,13 +1349,17 @@
     ntp = fn * nloc
     rows = qkv_weight.shape[0]
     ff = up_weight.shape[1]
-    wcol, fcol = width // fn, ff // fn
+    wcol, pcol = width // fn, ff // (2 * fn)
+    count = cn // 2
+    lo = lax.rem(ci, 2)
+    lines = [list(range(b, cn, 2)) for b in range(2)]
     heads = wcol // HEAD_DIM
     units = fn * seqs * heads // cn
     total = cn * length
     mixn = mix_in_weight.shape[1]
 
-    wdown = lax.all_gather(down_weight, "ctx", axis=0, tiled=True)
+    def line_gather(w):
+        return lax.all_gather(w, "ctx", axis=0, axis_index_groups=lines)
 
     parts = [
         norm_gain,
@@ -989,9 +1378,13 @@
         1,
         gather_small(flat),
         exchange_fsdp(qkv_weight.reshape(rows, 3, fn, wcol).transpose(2, 1, 0, 3)),
-        exchange_fsdp(up_weight.reshape(rows, fn, fcol).transpose(1, 0, 2)),
+        exchange_plane(
+            up_weight.reshape(rows, fn, count, 2, -1).transpose(1, 3, 0, 2, 4).reshape(fn, 2, rows, pcol),
+            plane_diagonals,
+        ),
     )
     flats = flats.reshape(dn, -1)
+    w12 = lax.all_gather(qkv_cols[:, 1:], "ctx", axis=0)
     pieces, at = [], 0
     for a in parts:
         pieces.append(flats[:, at : at + a.size])
@@ -1019,10 +1412,11 @@
     tables = rotary_tables(total)
     tables_l = lax.dynamic_slice_in_dim(tables, ci * length, length, 1)
 
-    def projected(x, w, s):
+    def projected(x, w, at, s):
         y = project(
             x.reshape(fn * seqs, length, width),
             w,
+            at,
             bias_cols[s : s + 1],
             tables_l if s < 2 else None,
         )
@@ -1038,18 +1432,19 @@
         x = x.reshape(fn * seqs, heads, length, HEAD_DIM)
         return x.transpose(0, 2, 1, 3).reshape(ntp, wcol)
 
-    cols_of = [qkv_cols[:, s] for s in range(3)]
-    g0, w0 = comm(9, gather_ctx(cols_of[0]), gather_fsdp(normed[0]))[::-1]
-    p0 = projected(g0, w0, 0)
-    q_u, w1, g1 = comm(4, exchange_ctx(p0, True), gather_ctx(cols_of[1]), gather_fsdp(normed[1]))
-    p1 = projected(g1, w1, 1)
-    p1, up_cols, out_rows, wdown = lax.optimization_barrier((p1, up_cols, out_weight, wdown))
+    w0, g0 = comm(9, gather_ctx(qkv_cols[:, 0]), gather_fsdp(normed[0]))
+    p0 = projected(g0, w0[:, :, None], 0, 0)
+    p0, w12, down_rows = lax.optimization_barrier((p0, w12, down_weight))
+    wdown = line_gather(down_rows).reshape(pcol, width)
+    q_u, g1 = comm(4, exchange_ctx(p0, True), gather_fsdp(normed[1]))
+    p1 = projected(g1, w12, 0, 1)
+    k_u, g2 = comm(4, exchange_ctx(p1, True), gather_fsdp(normed[2]))
+    p2 = projected(g2, w12, 1, 2)
+    p2, wdown, up_cols, out_rows = lax.optimization_barrier((p2, wdown, up_cols, out_weight))
     wout = lax.all_gather(out_rows, "ctx", axis=0, tiled=True)
-    up_g = lax.all_gather(up_cols, "ctx", axis=0)
-    k_u, w2, g2 = comm(4, exchange_ctx(p1, True), gather_ctx(cols_of[2]), gather_fsdp(normed[2]))
-    p2 = projected(g2, w2, 2)
+    up_g = line_gather(up_cols).reshape(count, fn, 2 * rows, pcol)
     (v_u,) = comm(5, exchange_ctx(p2, True))
-    wqkv = [w.transpose(1, 0, 2, 3).reshape(width, wcol) for w in (w0, w1, w2)]
+    wqkv = [w.transpose(1, 0, 2, 3).reshape(width, wcol) for w in (w0, w12[:, :, 0], w12[:, :, 1])]
     q_u, k_u, v_u = whole_units(q_u), whole_units(k_u), whole_units(v_u)
     normed_g = [g.reshape(ntp, width) for g in (g0, g1, g2)]
 
@@ -1070,12 +1465,20 @@
     def gather_tokens(x):
         return comm(3, gather_fsdp(x))[0].reshape(ntp, width)
 
+    def scatter_plane_tokens(x):
+        return comm(13, scatter_plane(x.astype(BF16).reshape(fn, 2, nloc, width)))[0]
+
+    def gather_plane_tokens(x):
+        return comm(14, gather_plane(x))[0].reshape(2 * ntp, width)
+
     hidden_res = streams[3] + scatter_tokens(dot("nd,de->ne", attended, wout)) + out_shift
     normed_mlp, mid_pull = jax.vjp(layer_norm, hidden_res, gain_all[3], shift_all[3])
-    mlp_g = gather_tokens(normed_mlp.astype(BF16))
-    up_bias_cols = lax.dynamic_slice_in_dim(up_shift, fi * fcol, fcol, 0)
+    mlp_g = gather_plane_tokens(normed_mlp.astype(BF16))
+    up_bias_cols = lax.dynamic_slice(
+        up_shift.reshape(fn, count, 2, -1), (fi, 0, lo, 0), (1, count, 1, ff // dn)
+    ).reshape(pcol)
     act_low, slope, wup = widen(mlp_g, up_g, up_bias_cols[None])
-    result = hidden_res + scatter_tokens(dot("nf,fd->nd", act_low, wdown)) + down_shift
+    result = hidden_res + scatter_plane_tokens(dot("nf,fd->nd", act_low, wdown)) + down_shift
     block_out = result.astype(BF16).reshape(seqs, length, width)
 
     next_rows, mixer_pull = jax.vjp(
@@ -1088,21 +1491,10 @@
     grad_result = grad_result + out_cotangent.reshape(nloc, width).astype(F32)
 
     grad_branch = grad_result.astype(BF16)
-    branch_g = gather_tokens(grad_branch)
+    branch_g = gather_plane_tokens(grad_branch)
     grad_down_shift = jnp.sum(grad_branch.astype(F32), axis=0)
 
-    low_bit = lax.rem(ci, 2)
-    pairs = [(i, i ^ 1) for i in range(cn)]
-    lines = [list(range(b, cn, 2)) for b in range(2)]
-
-    def halves(x):
-        x = x.reshape(cn // 2, 2, *x.shape[1:])
-        away = lax.dynamic_index_in_dim(x, 1 - low_bit, 1, keepdims=False)
-        kept = lax.dynamic_index_in_dim(x, low_bit, 1, keepdims=False)
-        return away, kept
-
-    def joined_half(kept, come):
-        return (kept.astype(F32) + come.astype(F32)).astype(BF16)
+    bit = lo.reshape(1)
 
     def line_scatter(x):
         y = lax.psum_scatter(
@@ -1116,21 +1508,15 @@
 
     down_part = dot("nf,nd->fd", act_low, branch_g).astype(BF16)
     down_part, wdown = lax.optimization_barrier((down_part, wdown))
-    grad_down = lax.psum_scatter(down_part, "ctx", scatter_dimension=0, tiled=True)
+    grad_down = line_scatter(down_part.reshape(count, -1, width))
     grad_active = dot("nd,fd->nf", branch_g, wdown)
     grad_upward = (grad_active * slope.astype(F32)).astype(BF16)
     grad_up_shift = jnp.sum(grad_upward.astype(F32), axis=0)
-    up_part = dot("nd,nf->df", mlp_g, grad_upward).astype(BF16)
-    up_part = up_part.reshape(fn, cn // 2, 2, rows, fcol)
-
-    def up_rows(bit):
-        x = lax.dynamic_index_in_dim(up_part, bit, 2, keepdims=False)
-        return x.transpose(1, 0, 2, 3).reshape(cn // 2, -1, fcol)
-
-    up_away, grad_upward = lax.optimization_barrier((up_rows(1 - low_bit), grad_upward))
-    up_half = joined_half(up_rows(low_bit), lax.ppermute(up_away, "ctx", pairs))
+    (up_part,) = halved_product(mlp_g, grad_upward, bit, fn, count, split=False)
+    up_part, grad_upward = lax.optimization_barrier((up_part, grad_upward))
+    grad_up = line_scatter(up_part.reshape(count, -1, pcol))
     mlp_part = dot("nf,df->nd", grad_upward, wup).astype(BF16)
-    grad_mlp = scatter_tokens(mlp_part)
+    grad_mlp = scatter_plane_tokens(mlp_part)
     grad_hidden, grad_gain_mid, grad_shift_mid = mid_pull(grad_mlp)
     grad_hidden = grad_hidden + grad_result
     grad_attn = grad_hidden.astype(BF16)
@@ -1139,51 +1525,42 @@
     out_part = dot("nd,ne->de", attended, attn_g).astype(BF16)
     grad_att = dot("ne,de->nd", attn_g, wout).astype(BF16)
     grad_att = grad_att.reshape(fn * seqs, length, heads, HEAD_DIM).transpose(0, 2, 1, 3)
-    out_away, out_kept = halves(out_part.reshape(cn, -1, width))
+    out_part, grad_att = lax.optimization_barrier((out_part, grad_att))
     (g_u,) = comm(5, exchange_ctx(grad_att.reshape(cn, units, length, HEAD_DIM), True))
-    g_u, grad_down, up_half = lax.optimization_barrier((g_u, grad_down, up_half))
-    grad_up = line_scatter(up_half)
+    g_u, grad_down, out_part = lax.optimization_barrier((g_u, grad_down, out_part))
+
+    def ctx_scatter(x):
+        return lax.psum_scatter(x, "ctx", scatter_dimension=0, tiled=True)
+
+    grad_out = ctx_scatter(out_part)
     gq, gk, gv = attend_back(q_u, k_u, v_u, first_key, lse_u, att_u, whole_units(g_u), tables)
-
-    def qkv_halves(p, s):
-        x = dot("nd,nc->dc", normed_g[s], p).astype(BF16).reshape(fn, cn, rows, wcol)
-        return halves(x.transpose(1, 0, 2, 3).reshape(cn, -1, wcol))
 
     def back_part(p, s):
         return dot("nc,dc->nd", p, wqkv[s]).astype(BF16).reshape(fn, nloc, width)
 
-    gp0, out_come = comm(12, from_units(gq), exchange_pair(out_away))
+    def qkv_part(p, i):
+        return halved_product(normed_g[i], p, bit, fn, cn, split=False)[0]
+
+    gp0, grad_up = lax.optimization_barrier((comm(6, from_units(gq))[0], grad_up))
     gp0 = columns(gp0)
-    q_away, q_kept = qkv_halves(gp0, 0)
-    gp1, q_come, gn0 = comm(
-        8, from_units(gk), exchange_pair(q_away), scatter_fsdp(back_part(gp0, 0))
+    q_part, gk = lax.optimization_barrier((qkv_part(gp0, 0), gk))
+    grad_q = ctx_scatter(q_part.reshape(-1, wcol)).reshape(fn, rows, wcol)
+    gp1, gn0 = comm(8, from_units(gk), scatter_fsdp(back_part(gp0, 0)))
+    gp1, grad_out = lax.optimization_barrier((gp1, grad_out))
+    gp1 = columns(gp1)
+    gp2, gn1 = comm(8, from_units(gv), scatter_fsdp(back_part(gp1, 1)))
+    gp2 = columns(gp2)
+    kv_part = jnp.stack([qkv_part(gp1, 1), qkv_part(gp2, 2)], axis=1)
+    kv_part, grad_up = lax.optimization_barrier((kv_part, grad_up))
+    grad_kv = ctx_scatter(kv_part.reshape(-1, wcol)).reshape(2, fn, rows, wcol)
+    grad_up, gn2, grad_q = comm(
+        7,
+        exchange_plane(grad_up.reshape(fn, 2, rows, pcol), plane_others),
+        scatter_fsdp(back_part(gp2, 2)),
+        exchange_fsdp(grad_q),
     )
-    gp1 = columns(gp1)
-    k_away, k_kept = qkv_halves(gp1, 1)
-    gp2, k_come, gn1 = comm(
-        8, from_units(gv), exchange_pair(k_away), scatter_fsdp(back_part(gp1, 1))
-    )
-    gp2, grad_up = lax.optimization_barrier((gp2, grad_up))
-    out_half = joined_half(out_kept, out_come).reshape(cn // 2, -1, wcol)
-    early = [joined_half(q_kept, q_come), joined_half(k_kept, k_come), out_half]
-    early = line_scatter(jnp.concatenate(early, axis=1))
-    grad_qk, grad_out = early[: 2 * fn * rows], early[2 * fn * rows :].reshape(rows, width)
-    gp2 = columns(gp2)
-    v_away, v_kept = qkv_halves(gp2, 2)
-    gn2, v_come, grad_up = comm(
-        7,
-        scatter_fsdp(back_part(gp2, 2)),
-        exchange_pair(v_away),
-        exchange_fsdp(grad_up.reshape(fn, rows, fcol)),
-    )
-    grad_up = grad_up.transpose(1, 0, 2).reshape(rows, ff)
-    grad_v = line_scatter(joined_half(v_kept, v_come))
+    grad_up = grad_up.reshape(fn, 2, rows, count, -1).transpose(2, 0, 3, 1, 4).reshape(rows, ff)
     grad_proj = (gp0, gp1, gp2)
-    grad_qkv = jnp.concatenate(
-        [grad_qk.reshape(2, fn, rows, wcol), grad_v.reshape(1, fn, rows, wcol)], axis=0
-    )
-    grad_qkv = lax.all_to_all(grad_qkv.transpose(1, 0, 2, 3), "fsdp", 0, 0, tiled=True)
-    grad_qkv = grad_qkv.transpose(2, 1, 0, 3).reshape(rows, 3, width).astype(F32)
     grad_qkv_shift = jnp.stack([jnp.sum(g.astype(F32), axis=0) for g in grad_proj])
 
     grad_history, grad_mix, grad_gain_front, grad_shift_front = last(
@@ -1196,30 +1573,48 @@
         zero = jnp.zeros((x.shape[0], full), F32)
         return lax.dynamic_update_slice_in_dim(zero, x, fi * x.shape[1], 1)
 
-    def parted(x):
-        k = x.shape[0]
-        return x.reshape(k, dn, -1).transpose(1, 0, 2).reshape(dn, -1)
-
-    sums = [
-        parted(jnp.concatenate([grad_gain_front, grad_gain_mid[None]], axis=0)),
-        parted(jnp.concatenate([grad_shift_front, grad_shift_mid[None]], axis=0)),
-        parted(own_columns(grad_qkv_shift, width)),
-        parted(grad_out_shift[None]),
-        parted(own_columns(grad_up_shift[None], ff)),
-        parted(grad_down_shift[None]),
-        parted(grad_root[None]),
-        grad_mix_in.reshape(dn, -1),
+    lines_14 = [
+        grad_gain_front,
+        grad_gain_mid[None],
+        grad_shift_front,
+        grad_shift_mid[None],
+        own_columns(grad_qkv_shift, width),
+        grad_out_shift[None],
+        grad_down_shift[None],
+        grad_root[None],
     ]
+    lines_14 = jnp.concatenate(lines_14, axis=0)
+    up_lines = lax.dynamic_update_slice(
+        jnp.zeros((fn, count, 2, ff // dn), F32),
+        grad_up_shift.reshape(1, count, 1, -1),
+        (fi, 0, lo, 0),
+    ).reshape(dn, -1)
     same = jnp.concatenate([grad_mix_out.reshape(-1), grad_mix_bias])
-    sums.append(jnp.broadcast_to(same[None], (dn, same.size)))
-    flat = jnp.concatenate(sums, axis=1)
+    flat = jnp.concatenate(
+        [
+            lines_14.reshape(-1, dn, width // dn).transpose(1, 0, 2).reshape(dn, -1),
+            up_lines,
+            grad_mix_in.reshape(dn, -1),
+            jnp.broadcast_to(same[None], (dn, same.size)),
+        ],
+        axis=1,
+    )
     flat = jnp.pad(flat, ((0, 0), (0, -flat.shape[1] % 1024)))
-    small = comm(2, scatter_small(flat.reshape(fn, cn, -1, 128)))[0].reshape(-1)
+    small, grad_k, grad_v = comm(
+        2,
+        scatter_small(flat.reshape(fn, cn, -1, 128)),
+        exchange_fsdp(grad_kv[0]),
+        exchange_fsdp(grad_kv[1]),
+    )
+    grad_qkv = jnp.stack([grad_q, grad_k, grad_v])
+    grad_qkv = grad_qkv.transpose(2, 0, 1, 3).reshape(rows, 3, width).astype(F32)
+    small = small.reshape(-1)
     out_small, at = [], 0
-    for s, shape in zip(sums[:-1], [a.shape for a in parts[:-1]], strict=True):
-        out_small.append(small[at : at + s.shape[1]].reshape(shape))
-        at += s.shape[1]
-    (g_gain, g_shift, g_qkv_b, g_out_b, g_up_b, g_down_b, g_root, g_mix_in) = out_small
+    order = [norm_gain, norm_bias, qkv_bias, out_bias, down_bias, root_gain, up_bias, mix_in_weight]
+    for a in order:
+        out_small.append(small[at : at + a.size].reshape(a.shape))
+        at += a.size
+    (g_gain, g_shift, g_qkv_b, g_out_b, g_down_b, g_root, g_up_b, g_mix_in) = out_small
     mix_sums = small[at : at + same.size]
     cut = grad_mix_out.size
     return (

time: 1140 us -> 1060 us (0.930)
  Pallas kernels: 871 us -> 798 us
    pallas_call x18, Pallas kernels: 756 us -> 649 us  [comm(): pl.pallas_call(kernel, out_shape=[t[2] for t in tasks], in_specs=[t[3] fo...]
    pallas_call x0 -> x4, Pallas kernels: none -> 32.9 us  [halved_product(): pl.pallas_call(kernel, grid_spec=pltpu.PrefetchScalarGridSpec(num_scalar_...]
    all_gather x2 -> x3, waiting for transfers between devices: 0.01 us -> 14.2 us  [the longest x2 13 us: line_gather(): return lax.all_gather(w, 'ctx', axis=0, axis_index_groups=lines)]
    unnamed x170 -> x144, local copies, waits for them, and re-layouts: 34.9 us -> 32.7 us
    dot_general x14 -> x10, matrix products: 86.6 us -> 87.1 us  [dot(): return jnp.einsum(pattern, left, right, preferred_element_type=F32)]
  transfers between devices with their start and end apart: 9 -> 9, of which waited for: 2 -> 2; matrix products, arithmetic and copies ran while one was open for 14% -> 13% of each run, Pallas kernels for 70% -> 61%
where the time goes in v3:
time: 1060 us
  Pallas kernels  798 us (75%)
  local copies, waits for them, and re-layouts  103 us (10%)
  matrix products  98.3 us (9%)
  other arithmetic  24.5 us (2%)
  between operations  15.7 us (1%)
  waiting for transfers between devices  14.9 us (1%)
    pallas_call x18, Pallas kernels, comm(): pl.pallas_call(kernel, out_shape=[t[2] for t in tasks], in_specs=[t[3] fo...  649 us
    dot_general x10, matrix products, dot(): return jnp.einsum(pattern, left, right, preferred_element_type=F32)  87.1 us
    pallas_call x4, Pallas kernels, halved_product(): pl.pallas_call(kernel, grid_spec=pltpu.PrefetchScalarGridSpec(num_scalar_...  32.9 us
    unnamed x144, local copies, waits for them, and re-layouts  32.7 us
    pallas_call x1, Pallas kernels, last(): pl.pallas_call(kernel, grid=(n // tokens,), in_specs=[pl.BlockSpec((h, to...  27.6 us
    pallas_call x1, Pallas kernels, attend_back(): pl.pallas_call(kernel, grid=(u, t // block), in_specs=[pl.BlockSpec(spec,...  25 us
  transfers between devices with their start and end apart: 9, of which 2 were waited for; matrix products, arithmetic and copies ran while one was open for 13% of the time, Pallas kernels for 61%

profile of v3, /device:TPU:1, one launch (start us, length us, event | category | flops | bytes accessed | tf_op | source)
XLA Modules:
  0.0 1055.5 jit_solution(12683863247214873587)
XLA Ops:
  13.3 34.8 %shard_map.340 = (f32[4,8,32,128]{3,2,1,0:T(8,128)}, bf16[4,3,64,512]{3,2,1,0:T(8,128)(2,1)}, bf16[4,2,64,1024]{3,2,1,0:T(8,128)(2,1)}) custom-call(f32[32,128]{1,0:T(8,128)} %pad_bitcast_fusion.1.refs_0_, bf16[4,3,64,512]{3,2,1,0:T(8,128)(2,1)} %bitcast.267, bf16[4,2,64,1024]{3,2,1,0:T(8,128)(2,1)} %reshape.453.refs_2_), custom_call_target="tpu_custom_call" | custom-call | bytes 15000000 | tf_op jit(solution)/shard_map/pallas_call | solution.py:142
  54.1 17.7 %shard_map.341 = (f32[4,256,2048]{2,1,0:T(8,128)}, bf16[3,256,2048]{2,1,0:T(8,128)(2,1)}) custom-call(bf16[9,256,2048]{2,1,0:T(8,128)(2,1)} %bitcast.236, f32[256,128]{1,0:T(8,128)} %pad.25.m_ref, f32[3,2048]{1,0:T(4,128)} %slice.139.g_ref, f32[3,2048]{1,0:T(4,128)} %slice.142.b_ref), custom_call_target="tpu_custom_call" | custom-call | flops 37748736 | bytes 20971520 | tf_op jit(solution)/shard_map/pallas_call | solution.py:1216
  73.5 3.6 slice_bitcast_fusion.2
  77.1 50.6 %shard_map.342 = (bf16[8,4,64,512]{3,2,1,0:T(8,128)(2,1)}, bf16[4,256,2048]{2,1,0:T(8,128)(2,1)}) custom-call(bf16[4,64,512]{2,1,0:T(8,128)(2,1)} %slice_bitcast_fusion.5.refs_0_, bf16[256,2048]{1,0:T(8,128)(2,1)} %get-tuple-element.260.refs_1_), custom_call_target="tpu_custom_call" | custom-call | bytes 15000000 | tf_op jit(solution)/shard_map/pallas_call | solution.py:142
  130.5 2.2 copy-done.18
  132.6 4.2 shard_map.343
  139.0 39.4 %shard_map.344 = (bf16[2,8,256,128]{3,2,1,0:T(8,128)(2,1)}, bf16[4,256,2048]{2,1,0:T(8,128)(2,1)}) custom-call(bf16[8,2,256,128]{3,2,1,0:T(8,128)(2,1)} %bitcast.225, bf16[256,2048]{1,0:T(8,128)(2,1)} %get-tuple-element.259.refs_1_), custom_call_target="tpu_custom_call" | custom-call | bytes 15000000 | tf_op jit(solution)/shard_map/pallas_call | solution.py:142
  178.4 2.2 copy-done.1
  180.6 2.2 copy-done.7
  182.8 4.2 shard_map.345
  188.0 48.3 %shard_map.346 = (bf16[2,8,256,128]{3,2,1,0:T(8,128)(2,1)}, bf16[4,256,2048]{2,1,0:T(8,128)(2,1)}) custom-call(bf16[8,2,256,128]{3,2,1,0:T(8,128)(2,1)} %bitcast.214, bf16[256,2048]{1,0:T(8,128)(2,1)} %get-tuple-element.258.refs_1_), custom_call_target="tpu_custom_call" | custom-call | bytes 15000000 | tf_op jit(solution)/shard_map/pallas_call | solution.py:142
  236.3 2.2 copy-done.4
  238.5 3.1 shard_map.347
  242.6 13.0 %all-gather.12.cloned.1.call-done = bf16[1024,2048]{1,0:T(8,128)(2,1)} async-done(((bf16[256,2048]{1,0:T(8,128)(2,1)}), bf16[1024,2048]{1,0:T(8,128)(2,1)}) %all-gather.12.cloned.1.call-update) | async-done | bytes 4194320 | tf_op jit(solution)/shard_map/all_gather | solution.py:1362
  261.6 29.9 %shard_map.348 = bf16[2,8,256,128]{3,2,1,0:T(8,128)(2,1)} custom-call(bf16[8,2,256,128]{3,2,1,0:T(8,128)(2,1)} %bitcast.211), custom_call_target="tpu_custom_call" | custom-call | bytes 15000000 | tf_op jit(solution)/shard_map/pallas_call | solution.py:142
  292.8 15.5 %shard_map.349 = (bf16[2,2048,128]{2,1,0:T(8,128)(2,1)S(1)}, f32[2,1,2048]{2,1,0:T(1,128)S(1)}) custom-call(bf16[2,2048,128]{2,1,0:T(8,128)(2,1)S(1)} %bitcast.232, bf16[2,2048,128]{2,1,0:T(8,128)(2,1)S(1)} %bitcast.234, bf16[2,2048,128]{2,1,0:T(8,128)(2,1)S(1)} %bitcast.223, s32[2,1,2048]{2,1,0:T(1,128)S(1)} %broadcast_in_dim.28.s_ref), custom_call_target="tpu_custom_call" | custom-call | flops 2147483648 | bytes 8388608 | tf_op jit(solution)/shard_map/pallas_call | solution.py:925
  309.3 27.3 %shard_map.350 = bf16[8,2,256,128]{3,2,1,0:T(8,128)(2,1)} custom-call(bf16[2,8,256,128]{3,2,1,0:T(8,128)(2,1)} %bitcast.224), custom_call_target="tpu_custom_call" | custom-call | bytes 15000000 | tf_op jit(solution)/shard_map/pallas_call | solution.py:142
  336.7 3.0 copy.175
  339.7 6.5 convolution_convert_fusion.6
  346.2 29.0 %shard_map.351 = f32[256,2048]{1,0:T(8,128)} custom-call(bf16[4,256,2048]{2,1,0:T(8,128)(2,1)} %bitcast.252), custom_call_target="tpu_custom_call" | custom-call | bytes 15000000 | tf_op jit(solution)/shard_map/pallas_call | solution.py:142
  375.2 2.6 fusion.39
  380.6 43.3 %shard_map.352 = bf16[4,2,256,2048]{3,2,1,0:T(8,128)(2,1)} custom-call(bf16[256,2048]{1,0:T(8,128)(2,1)} %add_convert_fusion.refs_0_), custom_call_target="tpu_custom_call" | custom-call | bytes 15000000 | tf_op jit(solution)/shard_map/pallas_call | solution.py:142
  423.9 19.3 %shard_map.353 = (bf16[2048,1024]{1,0:T(8,128)(2,1)S(1)}, bf16[2048,1024]{1,0:T(8,128)(2,1)}, bf16[2048,1024]{1,0:T(8,128)(2,1)}) custom-call(bf16[2048,2048]{1,0:T(8,128)(2,1)} %bitcast.243, bf16[4,4,128,1024]{3,2,1,0:T(8,128)(2,1)} %bitcast.304, f32[1,1024]{1,0:T(1,128)S(1)} %bitcast.230), custom_call_target="tpu_custom_call" | custom-call | flops 8589934592 | bytes 60000000 | tf_op jit(solution)/shard_map/pallas_call | solution.py:1125
  443.2 11.3 %convolution_convert_fusion.1 = bf16[2048,2048]{1,0:T(8,128)(2,1)} fusion(bf16[2048,1024]{1,0:T(8,128)(2,1)S(1)} %get-tuple-element.93, bf16[1024,2048]{1,0:T(8,128)(2,1)S(1)} %copy-done.61), kind=kOutput, calls=%fused_computation.4 | convolution fusion | flops 8594128896 | bytes 16777216 | tf_op jit(solution)/shard_map/nf,fd->nd/dot_general | solution.py:69
  454.5 41.5 %shard_map.354 = f32[256,2048]{1,0:T(8,128)} custom-call(bf16[4,2,256,2048]{3,2,1,0:T(8,128)(2,1)} %bitcast.242), custom_call_target="tpu_custom_call" | custom-call | bytes 15000000 | tf_op jit(solution)/shard_map/pallas_call | solution.py:142
  496.0 2.6 multiply_reduce_fusion.4
  498.6 2.0 fusion.17
  500.9 2.4 multiply_reduce_fusion
  505.2 39.6 %shard_map.355 = bf16[4,2,256,2048]{3,2,1,0:T(8,128)(2,1)} custom-call(bf16[256,2048]{1,0:T(8,128)(2,1)} %get-tuple-element.246.refs_0_), custom_call_target="tpu_custom_call" | custom-call | bytes 15000000 | tf_op jit(solution)/shard_map/pallas_call | solution.py:142
  544.8 13.3 %convolution_convert_fusion.5 = bf16[1024,2048]{1,0:T(8,128)(2,1)} fusion(bf16[2048,1024]{1,0:T(8,128)(2,1)S(1)} %get-tuple-element.93, bf16[2048,2048]{1,0:T(8,128)(2,1)} %bitcast.245), kind=kOutput, calls=%fused_computation.9 | convolution fusion | flops 8592031744 | bytes 16777216 | tf_op jit(solution)/shard_map/nf,nd->fd/dot_general | solution.py:69
  558.2 15.4 %convert_reduce_fusion = (f32[1024]{0:T(1024)S(1)}, bf16[2048,1024]{1,0:T(8,128)(2,1)}) fusion(bf16[2048,1024]{1,0:T(8,128)(2,1)} %get-tuple-element.97, bf16[2048,2048]{1,0:T(8,128)(2,1)} %bitcast.246, bf16[1024,2048]{1,0:T(8,128)(2,1)} %all-gather.12.cloned.1.call-done), kind=kOutput, calls=%fused_computation.1 | convolution fusion | flops 8600419328 | bytes 20975616 | tf_op jit(solution)/shard_map/nd,fd->nf/dot_general | solution.py:69
  573.6 18.1 %shard_map.356 = bf16[4,4,128,1024]{3,2,1,0:T(8,128)(2,1)S(1)} custom-call(s32[1]{0:T(128)} %bitcast.36.bit_ref, bf16[2048,2048]{1,0:T(8,128)(2,1)} %bitcast.244, bf16[2048,1024]{1,0:T(8,128)(2,1)} %get-tuple-element.98.g_ref), custom_call_target="tpu_custom_call" | custom-call | flops 8589934592 | bytes 16777216 | tf_op jit(solution)/shard_map/pallas_call | solution.py:1174
  591.7 2.0 copy-done.6
  593.7 14.3 %convolution_convert_fusion = bf16[2048,2048]{1,0:T(8,128)(2,1)} fusion(bf16[2048,1024]{1,0:T(8,128)(2,1)} %get-tuple-element.98.g_ref, bf16[2048,1024]{1,0:T(8,128)(2,1)} %get-tuple-element.99), kind=kOutput, calls=%fused_computation.3 | convolution fusion | flops 8594128896 | bytes 16777216 | tf_op jit(solution)/shard_map/nf,df->nd/dot_general | solution.py:69
  608.0 41.4 %shard_map.357 = f32[256,2048]{1,0:T(8,128)} custom-call(bf16[4,2,256,2048]{3,2,1,0:T(8,128)(2,1)} %bitcast.241), custom_call_target="tpu_custom_call" | custom-call | bytes 15000000 | tf_op jit(solution)/shard_map/pallas_call | solution.py:142
  649.4 2.5 multiply_reduce_fusion.1
  654.4 3.0 convert_reduce_fusion.2
  657.4 33.9 %shard_map.358 = bf16[4,256,2048]{2,1,0:T(8,128)(2,1)} custom-call(bf16[256,2048]{1,0:T(8,128)(2,1)} %get-tuple-element.248.refs_0_), custom_call_target="tpu_custom_call" | custom-call | bytes 15000000 | tf_op jit(solution)/shard_map/pallas_call | solution.py:142
  691.3 5.6 convolution_convert_fusion.8
  700.1 6.0 convolution_convert_fusion.7
  706.1 26.4 %shard_map.359 = bf16[2,8,256,128]{3,2,1,0:T(8,128)(2,1)} custom-call(bf16[8,2,256,128]{3,2,1,0:T(8,128)(2,1)} %bitcast.262), custom_call_target="tpu_custom_call" | custom-call | bytes 15000000 | tf_op jit(solution)/shard_map/pallas_call | solution.py:142
  732.6 25.0 %shard_map.360 = (bf16[2,2048,128]{2,1,0:T(8,128)(2,1)S(1)}, bf16[2,2048,128]{2,1,0:T(8,128)(2,1)S(1)}, bf16[2,2048,128]{2,1,0:T(8,128)(2,1)S(1)}) custom-call(bf16[2,2048,128]{2,1,0:T(8,128)(2,1)S(1)} %bitcast.233, bf16[2,2048,128]{2,1,0:T(8,128)(2,1)S(1)} %bitcast.235, bf16[2,2048,128]{2,1,0:T(8,128)(2,1)} %bitcast.222, ...), custom_call_target="tpu_custom_call" | custom-call | flops 5368709120 | bytes 20971520 | tf_op jit(solution)/shard_map/pallas_call | solution.py:1012
  760.6 26.8 %shard_map.361 = bf16[8,2,256,128]{3,2,1,0:T(8,128)(2,1)} custom-call(bf16[2,8,256,128]{3,2,1,0:T(8,128)(2,1)} %bitcast.227), custom_call_target="tpu_custom_call" | custom-call | bytes 15000000 | tf_op jit(solution)/shard_map/pallas_call | solution.py:142
  787.4 2.0 copy.177
  789.6 4.9 shard_map.362
  797.6 2.0 copy-done.3
  801.5 4.4 convolution_convert_fusion.4
  805.9 38.8 %shard_map.363 = (bf16[8,2,256,128]{3,2,1,0:T(8,128)(2,1)}, f32[256,2048]{1,0:T(8,128)}) custom-call(bf16[2,8,256,128]{3,2,1,0:T(8,128)(2,1)} %bitcast.221, bf16[4,256,2048]{2,1,0:T(8,128)(2,1)} %bitcast.251), custom_call_target="tpu_custom_call" | custom-call | bytes 15000000 | tf_op jit(solution)/shard_map/pallas_call | solution.py:142
  844.7 2.0 copy.179
  846.9 4.4 convolution_convert_fusion.3
  851.3 37.6 %shard_map.364 = (bf16[8,2,256,128]{3,2,1,0:T(8,128)(2,1)}, f32[256,2048]{1,0:T(8,128)}) custom-call(bf16[2,8,256,128]{3,2,1,0:T(8,128)(2,1)} %bitcast.220, bf16[4,256,2048]{2,1,0:T(8,128)(2,1)} %bitcast.250), custom_call_target="tpu_custom_call" | custom-call | bytes 15000000 | tf_op jit(solution)/shard_map/pallas_call | solution.py:142
  888.9 2.0 copy.181
  891.1 5.1 shard_map.365
  896.2 4.9 shard_map.366
  901.5 2.5 copy.186
  904.5 3.3 copy.182
  911.2 4.5 fusion.2
  921.3 2.9 convert_element_type.154
  927.6 6.0 convolution_convert_fusion.2
  933.6 41.1 %shard_map.367 = (bf16[4,2,64,1024]{3,2,1,0:T(8,128)(2,1)}, f32[256,2048]{1,0:T(8,128)}, bf16[4,64,512]{2,1,0:T(8,128)(2,1)}) custom-call(bf16[4,2,64,1024]{3,2,1,0:T(8,128)(2,1)} %bitcast.282, bf16[4,256,2048]{2,1,0:T(8,128)(2,1)} %bitcast.253, bf16[4,64,512]{2,1,0:T(8,128)(2,1)} %bitcast.294), custom_call_target="tpu_custom_call" | custom-call | bytes 15000000 | tf_op jit(solution)/shard_map/pallas_call | solution.py:142
  974.9 27.6 %shard_map.368 = (f32[9,256,2048]{2,1,0:T(8,128)}, f32[256,128]{1,0:T(8,128)}, f32[3,2048]{1,0:T(4,128)}, f32[3,2048]{1,0:T(4,128)}) custom-call(bf16[9,256,2048]{2,1,0:T(8,128)(2,1)} %bitcast.237, f32[256,128]{1,0:T(8,128)} %pad.25.m_ref, f32[4,256,2048]{2,1,0:T(8,128)} %get-tuple-element.76.s_ref, f32[3,2048]{1,0:T(4,128)} %slice.139.g_ref, ...), custom_call_target="tpu_custom_call" | custom-call | flops 75497472 | bytes 45088768 | tf_op jit(solution)/shard_map/pallas_call | solution.py:1290
  1007.5 3.0 copy.188
  1010.5 3.9 reshape.522
  1017.1 19.3 %shard_map.369 = (f32[48,128]{1,0:T(8,128)}, bf16[4,64,512]{2,1,0:T(8,128)(2,1)}, bf16[4,64,512]{2,1,0:T(8,128)(2,1)}) custom-call(f32[4,8,48,128]{3,2,1,0:T(8,128)} %copy.244, bf16[4,64,512]{2,1,0:T(8,128)(2,1)} %bitcast.281, bf16[4,64,512]{2,1,0:T(8,128)(2,1)} %bitcast.280), custom_call_target="tpu_custom_call" | custom-call | bytes 15000000 | tf_op jit(solution)/shard_map/pallas_call | solution.py:142
  (275 shorter events, 80.3 us)
Async XLA Ops:
  7.2 493.5 %copy-start = (f32[40,40]{1,0:T(8,128)S(1)}, f32[40,40]{1,0:T(8,128)}, u32[]{:S(2)}) copy-start(f32[40,40]{1,0:T(8,128)} %param.36) | copy-start | bytes 19204
  7.2 131.7 %all-gather.10.cloned.1.call-start = ((), (), s32[]{:S(2)}) async-start(), calls=%async_computation.11 | async-start | bytes 4718592 | tf_op jit(solution)/shard_map/all_gather | solution.py:1387
  9.1 2.1 copy-start.36
  9.5 2.6 copy-start.52
  9.5 2.8 copy-start.53
  9.5 2.9 copy-start.54
  9.6 2.9 copy-start.55
  9.6 3.0 copy-start.63
  9.6 3.0 copy-start.56
  9.6 3.0 copy-start.57
  9.6 3.0 copy-start.58
  9.6 3.0 copy-start.59
  48.1 5.0 copy-start.48
  50.0 205.6 %all-gather.12.cloned.1.call-start = ((), (), s32[]{:S(2)}) async-start(), calls=%async_computation.12 | async-start | bytes 5242880 | tf_op jit(solution)/shard_map/all_gather | solution.py:1362
  128.9 1.6 copy-start.9
  130.5 2.2 copy-start.18
  138.9 200.8 %all-gather.8.cloned.1.call-start = ((), (), s32[]{:S(2)}) async-start(), calls=%async_computation.5 | async-start | bytes 2359296 | tf_op jit(solution)/shard_map/all_gather | solution.py:1444
  178.4 2.2 copy-start.1
  180.6 2.2 copy-start.7
  182.8 53.5 %copy-start.2 = (bf16[32,2,64,512]{3,2,1,0:T(8,128)(2,1)S(1)}, bf16[32,2,64,512]{3,2,1,0:T(8,128)(2,1)}, u32[]{:S(2)}) copy-start(bf16[32,2,64,512]{3,2,1,0:T(8,128)(2,1)} %all-gather.10.cloned.1.call-done) | copy-start | bytes 12582916
  236.3 2.2 copy-start.4
  255.6 168.2 %all-gather.14.cloned.1.call-start = ((), (), s32[]{:S(2)}) async-start(), calls=%async_computation.13 | async-start | bytes 5242880 | tf_op jit(solution)/shard_map/all_gather | solution.py:1362
  256.2 476.3 %reduce-scatter.6.cloned.1.call-start = ((), (), s32[]{:S(2)}) async-start(), calls=%async_computation.6 | async-start | bytes 5242880 | tf_op jit(solution)/shard_map/reduce_scatter | solution.py:1500
  256.3 35.2 %copy-start.19 = (bf16[2,8,256,128]{3,2,1,0:T(8,128)(2,1)S(1)}, bf16[2,8,256,128]{3,2,1,0:T(8,128)(2,1)}, u32[]{:S(2)}) copy-start(bf16[2,8,256,128]{3,2,1,0:T(8,128)(2,1)} %get-tuple-element.82) | copy-start | bytes 3145732
  256.3 35.2 %copy-start.20 = (bf16[2,8,256,128]{3,2,1,0:T(8,128)(2,1)S(1)}, bf16[2,8,256,128]{3,2,1,0:T(8,128)(2,1)}, u32[]{:S(2)}) copy-start(bf16[2,8,256,128]{3,2,1,0:T(8,128)(2,1)} %get-tuple-element.85) | copy-start | bytes 3145732
  346.2 29.0 %copy-start.50 = (f32[2048]{0:T(1024)S(1)}, f32[2048]{0:T(1024)}, u32[]{:S(2)}) copy-start(f32[2048]{0:T(1024)} %add.158) | copy-start | bytes 24580
  377.8 1.3 copy-start.24
  377.8 1.3 copy-start.51
  423.9 19.3 %copy-start.61 = (bf16[1024,2048]{1,0:T(8,128)(2,1)S(1)}, bf16[1024,2048]{1,0:T(8,128)(2,1)}, u32[]{:S(2)}) copy-start(bf16[1024,2048]{1,0:T(8,128)(2,1)} %all-gather.12.cloned.1.call-done) | copy-start | bytes 12582916
  454.5 41.5 %copy-start.49 = (f32[2048]{0:T(1024)S(1)}, f32[2048]{0:T(1024)}, u32[]{:S(2)}) copy-start(f32[2048]{0:T(1024)} %add.169) | copy-start | bytes 24580
  498.6 4.7 copy-start.21
  498.6 2.1 copy-start.38
  500.6 2.7 copy-start.37
  500.8 2.5 copy-start.30
  503.3 1.9 copy-start.26
  558.1 229.3 %reduce-scatter.8.cloned.1.call-start = ((), (), s32[]{:S(2)}) async-start(), calls=%async_computation.7 | async-start | bytes 5242880 | tf_op jit(solution)/shard_map/reduce_scatter | solution.py:1500
  591.7 2.0 copy-start.6
  593.7 251.0 %reduce-scatter.10.cloned.1.call-start = ((), (), s32[]{:S(2)}) async-start(), calls=%async_computation.8 | async-start | bytes 2359296 | tf_op jit(solution)/shard_map/reduce_scatter | solution.py:1533
  608.0 41.4 %copy-start.25 = (f32[256,2048]{1,0:T(8,128)S(1)}, f32[256,2048]{1,0:T(8,128)}, u32[]{:S(2)}) copy-start(f32[256,2048]{1,0:T(8,128)} %copy-done.24) | copy-start | bytes 6291460
  649.4 2.6 copy-start.28
  651.9 1.6 copy-start.22
  652.0 2.2 copy-start.27
  652.0 2.5 copy-start.31
  657.4 33.9 %copy-start.62 = (bf16[512,2048]{1,0:T(8,128)(2,1)S(1)}, bf16[512,2048]{1,0:T(8,128)(2,1)}, u32[]{:S(2)}) copy-start(bf16[512,2048]{1,0:T(8,128)(2,1)} %all-gather.8.cloned.1.call-done) | copy-start | bytes 6291460
  698.7 1.5 copy-start.35
  732.5 201.1 %reduce-scatter.12.cloned.1.call-start = ((), (), s32[]{:S(2)}) async-start(), calls=%async_computation.9 | async-start | bytes 2359296 | tf_op jit(solution)/shard_map/reduce_scatter | solution.py:1533
  794.5 1.3 copy-start.11
  795.9 1.6 copy-start.10
  795.9 219.3 %reduce-scatter.14.cloned.1.call-start = ((), (), s32[]{:S(2)}) async-start(), calls=%async_computation.10 | async-start | bytes 4718592 | tf_op jit(solution)/shard_map/reduce_scatter | solution.py:1533
  797.5 2.2 copy-start.3
  904.5 6.7 copy-start.23
  911.2 8.4 copy-start.60
  917.4 6.8 copy-start.29
  921.3 4.0 copy-start.33
  921.3 5.1 copy-start.32
  974.8 29.4 %copy-start.47 = (f32[1,32,64]{2,1,0:T(8,128)S(1)}, f32[1,32,64]{2,1,0:T(8,128)}, u32[]{:S(2)}) copy-start(f32[1,32,64]{2,1,0:T(8,128)} %concatenate.43) | copy-start | bytes 24580
  974.8 29.4 %copy-start.46 = (f32[1,32,64]{2,1,0:T(8,128)S(1)}, f32[1,32,64]{2,1,0:T(8,128)}, u32[]{:S(2)}) copy-start(f32[1,32,64]{2,1,0:T(8,128)} %concatenate.45) | copy-start | bytes 24580
  974.8 29.5 %copy-start.43 = (f32[1,32,64]{2,1,0:T(8,128)S(1)}, f32[1,32,64]{2,1,0:T(8,128)}, u32[]{:S(2)}) copy-start(f32[1,32,64]{2,1,0:T(8,128)} %concatenate.47) | copy-start | bytes 24580
  974.8 29.5 %copy-start.44 = (f32[1,32,64]{2,1,0:T(8,128)S(1)}, f32[1,32,64]{2,1,0:T(8,128)}, u32[]{:S(2)}) copy-start(f32[1,32,64]{2,1,0:T(8,128)} %concatenate.48) | copy-start | bytes 24580
  974.8 29.5 %copy-start.45 = (f32[1,32,64]{2,1,0:T(8,128)S(1)}, f32[1,32,64]{2,1,0:T(8,128)}, u32[]{:S(2)}) copy-start(f32[1,32,64]{2,1,0:T(8,128)} %concatenate.49) | copy-start | bytes 24580
  974.8 29.7 %copy-start.41 = (f32[32,256]{1,0:T(8,128)S(1)}, f32[32,256]{1,0:T(8,128)}, u32[]{:S(2)}) copy-start(f32[32,256]{1,0:T(8,128)} %reshape.510) | copy-start | bytes 98308
  1004.6 1.9 copy-start.34
  1010.5 3.9 copy-start.39
  1014.4 28.3 %copy-start.40 = (bf16[4,64,512]{2,1,0:T(8,128)(2,1)S(1)}, bf16[4,64,512]{2,1,0:T(8,128)(2,1)}, u32[]{:S(2)}) copy-start(bf16[4,64,512]{2,1,0:T(8,128)(2,1)} %get-tuple-element.126) | copy-start | bytes 786436
  (9 other events, 9.2 us)
Sparse Core Ops, SparseCore 0:
  50.1 88.7 all-gather.9
  140.5 115.0 all-gather.11
  257.7 63.6 all-gather.7
  322.9 91.8 all-gather.13
  558.3 79.6 reduce-scatter.5
  640.2 77.4 reduce-scatter.7
  732.7 82.2 reduce-scatter.9
  818.5 84.7 reduce-scatter.11
  906.9 91.9 reduce-scatter.13

commit v4 on v3

--- a/solution.py
+++ b/solution.py
@@ -112,6 +112,11 @@
 def comm(cid, *tasks):
     n = len(tasks)
     counts = [len(t[5]) for t in tasks]
+    limit = 6 * 2**20
+    for t in tasks:
+        for x in t[5]:
+            if x.dtype in (BF16, F32):
+                limit += math.prod(x.shape) * jnp.dtype(x.dtype).itemsize
 
     def kernel(*refs):
         targets, seen = [], []
@@ -120,7 +125,7 @@
             (the_pair, [along_ctx]),
             (the_pair, [plane_others]),
             (links_and_twin, [plane_others]),
-            (along_fsdp, [plane_others]),
+            (links_and_twin, [along_fsdp]),
         ]
         for t in tasks:
             if t[0] not in seen and (t[0], seen[:1]) not in covered:
@@ -146,7 +151,7 @@
         out_specs=[t[4] for t in tasks],
         scratch_shapes=[x for t in tasks for x in t[5]],
         compiler_params=pltpu.CompilerParams(
-            collective_id=cid, has_side_effects=True, vmem_limit_bytes=56 * 2**20
+            collective_id=cid, has_side_effects=True, vmem_limit_bytes=limit
         ),
         cost_estimate=pl.CostEstimate(flops=0, bytes_accessed=15_000_000, transcendentals=0),
     )(*[t[1] for t in tasks])
@@ -498,11 +503,8 @@
     return [(lax.rem(f + a, fn), (c, pair[1])[b]) for a in range(fn) for b in range(2) if a or b]
 
 
-def plane_diagonals():
-    fn = lax.axis_size("fsdp")
-    f, _ = place()
-    (pair,) = the_pair()
-    return [(lax.rem(f + a, fn), pair[1]) for a in range(1, fn)]
+def plane_sides():
+    return [t for i, t in enumerate(plane_others()) if i > 0]
 
 
 def exchange_plane(x, peers):
@@ -547,11 +549,69 @@
     return (peers, x, shape, ANY, ANY, [dma(fn, 2), dma(fn, 2), dma()], body)
 
 
+def exchange_columns(x, wide, peers):
+    fn = lax.axis_size("fsdp")
+    _, _, rows, cols = x.shape
+    count = cols // wide
+
+    def body(x_ref, o_ref, s, r, own):
+        f, c = place()
+        lo = lax.rem(c, 2)
+        (pair,) = the_pair()
+
+        def index(a, b):
+            return lax.rem(f + a + fn, fn), (lo if b == 0 else 1 - lo)
+
+        def target(slot, h):
+            at = ((slot[0] * count + h) * 2 + slot[1]) * wide
+            return o_ref.at[:, pl.ds(pl.multiple_of(at, wide), wide)]
+
+        def copy(a, b, h, slot):
+            fa, lb = index(a, b)
+            return remote(
+                x_ref.at[fa, lb, :, pl.ds(h * wide, wide)],
+                target(slot, h),
+                s.at[a, b, h],
+                r.at[a, b, h],
+                (fa, c if b == 0 else pair[1]),
+            )
+
+        steps = [
+            (a, b, h) for a in range(fn) for b in range(2) for h in range(count) if a or b
+        ]
+        mine = [
+            pltpu.make_async_copy(
+                x_ref.at[f, lo, :, pl.ds(h * wide, wide)], target((f, lo), h), own.at[h]
+            )
+            for h in range(count)
+        ]
+
+        def start():
+            for a, b, h in steps:
+                copy(a, b, h, (f, lo)).start()
+            for m in mine:
+                m.start()
+
+        def end():
+            for m in mine:
+                m.wait()
+            for a, b, h in steps:
+                copy(a, b, h, index(-a, b)).wait_recv()
+            for a, b, h in steps:
+                copy(a, b, h, (f, lo)).wait_send()
+
+        return start, lambda: None, end
+
+    shape = jax.ShapeDtypeStruct((rows, fn * 2 * cols), x.dtype)
+    scratch = [dma(fn, 2, count), dma(fn, 2, count), dma(count)]
+    return (peers, x, shape, ANY, ANY, scratch, body)
+
+
 def links_twin_pair():
     return links_and_twin() + the_pair()
 
 
-def gather_plane(x, parts=4):
+def gather_plane(x, parts=8):
     fn = lax.axis_size("fsdp")
     chips = fn // 2
     n, d = x.shape
@@ -1193,25 +1253,27 @@
     )(bit, x, g)
 
 
-def front(hist, mix, gain, shift, tokens=16, wide=256):
+def front(hist, mix, gain, shift, tokens=16, wide=128):
     h, n, d = hist.shape
     rest = gain.shape[0]
 
-    def kernel(h_ref, m_ref, g_ref, b_ref, s_ref, n_ref):
+    def kernel(h_ref, m_ref, g_ref, b_ref, s_ref, *n_refs):
         m = m_ref[...]
+        across = [jnp.broadcast_to(m[:, i : i + 1], (tokens, wide)) for i in range(4 * h)]
         for at in range(0, d, wide):
             cut = slice(at, at + wide)
+            rows = [h_ref[j, :, cut].astype(F32) for j in range(h)]
             for s in range(4):
-                acc = m[:, s * h : s * h + 1] * h_ref[0, :, cut].astype(F32)
+                acc = across[s * h] * rows[0]
                 for j in range(1, h):
-                    acc += m[:, s * h + j : s * h + j + 1] * h_ref[j, :, cut].astype(F32)
+                    acc += across[s * h + j] * rows[j]
                 s_ref[s, :, cut] = acc
         for s in range(rest):
             x = s_ref[s]
             centre = x - jnp.mean(x, axis=-1, keepdims=True)
             spread = jnp.mean(centre * centre, axis=-1, keepdims=True)
             y = centre * lax.rsqrt(spread + EPS_NORM) * g_ref[s : s + 1] + b_ref[s : s + 1]
-            n_ref[s] = y.astype(BF16)
+            n_refs[s][...] = y.astype(BF16)
 
     return pl.pallas_call(
         kernel,
@@ -1224,12 +1286,10 @@
         ],
         out_specs=[
             pl.BlockSpec((4, tokens, d), lambda i: (0, i, 0)),
-            pl.BlockSpec((rest, tokens, d), lambda i: (0, i, 0)),
-        ],
-        out_shape=[
-            jax.ShapeDtypeStruct((4, n, d), F32),
-            jax.ShapeDtypeStruct((rest, n, d), BF16),
-        ],
+        ]
+        + [pl.BlockSpec((tokens, d), lambda i: (i, 0))] * rest,
+        out_shape=[jax.ShapeDtypeStruct((4, n, d), F32)]
+        + [jax.ShapeDtypeStruct((n, d), BF16)] * rest,
         compiler_params=pltpu.CompilerParams(vmem_limit_bytes=60 * 2**20),
         cost_estimate=pl.CostEstimate(
             flops=2 * 4 * h * n * d, bytes_accessed=n * d * (2 * h + 22), transcendentals=0
@@ -1263,20 +1323,23 @@
             )
         ds[rest] = r_ref[...]
         m = m_ref[...]
+        across = [jnp.broadcast_to(m[:, i : i + 1], (tokens, 128)) for i in range(4 * h)]
         sums = [[jnp.zeros((tokens, 128), F32) for _ in range(h)] for _ in range(4)]
         for at in range(0, d, wide):
-            cut = slice(at, at + wide)
-            parts = [ds[s, :, cut] for s in range(4)]
+            cuts = [slice(b, b + 128) for b in range(at, at + wide, 128)]
+            parts = [[ds[s, :, cut] for cut in cuts] for s in range(4)]
             for j in range(h):
-                row = h_ref[j, :, cut].astype(F32)
-                acc = m[:, j : j + 1] * parts[0]
-                for s in range(1, 4):
-                    acc += m[:, s * h + j : s * h + j + 1] * parts[s]
-                gh_ref[j, :, cut] = acc
+                for i, cut in enumerate(cuts):
+                    acc = across[j] * parts[0][i]
+                    for s in range(1, 4):
+                        acc += across[s * h + j] * parts[s][i]
+                    gh_ref[j, :, cut] = acc
+                rows = [h_ref[j, :, cut].astype(F32) for cut in cuts]
                 for s in range(4):
-                    prod = row * parts[s]
-                    for b in range(0, wide, 128):
-                        sums[s][j] += prod[:, b : b + 128]
+                    prod = rows[0] * parts[s][0]
+                    for i in range(1, len(cuts)):
+                        prod += rows[i] * parts[s][i]
+                    sums[s][j] += prod
         lane = lax.broadcasted_iota(jnp.int32, (tokens, 128), 1)
         total = jnp.zeros((tokens, 128), F32)
         for s in range(4):
@@ -1374,17 +1437,13 @@
     ]
     flat = jnp.concatenate([a.reshape(-1) for a in parts])
     flat = jnp.pad(flat, (0, -flat.size % 1024)).reshape(-1, 128)
-    flats, qkv_cols, up_cols = comm(
+    wout = lax.all_gather(out_weight, "ctx", axis=0, tiled=True)
+    flats, qkv_cols = comm(
         1,
         gather_small(flat),
         exchange_fsdp(qkv_weight.reshape(rows, 3, fn, wcol).transpose(2, 1, 0, 3)),
-        exchange_plane(
-            up_weight.reshape(rows, fn, count, 2, -1).transpose(1, 3, 0, 2, 4).reshape(fn, 2, rows, pcol),
-            plane_diagonals,
-        ),
     )
     flats = flats.reshape(dn, -1)
-    w12 = lax.all_gather(qkv_cols[:, 1:], "ctx", axis=0)
     pieces, at = [], 0
     for a in parts:
         pieces.append(flats[:, at : at + a.size])
@@ -1406,7 +1465,7 @@
     hist2 = history.reshape(hist, nloc, width)
     mix2 = dense_mix.reshape(dense_mix.shape[0], hist, nloc)
     mixes = jnp.pad(mix2.reshape(-1, nloc).T, ((0, 0), (0, 128 - mix2.shape[0] * hist)))
-    streams, normed = front(hist2, mixes, gain_all[:3], shift_all[:3])
+    streams, *normed = front(hist2, mixes, gain_all[:3], shift_all[:3])
 
     bias_cols = lax.dynamic_slice_in_dim(qkv_shift, fi * wcol, wcol, 1)
     tables = rotary_tables(total)
@@ -1432,19 +1491,26 @@
         x = x.reshape(fn * seqs, heads, length, HEAD_DIM)
         return x.transpose(0, 2, 1, 3).reshape(ntp, wcol)
 
-    w0, g0 = comm(9, gather_ctx(qkv_cols[:, 0]), gather_fsdp(normed[0]))
-    p0 = projected(g0, w0[:, :, None], 0, 0)
-    p0, w12, down_rows = lax.optimization_barrier((p0, w12, down_weight))
+    w01, g0 = comm(9, gather_ctx(qkv_cols[:, :2]), gather_fsdp(normed[0]))
+    g0, cols_2, wout = lax.optimization_barrier((g0, qkv_cols[:, 2], wout))
+    w2 = lax.all_gather(cols_2, "ctx", axis=0)
+    p0 = projected(g0, w01, 0, 0)
+    q_u, g1 = comm(4, exchange_ctx(p0, True), gather_fsdp(normed[1]))
+    p1 = projected(g1, w01, 1, 1)
+    p1, down_rows = lax.optimization_barrier((p1, down_weight))
     wdown = line_gather(down_rows).reshape(pcol, width)
-    q_u, g1 = comm(4, exchange_ctx(p0, True), gather_fsdp(normed[1]))
-    p1 = projected(g1, w12, 0, 1)
     k_u, g2 = comm(4, exchange_ctx(p1, True), gather_fsdp(normed[2]))
-    p2 = projected(g2, w12, 1, 2)
-    p2, wdown, up_cols, out_rows = lax.optimization_barrier((p2, wdown, up_cols, out_weight))
-    wout = lax.all_gather(out_rows, "ctx", axis=0, tiled=True)
+    p2 = projected(g2, w2[:, :, None], 0, 2)
+    v_u, up_cols = comm(
+        11,
+        exchange_ctx(p2, True),
+        exchange_plane(
+            up_weight.reshape(rows, fn, count, 2, -1).transpose(1, 3, 0, 2, 4).reshape(fn, 2, rows, pcol),
+            plane_sides,
+        ),
+    )
     up_g = line_gather(up_cols).reshape(count, fn, 2 * rows, pcol)
-    (v_u,) = comm(5, exchange_ctx(p2, True))
-    wqkv = [w.transpose(1, 0, 2, 3).reshape(width, wcol) for w in (w0, w12[:, :, 0], w12[:, :, 1])]
+    wqkv = [w.transpose(1, 0, 2, 3).reshape(width, wcol) for w in (w01[:, :, 0], w01[:, :, 1], w2)]
     q_u, k_u, v_u = whole_units(q_u), whole_units(k_u), whole_units(v_u)
     normed_g = [g.reshape(ntp, width) for g in (g0, g1, g2)]
 
@@ -1458,6 +1524,7 @@
     )[:, None, :]
     att_u, lse_u = attend(q_u, k_u, v_u, first_key)
     attended = columns(comm(6, from_units(att_u))[0])
+    attended, wdown = lax.optimization_barrier((attended, wdown))
 
     def scatter_tokens(x):
         return comm(10, scatter_fsdp(x.astype(BF16).reshape(fn, nloc, width)))[0]
@@ -1541,7 +1608,13 @@
     def qkv_part(p, i):
         return halved_product(normed_g[i], p, bit, fn, cn, split=False)[0]
 
-    gp0, grad_up = lax.optimization_barrier((comm(6, from_units(gq))[0], grad_up))
+    grad_up = grad_up.reshape(fn, 2, rows, pcol)
+    if ff // dn % 128 == 0:
+        gp0, grad_up = comm(12, from_units(gq), exchange_columns(grad_up, ff // dn, plane_sides))
+    else:
+        gp0, grad_up = comm(12, from_units(gq), exchange_plane(grad_up, plane_sides))
+        grad_up = grad_up.reshape(fn, 2, rows, count, -1).transpose(2, 0, 3, 1, 4)
+        grad_up = grad_up.reshape(rows, ff)
     gp0 = columns(gp0)
     q_part, gk = lax.optimization_barrier((qkv_part(gp0, 0), gk))
     grad_q = ctx_scatter(q_part.reshape(-1, wcol)).reshape(fn, rows, wcol)
@@ -1551,15 +1624,13 @@
     gp2, gn1 = comm(8, from_units(gv), scatter_fsdp(back_part(gp1, 1)))
     gp2 = columns(gp2)
     kv_part = jnp.stack([qkv_part(gp1, 1), qkv_part(gp2, 2)], axis=1)
-    kv_part, grad_up = lax.optimization_barrier((kv_part, grad_up))
+    kv_part, gp2 = lax.optimization_barrier((kv_part, gp2))
     grad_kv = ctx_scatter(kv_part.reshape(-1, wcol)).reshape(2, fn, rows, wcol)
-    grad_up, gn2, grad_q = comm(
+    grad_q, gn2 = comm(
         7,
-        exchange_plane(grad_up.reshape(fn, 2, rows, pcol), plane_others),
+        exchange_fsdp(grad_q),
         scatter_fsdp(back_part(gp2, 2)),
-        exchange_fsdp(grad_q),
     )
-    grad_up = grad_up.reshape(fn, 2, rows, count, -1).transpose(2, 0, 3, 1, 4).reshape(rows, ff)
     grad_proj = (gp0, gp1, gp2)
     grad_qkv_shift = jnp.stack([jnp.sum(g.astype(F32), axis=0) for g in grad_proj])
 

time: 1060 us -> 1020 us (0.962)
  Pallas kernels: 798 us -> 769 us
  matrix products: 98.3 us -> 85.5 us
    pallas_call x18, Pallas kernels: 649 us -> 620 us  [comm(): pl.pallas_call(kernel, out_shape=[t[2] for t in tasks], in_specs=[t[3] fo...]
    unnamed x144 -> x145, local copies, waits for them, and re-layouts: 32.7 us -> 52.8 us
    reduce_scatter x3, waiting for transfers between devices: 0.02 us -> 16.4 us  [ctx_scatter(): return lax.psum_scatter(x, 'ctx', scatter_dimension=0, tiled=True)]
    dot_general x10, matrix products: 87.1 us -> 72.7 us  [dot(): return jnp.einsum(pattern, left, right, preferred_element_type=F32)]
    all_gather x2, waiting for transfers between devices: 13 us -> 0.02 us  [line_gather(): return lax.all_gather(w, 'ctx', axis=0, axis_index_groups=lines)]
  transfers between devices with their start and end apart: 9 -> 9, of which waited for: 2 -> 1; matrix products, arithmetic and copies ran while one was open for 13% -> 12% of each run, Pallas kernels for 61% -> 65%
where the time goes in v4:
time: 1020 us; the launch traced here: 1010 us
  Pallas kernels  769 us (75%)
  local copies, waits for them, and re-layouts  101 us (10%)
  matrix products  85.5 us (8%)
  other arithmetic  19.1 us (2%)
  waiting for transfers between devices  17.3 us (2%)
  between operations  15.7 us (2%)
    pallas_call x18, Pallas kernels, comm(): pl.pallas_call(kernel, out_shape=[t[2] for t in tasks], in_specs=[t[3] fo...  620 us
    dot_general x10, matrix products, dot(): return jnp.einsum(pattern, left, right, preferred_element_type=F32)  72.7 us
    unnamed x145, local copies, waits for them, and re-layouts  52.8 us
    pallas_call x4, Pallas kernels, halved_product(): pl.pallas_call(kernel, grid_spec=pltpu.PrefetchScalarGridSpec(num_scalar_...  33.9 us
    pallas_call x1, Pallas kernels, last(): pl.pallas_call(kernel, grid=(n // tokens,), in_specs=[pl.BlockSpec((h, to...  27.3 us
    pallas_call x1, Pallas kernels, attend_back(): pl.pallas_call(kernel, grid=(u, t // block), in_specs=[pl.BlockSpec(spec,...  24.9 us
  transfers between devices with their start and end apart: 9, of which 1 were waited for; matrix products, arithmetic and copies ran while one was open for 12% of the time, Pallas kernels for 65%

profile of v4, /device:TPU:1, one launch (start us, length us, event | category | flops | bytes accessed | tf_op | source)
XLA Modules:
  0.0 1008.1 jit_solution(11922188032026193056)
XLA Ops:
  13.8 21.7 %shard_map.340 = (f32[4,8,32,128]{3,2,1,0:T(8,128)S(1)}, bf16[4,3,64,512]{3,2,1,0:T(8,128)(2,1)S(1)}) custom-call(f32[32,128]{1,0:T(8,128)S(1)} %pad_bitcast_fusion.1.refs_0_, bf16[4,3,64,512]{3,2,1,0:T(8,128)(2,1)S(1)} %bitcast.224), custom_call_target="tpu_custom_call" | custom-call | bytes 15000000 | tf_op jit(solution)/shard_map/pallas_call | solution.py:147
  38.4 16.9 %shard_map.341 = (f32[4,256,2048]{2,1,0:T(8,128)}, bf16[256,2048]{1,0:T(8,128)(2,1)}, bf16[256,2048]{1,0:T(8,128)(2,1)}, bf16[256,2048]{1,0:T(8,128)(2,1)}) custom-call(bf16[9,256,2048]{2,1,0:T(8,128)(2,1)} %bitcast.256, f32[256,128]{1,0:T(8,128)} %pad.25.m_ref, f32[3,2048]{1,0:T(4,128)} %slice.130.g_ref, f32[3,2048]{1,0:T(4,128)} %slice.133.b_ref), custom_call_target="tpu_custom_call" | custom-call | flops 37748736 | bytes 20971520 | tf_op jit(solution)/shard_map/pallas_call | solution.py:1278
  56.5 53.7 %shard_map.342 = (bf16[8,4,2,64,512]{4,3,2,1,0:T(8,128)(2,1)S(1)}, bf16[4,256,2048]{2,1,0:T(8,128)(2,1)S(1)}) custom-call(bf16[4,2,64,512]{3,2,1,0:T(8,128)(2,1)S(1)} %slice.135.refs_0_, bf16[256,2048]{1,0:T(8,128)(2,1)S(1)} %copy-done.18), custom_call_target="tpu_custom_call" | custom-call | bytes 15000000 | tf_op jit(solution)/shard_map/pallas_call | solution.py:147
  110.2 2.0 copy-done.1
  112.2 2.0 copy-done.8
  116.3 2.2 copy-done.2
  118.5 2.2 copy-done.9
  120.7 4.2 shard_map.343
  124.9 28.5 %shard_map.344 = (bf16[2,8,256,128]{3,2,1,0:T(8,128)(2,1)S(1)}, bf16[4,256,2048]{2,1,0:T(8,128)(2,1)S(1)}) custom-call(bf16[8,2,256,128]{3,2,1,0:T(8,128)(2,1)S(1)} %bitcast.223, bf16[256,2048]{1,0:T(8,128)(2,1)S(1)} %copy-done.22), custom_call_target="tpu_custom_call" | custom-call | bytes 15000000 | tf_op jit(solution)/shard_map/pallas_call | solution.py:147
  153.4 4.2 shard_map.345
  159.9 1.8 reshape.455.refs_1_
  161.7 33.9 %shard_map.346 = (bf16[2,8,256,128]{3,2,1,0:T(8,128)(2,1)S(1)}, bf16[4,256,2048]{2,1,0:T(8,128)(2,1)S(1)}) custom-call(bf16[8,2,256,128]{3,2,1,0:T(8,128)(2,1)S(1)} %bitcast.222, bf16[256,2048]{1,0:T(8,128)(2,1)S(1)} %copy-done.20), custom_call_target="tpu_custom_call" | custom-call | bytes 15000000 | tf_op jit(solution)/shard_map/pallas_call | solution.py:147
  195.6 2.0 copy-done.25
  200.3 2.2 copy-done.26
  202.5 3.1 shard_map.347
  205.7 39.8 %shard_map.348 = (bf16[2,8,256,128]{3,2,1,0:T(8,128)(2,1)S(1)}, bf16[4,2,64,1024]{3,2,1,0:T(8,128)(2,1)}) custom-call(bf16[8,2,256,128]{3,2,1,0:T(8,128)(2,1)S(1)} %bitcast.236, bf16[4,2,64,1024]{3,2,1,0:T(8,128)(2,1)S(1)} %reshape.455.refs_1_), custom_call_target="tpu_custom_call" | custom-call | bytes 15000000 | tf_op jit(solution)/shard_map/pallas_call | solution.py:147
  248.5 1.8 reshape.467
  252.8 15.3 %shard_map.349 = (bf16[2,2048,128]{2,1,0:T(8,128)(2,1)S(1)}, f32[2,1,2048]{2,1,0:T(1,128)S(1)}) custom-call(bf16[2,2048,128]{2,1,0:T(8,128)(2,1)S(1)} %bitcast.250, bf16[2,2048,128]{2,1,0:T(8,128)(2,1)S(1)} %bitcast.252, bf16[2,2048,128]{2,1,0:T(8,128)(2,1)S(1)} %bitcast.255, s32[2,1,2048]{2,1,0:T(1,128)S(1)} %broadcast_in_dim.28.s_ref), custom_call_target="tpu_custom_call" | custom-call | flops 2147483648 | bytes 8388608 | tf_op jit(solution)/shard_map/pallas_call | solution.py:985
  268.2 37.8 %shard_map.350 = bf16[8,2,256,128]{3,2,1,0:T(8,128)(2,1)S(1)} custom-call(bf16[2,8,256,128]{3,2,1,0:T(8,128)(2,1)S(1)} %bitcast.231), custom_call_target="tpu_custom_call" | custom-call | bytes 15000000 | tf_op jit(solution)/shard_map/pallas_call | solution.py:147
  307.1 4.3 convolution_convert_fusion.6
  311.4 28.2 %shard_map.351 = f32[256,2048]{1,0:T(8,128)S(1)} custom-call(bf16[4,256,2048]{2,1,0:T(8,128)(2,1)S(1)} %bitcast.208), custom_call_target="tpu_custom_call" | custom-call | bytes 15000000 | tf_op jit(solution)/shard_map/pallas_call | solution.py:147
  339.6 2.1 fusion.35
  343.0 41.5 %shard_map.352 = bf16[4,2,256,2048]{3,2,1,0:T(8,128)(2,1)S(1)} custom-call(bf16[256,2048]{1,0:T(8,128)(2,1)S(1)} %add_convert_fusion.refs_0_), custom_call_target="tpu_custom_call" | custom-call | bytes 15000000 | tf_op jit(solution)/shard_map/pallas_call | solution.py:147
  384.5 3.4 copy-done.3
  387.9 19.2 %shard_map.353 = (bf16[2048,1024]{1,0:T(8,128)(2,1)S(1)}, bf16[2048,1024]{1,0:T(8,128)(2,1)}, bf16[2048,1024]{1,0:T(8,128)(2,1)}) custom-call(bf16[2048,2048]{1,0:T(8,128)(2,1)} %bitcast.200, bf16[4,4,128,1024]{3,2,1,0:T(8,128)(2,1)} %bitcast.291, f32[1,1024]{1,0:T(1,128)S(1)} %bitcast.248), custom_call_target="tpu_custom_call" | custom-call | flops 8589934592 | bytes 60000000 | tf_op jit(solution)/shard_map/pallas_call | solution.py:1185
  407.1 9.6 convolution_convert_fusion.1
  416.7 40.4 %shard_map.354 = f32[256,2048]{1,0:T(8,128)S(1)} custom-call(bf16[4,2,256,2048]{3,2,1,0:T(8,128)(2,1)S(1)} %bitcast.199), custom_call_target="tpu_custom_call" | custom-call | bytes 15000000 | tf_op jit(solution)/shard_map/pallas_call | solution.py:147
  458.4 2.0 fusion.13
  460.6 2.4 multiply_reduce_fusion
  464.4 39.4 %shard_map.355 = bf16[4,2,256,2048]{3,2,1,0:T(8,128)(2,1)S(1)} custom-call(bf16[256,2048]{1,0:T(8,128)(2,1)S(1)} %get-tuple-element.268.refs_0_), custom_call_target="tpu_custom_call" | custom-call | bytes 15000000 | tf_op jit(solution)/shard_map/pallas_call | solution.py:147
  503.8 3.2 copy-done.4
  507.0 11.2 %convolution_convert_fusion.5 = bf16[1024,2048]{1,0:T(8,128)(2,1)} fusion(bf16[2048,1024]{1,0:T(8,128)(2,1)S(1)} %get-tuple-element.98, bf16[2048,2048]{1,0:T(8,128)(2,1)S(1)} %bitcast.202), kind=kOutput, calls=%fused_computation.9 | convolution fusion | flops 8592031744 | bytes 16777216 | tf_op jit(solution)/shard_map/nf,nd->fd/dot_general | solution.py:69
  518.3 16.1 %convert_reduce_fusion = (f32[1024]{0:T(1024)}, bf16[2048,1024]{1,0:T(8,128)(2,1)}) fusion(bf16[2048,1024]{1,0:T(8,128)(2,1)} %get-tuple-element.102, bf16[2048,2048]{1,0:T(8,128)(2,1)} %bitcast.203, bf16[1024,2048]{1,0:T(8,128)(2,1)} %all-gather.12.cloned.1.call-done), kind=kOutput, calls=%fused_computation.1 | convolution fusion | flops 8600419328 | bytes 20975616 | tf_op jit(solution)/shard_map/nd,fd->nf/dot_general | solution.py:69
  534.4 18.1 %shard_map.356 = bf16[4,4,128,1024]{3,2,1,0:T(8,128)(2,1)S(1)} custom-call(s32[1]{0:T(128)} %bitcast.32.bit_ref, bf16[2048,2048]{1,0:T(8,128)(2,1)} %bitcast.201, bf16[2048,1024]{1,0:T(8,128)(2,1)} %get-tuple-element.103.g_ref), custom_call_target="tpu_custom_call" | custom-call | flops 8589934592 | bytes 16777216 | tf_op jit(solution)/shard_map/pallas_call | solution.py:1234
  552.5 2.0 copy-done.6
  554.6 12.5 %convolution_convert_fusion = bf16[2048,2048]{1,0:T(8,128)(2,1)S(1)} fusion(bf16[2048,1024]{1,0:T(8,128)(2,1)} %get-tuple-element.103.g_ref, bf16[2048,1024]{1,0:T(8,128)(2,1)} %get-tuple-element.104), kind=kOutput, calls=%fused_computation.3 | convolution fusion | flops 8594128896 | bytes 16777216 | tf_op jit(solution)/shard_map/nf,df->nd/dot_general | solution.py:69
  567.1 40.4 %shard_map.357 = f32[256,2048]{1,0:T(8,128)S(1)} custom-call(bf16[4,2,256,2048]{3,2,1,0:T(8,128)(2,1)S(1)} %bitcast.198), custom_call_target="tpu_custom_call" | custom-call | bytes 15000000 | tf_op jit(solution)/shard_map/pallas_call | solution.py:147
  610.2 2.8 convert_reduce_fusion.2
  613.0 26.9 %shard_map.358 = bf16[4,256,2048]{2,1,0:T(8,128)(2,1)S(1)} custom-call(bf16[256,2048]{1,0:T(8,128)(2,1)S(1)} %get-tuple-element.270.refs_0_), custom_call_target="tpu_custom_call" | custom-call | bytes 15000000 | tf_op jit(solution)/shard_map/pallas_call | solution.py:147
  639.9 2.0 copy-done.5
  642.0 2.4 convolution_convert_fusion.8
  645.6 6.0 convolution_convert_fusion.7
  651.6 40.0 %shard_map.359 = bf16[2,8,256,128]{3,2,1,0:T(8,128)(2,1)S(1)} custom-call(bf16[8,2,256,128]{3,2,1,0:T(8,128)(2,1)S(1)} %bitcast.218), custom_call_target="tpu_custom_call" | custom-call | bytes 15000000 | tf_op jit(solution)/shard_map/pallas_call | solution.py:147
  695.1 24.9 %shard_map.360 = (bf16[2,2048,128]{2,1,0:T(8,128)(2,1)S(1)}, bf16[2,2048,128]{2,1,0:T(8,128)(2,1)S(1)}, bf16[2,2048,128]{2,1,0:T(8,128)(2,1)S(1)}) custom-call(bf16[2,2048,128]{2,1,0:T(8,128)(2,1)S(1)} %bitcast.251, bf16[2,2048,128]{2,1,0:T(8,128)(2,1)S(1)} %bitcast.253, bf16[2,2048,128]{2,1,0:T(8,128)(2,1)} %bitcast.254, ...), custom_call_target="tpu_custom_call" | custom-call | flops 5368709120 | bytes 20971520 | tf_op jit(solution)/shard_map/pallas_call | solution.py:1072
  722.3 38.5 %shard_map.361 = (bf16[8,2,256,128]{3,2,1,0:T(8,128)(2,1)S(1)}, bf16[64,8192]{1,0:T(8,128)(2,1)S(1)}) custom-call(bf16[2,8,256,128]{3,2,1,0:T(8,128)(2,1)S(1)} %bitcast.234, bf16[4,2,64,1024]{3,2,1,0:T(8,128)(2,1)S(1)} %bitcast.232), custom_call_target="tpu_custom_call" | custom-call | bytes 15000000 | tf_op jit(solution)/shard_map/pallas_call | solution.py:147
  762.8 5.8 shard_map.362
  768.6 2.5 slice_bitcast_fusion
  772.8 2.4 convolution_convert_fusion.4
  775.2 29.5 %shard_map.363 = (bf16[8,2,256,128]{3,2,1,0:T(8,128)(2,1)S(1)}, f32[256,2048]{1,0:T(8,128)S(1)}) custom-call(bf16[2,8,256,128]{3,2,1,0:T(8,128)(2,1)S(1)} %bitcast.230, bf16[4,256,2048]{2,1,0:T(8,128)(2,1)S(1)} %bitcast.207), custom_call_target="tpu_custom_call" | custom-call | bytes 15000000 | tf_op jit(solution)/shard_map/pallas_call | solution.py:147
  807.6 2.4 convolution_convert_fusion.3
  810.0 31.5 %shard_map.364 = (bf16[8,2,256,128]{3,2,1,0:T(8,128)(2,1)S(1)}, f32[256,2048]{1,0:T(8,128)S(1)}) custom-call(bf16[2,8,256,128]{3,2,1,0:T(8,128)(2,1)S(1)} %bitcast.229, bf16[4,256,2048]{2,1,0:T(8,128)(2,1)S(1)} %bitcast.206), custom_call_target="tpu_custom_call" | custom-call | bytes 15000000 | tf_op jit(solution)/shard_map/pallas_call | solution.py:147
  843.9 4.9 shard_map.365
  848.8 5.1 shard_map.366
  854.4 2.3 copy.200
  857.6 3.1 copy.196
  864.1 6.1 fusion.2
  870.2 1.8 reshape.503
  879.5 2.7 convert_element_type.140
  886.3 6.0 convolution_convert_fusion.2
  892.2 2.6 copy-done.7
  895.8 28.3 %shard_map.367 = (bf16[4,64,512]{2,1,0:T(8,128)(2,1)S(1)}, f32[256,2048]{1,0:T(8,128)S(1)}) custom-call(bf16[4,64,512]{2,1,0:T(8,128)(2,1)S(1)} %bitcast.241, bf16[4,256,2048]{2,1,0:T(8,128)(2,1)S(1)} %bitcast.210), custom_call_target="tpu_custom_call" | custom-call | bytes 15000000 | tf_op jit(solution)/shard_map/pallas_call | solution.py:147
  925.4 27.3 %shard_map.368 = (f32[9,256,2048]{2,1,0:T(8,128)}, f32[256,128]{1,0:T(8,128)}, f32[3,2048]{1,0:T(4,128)}, f32[3,2048]{1,0:T(4,128)}) custom-call(bf16[9,256,2048]{2,1,0:T(8,128)(2,1)} %bitcast.257, f32[256,128]{1,0:T(8,128)} %pad.25.m_ref, f32[4,256,2048]{2,1,0:T(8,128)} %get-tuple-element.78.s_ref, f32[3,2048]{1,0:T(4,128)} %slice.130.g_ref, ...), custom_call_target="tpu_custom_call" | custom-call | flops 75497472 | bytes 45088768 | tf_op jit(solution)/shard_map/pallas_call | solution.py:1353
  957.4 16.4 %reduce-scatter.14.cloned.1.call-done = bf16[512,512]{1,0:T(8,128)(2,1)} async-done(((bf16[4096,512]{1,0:T(8,128)(2,1)}), bf16[512,512]{1,0:T(8,128)(2,1)}) %reduce-scatter.14.cloned.1.call-update) | async-done | bytes 524304 | tf_op jit(solution)/shard_map/reduce_scatter | solution.py:1600
  974.9 19.6 %shard_map.369 = (f32[48,128]{1,0:T(8,128)S(1)}, bf16[4,64,512]{2,1,0:T(8,128)(2,1)S(1)}, bf16[4,64,512]{2,1,0:T(8,128)(2,1)S(1)}) custom-call(f32[4,8,48,128]{3,2,1,0:T(8,128)S(1)} %copy.247, bf16[4,64,512]{2,1,0:T(8,128)(2,1)S(1)} %bitcast.240, bf16[4,64,512]{2,1,0:T(8,128)(2,1)S(1)} %bitcast.239), custom_call_target="tpu_custom_call" | custom-call | bytes 15000000 | tf_op jit(solution)/shard_map/pallas_call | solution.py:147
  (273 shorter events, 77.3 us)
Async XLA Ops:
  7.2 453.2 %copy-start = (f32[40,40]{1,0:T(8,128)S(1)}, f32[40,40]{1,0:T(8,128)}, u32[]{:S(2)}) copy-start(f32[40,40]{1,0:T(8,128)} %param.36) | copy-start | bytes 19204
  7.2 107.7 %all-gather.8.cloned.1.call-start = ((), (), s32[]{:S(2)}) async-start(), calls=%async_computation.5 | async-start | bytes 2359296 | tf_op jit(solution)/shard_map/all_gather | solution.py:1440
  7.9 190.8 %all-gather.10.cloned.1.call-start = ((), (), s32[]{:S(2)}) async-start(), calls=%async_computation.11 | async-start | bytes 2359296 | tf_op jit(solution)/shard_map/all_gather | solution.py:1496
  8.0 29.5 %copy-start.61 = (f32[4,9,1,256]{3,2,1,0:T(1,128)S(1)}, f32[4,9,1,256]{3,2,1,0:T(1,128)}, u32[]{:S(2)}) copy-start(f32[4,9,1,256]{3,2,1,0:T(1,128)} %param.22) | copy-start | bytes 110596
  35.8 79.1 %copy-start.44 = (f32[4,8,32,128]{3,1,2,0:T(8,128)}, f32[4,8,32,128]{3,1,2,0:T(8,128)S(1)}, u32[]{:S(2)}) copy-start(f32[4,8,32,128]{3,1,2,0:T(8,128)S(1)} %copy.249) | copy-start | bytes 1572868
  110.2 2.0 copy-start.1
  112.2 2.0 copy-start.8
  114.9 192.2 %all-gather.12.cloned.1.call-start = ((), (), s32[]{:S(2)}) async-start(), calls=%async_computation.12 | async-start | bytes 5242880 | tf_op jit(solution)/shard_map/all_gather | solution.py:1425
  116.3 2.2 copy-start.2
  118.5 2.2 copy-start.9
  120.7 4.2 copy-start.22
  153.4 4.3 copy-start.10
  153.4 4.3 copy-start.27
  153.4 4.3 copy-start.48
  157.7 230.2 %all-gather.14.cloned.1.call-start = ((), (), s32[]{:S(2)}) async-start(), calls=%async_computation.13 | async-start | bytes 5242880 | tf_op jit(solution)/shard_map/all_gather | solution.py:1425
  158.6 3.2 copy-start.20
  195.6 2.1 copy-start.25
  198.7 1.6 copy-start.14
  200.3 2.2 copy-start.26
  205.6 41.5 %copy-start.45 = (f32[4,8,32,128]{3,1,2,0:T(8,128)S(1)}, f32[4,8,32,128]{3,1,2,0:T(8,128)}, u32[]{:S(2)}) copy-start(f32[4,8,32,128]{3,1,2,0:T(8,128)} %copy-done.44) | copy-start | bytes 1572868
  246.5 3.8 copy-start.28
  246.6 446.0 %reduce-scatter.6.cloned.1.call-start = ((), (), s32[]{:S(2)}) async-start(), calls=%async_computation.6 | async-start | bytes 5242880 | tf_op jit(solution)/shard_map/reduce_scatter | solution.py:1567
  250.3 1.2 copy-start.31
  251.6 1.2 copy-start.34
  268.2 38.7 %copy-start.19 = (bf16[2,2048,128]{2,1,0:T(8,128)(2,1)}, bf16[2,2048,128]{2,1,0:T(8,128)(2,1)S(1)}, u32[]{:S(2)}) copy-start(bf16[2,2048,128]{2,1,0:T(8,128)(2,1)S(1)} %get-tuple-element.93.o_ref) | copy-start | bytes 3145732
  307.1 4.3 copy-start.49
  341.7 1.3 copy-start.36
  384.5 3.4 copy-start.3
  387.9 19.2 %copy-start.62 = (bf16[1024,2048]{1,0:T(8,128)(2,1)S(1)}, bf16[1024,2048]{1,0:T(8,128)(2,1)}, u32[]{:S(2)}) copy-start(bf16[1024,2048]{1,0:T(8,128)(2,1)} %all-gather.12.cloned.1.call-done) | copy-start | bytes 12582916
  416.7 40.5 %copy-start.37 = (f32[256,2048]{1,0:T(8,128)S(1)}, f32[256,2048]{1,0:T(8,128)}, u32[]{:S(2)}) copy-start(f32[256,2048]{1,0:T(8,128)} %copy-done.36) | copy-start | bytes 6291460
  457.1 1.2 copy-start.41
  457.6 151.4 %copy-start.35 = (f32[256,2048]{1,0:T(8,128)}, f32[256,2048]{1,0:T(8,128)S(1)}, u32[]{:S(2)}) copy-start(f32[256,2048]{1,0:T(8,128)S(1)} %get-tuple-element.275) | copy-start | bytes 6291460
  457.6 2.8 copy-start.52
  460.4 2.7 copy-start.51
  460.6 2.5 copy-start.42
  463.0 1.3 copy-start.39
  503.8 3.3 copy-start.4
  518.3 202.7 %reduce-scatter.8.cloned.1.call-start = ((), (), s32[]{:S(2)}) async-start(), calls=%async_computation.7 | async-start | bytes 5242880 | tf_op jit(solution)/shard_map/reduce_scatter | solution.py:1567
  552.5 2.0 copy-start.6
  554.5 251.5 %reduce-scatter.10.cloned.1.call-start = ((), (), s32[]{:S(2)}) async-start(), calls=%async_computation.8 | async-start | bytes 2359296 | tf_op jit(solution)/shard_map/reduce_scatter | solution.py:1600
  567.1 40.4 %copy-start.38 = (f32[256,2048]{1,0:T(8,128)S(1)}, f32[256,2048]{1,0:T(8,128)}, u32[]{:S(2)}) copy-start(f32[256,2048]{1,0:T(8,128)} %copy-done.36) | copy-start | bytes 6291460
  608.3 1.6 copy-start.40
  608.3 1.9 copy-start.43
  613.0 29.0 %copy-start.63 = (bf16[512,2048]{1,0:T(8,128)(2,1)S(1)}, bf16[512,2048]{1,0:T(8,128)(2,1)}, u32[]{:S(2)}) copy-start(bf16[512,2048]{1,0:T(8,128)(2,1)} %all-gather.8.cloned.1.call-done) | copy-start | bytes 6291460
  639.9 2.1 copy-start.5
  644.4 1.2 copy-start.50
  692.6 199.6 %reduce-scatter.12.cloned.1.call-start = ((), (), s32[]{:S(2)}) async-start(), calls=%async_computation.9 | async-start | bytes 2359296 | tf_op jit(solution)/shard_map/reduce_scatter | solution.py:1600
  693.8 1.3 copy-start.32
  721.0 1.2 copy-start.21
  768.6 205.2 %reduce-scatter.14.cloned.1.call-start = ((), (), s32[]{:S(2)}) async-start(), calls=%async_computation.10 | async-start | bytes 4718592 | tf_op jit(solution)/shard_map/reduce_scatter | solution.py:1600
  772.8 2.4 copy-start.17
  804.7 1.3 copy-start.11
  806.0 1.6 copy-start.46
  841.6 1.3 copy-start.12
  876.9 5.3 copy-start.47
  892.2 2.6 copy-start.7
  924.1 1.3 copy-start.13
  925.4 29.1 %copy-start.60 = (f32[1,32,64]{2,1,0:T(8,128)S(1)}, f32[1,32,64]{2,1,0:T(8,128)}, u32[]{:S(2)}) copy-start(f32[1,32,64]{2,1,0:T(8,128)} %concatenate.43) | copy-start | bytes 24580
  925.4 29.1 %copy-start.59 = (f32[1,32,64]{2,1,0:T(8,128)S(1)}, f32[1,32,64]{2,1,0:T(8,128)}, u32[]{:S(2)}) copy-start(f32[1,32,64]{2,1,0:T(8,128)} %concatenate.45) | copy-start | bytes 24580
  925.4 29.1 %copy-start.56 = (f32[1,32,64]{2,1,0:T(8,128)S(1)}, f32[1,32,64]{2,1,0:T(8,128)}, u32[]{:S(2)}) copy-start(f32[1,32,64]{2,1,0:T(8,128)} %concatenate.47) | copy-start | bytes 24580
  925.4 29.1 %copy-start.57 = (f32[1,32,64]{2,1,0:T(8,128)S(1)}, f32[1,32,64]{2,1,0:T(8,128)}, u32[]{:S(2)}) copy-start(f32[1,32,64]{2,1,0:T(8,128)} %concatenate.48) | copy-start | bytes 24580
  925.4 29.2 %copy-start.58 = (f32[1,32,64]{2,1,0:T(8,128)S(1)}, f32[1,32,64]{2,1,0:T(8,128)}, u32[]{:S(2)}) copy-start(f32[1,32,64]{2,1,0:T(8,128)} %concatenate.49) | copy-start | bytes 24580
  925.4 29.4 %copy-start.54 = (f32[32,256]{1,0:T(8,128)S(1)}, f32[32,256]{1,0:T(8,128)}, u32[]{:S(2)}) copy-start(f32[32,256]{1,0:T(8,128)} %reshape.502) | copy-start | bytes 98308
  954.9 1.7 copy-start.53
  (9 other events, 9.2 us)
Sparse Core Ops, SparseCore 0:
  10.2 50.5 all-gather.7
  115.0 61.9 all-gather.9
  178.6 124.6 all-gather.11
  304.7 80.7 all-gather.13
  518.4 79.0 reduce-scatter.5
  600.4 94.1 reduce-scatter.7
  698.6 98.2 reduce-scatter.9
  800.5 80.8 reduce-scatter.11
  885.0 88.7 reduce-scatter.13

commit v5 on v4

--- a/solution.py
+++ b/solution.py
@@ -1204,76 +1204,68 @@
     )(x, w, bias)
 
 
-def halved_product(x, g, bit, groups, lines, tile=512, split=True):
+def line_product(x, g, groups, lines, tile=512, shelf=None):
     n, d = g.shape
     block = x.shape[1] // groups
-    r = block // lines // 2
+    r = block // lines
     tile = min(tile, d)
-
-    def kernel(bit_ref, x_ref, g_ref, *refs):
-        turned = refs[-1]
+    held, first, count = shelf or (None, 0, groups)
+
+    def kernel(x_ref, g_ref, *refs):
+        o_ref, turned = refs[-2:]
 
         @pl.when(pl.program_id(1) == 0)
         def _():
             turned[...] = x_ref[...].T
 
         y = nn(turned[...], g_ref[...]).astype(BF16)
-        if not split:
-            refs[0][:, 0] = y.reshape(lines, 2 * r, tile)
-            return
-        a_ref, k_ref = refs[:2]
-        y = y.reshape(lines, 2, r, tile)
-        first = bit_ref[0] == 0
-        a_ref[:, 0] = jnp.where(first, y[:, 1], y[:, 0])
-        k_ref[:, 0] = jnp.where(first, y[:, 0], y[:, 1])
-
-    size = r if split else 2 * r
-    half = pl.BlockSpec((lines, 1, size, tile), lambda i, j, b: (0, i, 0, j))
-    shape = jax.ShapeDtypeStruct((lines, groups, size, d), BF16)
-    outs = 2 if split else 1
+        o_ref[:, 0] = y.reshape(lines, r, tile)
+
+    extra = [] if held is None else [held]
     return pl.pallas_call(
         kernel,
-        grid_spec=pltpu.PrefetchScalarGridSpec(
-            num_scalar_prefetch=1,
-            grid=(groups, d // tile),
-            in_specs=[
-                pl.BlockSpec((n, block), lambda i, j, b: (0, i)),
-                pl.BlockSpec((n, tile), lambda i, j, b: (0, j)),
-            ],
-            out_specs=[half] * outs,
-            scratch_shapes=[pltpu.VMEM((block, n), BF16)],
-        ),
-        out_shape=[shape] * outs,
+        grid=(groups, d // tile),
+        in_specs=[
+            pl.BlockSpec((n, block), lambda i, j: (0, i)),
+            pl.BlockSpec((n, tile), lambda i, j: (0, j)),
+        ]
+        + [ANY] * len(extra),
+        out_specs=pl.BlockSpec((lines, 1, r, tile), lambda i, j: (0, first + i, 0, j)),
+        out_shape=jax.ShapeDtypeStruct((lines, count, r, d), BF16),
+        scratch_shapes=[pltpu.VMEM((block, n), BF16)],
+        input_output_aliases={2: 0} if extra else {},
         compiler_params=pltpu.CompilerParams(vmem_limit_bytes=48 * 2**20),
         cost_estimate=pl.CostEstimate(
             flops=2 * n * d * x.shape[1],
             bytes_accessed=2 * (n * d + n * x.shape[1] + d * x.shape[1]),
             transcendentals=0,
         ),
-    )(bit, x, g)
-
-
-def front(hist, mix, gain, shift, tokens=16, wide=128):
+    )(x, g, *extra)
+
+
+def front(hist, mix, gain, shift, tokens=32, wide=128):
     h, n, d = hist.shape
     rest = gain.shape[0]
 
     def kernel(h_ref, m_ref, g_ref, b_ref, s_ref, *n_refs):
-        m = m_ref[...]
-        across = [jnp.broadcast_to(m[:, i : i + 1], (tokens, wide)) for i in range(4 * h)]
-        for at in range(0, d, wide):
-            cut = slice(at, at + wide)
-            rows = [h_ref[j, :, cut].astype(F32) for j in range(h)]
-            for s in range(4):
-                acc = across[s * h] * rows[0]
-                for j in range(1, h):
-                    acc += across[s * h + j] * rows[j]
-                s_ref[s, :, cut] = acc
-        for s in range(rest):
-            x = s_ref[s]
-            centre = x - jnp.mean(x, axis=-1, keepdims=True)
-            spread = jnp.mean(centre * centre, axis=-1, keepdims=True)
-            y = centre * lax.rsqrt(spread + EPS_NORM) * g_ref[s : s + 1] + b_ref[s : s + 1]
-            n_refs[s][...] = y.astype(BF16)
+        for start in range(0, tokens, 16):
+            t = slice(start, start + 16)
+            m = m_ref[t]
+            across = [jnp.broadcast_to(m[:, i : i + 1], (16, wide)) for i in range(4 * h)]
+            for at in range(0, d, wide):
+                cut = slice(at, at + wide)
+                rows = [h_ref[j, t, cut].astype(F32) for j in range(h)]
+                for s in range(4):
+                    acc = across[s * h] * rows[0]
+                    for j in range(1, h):
+                        acc += across[s * h + j] * rows[j]
+                    s_ref[s, t, cut] = acc
+            for s in range(rest):
+                x = s_ref[s, t]
+                centre = x - jnp.mean(x, axis=-1, keepdims=True)
+                spread = jnp.mean(centre * centre, axis=-1, keepdims=True)
+                y = centre * lax.rsqrt(spread + EPS_NORM) * g_ref[s : s + 1] + b_ref[s : s + 1]
+                n_refs[s][t] = y.astype(BF16)
 
     return pl.pallas_call(
         kernel,
@@ -1297,7 +1289,7 @@
     )(hist, mix, gain, shift)
 
 
-def last(hist, mix, streams, gain, grads, grad_hidden, tokens=16, wide=256):
+def last(hist, mix, streams, gain, grads, grad_hidden, tokens=32, wide=256):
     h, n, d = hist.shape
     rest = gain.shape[0]
 
@@ -1307,46 +1299,48 @@
             gg_ref[...] = jnp.zeros_like(gg_ref)
             gb_ref[...] = jnp.zeros_like(gb_ref)
 
-        for s, d_ref in enumerate((d0, d1, d2)):
-            x = s_ref[s]
-            centre = x - jnp.mean(x, axis=-1, keepdims=True)
-            inverse = lax.rsqrt(jnp.mean(centre * centre, axis=-1, keepdims=True) + EPS_NORM)
-            unit = centre * inverse
-            dn = d_ref[...]
-            gg_ref[s : s + 1] += jnp.sum(dn * unit, axis=0, keepdims=True)
-            gb_ref[s : s + 1] += jnp.sum(dn, axis=0, keepdims=True)
-            du = dn * g_ref[s : s + 1]
-            ds[s] = inverse * (
-                du
-                - jnp.mean(du, axis=-1, keepdims=True)
-                - unit * jnp.mean(du * unit, axis=-1, keepdims=True)
-            )
-        ds[rest] = r_ref[...]
-        m = m_ref[...]
-        across = [jnp.broadcast_to(m[:, i : i + 1], (tokens, 128)) for i in range(4 * h)]
-        sums = [[jnp.zeros((tokens, 128), F32) for _ in range(h)] for _ in range(4)]
-        for at in range(0, d, wide):
-            cuts = [slice(b, b + 128) for b in range(at, at + wide, 128)]
-            parts = [[ds[s, :, cut] for cut in cuts] for s in range(4)]
-            for j in range(h):
-                for i, cut in enumerate(cuts):
-                    acc = across[j] * parts[0][i]
-                    for s in range(1, 4):
-                        acc += across[s * h + j] * parts[s][i]
-                    gh_ref[j, :, cut] = acc
-                rows = [h_ref[j, :, cut].astype(F32) for cut in cuts]
-                for s in range(4):
-                    prod = rows[0] * parts[s][0]
-                    for i in range(1, len(cuts)):
-                        prod += rows[i] * parts[s][i]
-                    sums[s][j] += prod
-        lane = lax.broadcasted_iota(jnp.int32, (tokens, 128), 1)
-        total = jnp.zeros((tokens, 128), F32)
-        for s in range(4):
-            for j in range(h):
-                value = jnp.sum(sums[s][j], axis=-1, keepdims=True)
-                total = jnp.where(lane == s * h + j, value, total)
-        gm_ref[...] = total
+        for start in range(0, tokens, 16):
+            t = slice(start, start + 16)
+            for s, d_ref in enumerate((d0, d1, d2)):
+                x = s_ref[s, t]
+                centre = x - jnp.mean(x, axis=-1, keepdims=True)
+                inverse = lax.rsqrt(jnp.mean(centre * centre, axis=-1, keepdims=True) + EPS_NORM)
+                unit = centre * inverse
+                dn = d_ref[t]
+                gg_ref[s : s + 1] += jnp.sum(dn * unit, axis=0, keepdims=True)
+                gb_ref[s : s + 1] += jnp.sum(dn, axis=0, keepdims=True)
+                du = dn * g_ref[s : s + 1]
+                ds[s] = inverse * (
+                    du
+                    - jnp.mean(du, axis=-1, keepdims=True)
+                    - unit * jnp.mean(du * unit, axis=-1, keepdims=True)
+                )
+            ds[rest] = r_ref[t]
+            m = m_ref[t]
+            across = [jnp.broadcast_to(m[:, i : i + 1], (16, 128)) for i in range(4 * h)]
+            sums = [[jnp.zeros((16, 128), F32) for _ in range(h)] for _ in range(4)]
+            for at in range(0, d, wide):
+                cuts = [slice(b, b + 128) for b in range(at, at + wide, 128)]
+                parts = [[ds[s, :, cut] for cut in cuts] for s in range(4)]
+                for j in range(h):
+                    for i, cut in enumerate(cuts):
+                        acc = across[j] * parts[0][i]
+                        for s in range(1, 4):
+                            acc += across[s * h + j] * parts[s][i]
+                        gh_ref[j, t, cut] = acc
+                    rows = [h_ref[j, t, cut].astype(F32) for cut in cuts]
+                    for s in range(4):
+                        prod = rows[0] * parts[s][0]
+                        for i in range(1, len(cuts)):
+                            prod += rows[i] * parts[s][i]
+                        sums[s][j] += prod
+            lane = lax.broadcasted_iota(jnp.int32, (16, 128), 1)
+            total = jnp.zeros((16, 128), F32)
+            for s in range(4):
+                for j in range(h):
+                    value = jnp.sum(sums[s][j], axis=-1, keepdims=True)
+                    total = jnp.where(lane == s * h + j, value, total)
+            gm_ref[t] = total
 
     row = pl.BlockSpec((tokens, d), lambda i: (i, 0))
     lines = pl.BlockSpec((rest, d), lambda i: (0, 0))
@@ -1356,7 +1350,7 @@
         in_specs=[
             pl.BlockSpec((h, tokens, d), lambda i: (0, i, 0)),
             pl.BlockSpec((tokens, 128), lambda i: (i, 0)),
-            pl.BlockSpec((4, tokens, d), lambda i: (0, i, 0)),
+            pl.BlockSpec((rest, tokens, d), lambda i: (0, i, 0)),
             lines,
             row,
             row,
@@ -1375,7 +1369,7 @@
             jax.ShapeDtypeStruct((rest, d), F32),
             jax.ShapeDtypeStruct((rest, d), F32),
         ],
-        scratch_shapes=[pltpu.VMEM((4, tokens, d), F32)],
+        scratch_shapes=[pltpu.VMEM((4, 16, d), F32)],
         compiler_params=pltpu.CompilerParams(vmem_limit_bytes=60 * 2**20),
         cost_estimate=pl.CostEstimate(
             flops=4 * 4 * h * n * d, bytes_accessed=n * d * (6 * h + 32), transcendentals=0
@@ -1561,8 +1555,6 @@
     branch_g = gather_plane_tokens(grad_branch)
     grad_down_shift = jnp.sum(grad_branch.astype(F32), axis=0)
 
-    bit = lo.reshape(1)
-
     def line_scatter(x):
         y = lax.psum_scatter(
             x.reshape(-1, x.shape[-1]),
@@ -1579,7 +1571,7 @@
     grad_active = dot("nd,fd->nf", branch_g, wdown)
     grad_upward = (grad_active * slope.astype(F32)).astype(BF16)
     grad_up_shift = jnp.sum(grad_upward.astype(F32), axis=0)
-    (up_part,) = halved_product(mlp_g, grad_upward, bit, fn, count, split=False)
+    up_part = line_product(mlp_g, grad_upward, fn, count)
     up_part, grad_upward = lax.optimization_barrier((up_part, grad_upward))
     grad_up = line_scatter(up_part.reshape(count, -1, pcol))
     mlp_part = dot("nf,df->nd", grad_upward, wup).astype(BF16)
@@ -1600,13 +1592,11 @@
         return lax.psum_scatter(x, "ctx", scatter_dimension=0, tiled=True)
 
     grad_out = ctx_scatter(out_part)
+
     gq, gk, gv = attend_back(q_u, k_u, v_u, first_key, lse_u, att_u, whole_units(g_u), tables)
 
     def back_part(p, s):
         return dot("nc,dc->nd", p, wqkv[s]).astype(BF16).reshape(fn, nloc, width)
-
-    def qkv_part(p, i):
-        return halved_product(normed_g[i], p, bit, fn, cn, split=False)[0]
 
     grad_up = grad_up.reshape(fn, 2, rows, pcol)
     if ff // dn % 128 == 0:
@@ -1616,14 +1606,16 @@
         grad_up = grad_up.reshape(fn, 2, rows, count, -1).transpose(2, 0, 3, 1, 4)
         grad_up = grad_up.reshape(rows, ff)
     gp0 = columns(gp0)
-    q_part, gk = lax.optimization_barrier((qkv_part(gp0, 0), gk))
+    q_part = line_product(normed_g[0], gp0, fn, cn)
+    q_part, gk = lax.optimization_barrier((q_part, gk))
     grad_q = ctx_scatter(q_part.reshape(-1, wcol)).reshape(fn, rows, wcol)
     gp1, gn0 = comm(8, from_units(gk), scatter_fsdp(back_part(gp0, 0)))
     gp1, grad_out = lax.optimization_barrier((gp1, grad_out))
     gp1 = columns(gp1)
     gp2, gn1 = comm(8, from_units(gv), scatter_fsdp(back_part(gp1, 1)))
     gp2 = columns(gp2)
-    kv_part = jnp.stack([qkv_part(gp1, 1), qkv_part(gp2, 2)], axis=1)
+    kv_part = line_product(normed_g[1], gp1, fn, cn, shelf=(None, 0, 2 * fn))
+    kv_part = line_product(normed_g[2], gp2, fn, cn, shelf=(kv_part, fn, 2 * fn))
     kv_part, gp2 = lax.optimization_barrier((kv_part, gp2))
     grad_kv = ctx_scatter(kv_part.reshape(-1, wcol)).reshape(2, fn, rows, wcol)
     grad_q, gn2 = comm(
@@ -1671,23 +1663,21 @@
         axis=1,
     )
     flat = jnp.pad(flat, ((0, 0), (0, -flat.shape[1] % 1024)))
-    small, grad_k, grad_v = comm(
-        2,
-        scatter_small(flat.reshape(fn, cn, -1, 128)),
-        exchange_fsdp(grad_kv[0]),
-        exchange_fsdp(grad_kv[1]),
-    )
-    grad_qkv = jnp.stack([grad_q, grad_k, grad_v])
-    grad_qkv = grad_qkv.transpose(2, 0, 1, 3).reshape(rows, 3, width).astype(F32)
+    (small,) = comm(2, scatter_small(flat.reshape(fn, cn, -1, 128)))
     small = small.reshape(-1)
     out_small, at = [], 0
     order = [norm_gain, norm_bias, qkv_bias, out_bias, down_bias, root_gain, up_bias, mix_in_weight]
     for a in order:
         out_small.append(small[at : at + a.size].reshape(a.shape))
         at += a.size
-    (g_gain, g_shift, g_qkv_b, g_out_b, g_down_b, g_root, g_up_b, g_mix_in) = out_small
     mix_sums = small[at : at + same.size]
     cut = grad_mix_out.size
+    out_small += [mix_sums[:cut].reshape(grad_mix_out.shape), mix_sums[cut:]]
+    out_small, grad_kv = lax.optimization_barrier((out_small, grad_kv))
+    (g_gain, g_shift, g_qkv_b, g_out_b, g_down_b, g_root, g_up_b, g_mix_in) = out_small[:-2]
+    grad_k, grad_v = comm(15, exchange_fsdp(grad_kv[0]), exchange_fsdp(grad_kv[1]))
+    grad_qkv = jnp.stack([grad_q, grad_k, grad_v])
+    grad_qkv = grad_qkv.transpose(2, 0, 1, 3).reshape(rows, 3, width).astype(F32)
     return (
         block_out,
         next_mix,
@@ -1705,8 +1695,8 @@
         g_down_b,
         g_root,
         g_mix_in,
-        mix_sums[:cut].reshape(grad_mix_out.shape),
-        mix_sums[cut:],
+        out_small[-2],
+        out_small[-1],
     )
 
 

time: 1020 us -> 1010 us (level)
  waiting for transfers between devices: 17.3 us -> 0.85 us
    pallas_call x18 -> x19, Pallas kernels: 620 us -> 638 us  [comm(): pl.pallas_call(kernel, out_shape=[t[2] for t in tasks], in_specs=[t[3] fo...]
    reduce_scatter x3, waiting for transfers between devices: 16.4 us -> 0.01 us  [ctx_scatter(): return lax.psum_scatter(x, 'ctx', scatter_dimension=0, tiled=True)]
    unnamed x145 -> x149, local copies, waits for them, and re-layouts: 52.8 us -> 54.1 us
  transfers between devices with their start and end apart: 9 -> 9, of which waited for: 1 -> 0; matrix products, arithmetic and copies ran while one was open for 12% -> 12% of each run, Pallas kernels for 65% -> 67%
where the time goes in v5:
time: 1010 us; the launch traced here: 1000 us
  Pallas kernels  779 us (77%)
  local copies, waits for them, and re-layouts  99.9 us (10%)
  matrix products  85.5 us (8%)
  other arithmetic  18.7 us (2%)
  between operations  15.7 us (2%)
    pallas_call x19, Pallas kernels, comm(): pl.pallas_call(kernel, out_shape=[t[2] for t in tasks], in_specs=[t[3] fo...  638 us
    dot_general x10, matrix products, dot(): return jnp.einsum(pattern, left, right, preferred_element_type=F32)  72.7 us
    unnamed x149, local copies, waits for them, and re-layouts  54.1 us
    pallas_call x4, Pallas kernels, line_product(): pl.pallas_call(kernel, grid=(groups, d // tile), in_specs=[pl.BlockSpec((...  32.9 us
    pallas_call x1, Pallas kernels, attend_back(): pl.pallas_call(kernel, grid=(u, t // block), in_specs=[pl.BlockSpec(spec,...  25 us
    pallas_call x1, Pallas kernels, last(): pl.pallas_call(kernel, grid=(n // tokens,), in_specs=[pl.BlockSpec((h, to...  22.8 us
  transfers between devices with their start and end apart: 9, of which 0 were waited for; matrix products, arithmetic and copies ran while one was open for 12% of the time, Pallas kernels for 67%

profile of v5, /device:TPU:1, one launch (start us, length us, event | category | flops | bytes accessed | tf_op | source)
XLA Modules:
  0.0 1000.4 jit_solution(9927488608417464936)
XLA Ops:
  13.8 21.7 %shard_map.340 = (f32[4,8,32,128]{3,2,1,0:T(8,128)S(1)}, bf16[4,3,64,512]{3,2,1,0:T(8,128)(2,1)S(1)}) custom-call(f32[32,128]{1,0:T(8,128)S(1)} %pad_bitcast_fusion.1.refs_0_, bf16[4,3,64,512]{3,2,1,0:T(8,128)(2,1)S(1)} %bitcast.227), custom_call_target="tpu_custom_call" | custom-call | bytes 15000000 | tf_op jit(solution)/shard_map/pallas_call | solution.py:147
  38.4 13.8 %shard_map.341 = (f32[4,256,2048]{2,1,0:T(8,128)}, bf16[256,2048]{1,0:T(8,128)(2,1)}, bf16[256,2048]{1,0:T(8,128)(2,1)}, bf16[256,2048]{1,0:T(8,128)(2,1)}) custom-call(bf16[9,256,2048]{2,1,0:T(8,128)(2,1)} %bitcast.254, f32[256,128]{1,0:T(8,128)} %pad.25.m_ref, f32[3,2048]{1,0:T(4,128)} %slice.128.g_ref, f32[3,2048]{1,0:T(4,128)} %slice.131.b_ref), custom_call_target="tpu_custom_call" | custom-call | flops 37748736 | bytes 20971520 | tf_op jit(solution)/shard_map/pallas_call | solution.py:1270
  53.5 56.7 %shard_map.342 = (bf16[8,4,2,64,512]{4,3,2,1,0:T(8,128)(2,1)S(1)}, bf16[4,256,2048]{2,1,0:T(8,128)(2,1)S(1)}) custom-call(bf16[4,2,64,512]{3,2,1,0:T(8,128)(2,1)S(1)} %slice.133.refs_0_, bf16[256,2048]{1,0:T(8,128)(2,1)S(1)} %copy-done.22), custom_call_target="tpu_custom_call" | custom-call | bytes 15000000 | tf_op jit(solution)/shard_map/pallas_call | solution.py:147
  110.2 1.9 copy-done.2
  112.2 2.0 copy-done.12
  116.3 2.2 copy-done.3
  118.5 2.2 copy-done.13
  120.7 4.2 shard_map.343
  124.9 28.5 %shard_map.344 = (bf16[2,8,256,128]{3,2,1,0:T(8,128)(2,1)S(1)}, bf16[4,256,2048]{2,1,0:T(8,128)(2,1)S(1)}) custom-call(bf16[8,2,256,128]{3,2,1,0:T(8,128)(2,1)S(1)} %bitcast.226, bf16[256,2048]{1,0:T(8,128)(2,1)S(1)} %copy-done.26), custom_call_target="tpu_custom_call" | custom-call | bytes 15000000 | tf_op jit(solution)/shard_map/pallas_call | solution.py:147
  153.4 4.2 shard_map.345
  159.9 1.8 reshape.450.refs_1_
  161.7 33.9 %shard_map.346 = (bf16[2,8,256,128]{3,2,1,0:T(8,128)(2,1)S(1)}, bf16[4,256,2048]{2,1,0:T(8,128)(2,1)S(1)}) custom-call(bf16[8,2,256,128]{3,2,1,0:T(8,128)(2,1)S(1)} %bitcast.225, bf16[256,2048]{1,0:T(8,128)(2,1)S(1)} %copy-done.24), custom_call_target="tpu_custom_call" | custom-call | bytes 15000000 | tf_op jit(solution)/shard_map/pallas_call | solution.py:147
  195.7 2.1 copy-done.8
  198.8 2.2 copy-done.9
  202.6 3.1 shard_map.347
  205.7 39.8 %shard_map.348 = (bf16[2,8,256,128]{3,2,1,0:T(8,128)(2,1)S(1)}, bf16[4,2,64,1024]{3,2,1,0:T(8,128)(2,1)}) custom-call(bf16[8,2,256,128]{3,2,1,0:T(8,128)(2,1)S(1)} %bitcast.237, bf16[4,2,64,1024]{3,2,1,0:T(8,128)(2,1)S(1)} %reshape.450.refs_1_), custom_call_target="tpu_custom_call" | custom-call | bytes 15000000 | tf_op jit(solution)/shard_map/pallas_call | solution.py:147
  248.5 1.8 reshape.462
  252.8 15.3 %shard_map.349 = (bf16[2,2048,128]{2,1,0:T(8,128)(2,1)S(1)}, f32[2,1,2048]{2,1,0:T(1,128)S(1)}) custom-call(bf16[2,2048,128]{2,1,0:T(8,128)(2,1)S(1)} %bitcast.248, bf16[2,2048,128]{2,1,0:T(8,128)(2,1)S(1)} %bitcast.250, bf16[2,2048,128]{2,1,0:T(8,128)(2,1)S(1)} %bitcast.253, s32[2,1,2048]{2,1,0:T(1,128)S(1)} %broadcast_in_dim.28.s_ref), custom_call_target="tpu_custom_call" | custom-call | flops 2147483648 | bytes 8388608 | tf_op jit(solution)/shard_map/pallas_call | solution.py:985
  268.2 37.8 %shard_map.350 = bf16[8,2,256,128]{3,2,1,0:T(8,128)(2,1)S(1)} custom-call(bf16[2,8,256,128]{3,2,1,0:T(8,128)(2,1)S(1)} %bitcast.233), custom_call_target="tpu_custom_call" | custom-call | bytes 15000000 | tf_op jit(solution)/shard_map/pallas_call | solution.py:147
  307.1 4.3 convolution_convert_fusion.6
  311.4 28.2 %shard_map.351 = f32[256,2048]{1,0:T(8,128)S(1)} custom-call(bf16[4,256,2048]{2,1,0:T(8,128)(2,1)S(1)} %bitcast.214), custom_call_target="tpu_custom_call" | custom-call | bytes 15000000 | tf_op jit(solution)/shard_map/pallas_call | solution.py:147
  339.6 2.1 fusion.35
  343.0 41.5 %shard_map.352 = bf16[4,2,256,2048]{3,2,1,0:T(8,128)(2,1)S(1)} custom-call(bf16[256,2048]{1,0:T(8,128)(2,1)S(1)} %add_convert_fusion.refs_0_), custom_call_target="tpu_custom_call" | custom-call | bytes 15000000 | tf_op jit(solution)/shard_map/pallas_call | solution.py:147
  384.5 3.4 copy-done.5
  387.9 19.2 %shard_map.353 = (bf16[2048,1024]{1,0:T(8,128)(2,1)S(1)}, bf16[2048,1024]{1,0:T(8,128)(2,1)}, bf16[2048,1024]{1,0:T(8,128)(2,1)}) custom-call(bf16[2048,2048]{1,0:T(8,128)(2,1)} %bitcast.205, bf16[4,4,128,1024]{3,2,1,0:T(8,128)(2,1)} %bitcast.289, f32[1,1024]{1,0:T(1,128)S(1)} %bitcast.247), custom_call_target="tpu_custom_call" | custom-call | flops 8589934592 | bytes 60000000 | tf_op jit(solution)/shard_map/pallas_call | solution.py:1185
  407.1 9.6 convolution_convert_fusion.1
  416.6 40.4 %shard_map.354 = f32[256,2048]{1,0:T(8,128)S(1)} custom-call(bf16[4,2,256,2048]{3,2,1,0:T(8,128)(2,1)S(1)} %bitcast.204), custom_call_target="tpu_custom_call" | custom-call | bytes 15000000 | tf_op jit(solution)/shard_map/pallas_call | solution.py:147
  458.3 2.0 fusion.13
  460.6 2.4 multiply_reduce_fusion
  464.3 39.4 %shard_map.355 = bf16[4,2,256,2048]{3,2,1,0:T(8,128)(2,1)S(1)} custom-call(bf16[256,2048]{1,0:T(8,128)(2,1)S(1)} %get-tuple-element.288.refs_0_), custom_call_target="tpu_custom_call" | custom-call | bytes 15000000 | tf_op jit(solution)/shard_map/pallas_call | solution.py:147
  503.8 3.2 copy-done.6
  507.0 11.2 %convolution_convert_fusion.5 = bf16[1024,2048]{1,0:T(8,128)(2,1)} fusion(bf16[2048,1024]{1,0:T(8,128)(2,1)S(1)} %get-tuple-element.108, bf16[2048,2048]{1,0:T(8,128)(2,1)S(1)} %bitcast.207), kind=kOutput, calls=%fused_computation.8 | convolution fusion | flops 8592031744 | bytes 16777216 | tf_op jit(solution)/shard_map/nf,nd->fd/dot_general | solution.py:69
  518.3 16.1 %convert_reduce_fusion = (f32[1024]{0:T(1024)}, bf16[2048,1024]{1,0:T(8,128)(2,1)}) fusion(bf16[2048,1024]{1,0:T(8,128)(2,1)} %get-tuple-element.112, bf16[2048,2048]{1,0:T(8,128)(2,1)} %bitcast.208, bf16[1024,2048]{1,0:T(8,128)(2,1)} %all-gather.12.cloned.1.call-done), kind=kOutput, calls=%fused_computation.1 | convolution fusion | flops 8600419328 | bytes 20975616 | tf_op jit(solution)/shard_map/nd,fd->nf/dot_general | solution.py:69
  534.4 18.1 %shard_map.356 = bf16[4,4,128,1024]{3,2,1,0:T(8,128)(2,1)S(1)} custom-call(bf16[2048,2048]{1,0:T(8,128)(2,1)} %bitcast.206, bf16[2048,1024]{1,0:T(8,128)(2,1)} %get-tuple-element.113.g_ref), custom_call_target="tpu_custom_call" | custom-call | flops 8589934592 | bytes 16777216 | tf_op jit(solution)/shard_map/pallas_call | solution.py:1225
  552.5 2.0 copy-done.10
  554.5 12.5 %convolution_convert_fusion = bf16[2048,2048]{1,0:T(8,128)(2,1)S(1)} fusion(bf16[2048,1024]{1,0:T(8,128)(2,1)} %get-tuple-element.113.g_ref, bf16[2048,1024]{1,0:T(8,128)(2,1)} %get-tuple-element.114), kind=kOutput, calls=%fused_computation.3 | convolution fusion | flops 8594128896 | bytes 16777216 | tf_op jit(solution)/shard_map/nf,df->nd/dot_general | solution.py:69
  567.1 40.3 %shard_map.357 = f32[256,2048]{1,0:T(8,128)S(1)} custom-call(bf16[4,2,256,2048]{3,2,1,0:T(8,128)(2,1)S(1)} %bitcast.203), custom_call_target="tpu_custom_call" | custom-call | bytes 15000000 | tf_op jit(solution)/shard_map/pallas_call | solution.py:147
  610.0 2.8 convert_reduce_fusion.2
  612.8 27.0 %shard_map.358 = bf16[4,256,2048]{2,1,0:T(8,128)(2,1)S(1)} custom-call(bf16[256,2048]{1,0:T(8,128)(2,1)S(1)} %get-tuple-element.290.refs_0_), custom_call_target="tpu_custom_call" | custom-call | bytes 15000000 | tf_op jit(solution)/shard_map/pallas_call | solution.py:147
  639.9 2.1 copy-done.7
  641.9 2.4 convolution_convert_fusion.8
  645.6 6.0 convolution_convert_fusion.7
  651.5 40.0 %shard_map.359 = bf16[2,8,256,128]{3,2,1,0:T(8,128)(2,1)S(1)} custom-call(bf16[8,2,256,128]{3,2,1,0:T(8,128)(2,1)S(1)} %bitcast.222), custom_call_target="tpu_custom_call" | custom-call | bytes 15000000 | tf_op jit(solution)/shard_map/pallas_call | solution.py:147
  693.8 25.0 %shard_map.360 = (bf16[2,2048,128]{2,1,0:T(8,128)(2,1)S(1)}, bf16[2,2048,128]{2,1,0:T(8,128)(2,1)S(1)}, bf16[2,2048,128]{2,1,0:T(8,128)(2,1)S(1)}) custom-call(bf16[2,2048,128]{2,1,0:T(8,128)(2,1)S(1)} %bitcast.249, bf16[2,2048,128]{2,1,0:T(8,128)(2,1)S(1)} %bitcast.251, bf16[2,2048,128]{2,1,0:T(8,128)(2,1)} %bitcast.252, ...), custom_call_target="tpu_custom_call" | custom-call | flops 5368709120 | bytes 20971520 | tf_op jit(solution)/shard_map/pallas_call | solution.py:1072
  721.1 38.4 %shard_map.361 = (bf16[8,2,256,128]{3,2,1,0:T(8,128)(2,1)S(1)}, bf16[64,8192]{1,0:T(8,128)(2,1)S(1)}) custom-call(bf16[2,8,256,128]{3,2,1,0:T(8,128)(2,1)S(1)} %bitcast.236, bf16[4,2,64,1024]{3,2,1,0:T(8,128)(2,1)S(1)} %bitcast.234), custom_call_target="tpu_custom_call" | custom-call | bytes 15000000 | tf_op jit(solution)/shard_map/pallas_call | solution.py:147
  761.4 4.9 shard_map.362
  767.7 2.5 slice_bitcast_fusion
  771.9 2.4 convolution_convert_fusion.4
  774.3 30.3 %shard_map.363 = (bf16[8,2,256,128]{3,2,1,0:T(8,128)(2,1)S(1)}, f32[256,2048]{1,0:T(8,128)S(1)}) custom-call(bf16[2,8,256,128]{3,2,1,0:T(8,128)(2,1)S(1)} %bitcast.232, bf16[4,256,2048]{2,1,0:T(8,128)(2,1)S(1)} %bitcast.212), custom_call_target="tpu_custom_call" | custom-call | bytes 15000000 | tf_op jit(solution)/shard_map/pallas_call | solution.py:147
  807.5 2.4 convolution_convert_fusion.3
  809.9 31.0 %shard_map.364 = (bf16[8,2,256,128]{3,2,1,0:T(8,128)(2,1)S(1)}, f32[256,2048]{1,0:T(8,128)S(1)}) custom-call(bf16[2,8,256,128]{3,2,1,0:T(8,128)(2,1)S(1)} %bitcast.231, bf16[4,256,2048]{2,1,0:T(8,128)(2,1)S(1)} %bitcast.211), custom_call_target="tpu_custom_call" | custom-call | bytes 15000000 | tf_op jit(solution)/shard_map/pallas_call | solution.py:147
  843.3 4.9 shard_map.365.refs_0_
  848.2 5.2 shard_map.366
  853.3 2.1 copy-done.1
  856.3 3.1 copy.192
  862.8 6.1 fusion.2
  868.9 1.8 reshape.497
  878.2 2.7 convert_element_type.140
  885.0 6.0 convolution_convert_fusion.2
  890.9 2.3 copy-done.11
  894.2 28.4 %shard_map.367 = (bf16[4,64,512]{2,1,0:T(8,128)(2,1)S(1)}, f32[256,2048]{1,0:T(8,128)S(1)}) custom-call(bf16[4,64,512]{2,1,0:T(8,128)(2,1)S(1)} %bitcast.240, bf16[4,256,2048]{2,1,0:T(8,128)(2,1)S(1)} %bitcast.217), custom_call_target="tpu_custom_call" | custom-call | bytes 15000000 | tf_op jit(solution)/shard_map/pallas_call | solution.py:147
  924.0 22.8 %shard_map.368 = (f32[9,256,2048]{2,1,0:T(8,128)}, f32[256,128]{1,0:T(8,128)}, f32[3,2048]{1,0:T(4,128)}, f32[3,2048]{1,0:T(4,128)}) custom-call(bf16[9,256,2048]{2,1,0:T(8,128)(2,1)} %bitcast.255, f32[256,128]{1,0:T(8,128)} %pad.25.m_ref, f32[4,256,2048]{2,1,0:T(8,128)} %get-tuple-element.88.s_ref, f32[3,2048]{1,0:T(4,128)} %slice.128.g_ref, ...), custom_call_target="tpu_custom_call" | custom-call | flops 75497472 | bytes 45088768 | tf_op jit(solution)/shard_map/pallas_call | solution.py:1347
  949.2 26.6 %shard_map.369 = f32[48,128]{1,0:T(8,128)S(1)} custom-call(f32[4,8,48,128]{3,2,1,0:T(8,128)S(1)} %copy.242), custom_call_target="tpu_custom_call" | custom-call | bytes 15000000 | tf_op jit(solution)/shard_map/pallas_call | solution.py:147
  983.0 8.3 shard_map.370
  (276 shorter events, 76.3 us)
Async XLA Ops:
  7.2 453.2 %copy-start = (f32[40,40]{1,0:T(8,128)S(1)}, f32[40,40]{1,0:T(8,128)}, u32[]{:S(2)}) copy-start(f32[40,40]{1,0:T(8,128)} %param.36) | copy-start | bytes 19204
  7.2 107.7 %all-gather.8.cloned.1.call-start = ((), (), s32[]{:S(2)}) async-start(), calls=%async_computation.5 | async-start | bytes 2359296 | tf_op jit(solution)/shard_map/all_gather | solution.py:1434
  7.9 190.8 %all-gather.10.cloned.1.call-start = ((), (), s32[]{:S(2)}) async-start(), calls=%async_computation.11 | async-start | bytes 2359296 | tf_op jit(solution)/shard_map/all_gather | solution.py:1490
  8.0 29.5 %copy-start.63 = (f32[4,9,1,256]{3,2,1,0:T(1,128)S(1)}, f32[4,9,1,256]{3,2,1,0:T(1,128)}, u32[]{:S(2)}) copy-start(f32[4,9,1,256]{3,2,1,0:T(1,128)} %param.22) | copy-start | bytes 110596
  35.8 79.1 %copy-start.46 = (f32[4,8,32,128]{3,1,2,0:T(8,128)}, f32[4,8,32,128]{3,1,2,0:T(8,128)S(1)}, u32[]{:S(2)}) copy-start(f32[4,8,32,128]{3,1,2,0:T(8,128)S(1)} %copy.244) | copy-start | bytes 1572868
  110.2 2.0 copy-start.2
  112.2 2.0 copy-start.12
  114.9 192.2 %all-gather.12.cloned.1.call-start = ((), (), s32[]{:S(2)}) async-start(), calls=%async_computation.12 | async-start | bytes 5242880 | tf_op jit(solution)/shard_map/all_gather | solution.py:1419
  116.3 2.2 copy-start.3
  118.5 2.2 copy-start.13
  120.7 4.2 copy-start.26
  153.4 4.3 copy-start.4
  153.4 4.3 copy-start.29
  153.4 4.3 copy-start.50
  157.7 230.2 %all-gather.14.cloned.1.call-start = ((), (), s32[]{:S(2)}) async-start(), calls=%async_computation.13 | async-start | bytes 5242880 | tf_op jit(solution)/shard_map/all_gather | solution.py:1419
  158.5 3.2 copy-start.24
  195.7 2.1 copy-start.8
  198.8 2.2 copy-start.9
  201.0 1.6 copy-start.17
  205.7 41.4 %copy-start.47 = (f32[4,8,32,128]{3,1,2,0:T(8,128)S(1)}, f32[4,8,32,128]{3,1,2,0:T(8,128)}, u32[]{:S(2)}) copy-start(f32[4,8,32,128]{3,1,2,0:T(8,128)} %copy-done.46) | copy-start | bytes 1572868
  246.5 3.8 copy-start.30
  246.6 446.0 %reduce-scatter.6.cloned.1.call-start = ((), (), s32[]{:S(2)}) async-start(), calls=%async_computation.6 | async-start | bytes 5242880 | tf_op jit(solution)/shard_map/reduce_scatter | solution.py:1559
  251.6 1.2 copy-start.36
  268.2 38.7 %copy-start.23 = (bf16[2,2048,128]{2,1,0:T(8,128)(2,1)}, bf16[2,2048,128]{2,1,0:T(8,128)(2,1)S(1)}, u32[]{:S(2)}) copy-start(bf16[2,2048,128]{2,1,0:T(8,128)(2,1)S(1)} %get-tuple-element.103.o_ref) | copy-start | bytes 3145732
  307.0 4.3 copy-start.51
  341.7 1.3 copy-start.38
  384.5 3.4 copy-start.5
  387.9 19.2 %copy-start.64 = (bf16[1024,2048]{1,0:T(8,128)(2,1)S(1)}, bf16[1024,2048]{1,0:T(8,128)(2,1)}, u32[]{:S(2)}) copy-start(bf16[1024,2048]{1,0:T(8,128)(2,1)} %all-gather.12.cloned.1.call-done) | copy-start | bytes 12582916
  416.6 40.5 %copy-start.39 = (f32[256,2048]{1,0:T(8,128)S(1)}, f32[256,2048]{1,0:T(8,128)}, u32[]{:S(2)}) copy-start(f32[256,2048]{1,0:T(8,128)} %copy-done.38) | copy-start | bytes 6291460
  457.5 151.3 %copy-start.37 = (f32[256,2048]{1,0:T(8,128)}, f32[256,2048]{1,0:T(8,128)S(1)}, u32[]{:S(2)}) copy-start(f32[256,2048]{1,0:T(8,128)S(1)} %get-tuple-element.295) | copy-start | bytes 6291460
  457.5 2.8 copy-start.54
  460.3 2.7 copy-start.53
  460.5 2.5 copy-start.44
  463.0 1.3 copy-start.41
  503.7 3.2 copy-start.6
  518.3 201.6 %reduce-scatter.8.cloned.1.call-start = ((), (), s32[]{:S(2)}) async-start(), calls=%async_computation.7 | async-start | bytes 5242880 | tf_op jit(solution)/shard_map/reduce_scatter | solution.py:1559
  552.5 2.0 copy-start.10
  554.5 251.4 %reduce-scatter.10.cloned.1.call-start = ((), (), s32[]{:S(2)}) async-start(), calls=%async_computation.8 | async-start | bytes 2359296 | tf_op jit(solution)/shard_map/reduce_scatter | solution.py:1592
  567.0 40.3 %copy-start.40 = (f32[256,2048]{1,0:T(8,128)S(1)}, f32[256,2048]{1,0:T(8,128)}, u32[]{:S(2)}) copy-start(f32[256,2048]{1,0:T(8,128)} %copy-done.38) | copy-start | bytes 6291460
  608.2 1.6 copy-start.42
  608.2 1.9 copy-start.45
  612.8 29.1 %copy-start.65 = (bf16[512,2048]{1,0:T(8,128)(2,1)S(1)}, bf16[512,2048]{1,0:T(8,128)(2,1)}, u32[]{:S(2)}) copy-start(bf16[512,2048]{1,0:T(8,128)(2,1)} %all-gather.8.cloned.1.call-done) | copy-start | bytes 6291460
  639.9 2.1 copy-start.7
  651.5 41.1 %copy-start.31 = (bf16[2,8,256,128]{3,2,1,0:T(8,128)(2,1)S(1)}, bf16[2,8,256,128]{3,2,1,0:T(8,128)(2,1)}, u32[]{:S(2)}) copy-start(bf16[2,8,256,128]{3,2,1,0:T(8,128)(2,1)} %copy-done.29) | copy-start | bytes 3145732
  692.5 198.4 %reduce-scatter.12.cloned.1.call-start = ((), (), s32[]{:S(2)}) async-start(), calls=%async_computation.9 | async-start | bytes 2359296 | tf_op jit(solution)/shard_map/reduce_scatter | solution.py:1592
  719.8 1.3 copy-start.25
  766.3 1.3 copy-start.18
  767.6 214.2 %reduce-scatter.14.cloned.1.call-start = ((), (), s32[]{:S(2)}) async-start(), calls=%async_computation.10 | async-start | bytes 4718592 | tf_op jit(solution)/shard_map/reduce_scatter | solution.py:1592
  771.9 2.4 copy-start.21
  804.6 1.3 copy-start.14
  805.9 1.6 copy-start.48
  840.9 1.3 copy-start.15
  853.3 2.1 copy-start.1
  875.6 5.3 copy-start.49
  890.9 2.3 copy-start.11
  922.7 1.3 copy-start.16
  924.0 24.5 %copy-start.62 = (f32[1,32,64]{2,1,0:T(8,128)S(1)}, f32[1,32,64]{2,1,0:T(8,128)}, u32[]{:S(2)}) copy-start(f32[1,32,64]{2,1,0:T(8,128)} %concatenate.43) | copy-start | bytes 24580
  924.0 24.6 %copy-start.61 = (f32[1,32,64]{2,1,0:T(8,128)S(1)}, f32[1,32,64]{2,1,0:T(8,128)}, u32[]{:S(2)}) copy-start(f32[1,32,64]{2,1,0:T(8,128)} %concatenate.45) | copy-start | bytes 24580
  924.0 24.6 %copy-start.58 = (f32[1,32,64]{2,1,0:T(8,128)S(1)}, f32[1,32,64]{2,1,0:T(8,128)}, u32[]{:S(2)}) copy-start(f32[1,32,64]{2,1,0:T(8,128)} %concatenate.47) | copy-start | bytes 24580
  924.0 24.6 %copy-start.59 = (f32[1,32,64]{2,1,0:T(8,128)S(1)}, f32[1,32,64]{2,1,0:T(8,128)}, u32[]{:S(2)}) copy-start(f32[1,32,64]{2,1,0:T(8,128)} %concatenate.48) | copy-start | bytes 24580
  924.0 24.6 %copy-start.60 = (f32[1,32,64]{2,1,0:T(8,128)S(1)}, f32[1,32,64]{2,1,0:T(8,128)}, u32[]{:S(2)}) copy-start(f32[1,32,64]{2,1,0:T(8,128)} %concatenate.49) | copy-start | bytes 24580
  924.0 24.9 %copy-start.56 = (f32[32,256]{1,0:T(8,128)S(1)}, f32[32,256]{1,0:T(8,128)}, u32[]{:S(2)}) copy-start(f32[32,256]{1,0:T(8,128)} %reshape.496) | copy-start | bytes 98308
  949.0 30.7 %copy-start.57 = (f32[256,128]{1,0:T(8,128)S(1)}, f32[256,128]{1,0:T(8,128)}, u32[]{:S(2)}) copy-start(f32[256,128]{1,0:T(8,128)} %get-tuple-element.135) | copy-start | bytes 393220
  949.0 31.5 %copy-start.55 = (bf16[64,2048]{1,0:T(8,128)(2,1)S(1)}, bf16[64,2048]{1,0:T(8,128)(2,1)}, u32[]{:S(2)}) copy-start(bf16[64,2048]{1,0:T(8,128)(2,1)} %reduce-scatter.10.cloned.1.call-done) | copy-start | bytes 786436
  (11 other events, 12.0 us)
Sparse Core Ops, SparseCore 0:
  10.2 52.9 all-gather.7
  115.0 61.9 all-gather.9
  178.6 124.5 all-gather.11
  304.6 80.7 all-gather.13
  518.4 79.0 reduce-scatter.5
  600.3 94.1 reduce-scatter.7
  698.6 97.0 reduce-scatter.9
  799.2 82.3 reduce-scatter.11
  885.3 88.7 reduce-scatter.13

commit v6 on v5

--- a/solution.py
+++ b/solution.py
@@ -112,6 +112,8 @@
 def comm(cid, *tasks):
     n = len(tasks)
     counts = [len(t[5]) for t in tasks]
+    given = [t[1] if isinstance(t[1], tuple) else (t[1],) for t in tasks]
+    many = sum(len(g) for g in given)
     limit = 6 * 2**20
     for t in tasks:
         for x in t[5]:
@@ -135,11 +137,12 @@
         for t in targets:
             pl.semaphore_signal(barrier, inc=1, device_id=t, device_id_type=MESH)
         pl.semaphore_wait(barrier, len(targets))
-        scratch = list(refs[2 * n :])
+        inputs, scratch = list(refs[:many]), list(refs[many + n :])
         phases = []
         for i, t in enumerate(tasks):
             mine, scratch = scratch[: counts[i]], scratch[counts[i] :]
-            phases.append(t[6](refs[i], refs[n + i], *mine))
+            own, inputs = inputs[: len(given[i])], inputs[len(given[i]) :]
+            phases.append(t[6](*own, refs[many + i], *mine))
         for p in range(3):
             for ph in phases:
                 ph[p]()
@@ -147,14 +150,14 @@
     out = pl.pallas_call(
         kernel,
         out_shape=[t[2] for t in tasks],
-        in_specs=[t[3] for t in tasks],
+        in_specs=[t[3] for t, g in zip(tasks, given, strict=True) for _ in g],
         out_specs=[t[4] for t in tasks],
         scratch_shapes=[x for t in tasks for x in t[5]],
         compiler_params=pltpu.CompilerParams(
             collective_id=cid, has_side_effects=True, vmem_limit_bytes=limit
         ),
         cost_estimate=pl.CostEstimate(flops=0, bytes_accessed=15_000_000, transcendentals=0),
-    )(*[t[1] for t in tasks])
+    )(*[x for g in given for x in g])
     return out
 
 
@@ -879,6 +882,64 @@
         dma(parts),
     ]
     return (links_twin_pair, x, jax.ShapeDtypeStruct((n, d), F32), ANY, ANY, scratch, body)
+
+
+def nobody():
+    return []
+
+
+def product_beside(x, g, groups, lines, tile=512):
+    n, d = g.shape
+    block = x.shape[1] // groups
+    r = block // lines
+
+    def body(x_ref, g_ref, o_ref, xs, gs, turned, ys, s_x, s_g, s_y):
+        def x_copy(i):
+            at = pl.ds(pl.multiple_of(i * block, block), block)
+            return pltpu.make_async_copy(x_ref.at[:, at], xs.at[i], s_x.at[i])
+
+        def y_copy(i):
+            return pltpu.make_async_copy(ys.at[i], o_ref.at[:, i], s_y.at[i])
+
+        g_copy = pltpu.make_async_copy(g_ref, gs, s_g)
+
+        def start():
+            g_copy.start()
+            for i in range(groups):
+                x_copy(i).start()
+
+        def middle():
+            g_copy.wait()
+
+            def one(i, _):
+                x_copy(i).wait()
+                turned[...] = xs[i].T
+                for j in range(0, d, tile):
+                    cut = slice(j, j + tile)
+                    y = nn(turned[...], gs[:, cut]).astype(BF16)
+                    ys[i, :, :, cut] = y.reshape(lines, r, tile)
+                y_copy(i).start()
+                return 0
+
+            lax.fori_loop(0, groups, one, 0)
+
+        def end():
+            for i in range(groups):
+                y_copy(i).wait()
+
+        return start, middle, end
+
+    shape = jax.ShapeDtypeStruct((lines, groups, r, d), BF16)
+    scratch = [
+        pltpu.VMEM((groups, n, block), BF16),
+        pltpu.VMEM((n, d), BF16),
+        pltpu.VMEM((block, n), BF16),
+        pltpu.VMEM((groups, lines, r, d), BF16),
+        dma(groups),
+        dma(),
+        dma(groups),
+    ]
+    return (nobody, (x, g), shape, ANY, ANY, scratch, body)
 
 
 def scatter_small(x):
@@ -1571,11 +1632,14 @@
     grad_active = dot("nd,fd->nf", branch_g, wdown)
     grad_upward = (grad_active * slope.astype(F32)).astype(BF16)
     grad_up_shift = jnp.sum(grad_upward.astype(F32), axis=0)
-    up_part = line_product(mlp_g, grad_upward, fn, count)
-    up_part, grad_upward = lax.optimization_barrier((up_part, grad_upward))
+    mlp_part = dot("nf,df->nd", grad_upward, wup).astype(BF16)
+    grad_mlp, up_part = comm(
+        17,
+        scatter_plane(mlp_part.reshape(fn, 2, nloc, width)),
+        product_beside(mlp_g, grad_upward, fn, count),
+    )
+    up_part, grad_mlp = lax.optimization_barrier((up_part, grad_mlp))
     grad_up = line_scatter(up_part.reshape(count, -1, pcol))
-    mlp_part = dot("nf,df->nd", grad_upward, wup).astype(BF16)
-    grad_mlp = scatter_plane_tokens(mlp_part)
     grad_hidden, grad_gain_mid, grad_shift_mid = mid_pull(grad_mlp)
     grad_hidden = grad_hidden + grad_result
     grad_attn = grad_hidden.astype(BF16)
@@ -1584,14 +1648,22 @@
     out_part = dot("nd,ne->de", attended, attn_g).astype(BF16)
     grad_att = dot("ne,de->nd", attn_g, wout).astype(BF16)
     grad_att = grad_att.reshape(fn * seqs, length, heads, HEAD_DIM).transpose(0, 2, 1, 3)
-    out_part, grad_att = lax.optimization_barrier((out_part, grad_att))
-    (g_u,) = comm(5, exchange_ctx(grad_att.reshape(cn, units, length, HEAD_DIM), True))
-    g_u, grad_down, out_part = lax.optimization_barrier((g_u, grad_down, out_part))
+    out_part = out_part.reshape(count, 2, rows, width)
+    out_away = lax.dynamic_index_in_dim(out_part, 1 - lo, 1, keepdims=False)
+    out_away, grad_att = lax.optimization_barrier((out_away, grad_att))
+    g_u, out_come = comm(
+        16,
+        exchange_ctx(grad_att.reshape(cn, units, length, HEAD_DIM), True),
+        exchange_pair(out_away),
+    )
+    out_half = lax.dynamic_index_in_dim(out_part, lo, 1, keepdims=False).astype(F32)
+    out_half = (out_half + out_come.astype(F32)).astype(BF16)
+    g_u, grad_down, out_half = lax.optimization_barrier((g_u, grad_down, out_half))
 
     def ctx_scatter(x):
         return lax.psum_scatter(x, "ctx", scatter_dimension=0, tiled=True)
 
-    grad_out = ctx_scatter(out_part)
+    grad_out = line_scatter(out_half)
 
     gq, gk, gv = attend_back(q_u, k_u, v_u, first_key, lse_u, att_u, whole_units(g_u), tables)
 

time: 1010 us -> 1010 us (level)
    pallas_call x4 -> x3, Pallas kernels: 32.9 us -> 14.8 us  [line_product(): pl.pallas_call(kernel, grid=(groups, d // tile), in_specs=[pl.BlockSpec((...]
    pallas_call x19, Pallas kernels: 638 us -> 656 us  [comm(): pl.pallas_call(kernel, out_shape=[t[2] for t in tasks], in_specs=[t[3] fo...]
    unnamed x149 -> x151, local copies, waits for them, and re-layouts: 54.1 us -> 54 us
where the time goes in v6:
time: 1010 us; the launch traced here: 998 us
  Pallas kernels  779 us (77%)
  local copies, waits for them, and re-layouts  99.7 us (10%)
  matrix products  80.7 us (8%)
  other arithmetic  21.9 us (2%)
  between operations  15.5 us (2%)
    pallas_call x19, Pallas kernels, comm(): pl.pallas_call(kernel, out_shape=[t[2] for t in tasks], in_specs=[t[3] fo...  656 us
    dot_general x10, matrix products, dot(): return jnp.einsum(pattern, left, right, preferred_element_type=F32)  67.9 us
    unnamed x151, local copies, waits for them, and re-layouts  54 us
    pallas_call x1, Pallas kernels, attend_back(): pl.pallas_call(kernel, grid=(u, t // block), in_specs=[pl.BlockSpec(spec,...  25 us
    pallas_call x1, Pallas kernels, last(): pl.pallas_call(kernel, grid=(n // tokens,), in_specs=[pl.BlockSpec((h, to...  22.7 us
  transfers between devices with their start and end apart: 9, of which 0 were waited for; matrix products, arithmetic and copies ran while one was open for 12% of the time, Pallas kernels for 67%

profile of v6, /device:TPU:1, one launch (start us, length us, event | category | flops | bytes accessed | tf_op | source)
XLA Modules:
  0.0 998.4 jit_solution(15222736149574193410)
XLA Ops:
  13.8 21.7 %shard_map.340 = (f32[4,8,32,128]{3,2,1,0:T(8,128)S(1)}, bf16[4,3,64,512]{3,2,1,0:T(8,128)(2,1)S(1)}) custom-call(f32[32,128]{1,0:T(8,128)S(1)} %pad_bitcast_fusion.1.refs_0_, bf16[4,3,64,512]{3,2,1,0:T(8,128)(2,1)S(1)} %bitcast.235), custom_call_target="tpu_custom_call" | custom-call | bytes 15000000 | tf_op jit(solution)/shard_map/pallas_call | solution.py:150
  38.4 13.8 %shard_map.341 = (f32[4,256,2048]{2,1,0:T(8,128)}, bf16[256,2048]{1,0:T(8,128)(2,1)}, bf16[256,2048]{1,0:T(8,128)(2,1)}, bf16[256,2048]{1,0:T(8,128)(2,1)}) custom-call(bf16[9,256,2048]{2,1,0:T(8,128)(2,1)} %bitcast.262, f32[256,128]{1,0:T(8,128)} %pad.25.m_ref, f32[3,2048]{1,0:T(4,128)} %slice.128.g_ref, f32[3,2048]{1,0:T(4,128)} %slice.131.b_ref), custom_call_target="tpu_custom_call" | custom-call | flops 37748736 | bytes 20971520 | tf_op jit(solution)/shard_map/pallas_call | solution.py:1331
  53.5 56.7 %shard_map.342 = (bf16[8,4,2,64,512]{4,3,2,1,0:T(8,128)(2,1)S(1)}, bf16[4,256,2048]{2,1,0:T(8,128)(2,1)S(1)}) custom-call(bf16[4,2,64,512]{3,2,1,0:T(8,128)(2,1)S(1)} %slice.133.refs_0_, bf16[256,2048]{1,0:T(8,128)(2,1)S(1)} %copy-done.22), custom_call_target="tpu_custom_call" | custom-call | bytes 15000000 | tf_op jit(solution)/shard_map/pallas_call | solution.py:150
  110.2 2.0 copy-done.2
  112.2 2.0 copy-done.12
  116.3 2.2 copy-done.3
  118.5 2.2 copy-done.13
  120.7 4.2 shard_map.343
  124.9 28.5 %shard_map.344 = (bf16[2,8,256,128]{3,2,1,0:T(8,128)(2,1)S(1)}, bf16[4,256,2048]{2,1,0:T(8,128)(2,1)S(1)}) custom-call(bf16[8,2,256,128]{3,2,1,0:T(8,128)(2,1)S(1)} %bitcast.234, bf16[256,2048]{1,0:T(8,128)(2,1)S(1)} %copy-done.26), custom_call_target="tpu_custom_call" | custom-call | bytes 15000000 | tf_op jit(solution)/shard_map/pallas_call | solution.py:150
  153.4 4.2 shard_map.345
  159.9 1.8 reshape.458.refs_1_
  161.7 33.9 %shard_map.346 = (bf16[2,8,256,128]{3,2,1,0:T(8,128)(2,1)S(1)}, bf16[4,256,2048]{2,1,0:T(8,128)(2,1)S(1)}) custom-call(bf16[8,2,256,128]{3,2,1,0:T(8,128)(2,1)S(1)} %bitcast.233, bf16[256,2048]{1,0:T(8,128)(2,1)S(1)} %copy-done.25), custom_call_target="tpu_custom_call" | custom-call | bytes 15000000 | tf_op jit(solution)/shard_map/pallas_call | solution.py:150
  195.7 2.1 copy-done.8
  198.8 2.2 copy-done.9
  202.6 3.1 shard_map.347
  205.7 39.8 %shard_map.348 = (bf16[2,8,256,128]{3,2,1,0:T(8,128)(2,1)S(1)}, bf16[4,2,64,1024]{3,2,1,0:T(8,128)(2,1)}) custom-call(bf16[8,2,256,128]{3,2,1,0:T(8,128)(2,1)S(1)} %bitcast.244, bf16[4,2,64,1024]{3,2,1,0:T(8,128)(2,1)S(1)} %reshape.458.refs_1_), custom_call_target="tpu_custom_call" | custom-call | bytes 15000000 | tf_op jit(solution)/shard_map/pallas_call | solution.py:150
  248.2 1.8 reshape.470
  252.4 15.3 %shard_map.349 = (bf16[2,2048,128]{2,1,0:T(8,128)(2,1)S(1)}, f32[2,1,2048]{2,1,0:T(1,128)S(1)}) custom-call(bf16[2,2048,128]{2,1,0:T(8,128)(2,1)S(1)} %bitcast.255, bf16[2,2048,128]{2,1,0:T(8,128)(2,1)S(1)} %bitcast.257, bf16[2,2048,128]{2,1,0:T(8,128)(2,1)S(1)} %bitcast.260, s32[2,1,2048]{2,1,0:T(1,128)S(1)} %broadcast_in_dim.28.s_ref), custom_call_target="tpu_custom_call" | custom-call | flops 2147483648 | bytes 8388608 | tf_op jit(solution)/shard_map/pallas_call | solution.py:1046
  267.8 38.1 %shard_map.350 = bf16[8,2,256,128]{3,2,1,0:T(8,128)(2,1)S(1)} custom-call(bf16[2,8,256,128]{3,2,1,0:T(8,128)(2,1)S(1)} %bitcast.241), custom_call_target="tpu_custom_call" | custom-call | bytes 15000000 | tf_op jit(solution)/shard_map/pallas_call | solution.py:150
  307.0 4.3 convolution_convert_fusion.6
  311.3 28.3 %shard_map.351 = f32[256,2048]{1,0:T(8,128)S(1)} custom-call(bf16[4,256,2048]{2,1,0:T(8,128)(2,1)S(1)} %bitcast.222), custom_call_target="tpu_custom_call" | custom-call | bytes 15000000 | tf_op jit(solution)/shard_map/pallas_call | solution.py:150
  339.6 2.1 fusion.36
  342.5 41.5 %shard_map.352 = bf16[4,2,256,2048]{3,2,1,0:T(8,128)(2,1)S(1)} custom-call(bf16[256,2048]{1,0:T(8,128)(2,1)S(1)} %add_convert_fusion.refs_0_), custom_call_target="tpu_custom_call" | custom-call | bytes 15000000 | tf_op jit(solution)/shard_map/pallas_call | solution.py:150
  384.1 3.4 copy-done.4
  387.5 19.2 %shard_map.353 = (bf16[2048,1024]{1,0:T(8,128)(2,1)S(1)}, bf16[2048,1024]{1,0:T(8,128)(2,1)}, bf16[2048,1024]{1,0:T(8,128)(2,1)}) custom-call(bf16[2048,2048]{1,0:T(8,128)(2,1)} %bitcast.208, bf16[4,4,128,1024]{3,2,1,0:T(8,128)(2,1)} %bitcast.301, f32[1,1024]{1,0:T(1,128)S(1)} %bitcast.254), custom_call_target="tpu_custom_call" | custom-call | flops 8589934592 | bytes 60000000 | tf_op jit(solution)/shard_map/pallas_call | solution.py:1246
  406.7 9.8 convolution_convert_fusion.1
  416.5 40.4 %shard_map.354 = f32[256,2048]{1,0:T(8,128)S(1)} custom-call(bf16[4,2,256,2048]{3,2,1,0:T(8,128)(2,1)S(1)} %bitcast.214), custom_call_target="tpu_custom_call" | custom-call | bytes 15000000 | tf_op jit(solution)/shard_map/pallas_call | solution.py:150
  458.1 2.0 fusion.14
  460.4 2.4 multiply_reduce_fusion
  464.2 39.4 %shard_map.355 = bf16[4,2,256,2048]{3,2,1,0:T(8,128)(2,1)S(1)} custom-call(bf16[256,2048]{1,0:T(8,128)(2,1)S(1)} %get-tuple-element.296.refs_0_), custom_call_target="tpu_custom_call" | custom-call | bytes 15000000 | tf_op jit(solution)/shard_map/pallas_call | solution.py:150
  503.6 3.3 copy-done.6
  506.8 11.2 %convolution_convert_fusion.5 = bf16[1024,2048]{1,0:T(8,128)(2,1)} fusion(bf16[2048,1024]{1,0:T(8,128)(2,1)S(1)} %get-tuple-element.112, bf16[2048,2048]{1,0:T(8,128)(2,1)S(1)} %bitcast.215), kind=kOutput, calls=%fused_computation.8 | convolution fusion | flops 8592031744 | bytes 16777216 | tf_op jit(solution)/shard_map/nf,nd->fd/dot_general | solution.py:69
  518.1 13.9 %convert_reduce_fusion = (f32[1024]{0:T(1024)}, bf16[2048,1024]{1,0:T(8,128)(2,1)S(1)}) fusion(bf16[2048,1024]{1,0:T(8,128)(2,1)} %get-tuple-element.116, bf16[2048,2048]{1,0:T(8,128)(2,1)} %bitcast.216, bf16[1024,2048]{1,0:T(8,128)(2,1)} %all-gather.12.cloned.1.call-done), kind=kOutput, calls=%fused_computation.1 | convolution fusion | flops 8600419328 | bytes 20975616 | tf_op jit(solution)/shard_map/nd,fd->nf/dot_general | solution.py:69
  532.1 10.9 %convolution_convert_fusion = bf16[2048,2048]{1,0:T(8,128)(2,1)} fusion(bf16[2048,1024]{1,0:T(8,128)(2,1)S(1)} %get-tuple-element.330.refs_2_, bf16[2048,1024]{1,0:T(8,128)(2,1)S(1)} %copy-done.66), kind=kOutput, calls=%fused_computation.3 | convolution fusion | flops 8594128896 | bytes 16777216 | tf_op jit(solution)/shard_map/nf,df->nd/dot_general | solution.py:69
  543.0 40.8 %shard_map.356 = (f32[256,2048]{1,0:T(8,128)S(1)}, bf16[4,4,128,1024]{3,2,1,0:T(8,128)(2,1)S(1)}) custom-call(bf16[4,2,256,2048]{3,2,1,0:T(8,128)(2,1)} %bitcast.264, bf16[2048,2048]{1,0:T(8,128)(2,1)} %bitcast.209, bf16[2048,1024]{1,0:T(8,128)(2,1)} %copy-done.44), custom_call_target="tpu_custom_call" | custom-call | bytes 15000000 | tf_op jit(solution)/shard_map/pallas_call | solution.py:150
  583.8 2.1 copy-done.10
  586.3 2.6 multiply_reduce_fusion.1
  591.1 2.8 convert_reduce_fusion.2
  593.9 26.9 %shard_map.357 = bf16[4,256,2048]{2,1,0:T(8,128)(2,1)S(1)} custom-call(bf16[256,2048]{1,0:T(8,128)(2,1)S(1)} %get-tuple-element.298.refs_0_), custom_call_target="tpu_custom_call" | custom-call | bytes 15000000 | tf_op jit(solution)/shard_map/pallas_call | solution.py:150
  620.8 2.0 copy-done.7
  622.8 2.4 convolution_convert_fusion.8
  626.4 4.6 convolution_convert_fusion.7
  631.2 42.1 %shard_map.358 = (bf16[2,8,256,128]{3,2,1,0:T(8,128)(2,1)S(1)}, bf16[4,64,2048]{2,1,0:T(8,128)(2,1)S(1)}) custom-call(bf16[8,2,256,128]{3,2,1,0:T(8,128)(2,1)S(1)} %bitcast.230, bf16[4,64,2048]{2,1,0:T(8,128)(2,1)S(1)} %dynamic-slice_bitcast_fusion.refs_1_), custom_call_target="tpu_custom_call" | custom-call | bytes 15000000 | tf_op jit(solution)/shard_map/pallas_call | solution.py:150
  677.0 25.0 %shard_map.359 = (bf16[2,2048,128]{2,1,0:T(8,128)(2,1)S(1)}, bf16[2,2048,128]{2,1,0:T(8,128)(2,1)S(1)}, bf16[2,2048,128]{2,1,0:T(8,128)(2,1)S(1)}) custom-call(bf16[2,2048,128]{2,1,0:T(8,128)(2,1)S(1)} %bitcast.256, bf16[2,2048,128]{2,1,0:T(8,128)(2,1)S(1)} %bitcast.258, bf16[2,2048,128]{2,1,0:T(8,128)(2,1)} %bitcast.259, ...), custom_call_target="tpu_custom_call" | custom-call | flops 5368709120 | bytes 20971520 | tf_op jit(solution)/shard_map/pallas_call | solution.py:1133
  704.1 45.0 %shard_map.360 = (bf16[8,2,256,128]{3,2,1,0:T(8,128)(2,1)S(1)}, bf16[64,8192]{1,0:T(8,128)(2,1)S(1)}) custom-call(bf16[2,8,256,128]{3,2,1,0:T(8,128)(2,1)S(1)} %bitcast.243, bf16[4,2,64,1024]{3,2,1,0:T(8,128)(2,1)S(1)} %bitcast.242), custom_call_target="tpu_custom_call" | custom-call | bytes 15000000 | tf_op jit(solution)/shard_map/pallas_call | solution.py:150
  751.2 4.9 shard_map.361
  757.6 2.5 slice_bitcast_fusion
  761.8 2.4 convolution_convert_fusion.4
  764.2 33.1 %shard_map.362 = (bf16[8,2,256,128]{3,2,1,0:T(8,128)(2,1)S(1)}, f32[256,2048]{1,0:T(8,128)S(1)}) custom-call(bf16[2,8,256,128]{3,2,1,0:T(8,128)(2,1)S(1)} %bitcast.240, bf16[4,256,2048]{2,1,0:T(8,128)(2,1)S(1)} %bitcast.220), custom_call_target="tpu_custom_call" | custom-call | bytes 15000000 | tf_op jit(solution)/shard_map/pallas_call | solution.py:150
  800.2 2.4 convolution_convert_fusion.3
  802.6 42.7 %shard_map.363 = (bf16[8,2,256,128]{3,2,1,0:T(8,128)(2,1)S(1)}, f32[256,2048]{1,0:T(8,128)S(1)}) custom-call(bf16[2,8,256,128]{3,2,1,0:T(8,128)(2,1)S(1)} %bitcast.239, bf16[4,256,2048]{2,1,0:T(8,128)(2,1)S(1)} %bitcast.219), custom_call_target="tpu_custom_call" | custom-call | bytes 15000000 | tf_op jit(solution)/shard_map/pallas_call | solution.py:150
  847.6 4.9 shard_map.364.refs_0_
  852.5 5.1 shard_map.365
  857.6 2.1 copy-done.1
  860.6 3.2 copy.198
  867.1 6.1 fusion.3
  873.2 1.8 reshape.507
  882.5 2.7 convert_element_type.156
  890.1 6.1 convolution_convert_fusion.2
  896.2 2.2 copy-done.11
  899.4 28.1 %shard_map.366 = (bf16[4,64,512]{2,1,0:T(8,128)(2,1)S(1)}, f32[256,2048]{1,0:T(8,128)S(1)}) custom-call(bf16[4,64,512]{2,1,0:T(8,128)(2,1)S(1)} %bitcast.247, bf16[4,256,2048]{2,1,0:T(8,128)(2,1)S(1)} %bitcast.225), custom_call_target="tpu_custom_call" | custom-call | bytes 15000000 | tf_op jit(solution)/shard_map/pallas_call | solution.py:150
  928.9 22.7 %shard_map.367 = (f32[9,256,2048]{2,1,0:T(8,128)}, f32[256,128]{1,0:T(8,128)}, f32[3,2048]{1,0:T(4,128)}, f32[3,2048]{1,0:T(4,128)}) custom-call(bf16[9,256,2048]{2,1,0:T(8,128)(2,1)} %bitcast.263, f32[256,128]{1,0:T(8,128)} %pad.25.m_ref, f32[4,256,2048]{2,1,0:T(8,128)} %get-tuple-element.92.s_ref, f32[3,2048]{1,0:T(4,128)} %slice.128.g_ref, ...), custom_call_target="tpu_custom_call" | custom-call | flops 75497472 | bytes 45088768 | tf_op jit(solution)/shard_map/pallas_call | solution.py:1408
  954.0 20.9 %shard_map.368 = f32[48,128]{1,0:T(8,128)S(1)} custom-call(f32[4,8,48,128]{3,2,1,0:T(8,128)S(1)} %copy.249), custom_call_target="tpu_custom_call" | custom-call | bytes 15000000 | tf_op jit(solution)/shard_map/pallas_call | solution.py:150
  981.2 8.3 shard_map.369
  (279 shorter events, 77.1 us)
Async XLA Ops:
  7.2 453.0 %copy-start = (f32[40,40]{1,0:T(8,128)S(1)}, f32[40,40]{1,0:T(8,128)}, u32[]{:S(2)}) copy-start(f32[40,40]{1,0:T(8,128)} %param.36) | copy-start | bytes 19204
  7.2 107.7 %all-gather.8.cloned.1.call-start = ((), (), s32[]{:S(2)}) async-start(), calls=%async_computation.5 | async-start | bytes 2359296 | tf_op jit(solution)/shard_map/all_gather | solution.py:1495
  7.9 190.8 %all-gather.10.cloned.1.call-start = ((), (), s32[]{:S(2)}) async-start(), calls=%async_computation.11 | async-start | bytes 2359296 | tf_op jit(solution)/shard_map/all_gather | solution.py:1551
  8.0 29.5 %copy-start.63 = (f32[4,9,1,256]{3,2,1,0:T(1,128)S(1)}, f32[4,9,1,256]{3,2,1,0:T(1,128)}, u32[]{:S(2)}) copy-start(f32[4,9,1,256]{3,2,1,0:T(1,128)} %param.22) | copy-start | bytes 110596
  35.8 79.1 %copy-start.46 = (f32[4,8,32,128]{3,1,2,0:T(8,128)}, f32[4,8,32,128]{3,1,2,0:T(8,128)S(1)}, u32[]{:S(2)}) copy-start(f32[4,8,32,128]{3,1,2,0:T(8,128)S(1)} %copy.251) | copy-start | bytes 1572868
  110.2 2.0 copy-start.2
  112.2 2.0 copy-start.12
  114.9 192.1 %all-gather.12.cloned.1.call-start = ((), (), s32[]{:S(2)}) async-start(), calls=%async_computation.12 | async-start | bytes 5242880 | tf_op jit(solution)/shard_map/all_gather | solution.py:1480
  116.3 2.2 copy-start.3
  118.5 2.2 copy-start.13
  120.7 4.2 copy-start.26
  153.4 4.3 copy-start.5
  153.4 4.3 copy-start.28
  153.4 4.3 copy-start.50
  157.7 229.8 %all-gather.14.cloned.1.call-start = ((), (), s32[]{:S(2)}) async-start(), calls=%async_computation.13 | async-start | bytes 5242880 | tf_op jit(solution)/shard_map/all_gather | solution.py:1480
  158.6 3.2 copy-start.25
  195.7 2.1 copy-start.8
  198.8 2.2 copy-start.9
  201.0 1.6 copy-start.17
  205.7 41.1 %copy-start.47 = (f32[4,8,32,128]{3,1,2,0:T(8,128)S(1)}, f32[4,8,32,128]{3,1,2,0:T(8,128)}, u32[]{:S(2)}) copy-start(f32[4,8,32,128]{3,1,2,0:T(8,128)} %copy-done.46) | copy-start | bytes 1572868
  246.5 3.5 copy-start.29
  246.5 429.1 %reduce-scatter.6.cloned.1.call-start = ((), (), s32[]{:S(2)}) async-start(), calls=%async_computation.6 | async-start | bytes 5242880 | tf_op jit(solution)/shard_map/reduce_scatter | solution.py:1620
  251.2 1.2 copy-start.35
  267.8 39.0 %copy-start.23 = (bf16[2,2048,128]{2,1,0:T(8,128)(2,1)}, bf16[2,2048,128]{2,1,0:T(8,128)(2,1)S(1)}, u32[]{:S(2)}) copy-start(bf16[2,2048,128]{2,1,0:T(8,128)(2,1)S(1)} %get-tuple-element.107.o_ref) | copy-start | bytes 3145732
  307.0 4.3 copy-start.51
  341.7 115.2 %copy-start.39 = (f32[256,2048]{1,0:T(8,128)}, f32[256,2048]{1,0:T(8,128)S(1)}, u32[]{:S(2)}) copy-start(f32[256,2048]{1,0:T(8,128)S(1)} %get-tuple-element.305) | copy-start | bytes 6291460
  384.1 3.4 copy-start.4
  387.5 19.2 %copy-start.64 = (bf16[1024,2048]{1,0:T(8,128)(2,1)S(1)}, bf16[1024,2048]{1,0:T(8,128)(2,1)}, u32[]{:S(2)}) copy-start(bf16[1024,2048]{1,0:T(8,128)(2,1)} %all-gather.12.cloned.1.call-done) | copy-start | bytes 12582916
  457.3 5.5 copy-start.37
  457.3 2.8 copy-start.54
  460.2 2.7 copy-start.53
  460.4 2.5 copy-start.45
  462.8 1.3 copy-start.41
  503.6 3.3 copy-start.6
  518.1 184.8 %reduce-scatter.8.cloned.1.call-start = ((), (), s32[]{:S(2)}) async-start(), calls=%async_computation.7 | async-start | bytes 5242880 | tf_op jit(solution)/shard_map/reduce_scatter | solution.py:1620
  518.1 13.9 %copy-start.66 = (bf16[2048,1024]{1,0:T(8,128)(2,1)S(1)}, bf16[2048,1024]{1,0:T(8,128)(2,1)}, u32[]{:S(2)}) copy-start(bf16[2048,1024]{1,0:T(8,128)(2,1)} %get-tuple-element.117) | copy-start | bytes 12582916
  532.1 10.9 %copy-start.44 = (bf16[2048,1024]{1,0:T(8,128)(2,1)}, bf16[2048,1024]{1,0:T(8,128)(2,1)S(1)}, u32[]{:S(2)}) copy-start(bf16[2048,1024]{1,0:T(8,128)(2,1)S(1)} %get-tuple-element.330.refs_2_) | copy-start | bytes 12582916
  583.7 2.1 copy-start.10
  585.9 212.7 %reduce-scatter.10.cloned.1.call-start = ((), (), s32[]{:S(2)}) async-start(), calls=%async_computation.8 | async-start | bytes 1310720 | tf_op jit(solution)/shard_map/reduce_scatter | solution.py:1620
  586.3 2.6 copy-start.40
  588.9 1.6 copy-start.38
  588.9 2.2 copy-start.42
  593.9 28.9 %copy-start.65 = (bf16[512,2048]{1,0:T(8,128)(2,1)S(1)}, bf16[512,2048]{1,0:T(8,128)(2,1)}, u32[]{:S(2)}) copy-start(bf16[512,2048]{1,0:T(8,128)(2,1)} %all-gather.8.cloned.1.call-done) | copy-start | bytes 6291460
  620.8 2.0 copy-start.7
  674.3 1.4 copy-start.30
  675.7 220.5 %reduce-scatter.12.cloned.1.call-start = ((), (), s32[]{:S(2)}) async-start(), calls=%async_computation.9 | async-start | bytes 2359296 | tf_op jit(solution)/shard_map/reduce_scatter | solution.py:1664
  756.1 1.3 copy-start.18
  757.4 222.7 %reduce-scatter.14.cloned.1.call-start = ((), (), s32[]{:S(2)}) async-start(), calls=%async_computation.10 | async-start | bytes 4718592 | tf_op jit(solution)/shard_map/reduce_scatter | solution.py:1664
  761.8 2.4 copy-start.21
  797.3 1.3 copy-start.14
  798.6 1.6 copy-start.48
  845.3 1.3 copy-start.15
  857.6 2.1 copy-start.1
  880.0 5.3 copy-start.49
  887.9 1.4 copy-start.55
  896.2 2.2 copy-start.11
  927.5 1.3 copy-start.16
  928.9 24.4 %copy-start.62 = (f32[1,32,64]{2,1,0:T(8,128)S(1)}, f32[1,32,64]{2,1,0:T(8,128)}, u32[]{:S(2)}) copy-start(f32[1,32,64]{2,1,0:T(8,128)} %concatenate.43) | copy-start | bytes 24580
  928.9 24.5 %copy-start.61 = (f32[1,32,64]{2,1,0:T(8,128)S(1)}, f32[1,32,64]{2,1,0:T(8,128)}, u32[]{:S(2)}) copy-start(f32[1,32,64]{2,1,0:T(8,128)} %concatenate.45) | copy-start | bytes 24580
  928.9 24.5 %copy-start.58 = (f32[1,32,64]{2,1,0:T(8,128)S(1)}, f32[1,32,64]{2,1,0:T(8,128)}, u32[]{:S(2)}) copy-start(f32[1,32,64]{2,1,0:T(8,128)} %concatenate.47) | copy-start | bytes 24580
  928.9 24.5 %copy-start.59 = (f32[1,32,64]{2,1,0:T(8,128)S(1)}, f32[1,32,64]{2,1,0:T(8,128)}, u32[]{:S(2)}) copy-start(f32[1,32,64]{2,1,0:T(8,128)} %concatenate.48) | copy-start | bytes 24580
  928.9 24.5 %copy-start.60 = (f32[1,32,64]{2,1,0:T(8,128)S(1)}, f32[1,32,64]{2,1,0:T(8,128)}, u32[]{:S(2)}) copy-start(f32[1,32,64]{2,1,0:T(8,128)} %concatenate.49) | copy-start | bytes 24580
  928.9 24.8 %copy-start.56 = (f32[32,256]{1,0:T(8,128)S(1)}, f32[32,256]{1,0:T(8,128)}, u32[]{:S(2)}) copy-start(f32[32,256]{1,0:T(8,128)} %reshape.506) | copy-start | bytes 98308
  953.7 25.0 %copy-start.57 = (f32[256,128]{1,0:T(8,128)S(1)}, f32[256,128]{1,0:T(8,128)}, u32[]{:S(2)}) copy-start(f32[256,128]{1,0:T(8,128)} %get-tuple-element.143) | copy-start | bytes 393220
  (12 other events, 13.2 us)
Sparse Core Ops, SparseCore 0:
  10.2 52.9 all-gather.7
  115.0 61.9 all-gather.9
  178.6 125.0 all-gather.11
  305.1 80.6 all-gather.13
  518.2 79.5 reduce-scatter.5
  600.0 94.1 reduce-scatter.7
  697.1 31.5 reduce-scatter.9
  757.5 93.3 reduce-scatter.11
  859.8 91.2 reduce-scatter.13

commit v7 on v6

--- a/solution.py
+++ b/solution.py
@@ -1304,7 +1304,7 @@
     )(x, g, *extra)
 
 
-def front(hist, mix, gain, shift, tokens=32, wide=128):
+def front(hist, mix, gain, shift, tokens=64, wide=128):
     h, n, d = hist.shape
     rest = gain.shape[0]
 
@@ -1350,7 +1350,7 @@
     )(hist, mix, gain, shift)
 
 
-def last(hist, mix, streams, gain, grads, grad_hidden, tokens=32, wide=256):
+def last(hist, mix, streams, gain, grads, grad_hidden, tokens=64, wide=256):
     h, n, d = hist.shape
     rest = gain.shape[0]
 

time: 1010 us -> 1010 us (level)
  no operation moved by 1% of the time
where the time goes in v7:
time: 1010 us; the launch traced here: 1000 us
  Pallas kernels  780 us (77%)
  local copies, waits for them, and re-layouts  99.8 us (10%)
  matrix products  80.6 us (8%)
  other arithmetic  21.9 us (2%)
  between operations  15.7 us (2%)
    pallas_call x19, Pallas kernels, comm(): pl.pallas_call(kernel, out_shape=[t[2] for t in tasks], in_specs=[t[3] fo...  657 us
    dot_general x10, matrix products, dot(): return jnp.einsum(pattern, left, right, preferred_element_type=F32)  67.9 us
    unnamed x151, local copies, waits for them, and re-layouts  54 us
    pallas_call x1, Pallas kernels, attend_back(): pl.pallas_call(kernel, grid=(u, t // block), in_specs=[pl.BlockSpec(spec,...  25 us
    pallas_call x1, Pallas kernels, last(): pl.pallas_call(kernel, grid=(n // tokens,), in_specs=[pl.BlockSpec((h, to...  24.2 us
  transfers between devices with their start and end apart: 9, of which 0 were waited for; matrix products, arithmetic and copies ran while one was open for 12% of the time, Pallas kernels for 67%

profile of v7, /device:TPU:1, one launch (start us, length us, event | category | flops | bytes accessed | tf_op | source)
XLA Modules:
  0.0 1000.1 jit_solution(9256786673561958161)
XLA Ops:
  13.8 21.7 %shard_map.340 = (f32[4,8,32,128]{3,2,1,0:T(8,128)S(1)}, bf16[4,3,64,512]{3,2,1,0:T(8,128)(2,1)S(1)}) custom-call(f32[32,128]{1,0:T(8,128)S(1)} %pad_bitcast_fusion.1.refs_0_, bf16[4,3,64,512]{3,2,1,0:T(8,128)(2,1)S(1)} %bitcast.235), custom_call_target="tpu_custom_call" | custom-call | bytes 15000000 | tf_op jit(solution)/shard_map/pallas_call | solution.py:150
  38.4 13.2 %shard_map.341 = (f32[4,256,2048]{2,1,0:T(8,128)}, bf16[256,2048]{1,0:T(8,128)(2,1)}, bf16[256,2048]{1,0:T(8,128)(2,1)}, bf16[256,2048]{1,0:T(8,128)(2,1)}) custom-call(bf16[9,256,2048]{2,1,0:T(8,128)(2,1)} %bitcast.262, f32[256,128]{1,0:T(8,128)} %pad.25.m_ref, f32[3,2048]{1,0:T(4,128)} %slice.128.g_ref, f32[3,2048]{1,0:T(4,128)} %slice.131.b_ref), custom_call_target="tpu_custom_call" | custom-call | flops 37748736 | bytes 20971520 | tf_op jit(solution)/shard_map/pallas_call | solution.py:1331
  52.9 57.2 %shard_map.342 = (bf16[8,4,2,64,512]{4,3,2,1,0:T(8,128)(2,1)S(1)}, bf16[4,256,2048]{2,1,0:T(8,128)(2,1)S(1)}) custom-call(bf16[4,2,64,512]{3,2,1,0:T(8,128)(2,1)S(1)} %slice.133.refs_0_, bf16[256,2048]{1,0:T(8,128)(2,1)S(1)} %copy-done.22), custom_call_target="tpu_custom_call" | custom-call | bytes 15000000 | tf_op jit(solution)/shard_map/pallas_call | solution.py:150
  110.1 2.0 copy-done.2
  112.1 2.0 copy-done.12
  116.2 2.2 copy-done.3
  118.4 2.2 copy-done.13
  120.6 4.2 shard_map.343
  124.8 28.6 %shard_map.344 = (bf16[2,8,256,128]{3,2,1,0:T(8,128)(2,1)S(1)}, bf16[4,256,2048]{2,1,0:T(8,128)(2,1)S(1)}) custom-call(bf16[8,2,256,128]{3,2,1,0:T(8,128)(2,1)S(1)} %bitcast.234, bf16[256,2048]{1,0:T(8,128)(2,1)S(1)} %copy-done.26), custom_call_target="tpu_custom_call" | custom-call | bytes 15000000 | tf_op jit(solution)/shard_map/pallas_call | solution.py:150
  153.4 4.2 shard_map.345
  159.9 1.8 reshape.458.refs_1_
  161.7 33.6 %shard_map.346 = (bf16[2,8,256,128]{3,2,1,0:T(8,128)(2,1)S(1)}, bf16[4,256,2048]{2,1,0:T(8,128)(2,1)S(1)}) custom-call(bf16[8,2,256,128]{3,2,1,0:T(8,128)(2,1)S(1)} %bitcast.233, bf16[256,2048]{1,0:T(8,128)(2,1)S(1)} %copy-done.25), custom_call_target="tpu_custom_call" | custom-call | bytes 15000000 | tf_op jit(solution)/shard_map/pallas_call | solution.py:150
  195.3 2.1 copy-done.8
  198.4 2.2 copy-done.9
  202.2 3.1 shard_map.347
  205.4 39.9 %shard_map.348 = (bf16[2,8,256,128]{3,2,1,0:T(8,128)(2,1)S(1)}, bf16[4,2,64,1024]{3,2,1,0:T(8,128)(2,1)}) custom-call(bf16[8,2,256,128]{3,2,1,0:T(8,128)(2,1)S(1)} %bitcast.244, bf16[4,2,64,1024]{3,2,1,0:T(8,128)(2,1)S(1)} %reshape.458.refs_1_), custom_call_target="tpu_custom_call" | custom-call | bytes 15000000 | tf_op jit(solution)/shard_map/pallas_call | solution.py:150
  248.0 1.8 reshape.470
  252.3 15.3 %shard_map.349 = (bf16[2,2048,128]{2,1,0:T(8,128)(2,1)S(1)}, f32[2,1,2048]{2,1,0:T(1,128)S(1)}) custom-call(bf16[2,2048,128]{2,1,0:T(8,128)(2,1)S(1)} %bitcast.255, bf16[2,2048,128]{2,1,0:T(8,128)(2,1)S(1)} %bitcast.257, bf16[2,2048,128]{2,1,0:T(8,128)(2,1)S(1)} %bitcast.260, s32[2,1,2048]{2,1,0:T(1,128)S(1)} %broadcast_in_dim.28.s_ref), custom_call_target="tpu_custom_call" | custom-call | flops 2147483648 | bytes 8388608 | tf_op jit(solution)/shard_map/pallas_call | solution.py:1046
  267.6 38.3 %shard_map.350 = bf16[8,2,256,128]{3,2,1,0:T(8,128)(2,1)S(1)} custom-call(bf16[2,8,256,128]{3,2,1,0:T(8,128)(2,1)S(1)} %bitcast.241), custom_call_target="tpu_custom_call" | custom-call | bytes 15000000 | tf_op jit(solution)/shard_map/pallas_call | solution.py:150
  306.9 4.3 convolution_convert_fusion.6
  311.3 28.1 %shard_map.351 = f32[256,2048]{1,0:T(8,128)S(1)} custom-call(bf16[4,256,2048]{2,1,0:T(8,128)(2,1)S(1)} %bitcast.222), custom_call_target="tpu_custom_call" | custom-call | bytes 15000000 | tf_op jit(solution)/shard_map/pallas_call | solution.py:150
  339.4 2.1 fusion.36
  342.3 41.9 %shard_map.352 = bf16[4,2,256,2048]{3,2,1,0:T(8,128)(2,1)S(1)} custom-call(bf16[256,2048]{1,0:T(8,128)(2,1)S(1)} %add_convert_fusion.refs_0_), custom_call_target="tpu_custom_call" | custom-call | bytes 15000000 | tf_op jit(solution)/shard_map/pallas_call | solution.py:150
  384.2 3.4 copy-done.4
  387.6 19.2 %shard_map.353 = (bf16[2048,1024]{1,0:T(8,128)(2,1)S(1)}, bf16[2048,1024]{1,0:T(8,128)(2,1)}, bf16[2048,1024]{1,0:T(8,128)(2,1)}) custom-call(bf16[2048,2048]{1,0:T(8,128)(2,1)} %bitcast.208, bf16[4,4,128,1024]{3,2,1,0:T(8,128)(2,1)} %bitcast.301, f32[1,1024]{1,0:T(1,128)S(1)} %bitcast.254), custom_call_target="tpu_custom_call" | custom-call | flops 8589934592 | bytes 60000000 | tf_op jit(solution)/shard_map/pallas_call | solution.py:1246
  406.8 9.8 convolution_convert_fusion.1
  416.6 40.4 %shard_map.354 = f32[256,2048]{1,0:T(8,128)S(1)} custom-call(bf16[4,2,256,2048]{3,2,1,0:T(8,128)(2,1)S(1)} %bitcast.214), custom_call_target="tpu_custom_call" | custom-call | bytes 15000000 | tf_op jit(solution)/shard_map/pallas_call | solution.py:150
  458.3 2.0 fusion.14
  460.6 2.4 multiply_reduce_fusion
  464.3 39.3 %shard_map.355 = bf16[4,2,256,2048]{3,2,1,0:T(8,128)(2,1)S(1)} custom-call(bf16[256,2048]{1,0:T(8,128)(2,1)S(1)} %get-tuple-element.296.refs_0_), custom_call_target="tpu_custom_call" | custom-call | bytes 15000000 | tf_op jit(solution)/shard_map/pallas_call | solution.py:150
  503.6 3.3 copy-done.6
  506.9 11.2 %convolution_convert_fusion.5 = bf16[1024,2048]{1,0:T(8,128)(2,1)} fusion(bf16[2048,1024]{1,0:T(8,128)(2,1)S(1)} %get-tuple-element.112, bf16[2048,2048]{1,0:T(8,128)(2,1)S(1)} %bitcast.215), kind=kOutput, calls=%fused_computation.8 | convolution fusion | flops 8592031744 | bytes 16777216 | tf_op jit(solution)/shard_map/nf,nd->fd/dot_general | solution.py:69
  518.2 13.9 %convert_reduce_fusion = (f32[1024]{0:T(1024)}, bf16[2048,1024]{1,0:T(8,128)(2,1)S(1)}) fusion(bf16[2048,1024]{1,0:T(8,128)(2,1)} %get-tuple-element.116, bf16[2048,2048]{1,0:T(8,128)(2,1)} %bitcast.216, bf16[1024,2048]{1,0:T(8,128)(2,1)} %all-gather.12.cloned.1.call-done), kind=kOutput, calls=%fused_computation.1 | convolution fusion | flops 8600419328 | bytes 20975616 | tf_op jit(solution)/shard_map/nd,fd->nf/dot_general | solution.py:69
  532.1 10.9 %convolution_convert_fusion = bf16[2048,2048]{1,0:T(8,128)(2,1)} fusion(bf16[2048,1024]{1,0:T(8,128)(2,1)S(1)} %get-tuple-element.330.refs_2_, bf16[2048,1024]{1,0:T(8,128)(2,1)S(1)} %copy-done.66), kind=kOutput, calls=%fused_computation.3 | convolution fusion | flops 8594128896 | bytes 16777216 | tf_op jit(solution)/shard_map/nf,df->nd/dot_general | solution.py:69
  543.0 40.8 %shard_map.356 = (f32[256,2048]{1,0:T(8,128)S(1)}, bf16[4,4,128,1024]{3,2,1,0:T(8,128)(2,1)S(1)}) custom-call(bf16[4,2,256,2048]{3,2,1,0:T(8,128)(2,1)} %bitcast.264, bf16[2048,2048]{1,0:T(8,128)(2,1)} %bitcast.209, bf16[2048,1024]{1,0:T(8,128)(2,1)} %copy-done.44), custom_call_target="tpu_custom_call" | custom-call | bytes 15000000 | tf_op jit(solution)/shard_map/pallas_call | solution.py:150
  583.8 2.1 copy-done.10
  586.4 2.6 multiply_reduce_fusion.1
  591.2 2.8 convert_reduce_fusion.2
  594.0 26.9 %shard_map.357 = bf16[4,256,2048]{2,1,0:T(8,128)(2,1)S(1)} custom-call(bf16[256,2048]{1,0:T(8,128)(2,1)S(1)} %get-tuple-element.298.refs_0_), custom_call_target="tpu_custom_call" | custom-call | bytes 15000000 | tf_op jit(solution)/shard_map/pallas_call | solution.py:150
  620.9 2.0 copy-done.7
  622.9 2.4 convolution_convert_fusion.8
  626.5 4.6 convolution_convert_fusion.7
  631.2 41.5 %shard_map.358 = (bf16[2,8,256,128]{3,2,1,0:T(8,128)(2,1)S(1)}, bf16[4,64,2048]{2,1,0:T(8,128)(2,1)S(1)}) custom-call(bf16[8,2,256,128]{3,2,1,0:T(8,128)(2,1)S(1)} %bitcast.230, bf16[4,64,2048]{2,1,0:T(8,128)(2,1)S(1)} %dynamic-slice_bitcast_fusion.refs_1_), custom_call_target="tpu_custom_call" | custom-call | bytes 15000000 | tf_op jit(solution)/shard_map/pallas_call | solution.py:150
  676.4 25.0 %shard_map.359 = (bf16[2,2048,128]{2,1,0:T(8,128)(2,1)S(1)}, bf16[2,2048,128]{2,1,0:T(8,128)(2,1)S(1)}, bf16[2,2048,128]{2,1,0:T(8,128)(2,1)S(1)}) custom-call(bf16[2,2048,128]{2,1,0:T(8,128)(2,1)S(1)} %bitcast.256, bf16[2,2048,128]{2,1,0:T(8,128)(2,1)S(1)} %bitcast.258, bf16[2,2048,128]{2,1,0:T(8,128)(2,1)} %bitcast.259, ...), custom_call_target="tpu_custom_call" | custom-call | flops 5368709120 | bytes 20971520 | tf_op jit(solution)/shard_map/pallas_call | solution.py:1133
  703.5 45.1 %shard_map.360 = (bf16[8,2,256,128]{3,2,1,0:T(8,128)(2,1)S(1)}, bf16[64,8192]{1,0:T(8,128)(2,1)S(1)}) custom-call(bf16[2,8,256,128]{3,2,1,0:T(8,128)(2,1)S(1)} %bitcast.243, bf16[4,2,64,1024]{3,2,1,0:T(8,128)(2,1)S(1)} %bitcast.242), custom_call_target="tpu_custom_call" | custom-call | bytes 15000000 | tf_op jit(solution)/shard_map/pallas_call | solution.py:150
  750.7 4.9 shard_map.361
  757.1 2.5 slice_bitcast_fusion
  761.3 2.4 convolution_convert_fusion.4
  763.7 32.8 %shard_map.362 = (bf16[8,2,256,128]{3,2,1,0:T(8,128)(2,1)S(1)}, f32[256,2048]{1,0:T(8,128)S(1)}) custom-call(bf16[2,8,256,128]{3,2,1,0:T(8,128)(2,1)S(1)} %bitcast.240, bf16[4,256,2048]{2,1,0:T(8,128)(2,1)S(1)} %bitcast.220), custom_call_target="tpu_custom_call" | custom-call | bytes 15000000 | tf_op jit(solution)/shard_map/pallas_call | solution.py:150
  799.3 2.4 convolution_convert_fusion.3
  801.7 42.6 %shard_map.363 = (bf16[8,2,256,128]{3,2,1,0:T(8,128)(2,1)S(1)}, f32[256,2048]{1,0:T(8,128)S(1)}) custom-call(bf16[2,8,256,128]{3,2,1,0:T(8,128)(2,1)S(1)} %bitcast.239, bf16[4,256,2048]{2,1,0:T(8,128)(2,1)S(1)} %bitcast.219), custom_call_target="tpu_custom_call" | custom-call | bytes 15000000 | tf_op jit(solution)/shard_map/pallas_call | solution.py:150
  846.7 4.9 shard_map.364.refs_0_
  851.5 5.1 shard_map.365
  856.7 2.1 copy-done.1
  859.6 3.2 copy.198
  866.1 6.1 fusion.3
  872.2 1.8 reshape.507
  881.5 2.7 convert_element_type.156
  889.2 6.0 convolution_convert_fusion.2
  895.2 2.2 copy-done.11
  898.3 28.1 %shard_map.366 = (bf16[4,64,512]{2,1,0:T(8,128)(2,1)S(1)}, f32[256,2048]{1,0:T(8,128)S(1)}) custom-call(bf16[4,64,512]{2,1,0:T(8,128)(2,1)S(1)} %bitcast.247, bf16[4,256,2048]{2,1,0:T(8,128)(2,1)S(1)} %bitcast.225), custom_call_target="tpu_custom_call" | custom-call | bytes 15000000 | tf_op jit(solution)/shard_map/pallas_call | solution.py:150
  927.8 24.2 %shard_map.367 = (f32[9,256,2048]{2,1,0:T(8,128)}, f32[256,128]{1,0:T(8,128)}, f32[3,2048]{1,0:T(4,128)}, f32[3,2048]{1,0:T(4,128)}) custom-call(bf16[9,256,2048]{2,1,0:T(8,128)(2,1)} %bitcast.263, f32[256,128]{1,0:T(8,128)} %pad.25.m_ref, f32[4,256,2048]{2,1,0:T(8,128)} %get-tuple-element.92.s_ref, f32[3,2048]{1,0:T(4,128)} %slice.128.g_ref, ...), custom_call_target="tpu_custom_call" | custom-call | flops 75497472 | bytes 45088768 | tf_op jit(solution)/shard_map/pallas_call | solution.py:1408
  954.4 22.0 %shard_map.368 = f32[48,128]{1,0:T(8,128)S(1)} custom-call(f32[4,8,48,128]{3,2,1,0:T(8,128)S(1)} %copy.249), custom_call_target="tpu_custom_call" | custom-call | bytes 15000000 | tf_op jit(solution)/shard_map/pallas_call | solution.py:150
  982.8 8.3 shard_map.369
  (279 shorter events, 77.2 us)
Async XLA Ops:
  7.2 453.2 %copy-start = (f32[40,40]{1,0:T(8,128)S(1)}, f32[40,40]{1,0:T(8,128)}, u32[]{:S(2)}) copy-start(f32[40,40]{1,0:T(8,128)} %param.36) | copy-start | bytes 19204
  7.2 107.6 %all-gather.8.cloned.1.call-start = ((), (), s32[]{:S(2)}) async-start(), calls=%async_computation.5 | async-start | bytes 2359296 | tf_op jit(solution)/shard_map/all_gather | solution.py:1495
  7.9 190.5 %all-gather.10.cloned.1.call-start = ((), (), s32[]{:S(2)}) async-start(), calls=%async_computation.11 | async-start | bytes 2359296 | tf_op jit(solution)/shard_map/all_gather | solution.py:1551
  8.0 29.5 %copy-start.63 = (f32[4,9,1,256]{3,2,1,0:T(1,128)S(1)}, f32[4,9,1,256]{3,2,1,0:T(1,128)}, u32[]{:S(2)}) copy-start(f32[4,9,1,256]{3,2,1,0:T(1,128)} %param.22) | copy-start | bytes 110596
  35.8 79.0 %copy-start.46 = (f32[4,8,32,128]{3,1,2,0:T(8,128)}, f32[4,8,32,128]{3,1,2,0:T(8,128)S(1)}, u32[]{:S(2)}) copy-start(f32[4,8,32,128]{3,1,2,0:T(8,128)S(1)} %copy.251) | copy-start | bytes 1572868
  110.1 2.0 copy-start.2
  112.1 2.0 copy-start.12
  114.8 192.1 %all-gather.12.cloned.1.call-start = ((), (), s32[]{:S(2)}) async-start(), calls=%async_computation.12 | async-start | bytes 5242880 | tf_op jit(solution)/shard_map/all_gather | solution.py:1480
  116.2 2.2 copy-start.3
  118.4 2.2 copy-start.13
  120.6 4.2 copy-start.26
  153.4 4.3 copy-start.5
  153.4 4.3 copy-start.28
  153.4 4.3 copy-start.50
  157.7 229.9 %all-gather.14.cloned.1.call-start = ((), (), s32[]{:S(2)}) async-start(), calls=%async_computation.13 | async-start | bytes 5242880 | tf_op jit(solution)/shard_map/all_gather | solution.py:1480
  158.5 3.2 copy-start.25
  195.3 2.1 copy-start.8
  198.4 2.2 copy-start.9
  200.6 1.6 copy-start.17
  205.3 41.2 %copy-start.47 = (f32[4,8,32,128]{3,1,2,0:T(8,128)S(1)}, f32[4,8,32,128]{3,1,2,0:T(8,128)}, u32[]{:S(2)}) copy-start(f32[4,8,32,128]{3,1,2,0:T(8,128)} %copy-done.46) | copy-start | bytes 1572868
  246.3 3.5 copy-start.29
  246.3 428.7 %reduce-scatter.6.cloned.1.call-start = ((), (), s32[]{:S(2)}) async-start(), calls=%async_computation.6 | async-start | bytes 5242880 | tf_op jit(solution)/shard_map/reduce_scatter | solution.py:1620
  267.6 39.1 %copy-start.23 = (bf16[2,2048,128]{2,1,0:T(8,128)(2,1)}, bf16[2,2048,128]{2,1,0:T(8,128)(2,1)S(1)}, u32[]{:S(2)}) copy-start(bf16[2,2048,128]{2,1,0:T(8,128)(2,1)S(1)} %get-tuple-element.107.o_ref) | copy-start | bytes 3145732
  306.9 4.3 copy-start.51
  341.4 115.6 %copy-start.39 = (f32[256,2048]{1,0:T(8,128)}, f32[256,2048]{1,0:T(8,128)S(1)}, u32[]{:S(2)}) copy-start(f32[256,2048]{1,0:T(8,128)S(1)} %get-tuple-element.305) | copy-start | bytes 6291460
  384.2 3.4 copy-start.4
  387.6 19.2 %copy-start.64 = (bf16[1024,2048]{1,0:T(8,128)(2,1)S(1)}, bf16[1024,2048]{1,0:T(8,128)(2,1)}, u32[]{:S(2)}) copy-start(bf16[1024,2048]{1,0:T(8,128)(2,1)} %all-gather.12.cloned.1.call-done) | copy-start | bytes 12582916
  457.5 5.5 copy-start.37
  457.5 2.8 copy-start.54
  460.3 2.7 copy-start.53
  460.5 2.5 copy-start.45
  463.0 1.3 copy-start.41
  503.6 3.3 copy-start.6
  518.1 184.1 %reduce-scatter.8.cloned.1.call-start = ((), (), s32[]{:S(2)}) async-start(), calls=%async_computation.7 | async-start | bytes 5242880 | tf_op jit(solution)/shard_map/reduce_scatter | solution.py:1620
  518.2 13.9 %copy-start.66 = (bf16[2048,1024]{1,0:T(8,128)(2,1)S(1)}, bf16[2048,1024]{1,0:T(8,128)(2,1)}, u32[]{:S(2)}) copy-start(bf16[2048,1024]{1,0:T(8,128)(2,1)} %get-tuple-element.117) | copy-start | bytes 12582916
  532.1 10.9 %copy-start.44 = (bf16[2048,1024]{1,0:T(8,128)(2,1)}, bf16[2048,1024]{1,0:T(8,128)(2,1)S(1)}, u32[]{:S(2)}) copy-start(bf16[2048,1024]{1,0:T(8,128)(2,1)S(1)} %get-tuple-element.330.refs_2_) | copy-start | bytes 12582916
  583.8 2.1 copy-start.10
  585.9 211.8 %reduce-scatter.10.cloned.1.call-start = ((), (), s32[]{:S(2)}) async-start(), calls=%async_computation.8 | async-start | bytes 1310720 | tf_op jit(solution)/shard_map/reduce_scatter | solution.py:1620
  586.3 2.6 copy-start.40
  588.9 1.6 copy-start.38
  588.9 2.2 copy-start.42
  594.0 28.9 %copy-start.65 = (bf16[512,2048]{1,0:T(8,128)(2,1)S(1)}, bf16[512,2048]{1,0:T(8,128)(2,1)}, u32[]{:S(2)}) copy-start(bf16[512,2048]{1,0:T(8,128)(2,1)} %all-gather.8.cloned.1.call-done) | copy-start | bytes 6291460
  620.9 2.0 copy-start.7
  625.2 1.3 copy-start.52
  673.7 1.4 copy-start.30
  675.1 220.1 %reduce-scatter.12.cloned.1.call-start = ((), (), s32[]{:S(2)}) async-start(), calls=%async_computation.9 | async-start | bytes 2359296 | tf_op jit(solution)/shard_map/reduce_scatter | solution.py:1664
  755.5 1.3 copy-start.18
  756.9 224.8 %reduce-scatter.14.cloned.1.call-start = ((), (), s32[]{:S(2)}) async-start(), calls=%async_computation.10 | async-start | bytes 4718592 | tf_op jit(solution)/shard_map/reduce_scatter | solution.py:1664
  761.3 2.4 copy-start.21
  796.4 1.3 copy-start.14
  797.7 1.6 copy-start.48
  844.3 1.3 copy-start.15
  856.6 2.1 copy-start.1
  879.0 5.3 copy-start.49
  886.9 1.4 copy-start.55
  895.2 2.2 copy-start.11
  926.4 1.3 copy-start.16
  927.8 26.0 %copy-start.62 = (f32[1,32,64]{2,1,0:T(8,128)S(1)}, f32[1,32,64]{2,1,0:T(8,128)}, u32[]{:S(2)}) copy-start(f32[1,32,64]{2,1,0:T(8,128)} %concatenate.43) | copy-start | bytes 24580
  927.8 26.0 %copy-start.61 = (f32[1,32,64]{2,1,0:T(8,128)S(1)}, f32[1,32,64]{2,1,0:T(8,128)}, u32[]{:S(2)}) copy-start(f32[1,32,64]{2,1,0:T(8,128)} %concatenate.45) | copy-start | bytes 24580
  927.8 26.0 %copy-start.58 = (f32[1,32,64]{2,1,0:T(8,128)S(1)}, f32[1,32,64]{2,1,0:T(8,128)}, u32[]{:S(2)}) copy-start(f32[1,32,64]{2,1,0:T(8,128)} %concatenate.47) | copy-start | bytes 24580
  927.8 26.1 %copy-start.59 = (f32[1,32,64]{2,1,0:T(8,128)S(1)}, f32[1,32,64]{2,1,0:T(8,128)}, u32[]{:S(2)}) copy-start(f32[1,32,64]{2,1,0:T(8,128)} %concatenate.48) | copy-start | bytes 24580
  927.8 26.1 %copy-start.60 = (f32[1,32,64]{2,1,0:T(8,128)S(1)}, f32[1,32,64]{2,1,0:T(8,128)}, u32[]{:S(2)}) copy-start(f32[1,32,64]{2,1,0:T(8,128)} %concatenate.49) | copy-start | bytes 24580
  927.8 26.3 %copy-start.56 = (f32[32,256]{1,0:T(8,128)S(1)}, f32[32,256]{1,0:T(8,128)}, u32[]{:S(2)}) copy-start(f32[32,256]{1,0:T(8,128)} %reshape.506) | copy-start | bytes 98308
  954.2 26.1 %copy-start.57 = (f32[256,128]{1,0:T(8,128)S(1)}, f32[256,128]{1,0:T(8,128)}, u32[]{:S(2)}) copy-start(f32[256,128]{1,0:T(8,128)} %get-tuple-element.143) | copy-start | bytes 393220
  (12 other events, 13.3 us)
Sparse Core Ops, SparseCore 0:
  10.2 53.7 all-gather.7
  114.9 61.8 all-gather.9
  178.4 124.7 all-gather.11
  304.6 80.3 all-gather.13
  518.3 78.7 reduce-scatter.5
  599.3 94.1 reduce-scatter.7
  696.4 31.5 reduce-scatter.9
  757.0 92.4 reduce-scatter.11
  858.9 92.3 reduce-scatter.13
